TPU v7x, 32 devices: a whole 2x2x4 slice. The times are simulated.
32 devices in a mesh: ia: 8 (over z, core), ka: 4 (over y, x).
Axes of the slice: x: 2, y: 2, z: 4, core: 2. Of those that a mesh axis runs over, the one named last changes fastest.
Arguments:
- amplitudes: float32 [8, 8, 1024, 1024], P('ia', 'ka'), may hold values from -3 to 3
- integrals: bfloat16 [8, 2, 8, 1024, 1024], P('ia', None, 'ka'), may hold values from -0.0625 to 0.0625
- tile_mask: int32 [8, 2, 8, 8, 8], P('ia', None, 'ka'), may hold values from 0 to 1, as said below
- pair_list: int32 [8, 2], replicated, may hold values from 0 to 7, as said below
Outputs:
- residual: float32 [8, 2, 1024, 1024], P('ia', None, 'ka')
Inputs may be any that keep to these rules, and one draw needn't show every extreme that they name: `tile_mask`: 1 marks a filled 128 x 128 tile of an integral block, 0 an empty one. `pair_list`: row i names two different occupied indices, neither equal to i; j stands in row i exactly when i stands in row j.
All inputs are finite; a program needn't handle non-finite values.
Results may differ from a plain program's by a relative error of at most 0.0003.
Values sent between devices are 32-bit elements; how exact they have to be, the bound alone decides.
No kernel may reach another device: no remote copies, remote signals or barrier semaphores. Data moves between devices by JAX's collectives and lax.ppermute only.
A program may use at most 192 MiB of HBM per device.

v0:
```python
import jax
import jax.numpy as jnp
from jax import lax
from jax.sharding import PartitionSpec as P


def expand_mask(tile_mask, tile_side):
    grown = jnp.repeat(jnp.repeat(tile_mask, tile_side, axis=-2), tile_side, axis=-1)
    return grown.astype(jnp.float32)


def mirror_sectioned(amplitudes):
    local_pairs = amplitudes.shape[1]
    virtuals = amplitudes.shape[3]
    across = lax.all_to_all(amplitudes, "ka", split_axis=2, concat_axis=1, tiled=True)
    crossed = lax.all_to_all(across, "ia", split_axis=1, concat_axis=0, tiled=True)
    settled = lax.all_to_all(crossed, "ka", split_axis=0, concat_axis=2, tiled=True)
    return settled.reshape(local_pairs, virtuals, virtuals)


def body(amplitudes, integrals, tile_mask, pair_list):
    mirrored = mirror_sectioned(amplitudes)
    mixed = 2.0 * amplitudes[0] - jnp.swapaxes(mirrored, 1, 2)
    tile_side = integrals.shape[-1] // tile_mask.shape[-1]
    masked = integrals[0].astype(jnp.float32) * expand_mask(tile_mask[0], tile_side)
    partial_value = jnp.einsum("kxy,skyz->sxz", mixed, masked, precision=lax.Precision.HIGHEST)
    own_rows = lax.psum_scatter(partial_value, "ka", scatter_dimension=1, tiled=True)
    columns = lax.all_to_all(own_rows, "ka", split_axis=2, concat_axis=1, tiled=True)
    flipped = jnp.swapaxes(columns, 1, 2)
    spread = lax.all_to_all(flipped, "ia", split_axis=1, concat_axis=0, tiled=True)
    occupied = pair_list.shape[0]
    owners = jnp.arange(occupied, dtype=jnp.int32)
    partner_slot = jnp.where(pair_list[pair_list, 0] == owners[:, None], 0, 1).astype(jnp.int32)
    source_row = pair_list * 2 + partner_slot
    routed = jnp.take(spread, source_row.reshape(-1), axis=0)
    routed = routed.reshape(occupied, 2, spread.shape[1], spread.shape[2])
    delivered = lax.all_to_all(routed, "ia", split_axis=0, concat_axis=2, tiled=True)
    return (own_rows + delivered[0])[None]


def solution(mesh):
    placed = (
        P("ia", "ka", None, None),
        P("ia", None, "ka", None, None),
        P("ia", None, "ka", None, None),
        P(),
    )
    return jax.shard_map(
        body, mesh=mesh, in_specs=placed, out_specs=P("ia", None, "ka", None), check_vma=False
    )
```

profile of v0, /device:TPU:0, one launch (start us, length us, event | category | flops | bytes accessed | tf_op | source)
XLA Modules:
  0.0 730.5 jit_solution(7266431080685342871)
XLA Ops:
  6.5 14.4 %copy.59 = f32[1,2,1024,1024]{3,1,0,2:T(2,128)S(1)} copy(f32[1,2,1024,1024]{3,2,1,0:T(8,128)} %param.4) | data formatting | bytes 16777216 | tf_op args[0]
  20.9 97.8 %all_to_all.96 = f32[1,2,1024,1024]{3,1,0,2:T(2,128)S(1)} all-to-all(f32[1,2,1024,1024]{3,1,0,2:T(2,128)S(1)} %copy.59), channel_id=1, replica_groups=mesh['ia'=8,'ka'=4] {'ka'}, dimensions={2} | all-to-all | bytes 16777216 | tf_op jit(solution)/shard_map/all_to_all | solution.py:15
  118.7 2.7 copy.60
  121.4 1.7 copy.61
  123.0 188.9 %all_to_all.97 = f32[1,8,256,1024]{3,2,0,1:T(8,128)} all-to-all(f32[1,8,256,1024]{3,2,0,1:T(8,128)S(1)} %bitcast.77), channel_id=1, replica_groups=mesh['ia'=8,'ka'=4] {'ia'}, dimensions={1} | all-to-all | bytes 16777216 | tf_op jit(solution)/shard_map/all_to_all | solution.py:16
  312.0 5.7 all-to-all-start.2
  317.7 8.7 %copy.58 = f32[1,2,1024,1024]{2,3,1,0:T(8,128)} copy(f32[1,2,1024,1024]{3,2,1,0:T(8,128)} %param.4) | data formatting | bytes 16777216 | tf_op args[0]
  326.4 0.1 broadcast_in_dim.29
  326.5 6.9 broadcast_in_dim.30
  333.5 18.0 %convert_element_type.25 = f32[2,2,1024,1024]{3,2,1,0:T(8,128)} reshape(f32[2,2,1024,8,128]{4,3,2,1,0:T(8,128)} %broadcast_in_dim.30) | data formatting | bytes 33554432 | tf_op jit(solution)/shard_map/convert_element_type | solution.py:9
  351.4 58.4 %all-to-all-done.2 = f32[8,1,256,1024]{3,2,1,0:T(8,128)} async-done(((f32[8,1,256,1024]{3,2,1,0:T(8,128)}), f32[8,1,256,1024]{3,2,1,0:T(8,128)}, u32[]{:S(2)}, u32[]{:S(2)}) %all-to-all-start.2) | async-done | bytes 8388640 | tf_op jit(solution)/shard_map/all_to_all | solution.py:17
  409.9 8.3 %copy.64 = f32[2,1,4,256,1024]{4,3,2,0,1:T(8,128)} copy(f32[2,1,4,256,1024]{4,3,0,2,1:T(8,128)} %bitcast.11) | data formatting | bytes 16777216 | tf_op jit(solution)/shard_map/all_to_all | solution.py:17
  418.2 62.7 %fusion.5 = f32[2,1024,1024]{1,2,0:T(8,128)} fusion(f32[2,1024,1024]{1,2,0:T(8,128)} %bitcast.80, f32[1,2,1024,1024]{2,3,1,0:T(8,128)} %copy.58, f32[2,2,1024,1024]{3,2,1,0:T(8,128)} %convert_element_type.25, bf16[1,2,2,1024,1024]{4,3,2,1,0:T(8,128)(2,1)} %param.5), kind=kOutput, calls=%fused_computation.9 | convolution fusion | flops 51552190464 | bytes 50331648 | tf_op jit(solution)/shard_map/kxy,skyz->sxz/dot_general | solution.py:26
  480.8 84.8 %reduce-scatter.2.cloned.1.call-done = f32[2,256,1024]{1,2,0:T(8,128)} async-done(((f32[2,1024,1024]{1,2,0:T(8,128)}), f32[2,256,1024]{1,2,0:T(8,128)}) %reduce-scatter.2.cloned.1.call-update) | async-done | bytes 2097168 | tf_op jit(solution)/shard_map/reduce_scatter | solution.py:27
  565.7 3.2 copy.71
  568.9 28.1 %all_to_all.98 = f32[2,256,1024]{1,0,2:T(2,128)S(1)} all-to-all(f32[2,256,1024]{1,0,2:T(2,128)S(1)} %copy.71), channel_id=1, replica_groups=mesh['ia'=8,'ka'=4] {'ka'}, dimensions={2} | all-to-all | bytes 4194304 | tf_op jit(solution)/shard_map/all_to_all | solution.py:28
  597.0 0.2 copy.72
  597.1 1.8 copy.73
  599.0 4.2 copy.74
  603.2 4.6 all-to-all-start.4
  607.8 0.1 reshape.60
  607.9 0.7 gather_fusion
  608.8 48.0 %all-to-all-done.4 = f32[2,256,1024]{2,0,1:T(2,128)S(1)} async-done(((f32[2,256,1024]{2,0,1:T(2,128)}), f32[2,256,1024]{2,0,1:T(2,128)S(1)}, u32[]{:S(2)}, u32[]{:S(2)}) %all-to-all-start.4) | async-done | bytes 2097184 | tf_op jit(solution)/shard_map/all_to_all | solution.py:30
  656.8 0.7 copy.75
  657.5 0.2 copy.76
  657.7 2.0 gather_fusion.1
  659.8 2.0 broadcast_select_fusion
  661.8 51.5 %all_to_all.99 = f32[8,2,32,1024]{3,2,1,0:T(8,128)S(1)} all-to-all(f32[8,2,32,1024]{3,2,1,0:T(8,128)S(1)} %broadcast_select_fusion), channel_id=1, replica_groups=mesh['ia'=8,'ka'=4] {'ia'}, dimensions={0} | all-to-all | bytes 4194304 | tf_op jit(solution)/shard_map/all_to_all | solution.py:37
  713.3 1.5 copy.77
  714.7 2.9 copy.78
  717.6 3.2 add_bitcast_fusion
  720.8 2.9 copy.79
  (16 shorter events, 0.4 us)
Async XLA Ops:
  312.0 97.9 %all-to-all-start.2 = ((f32[8,1,256,1024]{3,2,1,0:T(8,128)}), f32[8,1,256,1024]{3,2,1,0:T(8,128)}, u32[]{:S(2)}, u32[]{:S(2)}) async-start(f32[8,1,256,1024]{3,2,1,0:T(8,128)} %bitcast.75), calls=%async_computation.2 | async-start | bytes 16777216 | tf_op jit(solution)/shard_map/all_to_all | solution.py:17
  317.6 8.8 %copy-start.2 = (s32[1,2,2,8,8]{4,3,2,1,0:T(8,128)S(1)}, s32[1,2,2,8,8]{4,3,2,1,0:T(8,128)}, u32[]{:S(2)}) copy-start(s32[1,2,2,8,8]{4,3,2,1,0:T(8,128)} %param.6) | copy-start | bytes 3076
  317.6 248.0 %reduce-scatter.2.cloned.1.call-start = ((), (), s32[]{:S(2)}) async-start(), calls=%async_computation.7 | async-start | bytes 10485760 | tf_op jit(solution)/shard_map/reduce_scatter | solution.py:27
  597.0 10.8 %copy-start = (s32[8,2]{0,1:T(2,128)S(1)}, s32[8,2]{0,1:T(2,128)}, u32[]{:S(2)}) copy-start(s32[8,2]{0,1:T(2,128)} %param.7) | copy-start | bytes 196
  603.2 53.7 %all-to-all-start.4 = ((f32[2,256,1024]{2,0,1:T(2,128)}), f32[2,256,1024]{2,0,1:T(2,128)S(1)}, u32[]{:S(2)}, u32[]{:S(2)}) async-start(f32[2,256,1024]{2,0,1:T(2,128)} %copy.74), calls=%async_computation.5 | async-start | bytes 4194304 | tf_op jit(solution)/shard_map/all_to_all | solution.py:30
  659.7 57.9 %copy-start.1 = (f32[2,256,1024]{1,2,0:T(8,128)S(1)}, f32[2,256,1024]{1,2,0:T(8,128)}, u32[]{:S(2)}) copy-start(f32[2,256,1024]{1,2,0:T(8,128)} %reduce-scatter.2.cloned.1.call-done) | copy-start | bytes 6291460
Sparse Core Ops, SparseCore 0:
  481.0 84.6 reduce-scatter.1
where the time goes:
time: 732 us; the launch traced here: 730 us
  blocking collectives  366 us (50%)
  waiting for transfers between devices  191 us (26%)
  local copies, waits for them, and re-layouts  81.3 us (11%)
  matrix products  62.7 us (9%)
  between operations  13.5 us (2%)
  starting transfers between devices  10.3 us (1%)
    all_to_all x1, blocking collectives, mirror_sectioned(): lax.all_to_all(across, 'ia', split_axis=1, concat_axis=0, tiled=True)  189 us
    all_to_all x1, blocking collectives, mirror_sectioned(): lax.all_to_all(amplitudes, 'ka', split_axis=2, concat_axis=1, tiled=True)  97.8 us
    reduce_scatter x1, waiting for transfers between devices, body(): lax.psum_scatter(partial_value, 'ka', scatter_dimension=1, tiled=True)  84.8 us
    dot_general x1, matrix products, body(): jnp.einsum('kxy,skyz->sxz', mixed, masked, precision=lax.Precision.HIGHEST)  62.7 us
    all_to_all x1, waiting for transfers between devices, mirror_sectioned(): lax.all_to_all(crossed, 'ka', split_axis=0, concat_axis=2, tiled=True)  58.4 us
    all_to_all x1, blocking collectives, body(): lax.all_to_all(routed, 'ia', split_axis=0, concat_axis=2, tiled=True)  51.5 us
    all_to_all x1, waiting for transfers between devices, body(): lax.all_to_all(flipped, 'ia', split_axis=1, concat_axis=0, tiled=True)  48 us
    all_to_all x1, blocking collectives, body(): lax.all_to_all(own_rows, 'ka', split_axis=2, concat_axis=1, tiled=True)  28.1 us
  transfers between devices with their start and end apart: 3, of which 3 were waited for; matrix products, arithmetic and copies ran while one was open for 5% of the time, Pallas kernels for 0%

commit v1 on v0

v1 whole, which is shorter than its diff:
```python
import functools

import jax
import jax.numpy as jnp
from jax import lax
from jax.experimental import pallas as pl
from jax.experimental.pallas import tpu as pltpu
from jax.sharding import PartitionSpec as P

CHUNKS = 4
VMEM_BYTES = 48 * 1024 * 1024


def flip_kernel(blocks_ref, *chunk_refs):
    flipped = blocks_ref[0, 0].T
    rows = chunk_refs[0].shape[2]
    for chunk, chunk_ref in enumerate(chunk_refs):
        chunk_ref[0, 0] = flipped[chunk * rows : (chunk + 1) * rows]


def flip_chunks(amplitudes, sections, chunks):
    pairs, virtuals = amplitudes.shape[1], amplitudes.shape[3]
    wide = virtuals // sections
    rows = wide // chunks
    piece = jax.ShapeDtypeStruct((sections, pairs, rows, virtuals), jnp.float32)
    return pl.pallas_call(
        flip_kernel,
        grid=(pairs, sections),
        in_specs=[pl.BlockSpec((1, 1, virtuals, wide), lambda d, q: (0, d, 0, q))],
        out_specs=[pl.BlockSpec((1, 1, rows, virtuals), lambda d, q: (q, d, 0, 0))] * chunks,
        out_shape=[piece] * chunks,
        compiler_params=pltpu.CompilerParams(vmem_limit_bytes=VMEM_BYTES),
        cost_estimate=pl.CostEstimate(
            flops=0, bytes_accessed=2 * amplitudes.size * 4, transcendentals=0
        ),
        name="flip",
    )(amplitudes)


def mask_kernel(tiles, mask_ref, integrals_ref, masked_ref):
    side = integrals_ref.shape[-1] // tiles
    slot, pair = pl.program_id(0), pl.program_id(1)
    for r in range(tiles):
        for c in range(tiles):
            keep = mask_ref[slot, pair, r, c] != 0
            spot = (pl.ds(r * side, side), pl.ds(c * side, side))
            tile = integrals_ref[0, 0, 0, spot[0], spot[1]]
            masked_ref[0, 0, spot[0], spot[1]] = jnp.where(keep, tile, jnp.zeros_like(tile))


def mask_blocks(integrals, tile_mask):
    _, slots, pairs, virtuals, _ = integrals.shape
    return pl.pallas_call(
        functools.partial(mask_kernel, tile_mask.shape[-1]),
        grid=(slots, pairs),
        in_specs=[
            pl.BlockSpec(memory_space=pltpu.SMEM),
            pl.BlockSpec((1, 1, 1, virtuals, virtuals), lambda s, k: (0, s, k, 0, 0)),
        ],
        out_specs=pl.BlockSpec((1, 1, virtuals, virtuals), lambda s, k: (s, k, 0, 0)),
        out_shape=jax.ShapeDtypeStruct((slots, pairs, virtuals, virtuals), jnp.bfloat16),
        compiler_params=pltpu.CompilerParams(vmem_limit_bytes=VMEM_BYTES),
        cost_estimate=pl.CostEstimate(
            flops=0, bytes_accessed=2 * integrals.size * 2, transcendentals=0
        ),
        name="mask",
    )(tile_mask[0], integrals)


def product_kernel(own_ref, mirrored_ref, masked_ref, out_ref, split_ref):
    sections, pairs, rows, virtuals = mirrored_ref.shape
    tall = sections * rows

    @pl.when((pl.program_id(0) == 0) & (pl.program_id(1) == 0))
    def _():
        for q in range(sections):
            for k in range(pairs):
                mixed = 2.0 * own_ref[0, k, q, 0] - mirrored_ref[q, k]
                high = mixed.astype(jnp.bfloat16)
                low = (mixed - high.astype(jnp.float32)).astype(jnp.bfloat16)
                split_ref[k, pl.ds(q * rows, rows)] = high
                split_ref[k, pl.ds(tall + q * rows, rows)] = low

    total = None
    for k in range(pairs):
        both = jnp.dot(split_ref[k], masked_ref[0, k], preferred_element_type=jnp.float32)
        both = both[:tall] + both[tall:]
        total = both if total is None else total + both
    out_ref[:, 0] = total.reshape(sections, rows, total.shape[-1])


def product(own, mirrored, masked, chunk):
    sections, pairs, rows, virtuals = mirrored.shape
    slots = masked.shape[0]
    wide = min(virtuals, 512)
    return pl.pallas_call(
        product_kernel,
        grid=(slots, virtuals // wide),
        in_specs=[
            pl.BlockSpec(
                (1, pairs, sections, 1, rows, virtuals), lambda s, n: (0, 0, 0, chunk, 0, 0)
            ),
            pl.BlockSpec((sections, pairs, rows, virtuals), lambda s, n: (0, 0, 0, 0)),
            pl.BlockSpec((1, pairs, virtuals, wide), lambda s, n: (s, 0, 0, n)),
        ],
        out_specs=pl.BlockSpec((sections, 1, rows, wide), lambda s, n: (0, s, 0, n)),
        out_shape=jax.ShapeDtypeStruct((sections, slots, rows, virtuals), jnp.float32),
        scratch_shapes=[pltpu.VMEM((pairs, 2 * sections * rows, virtuals), jnp.bfloat16)],
        compiler_params=pltpu.CompilerParams(vmem_limit_bytes=VMEM_BYTES),
        cost_estimate=pl.CostEstimate(
            flops=4 * sections * rows * pairs * virtuals * virtuals * slots,
            bytes_accessed=masked.size * 2 + 3 * mirrored.size * 4,
            transcendentals=0,
        ),
        name="product",
    )(own, mirrored, masked)


def finish_kernel(chunks, *refs):
    own_refs, delivered_refs = refs[:chunks], refs[chunks : 2 * chunks]
    out_ref, columns_ref = refs[2 * chunks :]
    rows = own_refs[0].shape[1]
    sections = columns_ref.shape[0] // (rows * chunks)
    pieces, _, short, _ = delivered_refs[0].shape
    parts = pieces // sections
    for chunk in range(chunks):
        for q in range(sections):
            for part in range(parts):
                start = (q * chunks + chunk) * rows + part * short
                columns_ref[pl.ds(start, short)] = delivered_refs[chunk][q * parts + part, 0]
    turned = columns_ref[...].T
    for chunk in range(chunks):
        spot = slice(chunk * rows, (chunk + 1) * rows)
        out_ref[0, 0, spot] = own_refs[chunk][0] + turned[spot]


def finish(own, delivered):
    chunks = len(own)
    slots, rows, virtuals = own[0].shape
    pieces, _, short, wide = delivered[0].shape
    return pl.pallas_call(
        functools.partial(finish_kernel, chunks),
        grid=(slots,),
        in_specs=[pl.BlockSpec((1, rows, virtuals), lambda s: (s, 0, 0))] * chunks
        + [pl.BlockSpec((pieces, 1, short, wide), lambda s: (0, s, 0, 0))] * chunks,
        out_specs=pl.BlockSpec((1, 1, wide, virtuals), lambda s: (0, s, 0, 0)),
        out_shape=jax.ShapeDtypeStruct((1, slots, wide, virtuals), jnp.float32),
        scratch_shapes=[pltpu.VMEM((virtuals, wide), jnp.float32)],
        compiler_params=pltpu.CompilerParams(vmem_limit_bytes=VMEM_BYTES),
        name="finish",
    )(*own, *delivered)


def swap(array, axis):
    return lax.all_to_all(array, axis, split_axis=0, concat_axis=0, tiled=True)


def body(sections, amplitudes, integrals, tile_mask, pair_list):
    _, pairs, virtuals, _ = amplitudes.shape
    occupied, slots = pair_list.shape
    wide = virtuals // sections
    chunks = CHUNKS
    rows = wide // chunks
    short = rows // pairs

    owners = jnp.arange(occupied, dtype=jnp.int32)
    partner_slot = jnp.where(pair_list[pair_list, 0] == owners[:, None], 0, 1).astype(jnp.int32)
    source_row = (pair_list * slots + partner_slot).reshape(-1)

    own_view = amplitudes.reshape(1, pairs, sections, chunks, rows, virtuals)
    flipped = flip_chunks(amplitudes, sections, chunks)
    masked = mask_blocks(integrals, tile_mask)

    own, delivered = [], []
    for chunk in range(chunks):
        across = swap(flipped[chunk], "ka").reshape(occupied, rows, virtuals)
        crossed = swap(across, "ia").reshape(sections, pairs, rows, virtuals)
        mirrored = swap(crossed, "ka")
        partial_rows = product(own_view, mirrored, masked, chunk)
        summed = lax.psum_scatter(partial_rows, "ka", scatter_dimension=0, tiled=False)
        own.append(summed)
        cut = summed.reshape(slots, pairs, short, sections, wide).transpose(3, 1, 0, 2, 4)
        columns = swap(cut, "ka").reshape(occupied, slots, short, wide)
        spread = swap(columns, "ia").reshape(occupied * slots, short, wide)
        routed = jnp.take(spread, source_row, axis=0).reshape(occupied, slots, short, wide)
        delivered.append(swap(routed, "ia"))
    return finish(own, delivered)


def solution(mesh):
    placed = (
        P("ia", "ka", None, None),
        P("ia", None, "ka", None, None),
        P("ia", None, "ka", None, None),
        P(),
    )
    return jax.shard_map(
        functools.partial(body, mesh.shape["ka"]),
        mesh=mesh,
        in_specs=placed,
        out_specs=P("ia", None, "ka", None),
        check_vma=False,
    )
```

time: 732 us -> 680 us (0.929)
  local copies, waits for them, and re-layouts: 81.3 us -> 15.4 us
  matrix products: 62.7 us -> 0 us
  Pallas kernels: 0 us -> 55 us
  starting transfers between devices: 10.3 us -> 42.3 us
  blocking collectives: 366 us -> 348 us
  waiting for transfers between devices: 191 us -> 203 us
    reduce_scatter x1 -> x0, waiting for transfers between devices: 84.8 us -> none  [body(): lax.psum_scatter(partial_value, 'ka', scatter_dimension=1, tiled=True)]
    all_to_all x2 -> x11, waiting for transfers between devices: 106 us -> 191 us  [swap(): return lax.all_to_all(array, axis, split_axis=0, concat_axis=0, tiled=True)]
    dot_general x1 -> x0, matrix products: 62.7 us -> none  [body(): jnp.einsum('kxy,skyz->sxz', mixed, masked, precision=lax.Precision.HIGHEST)]
    pallas_call x0 -> x7, Pallas kernels: none -> 55 us  [the longest x4 36.5 us: product(): pl.pallas_call(product_kernel, grid=(slots, virtuals // wide), in_specs=[...]
    all_to_all x2 -> x11, starting transfers between devices: 10.3 us -> 42.2 us  [swap(): return lax.all_to_all(array, axis, split_axis=0, concat_axis=0, tiled=True)]
    unnamed x9 -> x17, local copies, waits for them, and re-layouts: 23.2 us -> 0.11 us
    all_to_all x4 -> x13, blocking collectives: 366 us -> 348 us  [swap(): return lax.all_to_all(array, axis, split_axis=0, concat_axis=0, tiled=True)]
    convert_element_type x1 -> x0, local copies, waits for them, and re-layouts: 18 us -> none  [expand_mask(): return grown.astype(jnp.float32)]
  transfers between devices with their start and end apart: 3 -> 15, of which waited for: 3 -> 11; matrix products, arithmetic and copies ran while one was open for 5% -> 2% of each run, Pallas kernels for 0% -> 7%
where the time goes in v1:
time: 680 us; the launch traced here: 677 us
  blocking collectives  348 us (51%)
  waiting for transfers between devices  203 us (30%)
  Pallas kernels  55 us (8%)
  starting transfers between devices  42.3 us (6%)
  local copies, waits for them, and re-layouts  15.4 us (2%)
  between operations  13.4 us (2%)
    all_to_all x13, blocking collectives, swap(): return lax.all_to_all(array, axis, split_axis=0, concat_axis=0, tiled=True)  348 us
    all_to_all x11, waiting for transfers between devices, swap(): return lax.all_to_all(array, axis, split_axis=0, concat_axis=0, tiled=True)  191 us
    all_to_all x11, starting transfers between devices, swap(): return lax.all_to_all(array, axis, split_axis=0, concat_axis=0, tiled=True)  42.2 us
    pallas_call x4, Pallas kernels, product(): pl.pallas_call(product_kernel, grid=(slots, virtuals // wide), in_specs=[...  36.5 us
  transfers between devices with their start and end apart: 15, of which 11 were waited for; matrix products, arithmetic and copies ran while one was open for 2% of the time, Pallas kernels for 7%

profile of v1, /device:TPU:0, one launch (start us, length us, event | category | flops | bytes accessed | tf_op | source)
XLA Modules:
  0.0 677.4 jit_solution(11426233447346713520)
XLA Ops:
  6.5 8.7 %flip.1 = (f32[4,2,64,1024]{3,2,1,0:T(8,128)S(1)}, f32[4,2,64,1024]{3,2,1,0:T(8,128)S(1)}, f32[4,2,64,1024]{3,2,1,0:T(8,128)}, f32[4,2,64,1024]{3,2,1,0:T(8,128)}) custom-call(f32[1,2,1024,1024]{3,2,1,0:T(8,128)} %blocks_ref.1), custom_call_target="tpu_custom_call" | custom-call | bytes 16777216 | tf_op jit(solution)/shard_map/flip/pallas_call | solution.py:26
  15.2 30.3 %all_to_all.120 = f32[4,2,64,1024]{3,2,1,0:T(8,128)S(1)} all-to-all(f32[4,2,64,1024]{3,2,1,0:T(8,128)S(1)} %get-tuple-element.10), channel_id=1, replica_groups=mesh['ia'=8,'ka'=4] {'ka'}, dimensions={0} | all-to-all | bytes 4194304 | tf_op jit(solution)/shard_map/all_to_all | solution.py:155
  45.5 27.5 %all_to_all.121 = f32[4,2,64,1024]{3,2,1,0:T(8,128)} all-to-all(f32[4,2,64,1024]{3,2,1,0:T(8,128)S(1)} %get-tuple-element.11), channel_id=1, replica_groups=mesh['ia'=8,'ka'=4] {'ka'}, dimensions={0} | all-to-all | bytes 4194304 | tf_op jit(solution)/shard_map/all_to_all | solution.py:155
  73.0 26.1 %all_to_all.122 = f32[4,2,64,1024]{3,2,1,0:T(8,128)} all-to-all(f32[4,2,64,1024]{3,2,1,0:T(8,128)S(1)} %copy-done.7), channel_id=1, replica_groups=mesh['ia'=8,'ka'=4] {'ka'}, dimensions={0} | all-to-all | bytes 4194304 | tf_op jit(solution)/shard_map/all_to_all | solution.py:155
  99.1 24.6 %all_to_all.123 = f32[4,2,64,1024]{3,2,1,0:T(8,128)} all-to-all(f32[4,2,64,1024]{3,2,1,0:T(8,128)S(1)} %copy-done.6), channel_id=1, replica_groups=mesh['ia'=8,'ka'=4] {'ka'}, dimensions={0} | all-to-all | bytes 4194304 | tf_op jit(solution)/shard_map/all_to_all | solution.py:155
  123.7 53.7 %all_to_all.124 = f32[8,64,1024]{2,1,0:T(8,128)S(1)} all-to-all(f32[8,64,1024]{2,1,0:T(8,128)S(1)} %bitcast.51), channel_id=1, replica_groups=mesh['ia'=8,'ka'=4] {'ia'}, dimensions={0} | all-to-all | bytes 4194304 | tf_op jit(solution)/shard_map/all_to_all | solution.py:155
  177.4 27.7 %all_to_all.125.mirrored_ref = f32[4,2,64,1024]{3,2,1,0:T(8,128)S(1)} all-to-all(f32[4,2,64,1024]{3,2,1,0:T(8,128)S(1)} %bitcast.52), channel_id=1, replica_groups=mesh['ia'=8,'ka'=4] {'ka'}, dimensions={0} | all-to-all | bytes 4194304 | tf_op jit(solution)/shard_map/all_to_all | solution.py:155
  205.2 4.5 all-to-all-start.4
  209.7 7.9 %mask.1.masked_ref = bf16[2,2,1024,1024]{3,2,1,0:T(8,128)(2,1)} custom-call(s32[2,2,8,8]{3,2,1,0:T(8,128)S(1)} %bitcast.43, bf16[1,2,2,1024,1024]{4,3,2,1,0:T(8,128)(2,1)} %integrals_ref.1), custom_call_target="tpu_custom_call" | custom-call | bytes 16777216 | tf_op jit(solution)/shard_map/mask/pallas_call | solution.py:53
  217.7 9.1 %product.4 = f32[4,2,64,1024]{3,2,1,0:T(8,128)} custom-call(f32[1,2,4,4,64,1024]{5,4,3,2,1,0:T(8,128)} %bitcast.44, f32[4,2,64,1024]{3,2,1,0:T(8,128)S(1)} %all_to_all.125.mirrored_ref, bf16[2,2,1024,1024]{3,2,1,0:T(8,128)(2,1)} %mask.1.masked_ref), custom_call_target="tpu_custom_call" | custom-call | flops 4294967296 | bytes 14680064 | tf_op jit(solution)/shard_map/product/pallas_call | solution.py:96
  226.8 31.9 %all-to-all-done.4 = f32[8,64,1024]{2,1,0:T(8,128)} async-done(((f32[8,64,1024]{2,1,0:T(8,128)}), f32[8,64,1024]{2,1,0:T(8,128)}, u32[]{:S(2)}, u32[]{:S(2)}) %all-to-all-start.4) | async-done | bytes 2097184 | tf_op jit(solution)/shard_map/all_to_all | solution.py:155
  258.8 29.0 %all_to_all.126.mirrored_ref = f32[4,2,64,1024]{3,2,1,0:T(8,128)S(1)} all-to-all(f32[4,2,64,1024]{3,2,1,0:T(8,128)} %bitcast.7), channel_id=1, replica_groups=mesh['ia'=8,'ka'=4] {'ka'}, dimensions={0} | all-to-all | bytes 4194304 | tf_op jit(solution)/shard_map/all_to_all | solution.py:155
  287.8 4.4 all-to-all-start.7
  292.2 9.1 %product.5 = f32[4,2,64,1024]{3,2,1,0:T(8,128)} custom-call(f32[1,2,4,4,64,1024]{5,4,3,2,1,0:T(8,128)} %bitcast.45, f32[4,2,64,1024]{3,2,1,0:T(8,128)S(1)} %all_to_all.126.mirrored_ref, bf16[2,2,1024,1024]{3,2,1,0:T(8,128)(2,1)} %mask.1.masked_ref), custom_call_target="tpu_custom_call" | custom-call | flops 4294967296 | bytes 14680064 | tf_op jit(solution)/shard_map/product/pallas_call | solution.py:96
  301.4 39.8 %all-to-all-done.7 = f32[8,64,1024]{2,1,0:T(8,128)} async-done(((f32[8,64,1024]{2,1,0:T(8,128)}), f32[8,64,1024]{2,1,0:T(8,128)}, u32[]{:S(2)}, u32[]{:S(2)}) %all-to-all-start.7) | async-done | bytes 2097184 | tf_op jit(solution)/shard_map/all_to_all | solution.py:155
  341.2 29.0 %all_to_all.127.mirrored_ref = f32[4,2,64,1024]{3,2,1,0:T(8,128)S(1)} all-to-all(f32[4,2,64,1024]{3,2,1,0:T(8,128)} %bitcast.10), channel_id=1, replica_groups=mesh['ia'=8,'ka'=4] {'ka'}, dimensions={0} | all-to-all | bytes 4194304 | tf_op jit(solution)/shard_map/all_to_all | solution.py:155
  374.7 9.1 %product.6 = f32[4,2,64,1024]{3,2,1,0:T(8,128)} custom-call(f32[1,2,4,4,64,1024]{5,4,3,2,1,0:T(8,128)} %bitcast.46, f32[4,2,64,1024]{3,2,1,0:T(8,128)S(1)} %all_to_all.127.mirrored_ref, bf16[2,2,1024,1024]{3,2,1,0:T(8,128)(2,1)} %mask.1.masked_ref), custom_call_target="tpu_custom_call" | custom-call | flops 4294967296 | bytes 14680064 | tf_op jit(solution)/shard_map/product/pallas_call | solution.py:96
  383.9 39.8 %all-to-all-done.10 = f32[8,64,1024]{2,1,0:T(8,128)} async-done(((f32[8,64,1024]{2,1,0:T(8,128)}), f32[8,64,1024]{2,1,0:T(8,128)}, u32[]{:S(2)}, u32[]{:S(2)}) %all-to-all-start.10) | async-done | bytes 2097184 | tf_op jit(solution)/shard_map/all_to_all | solution.py:155
  423.7 29.0 %all_to_all.128.mirrored_ref = f32[4,2,64,1024]{3,2,1,0:T(8,128)S(1)} all-to-all(f32[4,2,64,1024]{3,2,1,0:T(8,128)} %bitcast.13), channel_id=1, replica_groups=mesh['ia'=8,'ka'=4] {'ka'}, dimensions={0} | all-to-all | bytes 4194304 | tf_op jit(solution)/shard_map/all_to_all | solution.py:155
  452.7 9.2 %product.7 = f32[4,2,64,1024]{3,2,1,0:T(8,128)} custom-call(f32[1,2,4,4,64,1024]{5,4,3,2,1,0:T(8,128)} %bitcast.47, f32[4,2,64,1024]{3,2,1,0:T(8,128)S(1)} %all_to_all.128.mirrored_ref, bf16[2,2,1024,1024]{3,2,1,0:T(8,128)(2,1)} %mask.1.masked_ref), custom_call_target="tpu_custom_call" | custom-call | flops 4294967296 | bytes 14680064 | tf_op jit(solution)/shard_map/product/pallas_call | solution.py:96
  469.8 11.8 %all-to-all-done.12 = f32[4,2,2,32,256]{4,3,1,2,0:T(8,128)S(1)} async-done(((f32[4,2,2,32,256]{4,3,1,2,0:T(8,128)}), f32[4,2,2,32,256]{4,3,1,2,0:T(8,128)S(1)}, u32[]{:S(2)}, u32[]{:S(2)}) %all-to-all-start.12) | async-done | bytes 524320 | tf_op jit(solution)/shard_map/all_to_all | solution.py:155
  495.1 11.5 %reduce-scatter.19.cloned.1.call-done = f32[1,2,64,1024]{3,2,1,0:T(8,128)} async-done(((f32[4,2,64,1024]{3,2,1,0:T(8,128)}), f32[1,2,64,1024]{3,2,1,0:T(8,128)}) %reduce-scatter.19.cloned.1.call-update) | async-done | bytes 524304
  513.1 7.6 %all-to-all-done.21 = f32[4,2,2,32,256]{4,3,1,2,0:T(8,128)S(1)} async-done(((f32[4,2,2,32,256]{4,3,1,2,0:T(8,128)}), f32[4,2,2,32,256]{4,3,1,2,0:T(8,128)S(1)}, u32[]{:S(2)}, u32[]{:S(2)}) %all-to-all-start.21) | async-done | bytes 524320 | tf_op jit(solution)/shard_map/all_to_all | solution.py:155
  520.7 4.6 all-to-all-start.13
  526.1 14.5 %all-to-all-done.13 = f32[8,2,32,256]{3,2,1,0:T(8,128)S(1)} async-done(((f32[8,2,32,256]{3,2,1,0:T(8,128)}), f32[8,2,32,256]{3,2,1,0:T(8,128)S(1)}, u32[]{:S(2)}, u32[]{:S(2)}) %all-to-all-start.13) | async-done | bytes 524320 | tf_op jit(solution)/shard_map/all_to_all | solution.py:155
  545.0 14.4 %all-to-all-done.16 = f32[8,2,32,256]{3,2,1,0:T(8,128)S(1)} async-done(((f32[8,2,32,256]{3,2,1,0:T(8,128)}), f32[8,2,32,256]{3,2,1,0:T(8,128)S(1)}, u32[]{:S(2)}, u32[]{:S(2)}) %all-to-all-start.16) | async-done | bytes 524320 | tf_op jit(solution)/shard_map/all_to_all | solution.py:155
  563.8 14.3 %all-to-all-done.19 = f32[8,2,32,256]{3,2,1,0:T(8,128)S(1)} async-done(((f32[8,2,32,256]{3,2,1,0:T(8,128)}), f32[8,2,32,256]{3,2,1,0:T(8,128)S(1)}, u32[]{:S(2)}, u32[]{:S(2)}) %all-to-all-start.19) | async-done | bytes 524320 | tf_op jit(solution)/shard_map/all_to_all | solution.py:155
  584.4 12.5 %all-to-all-done.22 = f32[8,2,32,256]{3,2,1,0:T(8,128)S(1)} async-done(((f32[8,2,32,256]{3,2,1,0:T(8,128)}), f32[8,2,32,256]{3,2,1,0:T(8,128)S(1)}, u32[]{:S(2)}, u32[]{:S(2)}) %all-to-all-start.22) | async-done | bytes 524320 | tf_op jit(solution)/shard_map/all_to_all | solution.py:155
  597.8 17.9 %all_to_all.129.refs_4_ = f32[8,2,32,256]{3,2,1,0:T(8,128)S(1)} all-to-all(f32[8,2,32,256]{3,2,1,0:T(8,128)S(1)} %bitcast.56), channel_id=1, replica_groups=mesh['ia'=8,'ka'=4] {'ia'}, dimensions={0} | all-to-all | bytes 1048576 | tf_op jit(solution)/shard_map/all_to_all | solution.py:155
  615.7 17.8 %all_to_all.130.refs_5_ = f32[8,2,32,256]{3,2,1,0:T(8,128)S(1)} all-to-all(f32[8,2,32,256]{3,2,1,0:T(8,128)S(1)} %bitcast.55), channel_id=1, replica_groups=mesh['ia'=8,'ka'=4] {'ia'}, dimensions={0} | all-to-all | bytes 1048576 | tf_op jit(solution)/shard_map/all_to_all | solution.py:155
  633.5 17.8 %all_to_all.131.refs_6_ = f32[8,2,32,256]{3,2,1,0:T(8,128)S(1)} all-to-all(f32[8,2,32,256]{3,2,1,0:T(8,128)S(1)} %bitcast.54), channel_id=1, replica_groups=mesh['ia'=8,'ka'=4] {'ia'}, dimensions={0} | all-to-all | bytes 1048576 | tf_op jit(solution)/shard_map/all_to_all | solution.py:155
  651.3 17.8 %all_to_all.132.refs_7_ = f32[8,2,32,256]{3,2,1,0:T(8,128)S(1)} all-to-all(f32[8,2,32,256]{3,2,1,0:T(8,128)S(1)} %bitcast.53), channel_id=1, replica_groups=mesh['ia'=8,'ka'=4] {'ia'}, dimensions={0} | all-to-all | bytes 1048576 | tf_op jit(solution)/shard_map/all_to_all | solution.py:155
  (65 shorter events, 50.9 us)
Async XLA Ops:
  45.5 27.5 %copy-start.7 = (f32[4,2,64,1024]{3,2,1,0:T(8,128)S(1)}, f32[4,2,64,1024]{3,2,1,0:T(8,128)}, u32[]{:S(2)}) copy-start(f32[4,2,64,1024]{3,2,1,0:T(8,128)} %get-tuple-element.12) | copy-start | bytes 6291460
  73.0 26.1 %copy-start.6 = (f32[4,2,64,1024]{3,2,1,0:T(8,128)S(1)}, f32[4,2,64,1024]{3,2,1,0:T(8,128)}, u32[]{:S(2)}) copy-start(f32[4,2,64,1024]{3,2,1,0:T(8,128)} %get-tuple-element.13) | copy-start | bytes 6291460
  205.2 4.6 copy-start.4
  205.2 53.6 %all-to-all-start.4 = ((f32[8,64,1024]{2,1,0:T(8,128)}), f32[8,64,1024]{2,1,0:T(8,128)}, u32[]{:S(2)}, u32[]{:S(2)}) async-start(f32[8,64,1024]{2,1,0:T(8,128)} %bitcast.50), calls=%async_computation.4 | async-start | bytes 4194304 | tf_op jit(solution)/shard_map/all_to_all | solution.py:155
  209.7 252.2 %reduce-scatter.13.cloned.1.call-start = ((), (), s32[]{:S(2)}) async-start(), calls=%async_computation.28 | async-start | bytes 2621440
  287.8 53.4 %all-to-all-start.7 = ((f32[8,64,1024]{2,1,0:T(8,128)}), f32[8,64,1024]{2,1,0:T(8,128)}, u32[]{:S(2)}, u32[]{:S(2)}) async-start(f32[8,64,1024]{2,1,0:T(8,128)} %bitcast.49), calls=%async_computation.7 | async-start | bytes 4194304 | tf_op jit(solution)/shard_map/all_to_all | solution.py:155
  292.2 175.5 %reduce-scatter.15.cloned.1.call-start = ((), (), s32[]{:S(2)}) async-start(), calls=%async_computation.29 | async-start | bytes 2621440
  370.3 53.4 %all-to-all-start.10 = ((f32[8,64,1024]{2,1,0:T(8,128)}), f32[8,64,1024]{2,1,0:T(8,128)}, u32[]{:S(2)}, u32[]{:S(2)}) async-start(f32[8,64,1024]{2,1,0:T(8,128)} %bitcast.48), calls=%async_computation.10 | async-start | bytes 4194304 | tf_op jit(solution)/shard_map/all_to_all | solution.py:155
  374.6 110.5 %reduce-scatter.17.cloned.1.call-start = ((), (), s32[]{:S(2)}) async-start(), calls=%async_computation.30 | async-start | bytes 2621440
  383.8 122.8 %reduce-scatter.19.cloned.1.call-start = ((), (), s32[]{:S(2)}) async-start(), calls=%async_computation.31 | async-start | bytes 2621440
  464.1 17.5 %all-to-all-start.12 = ((f32[4,2,2,32,256]{4,3,1,2,0:T(8,128)}), f32[4,2,2,32,256]{4,3,1,2,0:T(8,128)S(1)}, u32[]{:S(2)}, u32[]{:S(2)}) async-start(f32[4,2,2,32,256]{4,3,1,2,0:T(8,128)} %copy.33), calls=%async_computation.12 | async-start | bytes 1048576 | tf_op jit(solution)/shard_map/all_to_all | solution.py:155
  481.6 10.0 %all-to-all-start.15 = ((f32[4,2,2,32,256]{4,3,1,2,0:T(8,128)}), f32[4,2,2,32,256]{4,3,1,2,0:T(8,128)S(1)}, u32[]{:S(2)}, u32[]{:S(2)}) async-start(f32[4,2,2,32,256]{4,3,1,2,0:T(8,128)} %copy.35), calls=%async_computation.15 | async-start | bytes 1048576 | tf_op jit(solution)/shard_map/all_to_all | solution.py:155
  491.6 17.1 %all-to-all-start.18 = ((f32[4,2,2,32,256]{4,3,1,2,0:T(8,128)}), f32[4,2,2,32,256]{4,3,1,2,0:T(8,128)S(1)}, u32[]{:S(2)}, u32[]{:S(2)}) async-start(f32[4,2,2,32,256]{4,3,1,2,0:T(8,128)} %copy.37), calls=%async_computation.18 | async-start | bytes 1048576 | tf_op jit(solution)/shard_map/all_to_all | solution.py:155
  508.8 11.9 %all-to-all-start.21 = ((f32[4,2,2,32,256]{4,3,1,2,0:T(8,128)}), f32[4,2,2,32,256]{4,3,1,2,0:T(8,128)S(1)}, u32[]{:S(2)}, u32[]{:S(2)}) async-start(f32[4,2,2,32,256]{4,3,1,2,0:T(8,128)} %copy.39), calls=%async_computation.21 | async-start | bytes 1048576 | tf_op jit(solution)/shard_map/all_to_all | solution.py:155
  520.7 19.9 %all-to-all-start.13 = ((f32[8,2,32,256]{3,2,1,0:T(8,128)}), f32[8,2,32,256]{3,2,1,0:T(8,128)S(1)}, u32[]{:S(2)}, u32[]{:S(2)}) async-start(f32[8,2,32,256]{3,2,1,0:T(8,128)} %bitcast.16), calls=%async_computation.13 | async-start | bytes 1048576 | tf_op jit(solution)/shard_map/all_to_all | solution.py:155
  525.3 37.6 %copy-start.5 = (s32[8,2]{0,1:T(2,128)S(1)}, s32[8,2]{0,1:T(2,128)}, u32[]{:S(2)}) copy-start(s32[8,2]{0,1:T(2,128)} %param.9) | copy-start | bytes 196
  540.6 18.8 %all-to-all-start.16 = ((f32[8,2,32,256]{3,2,1,0:T(8,128)}), f32[8,2,32,256]{3,2,1,0:T(8,128)S(1)}, u32[]{:S(2)}, u32[]{:S(2)}) async-start(f32[8,2,32,256]{3,2,1,0:T(8,128)} %bitcast.20), calls=%async_computation.16 | async-start | bytes 1048576 | tf_op jit(solution)/shard_map/all_to_all | solution.py:155
  559.4 18.8 %all-to-all-start.19 = ((f32[8,2,32,256]{3,2,1,0:T(8,128)}), f32[8,2,32,256]{3,2,1,0:T(8,128)S(1)}, u32[]{:S(2)}, u32[]{:S(2)}) async-start(f32[8,2,32,256]{3,2,1,0:T(8,128)} %bitcast.24), calls=%async_computation.19 | async-start | bytes 1048576 | tf_op jit(solution)/shard_map/all_to_all | solution.py:155
  578.2 18.8 %all-to-all-start.22 = ((f32[8,2,32,256]{3,2,1,0:T(8,128)}), f32[8,2,32,256]{3,2,1,0:T(8,128)S(1)}, u32[]{:S(2)}, u32[]{:S(2)}) async-start(f32[8,2,32,256]{3,2,1,0:T(8,128)} %bitcast.28), calls=%async_computation.22 | async-start | bytes 1048576 | tf_op jit(solution)/shard_map/all_to_all | solution.py:155
  597.8 71.2 %copy-start = (f32[1,2,64,1024]{3,2,1,0:T(8,128)S(1)}, f32[1,2,64,1024]{3,2,1,0:T(8,128)}, u32[]{:S(2)}) copy-start(f32[1,2,64,1024]{3,2,1,0:T(8,128)} %reduce-scatter.13.cloned.1.call-done) | copy-start | bytes 1572868
  597.8 71.2 %copy-start.1 = (f32[1,2,64,1024]{3,2,1,0:T(8,128)S(1)}, f32[1,2,64,1024]{3,2,1,0:T(8,128)}, u32[]{:S(2)}) copy-start(f32[1,2,64,1024]{3,2,1,0:T(8,128)} %reduce-scatter.15.cloned.1.call-done) | copy-start | bytes 1572868
  597.8 71.2 %copy-start.2 = (f32[1,2,64,1024]{3,2,1,0:T(8,128)S(1)}, f32[1,2,64,1024]{3,2,1,0:T(8,128)}, u32[]{:S(2)}) copy-start(f32[1,2,64,1024]{3,2,1,0:T(8,128)} %reduce-scatter.17.cloned.1.call-done) | copy-start | bytes 1572868
  597.8 71.2 %copy-start.3 = (f32[1,2,64,1024]{3,2,1,0:T(8,128)S(1)}, f32[1,2,64,1024]{3,2,1,0:T(8,128)}, u32[]{:S(2)}) copy-start(f32[1,2,64,1024]{3,2,1,0:T(8,128)} %reduce-scatter.19.cloned.1.call-done) | copy-start | bytes 1572868
Sparse Core Ops, SparseCore 0:
  226.9 34.9 reduce-scatter.12
  301.5 34.9 reduce-scatter.14
  384.0 34.9 reduce-scatter.16
  462.0 44.5 reduce-scatter.18

commit v2 on v0

v2 whole, which is shorter than its diff:
```python
import functools

import jax
import jax.numpy as jnp
from jax import lax
from jax.experimental import pallas as pl
from jax.experimental.pallas import tpu as pltpu
from jax.sharding import PartitionSpec as P

ROUNDS = 4
VMEM_BYTES = 48 * 1024 * 1024


def call(kernel, name, scalars, operands, in_specs, out_specs, out_shape, grid, scratch=(), flops=0):
    moved = sum(x.size * x.dtype.itemsize for x in jax.tree.leaves(out_shape)) * 2
    return pl.pallas_call(
        kernel,
        grid_spec=pltpu.PrefetchScalarGridSpec(
            num_scalar_prefetch=1,
            grid=grid,
            in_specs=in_specs,
            out_specs=out_specs,
            scratch_shapes=list(scratch),
        ),
        out_shape=out_shape,
        compiler_params=pltpu.CompilerParams(vmem_limit_bytes=VMEM_BYTES),
        cost_estimate=pl.CostEstimate(flops=flops, bytes_accessed=moved, transcendentals=0),
        name=name,
    )(scalars, *operands)


def flip_kernel(pairs, place_ref, *refs):
    blocks, pieces = refs[:pairs], refs[pairs:]
    rounds = len(pieces) // pairs
    for e in range(pairs):
        flipped = blocks[e][0, 0].T
        rows = flipped.shape[0] // rounds
        for r in range(rounds):
            pieces[r * pairs + e][...] = flipped[r * rows : (r + 1) * rows]


def flip(place, amplitudes, section, sections, rounds):
    pairs, virtuals = amplitudes.shape[1], amplitudes.shape[3]
    wide = virtuals // sections
    rows = wide // rounds
    out = call(
        functools.partial(flip_kernel, pairs),
        "flip",
        place,
        [amplitudes] * pairs,
        [
            pl.BlockSpec((1, 1, virtuals, wide), lambda n, at, e=e: (0, at[1] ^ e, 0, section))
            for e in range(pairs)
        ],
        [pl.BlockSpec((rows, virtuals), lambda n, at: (0, 0))] * (rounds * pairs),
        [jax.ShapeDtypeStruct((rows, virtuals), jnp.float32)] * (rounds * pairs),
        (1,),
    )
    return [out[r * pairs : (r + 1) * pairs] for r in range(rounds)]


def mask_kernel(tiles, mask_ref, integrals_ref, masked_ref):
    side = integrals_ref.shape[-1] // tiles
    slot, pair = pl.program_id(0), pl.program_id(1)
    for r in range(tiles):
        for c in range(tiles):
            keep = mask_ref[slot, pair, r, c] != 0
            spot = (pl.ds(r * side, side), pl.ds(c * side, side))
            tile = integrals_ref[0, 0, 0, spot[0], spot[1]]
            masked_ref[0, 0, spot[0], spot[1]] = jnp.where(keep, tile, jnp.zeros_like(tile))


def mask_blocks(integrals, tile_mask):
    _, slots, pairs, virtuals, _ = integrals.shape
    out_shape = jax.ShapeDtypeStruct((slots, pairs, virtuals, virtuals), jnp.bfloat16)
    return call(
        functools.partial(mask_kernel, tile_mask.shape[-1]),
        "mask",
        tile_mask[0],
        [integrals],
        [pl.BlockSpec((1, 1, 1, virtuals, virtuals), lambda s, k, mask: (0, s, k, 0, 0))],
        pl.BlockSpec((1, 1, virtuals, virtuals), lambda s, k, mask: (s, k, 0, 0)),
        out_shape,
        (slots, pairs),
    )


def product_kernel(sections, pairs, place_ref, *refs):
    own_refs, refs = refs[:pairs], refs[pairs:]
    mirrored_refs, refs = refs[: sections * pairs], refs[sections * pairs :]
    masked_refs, refs = refs[:pairs], refs[pairs:]
    out_refs, split_ref = refs[:sections], refs[sections]
    rows = mirrored_refs[0].shape[0]
    tall = sections * rows
    here = place_ref[2]

    @pl.when((pl.program_id(0) == 0) & (pl.program_id(1) == 0))
    def _():
        for g in range(sections):
            start = pl.multiple_of((here ^ g) * rows, rows)
            for e in range(pairs):
                mixed = 2.0 * own_refs[e][0, 0, g, 0] - mirrored_refs[g * pairs + e][...]
                high = mixed.astype(jnp.bfloat16)
                low = (mixed - high.astype(jnp.float32)).astype(jnp.bfloat16)
                split_ref[e, pl.ds(start, rows)] = high
                split_ref[e, pl.ds(tall + start, rows)] = low

    total = None
    for e in range(pairs):
        both = jnp.dot(split_ref[e], masked_refs[e][0, 0], preferred_element_type=jnp.float32)
        both = both[:tall] + both[tall:]
        total = both if total is None else total + both
    for d in range(sections):
        out_refs[d][0] = total[d * rows : (d + 1) * rows]


def product(place, own, mirrored, masked, turn):
    sections, pairs = len(mirrored), len(mirrored[0])
    rows, virtuals = mirrored[0][0].shape
    slots = masked.shape[0]
    wide = min(virtuals, 512)
    flat = [piece for section in mirrored for piece in section]
    return call(
        functools.partial(product_kernel, sections, pairs),
        "product",
        place,
        [own] * pairs + flat + [masked] * pairs,
        [
            pl.BlockSpec(
                (1, 1, sections, 1, rows, virtuals),
                lambda s, n, at, e=e: (0, at[1] ^ e, 0, turn, 0, 0),
            )
            for e in range(pairs)
        ]
        + [pl.BlockSpec((rows, virtuals), lambda s, n, at: (0, 0))] * len(flat)
        + [
            pl.BlockSpec((1, 1, virtuals, wide), lambda s, n, at, e=e: (s, at[1] ^ e, 0, n))
            for e in range(pairs)
        ],
        [pl.BlockSpec((1, rows, wide), lambda s, n, at: (s, 0, n))] * sections,
        [jax.ShapeDtypeStruct((slots, rows, virtuals), jnp.float32)] * sections,
        (slots, virtuals // wide),
        scratch=[pltpu.VMEM((pairs, 2 * sections * rows, virtuals), jnp.bfloat16)],
        flops=4 * sections * rows * pairs * virtuals * virtuals * slots,
    )


def total_kernel(sections, place_ref, *refs):
    part_refs, total_ref, cut_refs = refs[:sections], refs[sections], refs[sections + 1 :]
    total_ref[...] = sum((part[...] for part in part_refs[1:]), part_refs[0][...])
    wide = cut_refs[0].shape[-1]
    for d in range(sections):
        start = pl.multiple_of((place_ref[2] ^ d) * wide, wide)
        cut_refs[d][...] = total_ref[:, :, pl.ds(start, wide)]


def total(place, parts):
    sections = len(parts)
    slots, rows, virtuals = parts[0].shape
    wide = virtuals // sections
    full = pl.BlockSpec((slots, rows, virtuals), lambda n, at: (0, 0, 0))
    out = call(
        functools.partial(total_kernel, sections),
        "total",
        place,
        parts,
        [full] * sections,
        [full] + [pl.BlockSpec((slots, rows, wide), lambda n, at: (0, 0, 0))] * sections,
        [jax.ShapeDtypeStruct((slots, rows, virtuals), jnp.float32)]
        + [jax.ShapeDtypeStruct((slots, rows, wide), jnp.float32)] * sections,
        (1,),
    )
    return out[0], out[1:]


def finish_kernel(rounds, place_ref, *refs):
    own_refs, delivered_refs = refs[:rounds], refs[rounds : 2 * rounds]
    out_ref, columns_ref = refs[2 * rounds :]
    rows = own_refs[0].shape[1]
    sections = columns_ref.shape[0] // (rows * rounds)
    pieces, _, short, _ = delivered_refs[0].shape
    parts = pieces // sections
    for r in range(rounds):
        for d in range(sections):
            base = pl.multiple_of(((place_ref[2] ^ d) * rounds + r) * rows, rows)
            for part in range(parts):
                columns_ref[pl.ds(base + part * short, short)] = delivered_refs[r][d * parts + part, 0]
    turned = columns_ref[...].T
    for r in range(rounds):
        spot = slice(r * rows, (r + 1) * rows)
        out_ref[0, 0, spot] = own_refs[r][0] + turned[spot]


def finish(place, own, delivered):
    rounds = len(own)
    slots, rows, virtuals = own[0].shape
    pieces, _, short, wide = delivered[0].shape
    return call(
        functools.partial(finish_kernel, rounds),
        "finish",
        place,
        list(own) + list(delivered),
        [pl.BlockSpec((1, rows, virtuals), lambda s, at: (s, 0, 0))] * rounds
        + [pl.BlockSpec((pieces, 1, short, wide), lambda s, at: (0, s, 0, 0))] * rounds,
        pl.BlockSpec((1, 1, wide, virtuals), lambda s, at: (0, s, 0, 0)),
        jax.ShapeDtypeStruct((1, slots, wide, virtuals), jnp.float32),
        (slots,),
        scratch=[pltpu.VMEM((virtuals, wide), jnp.float32)],
    )


def swap(array, axis):
    return lax.all_to_all(array, axis, split_axis=0, concat_axis=0, tiled=True)


def route(array, sections, pairs, move):
    moves = []
    for plane in range(sections):
        for core in range(pairs):
            for line in range(sections):
                to_plane, to_core, to_line = move(plane, core, line)
                source = (plane * pairs + core) * sections + line
                moves.append((source, (to_plane * pairs + to_core) * sections + to_line))
    return lax.ppermute(array, ("ia", "ka"), moves)


def body(sections, amplitudes, integrals, tile_mask, pair_list):
    _, pairs, virtuals, _ = amplitudes.shape
    occupied, slots = pair_list.shape
    wide = virtuals // sections
    rounds = ROUNDS
    rows = wide // rounds
    short = rows // pairs
    here, there = lax.axis_index("ka"), lax.axis_index("ia")
    place = jnp.stack([there // pairs, there % pairs, here]).astype(jnp.int32)

    owners = jnp.arange(occupied, dtype=jnp.int32)
    partner_slot = jnp.where(pair_list[pair_list, 0] == owners[:, None], 0, 1).astype(jnp.int32)
    source_row = (pair_list * slots + partner_slot).reshape(-1)

    own_view = amplitudes.reshape(1, pairs, sections, rounds, rows, virtuals)
    flipped = [flip(place, amplitudes, g, sections, rounds) for g in range(sections)]
    masked = mask_blocks(integrals, tile_mask)

    own, delivered = [], []
    for r in range(rounds):
        mirrored = []
        for g in range(sections):
            landed = []
            for e in range(pairs):
                piece = flipped[g][r][e]
                piece = route(piece, sections, pairs, lambda a, c, q: (a, c, a ^ q ^ g))
                piece = route(piece, sections, pairs, lambda a, c, l: (a ^ l ^ g, c ^ e, l))
                piece = route(piece, sections, pairs, lambda q, c, l: (q, c, q ^ l ^ g))
                landed.append(piece)
            mirrored.append(landed)
        parts = product(place, own_view, mirrored, masked, r)
        parts = [parts[0]] + [
            route(parts[d], sections, pairs, lambda a, c, q: (a, c, q ^ d))
            for d in range(1, sections)
        ]
        summed, cuts = total(place, parts)
        own.append(summed)
        columns = [cuts[0]] + [
            route(cuts[d], sections, pairs, lambda a, c, q: (a, c, q ^ d))
            for d in range(1, sections)
        ]
        columns = jnp.stack(columns).reshape(sections, slots, pairs, short, wide)
        columns = columns.swapaxes(1, 2).reshape(occupied, slots, short, wide)
        spread = swap(columns, "ia").reshape(occupied * slots, short, wide)
        routed = jnp.take(spread, source_row, axis=0).reshape(occupied, slots, short, wide)
        delivered.append(swap(routed, "ia"))
    return finish(place, own, delivered)


def solution(mesh):
    placed = (
        P("ia", "ka", None, None),
        P("ia", None, "ka", None, None),
        P("ia", None, "ka", None, None),
        P(),
    )
    return jax.shard_map(
        functools.partial(body, mesh.shape["ka"]),
        mesh=mesh,
        in_specs=placed,
        out_specs=P("ia", None, "ka", None),
        check_vma=False,
    )
```

time: 732 us -> 704 us (0.962)
  blocking collectives: 366 us -> 71 us
  starting transfers between devices: 10.3 us -> 299 us
  Pallas kernels: 0 us -> 63.7 us
  matrix products: 62.7 us -> 0 us
  local copies, waits for them, and re-layouts: 81.3 us -> 29.7 us
  waiting for transfers between devices: 191 us -> 230 us
  between operations: 13.5 us -> 1.64 us
    all_to_all x4, blocking collectives: 366 us -> 71 us  [swap(): return lax.all_to_all(array, axis, split_axis=0, concat_axis=0, tiled=True)]
    ppermute x0 -> x120, starting transfers between devices: none -> 281 us  [route(): return lax.ppermute(array, ('ia', 'ka'), moves)]
    ppermute x0 -> x120, waiting for transfers between devices: none -> 221 us  [route(): return lax.ppermute(array, ('ia', 'ka'), moves)]
    all_to_all x2 -> x4, waiting for transfers between devices: 106 us -> 8.81 us  [swap(): return lax.all_to_all(array, axis, split_axis=0, concat_axis=0, tiled=True)]
    reduce_scatter x1 -> x0, waiting for transfers between devices: 84.8 us -> none  [body(): lax.psum_scatter(partial_value, 'ka', scatter_dimension=1, tiled=True)]
    pallas_call x0 -> x14, Pallas kernels: none -> 63.7 us  [call(): pl.pallas_call(kernel, grid_spec=pltpu.PrefetchScalarGridSpec(num_scalar_...]
    dot_general x1 -> x0, matrix products: 62.7 us -> none  [body(): jnp.einsum('kxy,skyz->sxz', mixed, masked, precision=lax.Precision.HIGHEST)]
    convert_element_type x1 -> x0, local copies, waits for them, and re-layouts: 18 us -> none  [expand_mask(): return grown.astype(jnp.float32)]
  transfers between devices with their start and end apart: 3 -> 124, of which waited for: 3 -> 27; matrix products, arithmetic and copies ran while one was open for 5% -> 1% of each run, Pallas kernels for 0% -> 8%
where the time goes in v2:
time: 704 us; the launch traced here: 700 us
  starting transfers between devices  299 us (42%)
  waiting for transfers between devices  230 us (33%)
  blocking collectives  71 us (10%)
  Pallas kernels  63.7 us (9%)
  local copies, waits for them, and re-layouts  29.7 us (4%)
    ppermute x120, starting transfers between devices, route(): return lax.ppermute(array, ('ia', 'ka'), moves)  281 us
    ppermute x120, waiting for transfers between devices, route(): return lax.ppermute(array, ('ia', 'ka'), moves)  221 us
    all_to_all x4, blocking collectives, swap(): return lax.all_to_all(array, axis, split_axis=0, concat_axis=0, tiled=True)  71 us
    pallas_call x14, Pallas kernels, call(): pl.pallas_call(kernel, grid_spec=pltpu.PrefetchScalarGridSpec(num_scalar_...  63.7 us
    unnamed x73, local copies, waits for them, and re-layouts  20.5 us
    all_to_all x4, starting transfers between devices, swap(): return lax.all_to_all(array, axis, split_axis=0, concat_axis=0, tiled=True)  18 us
  transfers between devices with their start and end apart: 124, of which 27 were waited for; matrix products, arithmetic and copies ran while one was open for 1% of the time, Pallas kernels for 8%

profile of v2, /device:TPU:0, one launch (start us, length us, event | category | flops | bytes accessed | tf_op | source)
XLA Modules:
  0.0 699.9 jit_solution(1056247005017581789)
XLA Ops:
  2.8 4.8 collective-permute-start.9
  35.0 4.9 collective-permute-done.21
  59.8 8.3 %collective-permute-done.69 = f32[64,1024]{1,0:T(8,128)S(1)} collective-permute-done((f32[64,1024]{1,0:T(8,128)S(1)}, f32[64,1024]{1,0:T(8,128)S(1)}, u32[]{:S(2)}, u32[]{:S(2)}) %collective-permute-start.69) | collective-permute-done | bytes 262176 | tf_op jit(solution)/shard_map/ppermute | solution.py:224
  117.2 16.5 %collective-permute-start.13 = (f32[64,1024]{1,0:T(8,128)S(1)}, f32[64,1024]{1,0:T(8,128)S(1)}, u32[]{:S(2)}, u32[]{:S(2)}) collective-permute-start(f32[64,1024]{1,0:T(8,128)S(1)} %collective-permute-done.12), channel_id=1, source_target_pairs={{0,16},{1,25},{2,2},{3,11},{4,20},{5,29},{6,6},{7,15},{8,24},{9,17... | collective-permute-start | bytes 786440 | tf_op jit(solution)/shard_map/ppermute | solution.py:224
  140.6 16.4 %collective-permute-done.13 = f32[64,1024]{1,0:T(8,128)S(1)} collective-permute-done((f32[64,1024]{1,0:T(8,128)S(1)}, f32[64,1024]{1,0:T(8,128)S(1)}, u32[]{:S(2)}, u32[]{:S(2)}) %collective-permute-start.13) | collective-permute-done | bytes 262176 | tf_op jit(solution)/shard_map/ppermute | solution.py:224
  160.2 5.4 collective-permute-start.58
  165.6 5.3 collective-permute-start.61
  184.4 6.0 collective-permute-done.64
  191.2 22.8 %collective-permute-done.70 = f32[64,1024]{1,0:T(8,128)S(1)} collective-permute-done((f32[64,1024]{1,0:T(8,128)S(1)}, f32[64,1024]{1,0:T(8,128)S(1)}, u32[]{:S(2)}, u32[]{:S(2)}) %collective-permute-start.70) | collective-permute-done | bytes 262176 | tf_op jit(solution)/shard_map/ppermute | solution.py:224
  219.9 7.6 %collective-permute-start.40 = (f32[64,1024]{1,0:T(8,128)S(1)}, f32[64,1024]{1,0:T(8,128)S(1)}, u32[]{:S(2)}, u32[]{:S(2)}) collective-permute-start(f32[64,1024]{1,0:T(8,128)S(1)} %collective-permute-done.39), channel_id=1, source_target_pairs={{0,16},{1,25},{2,2},{3,11},{4,20},{5,29},{6,6},{7,15},{8,24},{9,17... | collective-permute-start | bytes 786440 | tf_op jit(solution)/shard_map/ppermute | solution.py:224
  237.1 25.3 %collective-permute-done.40 = f32[64,1024]{1,0:T(8,128)S(1)} collective-permute-done((f32[64,1024]{1,0:T(8,128)S(1)}, f32[64,1024]{1,0:T(8,128)S(1)}, u32[]{:S(2)}, u32[]{:S(2)}) %collective-permute-start.40) | collective-permute-done | bytes 262176 | tf_op jit(solution)/shard_map/ppermute | solution.py:224
  262.5 11.8 %collective-permute-done.43 = f32[64,1024]{1,0:T(8,128)S(1)} collective-permute-done((f32[64,1024]{1,0:T(8,128)S(1)}, f32[64,1024]{1,0:T(8,128)S(1)}, u32[]{:S(2)}, u32[]{:S(2)}) %collective-permute-start.43) | collective-permute-done | bytes 262176 | tf_op jit(solution)/shard_map/ppermute | solution.py:224
  289.6 9.0 %collective-permute-done.14.refs_6_ = f32[64,1024]{1,0:T(8,128)S(1)} collective-permute-done((f32[64,1024]{1,0:T(8,128)S(1)}, f32[64,1024]{1,0:T(8,128)S(1)}, u32[]{:S(2)}, u32[]{:S(2)}) %collective-permute-start.14) | collective-permute-done | bytes 262176 | tf_op jit(solution)/shard_map/ppermute | solution.py:224
  304.7 8.8 %mask.1.refs_10_.refs_11_ = bf16[2,2,1024,1024]{3,2,1,0:T(8,128)(2,1)} custom-call(s32[2,2,8,8]{3,2,1,0:T(8,128)S(1)} %bitcast.37, bf16[1,2,2,1024,1024]{4,3,2,1,0:T(8,128)(2,1)} %integrals_ref.1), custom_call_target="tpu_custom_call" | custom-call | bytes 16777216 | tf_op jit(solution)/shard_map/mask/pallas_call | solution.py:16
  315.6 6.1 collective-permute-start.62
  321.7 8.8 %product.4 = (f32[2,64,1024]{2,1,0:T(8,128)S(1)}, f32[2,64,1024]{2,1,0:T(8,128)S(1)}, f32[2,64,1024]{2,1,0:T(8,128)S(1)}, f32[2,64,1024]{2,1,0:T(8,128)S(1)}) custom-call(s32[3]{0:T(128)S(1)} %pad_add_fusion.place_ref, f32[1,2,4,4,64,1024]{5,4,3,2,1,0:T(8,128)} %bitcast.38, f32[1,2,4,4,64,1024]{5,4,3,2,1,0:T(8,128)} %bitcast.39, ...), custom_call_target="tpu_custom_call" | custom-call | flops 4294967296 | bytes 4194304 | tf_op jit(solution)/shard_map/product/pallas_call | solution.py:16
  332.5 10.5 %collective-permute-start.68 = (f32[64,1024]{1,0:T(8,128)S(1)}, f32[64,1024]{1,0:T(8,128)S(1)}, u32[]{:S(2)}, u32[]{:S(2)}) collective-permute-start(f32[64,1024]{1,0:T(8,128)S(1)} %collective-permute-done.67), channel_id=1, source_target_pairs={{0,2},{1,3},{2,0},{3,1},{4,6},{5,7},{6,4},{7,5},{8,11},{9,10},{10,... | collective-permute-start | bytes 786440 | tf_op jit(solution)/shard_map/ppermute | solution.py:224
  352.1 31.2 %collective-permute-done.71.refs_7_ = f32[64,1024]{1,0:T(8,128)S(1)} collective-permute-done((f32[64,1024]{1,0:T(8,128)S(1)}, f32[64,1024]{1,0:T(8,128)S(1)}, u32[]{:S(2)}, u32[]{:S(2)}) %collective-permute-start.71) | collective-permute-done | bytes 262176 | tf_op jit(solution)/shard_map/ppermute | solution.py:224
  386.6 5.1 collective-permute-start.35
  407.7 9.5 %product.6 = (f32[2,64,1024]{2,1,0:T(8,128)S(1)}, f32[2,64,1024]{2,1,0:T(8,128)}, f32[2,64,1024]{2,1,0:T(8,128)}, f32[2,64,1024]{2,1,0:T(8,128)}) custom-call(s32[3]{0:T(128)S(1)} %pad_add_fusion.place_ref, f32[1,2,4,4,64,1024]{5,4,3,2,1,0:T(8,128)} %bitcast.40, f32[1,2,4,4,64,1024]{5,4,3,2,1,0:T(8,128)} %bitcast.41, ...), custom_call_target="tpu_custom_call" | custom-call | flops 4294967296 | bytes 4194304 | tf_op jit(solution)/shard_map/product/pallas_call | solution.py:16
  434.0 14.5 %collective-permute-done.47.refs_8_ = f32[64,1024]{1,0:T(8,128)S(1)} collective-permute-done((f32[64,1024]{1,0:T(8,128)}, f32[64,1024]{1,0:T(8,128)S(1)}, u32[]{:S(2)}, u32[]{:S(2)}) %collective-permute-start.47) | collective-permute-done | bytes 262176 | tf_op jit(solution)/shard_map/ppermute | solution.py:224
  469.7 8.8 %product.5 = (f32[2,64,1024]{2,1,0:T(8,128)S(1)}, f32[2,64,1024]{2,1,0:T(8,128)S(1)}, f32[2,64,1024]{2,1,0:T(8,128)S(1)}, f32[2,64,1024]{2,1,0:T(8,128)S(1)}) custom-call(s32[3]{0:T(128)S(1)} %pad_add_fusion.place_ref, f32[1,2,4,4,64,1024]{5,4,3,2,1,0:T(8,128)} %bitcast.42, f32[1,2,4,4,64,1024]{5,4,3,2,1,0:T(8,128)} %bitcast.43, f32[64,1024]{1,0:T(8,128)S(1)} %copy-done.7, ...), custom_call_target="tpu_custom_call" | custom-call | flops 4294967296 | bytes 4194304 | tf_op jit(solution)/shard_map/product/pallas_call | solution.py:16
  488.2 27.5 %collective-permute-done.115 = f32[2,64,256]{2,1,0:T(8,128)S(1)} collective-permute-done((f32[2,64,256]{2,1,0:T(8,128)S(1)}, f32[2,64,256]{2,1,0:T(8,128)S(1)}, u32[]{:S(2)}, u32[]{:S(2)}) %collective-permute-start.115) | collective-permute-done | bytes 131104 | tf_op jit(solution)/shard_map/ppermute | solution.py:224
  554.2 9.9 %product.7 = (f32[2,64,1024]{2,1,0:T(8,128)S(1)}, f32[2,64,1024]{2,1,0:T(8,128)}, f32[2,64,1024]{2,1,0:T(8,128)}, f32[2,64,1024]{2,1,0:T(8,128)}) custom-call(s32[3]{0:T(128)S(1)} %pad_add_fusion.place_ref, f32[1,2,4,4,64,1024]{5,4,3,2,1,0:T(8,128)} %bitcast.44, f32[1,2,4,4,64,1024]{5,4,3,2,1,0:T(8,128)} %bitcast.45, f32[64,1024]{1,0:T(8,128)S(1)} %copy-done.21, ...), custom_call_target="tpu_custom_call" | custom-call | flops 4294967296 | bytes 4194304 | tf_op jit(solution)/shard_map/product/pallas_call | solution.py:16
  568.5 5.0 all-to-all-start.2
  573.5 5.7 collective-permute-done.105.refs_1_
  579.1 9.9 %collective-permute-done.106.refs_2_ = f32[2,64,1024]{2,1,0:T(8,128)S(1)} collective-permute-done((f32[2,64,1024]{2,1,0:T(8,128)}, f32[2,64,1024]{2,1,0:T(8,128)S(1)}, u32[]{:S(2)}, u32[]{:S(2)}) %collective-permute-start.106) | collective-permute-done | bytes 524320 | tf_op jit(solution)/shard_map/ppermute | solution.py:224
  613.6 8.8 %all-to-all-done.6 = f32[8,2,32,256]{3,2,1,0:T(8,128)} async-done(((f32[8,2,32,256]{3,2,1,0:T(8,128)}), f32[8,2,32,256]{3,2,1,0:T(8,128)}, u32[]{:S(2)}, u32[]{:S(2)}) %all-to-all-start.6) | async-done | bytes 524320 | tf_op jit(solution)/shard_map/all_to_all | solution.py:213
  626.4 17.8 %all_to_all.40.refs_4_ = f32[8,2,32,256]{3,2,1,0:T(8,128)S(1)} all-to-all(f32[8,2,32,256]{3,2,1,0:T(8,128)S(1)} %bitcast.49), channel_id=1, replica_groups=mesh['ia'=8,'ka'=4] {'ia'}, dimensions={0} | all-to-all | bytes 1048576 | tf_op jit(solution)/shard_map/all_to_all | solution.py:213
  644.1 17.8 %all_to_all.41.refs_5_ = f32[8,2,32,256]{3,2,1,0:T(8,128)S(1)} all-to-all(f32[8,2,32,256]{3,2,1,0:T(8,128)S(1)} %bitcast.48), channel_id=1, replica_groups=mesh['ia'=8,'ka'=4] {'ia'}, dimensions={0} | all-to-all | bytes 1048576 | tf_op jit(solution)/shard_map/all_to_all | solution.py:213
  661.9 17.8 %all_to_all.42.refs_6_ = f32[8,2,32,256]{3,2,1,0:T(8,128)S(1)} all-to-all(f32[8,2,32,256]{3,2,1,0:T(8,128)S(1)} %bitcast.47), channel_id=1, replica_groups=mesh['ia'=8,'ka'=4] {'ia'}, dimensions={0} | all-to-all | bytes 1048576 | tf_op jit(solution)/shard_map/all_to_all | solution.py:213
  679.6 17.8 %all_to_all.43.refs_7_ = f32[8,2,32,256]{3,2,1,0:T(8,128)S(1)} all-to-all(f32[8,2,32,256]{3,2,1,0:T(8,128)S(1)} %bitcast.46), channel_id=1, replica_groups=mesh['ia'=8,'ka'=4] {'ia'}, dimensions={0} | all-to-all | bytes 1048576 | tf_op jit(solution)/shard_map/all_to_all | solution.py:213
  (334 shorter events, 313.0 us)
Async XLA Ops:
  104.4 29.3 %collective-permute-start.90 = (f32[64,1024]{1,0:T(8,128)S(1)}, f32[64,1024]{1,0:T(8,128)S(1)}, u32[]{:S(2)}, u32[]{:S(2)}) collective-permute-start(f32[64,1024]{1,0:T(8,128)S(1)} %get-tuple-element.116), channel_id=1, source_target_pairs={{0,1},{1,0},{2,3},{3,2},{4,5},{5,4},{6,7},{7,6},{8,8},{9,9},{10,10... | collective-permute-start | bytes 786440 | tf_op jit(solution)/shard_map/ppermute | solution.py:224
  117.2 39.8 %collective-permute-start.13 = (f32[64,1024]{1,0:T(8,128)S(1)}, f32[64,1024]{1,0:T(8,128)S(1)}, u32[]{:S(2)}, u32[]{:S(2)}) collective-permute-start(f32[64,1024]{1,0:T(8,128)S(1)} %collective-permute-done.12), channel_id=1, source_target_pairs={{0,16},{1,25},{2,2},{3,11},{4,20},{5,29},{6,6},{7,15},{8,24},{9,17... | collective-permute-start | bytes 786440 | tf_op jit(solution)/shard_map/ppermute | solution.py:224
  177.4 36.6 %collective-permute-start.70 = (f32[64,1024]{1,0:T(8,128)S(1)}, f32[64,1024]{1,0:T(8,128)S(1)}, u32[]{:S(2)}, u32[]{:S(2)}) collective-permute-start(f32[64,1024]{1,0:T(8,128)S(1)} %collective-permute-done.69), channel_id=1, source_target_pairs={{0,20},{1,29},{2,6},{3,15},{4,16},{5,25},{6,2},{7,11},{8,28},{9,21... | collective-permute-start | bytes 786440 | tf_op jit(solution)/shard_map/ppermute | solution.py:224
  179.2 36.9 %collective-permute-start.73 = (f32[64,1024]{1,0:T(8,128)S(1)}, f32[64,1024]{1,0:T(8,128)S(1)}, u32[]{:S(2)}, u32[]{:S(2)}) collective-permute-start(f32[64,1024]{1,0:T(8,128)S(1)} %collective-permute-done.72), channel_id=1, source_target_pairs={{0,24},{1,17},{2,10},{3,3},{4,28},{5,21},{6,14},{7,7},{8,16},{9,25... | collective-permute-start | bytes 786440 | tf_op jit(solution)/shard_map/ppermute | solution.py:224
  183.2 36.8 %collective-permute-start.76 = (f32[64,1024]{1,0:T(8,128)S(1)}, f32[64,1024]{1,0:T(8,128)S(1)}, u32[]{:S(2)}, u32[]{:S(2)}) collective-permute-start(f32[64,1024]{1,0:T(8,128)S(1)} %collective-permute-done.75), channel_id=1, source_target_pairs={{0,28},{1,21},{2,14},{3,7},{4,24},{5,17},{6,10},{7,3},{8,20},{9,29... | collective-permute-start | bytes 786440 | tf_op jit(solution)/shard_map/ppermute | solution.py:224
  190.4 37.1 %collective-permute-start.28 = (f32[64,1024]{1,0:T(8,128)S(1)}, f32[64,1024]{1,0:T(8,128)S(1)}, u32[]{:S(2)}, u32[]{:S(2)}) collective-permute-start(f32[64,1024]{1,0:T(8,128)S(1)} %collective-permute-done.27), channel_id=1, source_target_pairs={{0,0},{1,9},{2,18},{3,27},{4,4},{5,13},{6,22},{7,31},{8,8},{9,1},{... | collective-permute-start | bytes 786440 | tf_op jit(solution)/shard_map/ppermute | solution.py:224
  191.1 37.1 %collective-permute-start.31 = (f32[64,1024]{1,0:T(8,128)S(1)}, f32[64,1024]{1,0:T(8,128)S(1)}, u32[]{:S(2)}, u32[]{:S(2)}) collective-permute-start(f32[64,1024]{1,0:T(8,128)S(1)} %collective-permute-done.30), channel_id=1, source_target_pairs={{0,4},{1,13},{2,22},{3,31},{4,0},{5,9},{6,18},{7,27},{8,12},{9,5},... | collective-permute-start | bytes 786440 | tf_op jit(solution)/shard_map/ppermute | solution.py:224
  219.9 42.6 %collective-permute-start.40 = (f32[64,1024]{1,0:T(8,128)S(1)}, f32[64,1024]{1,0:T(8,128)S(1)}, u32[]{:S(2)}, u32[]{:S(2)}) collective-permute-start(f32[64,1024]{1,0:T(8,128)S(1)} %collective-permute-done.39), channel_id=1, source_target_pairs={{0,16},{1,25},{2,2},{3,11},{4,20},{5,29},{6,6},{7,15},{8,24},{9,17... | collective-permute-start | bytes 786440 | tf_op jit(solution)/shard_map/ppermute | solution.py:224
  227.6 46.7 %collective-permute-start.43 = (f32[64,1024]{1,0:T(8,128)S(1)}, f32[64,1024]{1,0:T(8,128)S(1)}, u32[]{:S(2)}, u32[]{:S(2)}) collective-permute-start(f32[64,1024]{1,0:T(8,128)S(1)} %collective-permute-done.42), channel_id=1, source_target_pairs={{0,20},{1,29},{2,6},{3,15},{4,16},{5,25},{6,2},{7,11},{8,28},{9,21... | collective-permute-start | bytes 786440 | tf_op jit(solution)/shard_map/ppermute | solution.py:224
  228.2 48.0 %collective-permute-start.46 = (f32[64,1024]{1,0:T(8,128)S(1)}, f32[64,1024]{1,0:T(8,128)}, u32[]{:S(2)}, u32[]{:S(2)}) collective-permute-start(f32[64,1024]{1,0:T(8,128)S(1)} %collective-permute-done.45), channel_id=1, source_target_pairs={{0,24},{1,17},{2,10},{3,3},{4,28},{5,21},{6,14},{7,7},{8,16},{9,25... | collective-permute-start | bytes 786440 | tf_op jit(solution)/shard_map/ppermute | solution.py:224
  231.4 46.7 %collective-permute-start.49 = (f32[64,1024]{1,0:T(8,128)S(1)}, f32[64,1024]{1,0:T(8,128)}, u32[]{:S(2)}, u32[]{:S(2)}) collective-permute-start(f32[64,1024]{1,0:T(8,128)S(1)} %collective-permute-done.48), channel_id=1, source_target_pairs={{0,28},{1,21},{2,14},{3,7},{4,24},{5,17},{6,10},{7,3},{8,20},{9,29... | collective-permute-start | bytes 786440 | tf_op jit(solution)/shard_map/ppermute | solution.py:224
  233.5 48.6 %collective-permute-start.100 = (f32[64,1024]{1,0:T(8,128)S(1)}, f32[64,1024]{1,0:T(8,128)S(1)}, u32[]{:S(2)}, u32[]{:S(2)}) collective-permute-start(f32[64,1024]{1,0:T(8,128)S(1)} %collective-permute-done.99), channel_id=1, source_target_pairs={{0,24},{1,17},{2,10},{3,3},{4,28},{5,21},{6,14},{7,7},{8,16},{9,25... | collective-permute-start | bytes 786440 | tf_op jit(solution)/shard_map/ppermute | solution.py:224
  282.1 31.4 %collective-permute-start.2 = (f32[64,1024]{1,0:T(8,128)S(1)}, f32[64,1024]{1,0:T(8,128)S(1)}, u32[]{:S(2)}, u32[]{:S(2)}) collective-permute-start(f32[64,1024]{1,0:T(8,128)S(1)} %collective-permute-done.1), channel_id=1, source_target_pairs={{0,0},{1,1},{2,2},{3,3},{4,4},{5,5},{6,6},{7,7},{8,9},{9,8},{10,11... | collective-permute-start | bytes 786440 | tf_op jit(solution)/shard_map/ppermute | solution.py:224
  282.8 31.3 %collective-permute-start.20 = (f32[64,1024]{1,0:T(8,128)S(1)}, f32[64,1024]{1,0:T(8,128)S(1)}, u32[]{:S(2)}, u32[]{:S(2)}) collective-permute-start(f32[64,1024]{1,0:T(8,128)S(1)} %collective-permute-done.19), channel_id=1, source_target_pairs={{0,3},{1,2},{2,1},{3,0},{4,7},{5,6},{6,5},{7,4},{8,10},{9,11},{10,... | collective-permute-start | bytes 786440 | tf_op jit(solution)/shard_map/ppermute | solution.py:224
  343.0 42.9 %collective-permute-start.24 = (f32[2,64,1024]{2,1,0:T(8,128)S(1)}, f32[2,64,1024]{2,1,0:T(8,128)S(1)}, u32[]{:S(2)}, u32[]{:S(2)}) collective-permute-start(f32[2,64,1024]{2,1,0:T(8,128)S(1)} %get-tuple-element.83), channel_id=1, source_target_pairs={{0,1},{1,0},{2,3},{3,2},{4,5},{5,4},{6,7},{7,6},{8,9},{9,8},{10,11... | collective-permute-start | bytes 1572872 | tf_op jit(solution)/shard_map/ppermute | solution.py:224
  343.1 43.5 %collective-permute-start.25 = (f32[2,64,1024]{2,1,0:T(8,128)S(1)}, f32[2,64,1024]{2,1,0:T(8,128)S(1)}, u32[]{:S(2)}, u32[]{:S(2)}) collective-permute-start(f32[2,64,1024]{2,1,0:T(8,128)S(1)} %get-tuple-element.84), channel_id=1, source_target_pairs={{0,2},{1,3},{2,0},{3,1},{4,6},{5,7},{6,4},{7,5},{8,10},{9,11},{10,... | collective-permute-start | bytes 1572872 | tf_op jit(solution)/shard_map/ppermute | solution.py:224
  343.2 48.5 %collective-permute-start.26 = (f32[2,64,1024]{2,1,0:T(8,128)S(1)}, f32[2,64,1024]{2,1,0:T(8,128)S(1)}, u32[]{:S(2)}, u32[]{:S(2)}) collective-permute-start(f32[2,64,1024]{2,1,0:T(8,128)S(1)} %get-tuple-element.85), channel_id=1, source_target_pairs={{0,3},{1,2},{2,1},{3,0},{4,7},{5,6},{6,5},{7,4},{8,11},{9,10},{10,... | collective-permute-start | bytes 1572872 | tf_op jit(solution)/shard_map/ppermute | solution.py:224
  346.7 36.6 %collective-permute-start.71 = (f32[64,1024]{1,0:T(8,128)S(1)}, f32[64,1024]{1,0:T(8,128)S(1)}, u32[]{:S(2)}, u32[]{:S(2)}) collective-permute-start(f32[64,1024]{1,0:T(8,128)S(1)} %collective-permute-done.70), channel_id=1, source_target_pairs={{0,2},{1,3},{2,0},{3,1},{4,6},{5,7},{6,4},{7,5},{8,11},{9,10},{10,... | collective-permute-start | bytes 786440 | tf_op jit(solution)/shard_map/ppermute | solution.py:224
  350.1 35.1 %collective-permute-start.74 = (f32[64,1024]{1,0:T(8,128)S(1)}, f32[64,1024]{1,0:T(8,128)S(1)}, u32[]{:S(2)}, u32[]{:S(2)}) collective-permute-start(f32[64,1024]{1,0:T(8,128)S(1)} %collective-permute-done.73), channel_id=1, source_target_pairs={{0,3},{1,2},{2,1},{3,0},{4,7},{5,6},{6,5},{7,4},{8,10},{9,11},{10,... | collective-permute-start | bytes 786440 | tf_op jit(solution)/shard_map/ppermute | solution.py:224
  417.2 35.6 %collective-permute-start.78 = (f32[2,64,1024]{2,1,0:T(8,128)}, f32[2,64,1024]{2,1,0:T(8,128)S(1)}, u32[]{:S(2)}, u32[]{:S(2)}) collective-permute-start(f32[2,64,1024]{2,1,0:T(8,128)} %get-tuple-element.109), channel_id=1, source_target_pairs={{0,1},{1,0},{2,3},{3,2},{4,5},{5,4},{6,7},{7,6},{8,9},{9,8},{10,11... | collective-permute-start | bytes 1572872 | tf_op jit(solution)/shard_map/ppermute | solution.py:224
  418.9 36.7 %collective-permute-start.79 = (f32[2,64,1024]{2,1,0:T(8,128)}, f32[2,64,1024]{2,1,0:T(8,128)S(1)}, u32[]{:S(2)}, u32[]{:S(2)}) collective-permute-start(f32[2,64,1024]{2,1,0:T(8,128)} %get-tuple-element.110), channel_id=1, source_target_pairs={{0,2},{1,3},{2,0},{3,1},{4,6},{5,7},{6,4},{7,5},{8,10},{9,11},{10,... | collective-permute-start | bytes 1572872 | tf_op jit(solution)/shard_map/ppermute | solution.py:224
  420.3 37.9 %collective-permute-start.80 = (f32[2,64,1024]{2,1,0:T(8,128)}, f32[2,64,1024]{2,1,0:T(8,128)S(1)}, u32[]{:S(2)}, u32[]{:S(2)}) collective-permute-start(f32[2,64,1024]{2,1,0:T(8,128)} %get-tuple-element.111), channel_id=1, source_target_pairs={{0,3},{1,2},{2,1},{3,0},{4,7},{5,6},{6,5},{7,4},{8,11},{9,10},{10,... | collective-permute-start | bytes 1572872 | tf_op jit(solution)/shard_map/ppermute | solution.py:224
  429.8 112.9 %all-to-all-start = ((f32[8,2,32,256]{3,2,1,0:T(8,128)}), f32[8,2,32,256]{3,2,1,0:T(8,128)}, u32[]{:S(2)}, u32[]{:S(2)}) async-start(f32[8,2,32,256]{3,2,1,0:T(8,128)} %bitcast.50), calls=%async_computation | async-start | bytes 1048576 | tf_op jit(solution)/shard_map/all_to_all | solution.py:213
  449.2 31.1 %collective-permute-start.88 = (f32[64,1024]{1,0:T(8,128)}, f32[64,1024]{1,0:T(8,128)}, u32[]{:S(2)}, u32[]{:S(2)}) collective-permute-start(f32[64,1024]{1,0:T(8,128)} %copy-done.28), channel_id=1, source_target_pairs={{0,8},{1,1},{2,26},{3,19},{4,12},{5,5},{6,30},{7,23},{8,0},{9,9},{... | collective-permute-start | bytes 786440 | tf_op jit(solution)/shard_map/ppermute | solution.py:224
  452.8 29.6 %collective-permute-start.91 = (f32[64,1024]{1,0:T(8,128)}, f32[64,1024]{1,0:T(8,128)}, u32[]{:S(2)}, u32[]{:S(2)}) collective-permute-start(f32[64,1024]{1,0:T(8,128)} %copy-done.29), channel_id=1, source_target_pairs={{0,12},{1,5},{2,30},{3,23},{4,8},{5,1},{6,26},{7,19},{8,4},{9,13},... | collective-permute-start | bytes 786440 | tf_op jit(solution)/shard_map/ppermute | solution.py:224
  452.8 29.7 %collective-permute-start.94 = (f32[64,1024]{1,0:T(8,128)}, f32[64,1024]{1,0:T(8,128)}, u32[]{:S(2)}, u32[]{:S(2)}) collective-permute-start(f32[64,1024]{1,0:T(8,128)} %copy-done.30), channel_id=1, source_target_pairs={{0,16},{1,25},{2,2},{3,11},{4,20},{5,29},{6,6},{7,15},{8,24},{9,17... | collective-permute-start | bytes 786440 | tf_op jit(solution)/shard_map/ppermute | solution.py:224
  482.4 49.6 %collective-permute-start.51 = (f32[2,64,1024]{2,1,0:T(8,128)S(1)}, f32[2,64,1024]{2,1,0:T(8,128)S(1)}, u32[]{:S(2)}, u32[]{:S(2)}) collective-permute-start(f32[2,64,1024]{2,1,0:T(8,128)S(1)} %get-tuple-element.96), channel_id=1, source_target_pairs={{0,1},{1,0},{2,3},{3,2},{4,5},{5,4},{6,7},{7,6},{8,9},{9,8},{10,11... | collective-permute-start | bytes 1572872 | tf_op jit(solution)/shard_map/ppermute | solution.py:224
  482.5 53.4 %collective-permute-start.52 = (f32[2,64,1024]{2,1,0:T(8,128)S(1)}, f32[2,64,1024]{2,1,0:T(8,128)S(1)}, u32[]{:S(2)}, u32[]{:S(2)}) collective-permute-start(f32[2,64,1024]{2,1,0:T(8,128)S(1)} %get-tuple-element.97), channel_id=1, source_target_pairs={{0,2},{1,3},{2,0},{3,1},{4,6},{5,7},{6,4},{7,5},{8,10},{9,11},{10,... | collective-permute-start | bytes 1572872 | tf_op jit(solution)/shard_map/ppermute | solution.py:224
  484.5 53.5 %collective-permute-start.53 = (f32[2,64,1024]{2,1,0:T(8,128)S(1)}, f32[2,64,1024]{2,1,0:T(8,128)S(1)}, u32[]{:S(2)}, u32[]{:S(2)}) collective-permute-start(f32[2,64,1024]{2,1,0:T(8,128)S(1)} %get-tuple-element.98), channel_id=1, source_target_pairs={{0,3},{1,2},{2,1},{3,0},{4,7},{5,6},{6,5},{7,4},{8,11},{9,10},{10,... | collective-permute-start | bytes 1572872 | tf_op jit(solution)/shard_map/ppermute | solution.py:224
  485.9 29.8 %collective-permute-start.115 = (f32[2,64,256]{2,1,0:T(8,128)S(1)}, f32[2,64,256]{2,1,0:T(8,128)S(1)}, u32[]{:S(2)}, u32[]{:S(2)}) collective-permute-start(f32[2,64,256]{2,1,0:T(8,128)S(1)} %get-tuple-element.136), channel_id=1, source_target_pairs={{0,2},{1,3},{2,0},{3,1},{4,6},{5,7},{6,4},{7,5},{8,10},{9,11},{10,... | collective-permute-start | bytes 393224 | tf_op jit(solution)/shard_map/ppermute | solution.py:224
  486.7 32.4 %collective-permute-start.116 = (f32[2,64,256]{2,1,0:T(8,128)S(1)}, f32[2,64,256]{2,1,0:T(8,128)S(1)}, u32[]{:S(2)}, u32[]{:S(2)}) collective-permute-start(f32[2,64,256]{2,1,0:T(8,128)S(1)} %get-tuple-element.137), channel_id=1, source_target_pairs={{0,3},{1,2},{2,1},{3,0},{4,7},{5,6},{6,5},{7,4},{8,11},{9,10},{10,... | collective-permute-start | bytes 393224 | tf_op jit(solution)/shard_map/ppermute | solution.py:224
  568.5 33.7 %all-to-all-start.2 = ((f32[8,2,32,256]{3,2,1,0:T(8,128)}), f32[8,2,32,256]{3,2,1,0:T(8,128)}, u32[]{:S(2)}, u32[]{:S(2)}) async-start(f32[8,2,32,256]{3,2,1,0:T(8,128)} %bitcast.52), calls=%async_computation.2 | async-start | bytes 1048576 | tf_op jit(solution)/shard_map/all_to_all | solution.py:213
  (128 other events, 2845.7 us)

commit v3 on v0

v3 whole, which is shorter than its diff:
```python
import functools

import jax
import jax.numpy as jnp
from jax import lax
from jax.experimental import pallas as pl
from jax.experimental.pallas import tpu as pltpu
from jax.sharding import PartitionSpec as P

CHUNKS = (2, 3, 2, 1)
LANES = 128
VMEM_BYTES = 48 * 1024 * 1024


def call(kernel, name, scalars, operands, in_specs, out_specs, out_shape, grid, scratch=(), flops=0):
    moved = sum(x.size * x.dtype.itemsize for x in jax.tree.leaves(out_shape)) * 2
    return pl.pallas_call(
        kernel,
        grid_spec=pltpu.PrefetchScalarGridSpec(
            num_scalar_prefetch=1,
            grid=grid,
            in_specs=in_specs,
            out_specs=out_specs,
            scratch_shapes=list(scratch),
        ),
        out_shape=out_shape,
        compiler_params=pltpu.CompilerParams(vmem_limit_bytes=VMEM_BYTES),
        cost_estimate=pl.CostEstimate(flops=flops, bytes_accessed=moved, transcendentals=0),
        name=name,
    )(scalars, *operands)


def whole(shape):
    return pl.BlockSpec(shape, lambda *_: (0,) * len(shape))


def first_flip_kernel(place_ref, blocks_ref, piece_ref):
    piece_ref[0, 0] = blocks_ref[0, 0].T[: piece_ref.shape[2]]


def first_flip(place, amplitudes, sections, rows):
    pairs, virtuals = amplitudes.shape[1], amplitudes.shape[3]
    steps = virtuals // sections // LANES
    return call(
        first_flip_kernel,
        "first_flip",
        place,
        [amplitudes],
        [pl.BlockSpec((1, 1, virtuals, LANES), lambda d, q, at: (0, d, 0, q * steps))],
        pl.BlockSpec((1, 1, rows, virtuals), lambda d, q, at: (q, d, 0, 0)),
        jax.ShapeDtypeStruct((sections, pairs, rows, virtuals), jnp.float32),
        (pairs, sections),
    )


def flip_kernel(spans, place_ref, blocks_ref, *pieces):
    flipped = blocks_ref[0, 0].T
    for (start, rows), piece in zip(spans, pieces):
        piece[0] = flipped[start : start + rows]


def flip(place, amplitudes, sections, e, spans):
    pairs, virtuals = amplitudes.shape[1], amplitudes.shape[3]
    wide = virtuals // sections
    return call(
        functools.partial(flip_kernel, spans),
        "flip",
        place,
        [amplitudes],
        [pl.BlockSpec((1, 1, virtuals, wide), lambda d, at: (0, d, 0, at[0] ^ e))],
        [pl.BlockSpec((1, rows, virtuals), lambda d, at: (d, 0, 0)) for _, rows in spans],
        [jax.ShapeDtypeStruct((pairs, rows, virtuals), jnp.float32) for _, rows in spans],
        (pairs,),
    )


def gather_kernel(place_ref, *refs):
    pieces, out_ref = refs[:-1], refs[-1]
    for e, piece in enumerate(pieces):
        out_ref[place_ref[0] ^ e] = piece[...]


def gather(place, pieces):
    shape = (len(pieces), *pieces[0].shape)
    return call(
        gather_kernel,
        "gather",
        place,
        pieces,
        [whole(pieces[0].shape)] * len(pieces),
        whole(shape),
        jax.ShapeDtypeStruct(shape, jnp.float32),
        (1,),
    )


def scatter_kernel(place_ref, stacked_ref, *pieces):
    for e, piece in enumerate(pieces):
        piece[...] = stacked_ref[place_ref[0] ^ e]


def scatter(place, stacked):
    count, shape = stacked.shape[0], stacked.shape[1:]
    return call(
        scatter_kernel,
        "scatter",
        place,
        [stacked],
        [whole(stacked.shape)],
        [whole(shape)] * count,
        [jax.ShapeDtypeStruct(shape, jnp.float32)] * count,
        (1,),
    )


def mask_kernel(tiles, mask_ref, integrals_ref, masked_ref):
    side = integrals_ref.shape[-1] // tiles
    slot, pair = pl.program_id(0), pl.program_id(1)
    for r in range(tiles):
        for c in range(tiles):
            keep = mask_ref[slot, pair, r, c] != 0
            spot = (pl.ds(r * side, side), pl.ds(c * side, side))
            tile = integrals_ref[0, 0, 0, spot[0], spot[1]]
            masked_ref[0, 0, spot[0], spot[1]] = jnp.where(keep, tile, jnp.zeros_like(tile))


def mask_blocks(integrals, tile_mask):
    _, slots, pairs, virtuals, _ = integrals.shape
    out_shape = jax.ShapeDtypeStruct((slots, pairs, virtuals, virtuals), jnp.bfloat16)
    return call(
        functools.partial(mask_kernel, tile_mask.shape[-1]),
        "mask",
        tile_mask[0],
        [integrals],
        [pl.BlockSpec((1, 1, 1, virtuals, virtuals), lambda s, k, mask: (0, s, k, 0, 0))],
        pl.BlockSpec((1, 1, virtuals, virtuals), lambda s, k, mask: (s, k, 0, 0)),
        out_shape,
        (slots, pairs),
    )


def product_kernel(sections, place_ref, *refs):
    own_refs, mirrored_refs, refs = refs[:sections], refs[sections : 2 * sections], refs[2 * sections :]
    masked_ref, out_ref, split_ref = refs
    pairs, rows, _ = mirrored_refs[0].shape
    tall = sections * rows

    @pl.when((pl.program_id(0) == 0) & (pl.program_id(1) == 0))
    def _():
        for e in range(sections):
            for k in range(pairs):
                mixed = 2.0 * own_refs[e][0, k] - mirrored_refs[e][k]
                high = mixed.astype(jnp.bfloat16)
                low = (mixed - high.astype(jnp.float32)).astype(jnp.bfloat16)
                split_ref[k, pl.ds(e * rows, rows)] = high
                split_ref[k, pl.ds(tall + e * rows, rows)] = low

    total = None
    for k in range(pairs):
        both = jnp.dot(split_ref[k], masked_ref[0, k], preferred_element_type=jnp.float32)
        both = both[:tall] + both[tall:]
        total = both if total is None else total + both
    for e in range(sections):
        out_ref[place_ref[0] ^ e, 0] = total[e * rows : (e + 1) * rows]


def product(place, own, mirrored, masked, start):
    sections = len(mirrored)
    pairs, rows, virtuals = mirrored[0].shape
    slots = masked.shape[0]
    deep = virtuals // sections
    wide = min(virtuals, 512)
    return call(
        functools.partial(product_kernel, sections),
        "product",
        place,
        [own] * sections + list(mirrored) + [masked],
        [
            pl.BlockSpec(
                tuple(pl.Element(size) for size in (1, pairs, rows, virtuals)),
                lambda s, n, at, e=e: (0, 0, pl.multiple_of((at[0] ^ e) * deep + start, 8), 0),
            )
            for e in range(sections)
        ]
        + [whole(mirrored[0].shape)] * sections
        + [pl.BlockSpec((1, pairs, virtuals, wide), lambda s, n, at: (s, 0, 0, n))],
        pl.BlockSpec((sections, 1, rows, wide), lambda s, n, at: (0, s, 0, n)),
        jax.ShapeDtypeStruct((sections, slots, rows, virtuals), jnp.float32),
        (slots, virtuals // wide),
        scratch=[pltpu.VMEM((pairs, 2 * sections * rows, virtuals), jnp.bfloat16)],
        flops=4 * sections * rows * pairs * virtuals * virtuals * slots,
    )


def cut_kernel(place_ref, total_ref, *cut_refs):
    parts, _, short, wide = cut_refs[0].shape
    for e, cut_ref in enumerate(cut_refs):
        start = pl.multiple_of((place_ref[0] ^ e) * wide, wide)
        for part in range(parts):
            cut_ref[part] = total_ref[:, part * short : (part + 1) * short, pl.ds(start, wide)]


def cut(place, total, sections, parts):
    slots, rows, virtuals = total.shape
    shape = (parts, slots, rows // parts, virtuals // sections)
    return call(
        cut_kernel,
        "cut",
        place,
        [total],
        [whole(total.shape)],
        [whole(shape)] * sections,
        [jax.ShapeDtypeStruct(shape, jnp.float32)] * sections,
        (1,),
    )


def finish_kernel(spans, place_ref, *refs):
    chunks = len(spans)
    own_refs, delivered_refs = refs[:chunks], refs[chunks : 2 * chunks]
    out_ref, columns_ref = refs[2 * chunks :]
    wide = out_ref.shape[2]
    sections = columns_ref.shape[0] // wide
    for (start, _), delivered_ref in zip(spans, delivered_refs):
        pieces, _, short, _ = delivered_ref.shape
        parts = pieces // sections
        for e in range(sections):
            base = (place_ref[0] ^ e) * wide + start
            for part in range(parts):
                spot = pl.multiple_of(base + part * short, 8)
                columns_ref[pl.ds(spot, short)] = delivered_ref[e * parts + part, 0]
    turned = columns_ref[...].T
    for (start, rows), own_ref in zip(spans, own_refs):
        out_ref[0, 0, start : start + rows] = own_ref[0] + turned[start : start + rows]


def finish(place, spans, own, delivered):
    slots, _, virtuals = own[0].shape
    wide = delivered[0].shape[-1]
    return call(
        functools.partial(finish_kernel, spans),
        "finish",
        place,
        list(own) + list(delivered),
        [pl.BlockSpec((1, *x.shape[1:]), lambda s, at: (s, 0, 0)) for x in own]
        + [
            pl.BlockSpec((x.shape[0], 1, *x.shape[2:]), lambda s, at: (0, s, 0, 0))
            for x in delivered
        ],
        pl.BlockSpec((1, 1, wide, virtuals), lambda s, at: (0, s, 0, 0)),
        jax.ShapeDtypeStruct((1, slots, wide, virtuals), jnp.float32),
        (slots,),
        scratch=[pltpu.VMEM((virtuals, wide), jnp.float32)],
    )


def swap(array, axis):
    return lax.all_to_all(array, axis, split_axis=0, concat_axis=0, tiled=True)


def spread(pieces):
    count = len(pieces)
    return [pieces[0]] + [
        lax.ppermute(pieces[e], "ka", [(q, q ^ e) for q in range(count)]) for e in range(1, count)
    ]


def body(sections, amplitudes, integrals, tile_mask, pair_list):
    _, pairs, virtuals, _ = amplitudes.shape
    occupied, slots = pair_list.shape
    wide = virtuals // sections
    sizes = [wide * part // sum(CHUNKS) for part in CHUNKS]
    spans = [(sum(sizes[:at]), size) for at, size in enumerate(sizes)]
    place = lax.axis_index("ka").astype(jnp.int32).reshape(1)

    owners = jnp.arange(occupied, dtype=jnp.int32)
    partner_slot = jnp.where(pair_list[pair_list, 0] == owners[:, None], 0, 1).astype(jnp.int32)
    source_row = (pair_list * slots + partner_slot).reshape(-1)

    first = first_flip(place, amplitudes, sections, sizes[0])
    flipped = [flip(place, amplitudes, sections, e, spans[1:]) for e in range(sections)]
    masked = mask_blocks(integrals, tile_mask)

    own, delivered = [], []
    for at, (start, rows) in enumerate(spans):
        short = rows // pairs
        if at == 0:
            across = swap(first, "ka")
        else:
            across = gather(place, spread([pieces[at - 1] for pieces in flipped]))
        crossed = swap(across.reshape(occupied, rows, virtuals), "ia")
        crossed = crossed.reshape(sections, pairs, rows, virtuals)
        mirrored = spread(scatter(place, crossed))
        partial_rows = product(place, amplitudes, mirrored, masked, start)
        summed = lax.psum_scatter(partial_rows, "ka", scatter_dimension=0, tiled=False)
        own.append(summed)
        columns = jnp.concatenate(spread(cut(place, summed, sections, pairs)))
        met = swap(columns, "ia").reshape(occupied * slots, short, wide)
        routed = jnp.take(met, source_row, axis=0).reshape(occupied, slots, short, wide)
        delivered.append(swap(routed, "ia"))
    return finish(place, spans, own, delivered)


def solution(mesh):
    placed = (
        P("ia", "ka", None, None),
        P("ia", None, "ka", None, None),
        P("ia", None, "ka", None, None),
        P(),
    )
    return jax.shard_map(
        functools.partial(body, mesh.shape["ka"]),
        mesh=mesh,
        in_specs=placed,
        out_specs=P("ia", None, "ka", None),
        check_vma=False,
    )
```

time: 732 us -> 560 us (0.77)
  blocking collectives: 366 us -> 48.8 us
  waiting for transfers between devices: 191 us -> 317 us
  starting transfers between devices: 10.3 us -> 86.5 us
  Pallas kernels: 0 us -> 68.1 us
  local copies, waits for them, and re-layouts: 81.3 us -> 17.7 us
  matrix products: 62.7 us -> 0 us
    all_to_all x4 -> x2, blocking collectives: 366 us -> 48.8 us  [swap(): return lax.all_to_all(array, axis, split_axis=0, concat_axis=0, tiled=True)]
    ppermute x0 -> x33, waiting for transfers between devices: none -> 216 us  [spread(): lax.ppermute(pieces[e], 'ka', [(q, q ^ e) for q in range(count)])]
    reduce_scatter x1 -> x0, waiting for transfers between devices: 84.8 us -> none  [body(): lax.psum_scatter(partial_value, 'ka', scatter_dimension=1, tiled=True)]
    pallas_call x0 -> x22, Pallas kernels: none -> 68.1 us  [call(): pl.pallas_call(kernel, grid_spec=pltpu.PrefetchScalarGridSpec(num_scalar_...]
    dot_general x1 -> x0, matrix products: 62.7 us -> none  [body(): jnp.einsum('kxy,skyz->sxz', mixed, masked, precision=lax.Precision.HIGHEST)]
    ppermute x0 -> x33, starting transfers between devices: none -> 39.2 us  [spread(): lax.ppermute(pieces[e], 'ka', [(q, q ^ e) for q in range(count)])]
    all_to_all x2 -> x11, starting transfers between devices: 10.3 us -> 47.1 us  [swap(): return lax.all_to_all(array, axis, split_axis=0, concat_axis=0, tiled=True)]
    convert_element_type x1 -> x0, local copies, waits for them, and re-layouts: 18 us -> none  [expand_mask(): return grown.astype(jnp.float32)]
  transfers between devices with their start and end apart: 3 -> 48, of which waited for: 3 -> 32; matrix products, arithmetic and copies ran while one was open for 5% -> 2% of each run, Pallas kernels for 0% -> 11%
where the time goes in v3:
time: 560 us; the launch traced here: 558 us
  waiting for transfers between devices  317 us (57%)
  starting transfers between devices  86.5 us (15%)
  Pallas kernels  68.1 us (12%)
  blocking collectives  48.8 us (9%)
  local copies, waits for them, and re-layouts  17.7 us (3%)
  between operations  13.5 us (2%)
  other arithmetic  6.5 us (1%)
    ppermute x33, waiting for transfers between devices, spread(): lax.ppermute(pieces[e], 'ka', [(q, q ^ e) for q in range(count)])  216 us
    all_to_all x11, waiting for transfers between devices, swap(): return lax.all_to_all(array, axis, split_axis=0, concat_axis=0, tiled=True)  101 us
    pallas_call x22, Pallas kernels, call(): pl.pallas_call(kernel, grid_spec=pltpu.PrefetchScalarGridSpec(num_scalar_...  68.1 us
    all_to_all x2, blocking collectives, swap(): return lax.all_to_all(array, axis, split_axis=0, concat_axis=0, tiled=True)  48.8 us
    all_to_all x11, starting transfers between devices, swap(): return lax.all_to_all(array, axis, split_axis=0, concat_axis=0, tiled=True)  47.1 us
    ppermute x33, starting transfers between devices, spread(): lax.ppermute(pieces[e], 'ka', [(q, q ^ e) for q in range(count)])  39.2 us
    unnamed x37, local copies, waits for them, and re-layouts  12.2 us
  transfers between devices with their start and end apart: 48, of which 32 were waited for; matrix products, arithmetic and copies ran while one was open for 2% of the time, Pallas kernels for 11%

profile of v3, /device:TPU:0, one launch (start us, length us, event | category | flops | bytes accessed | tf_op | source)
XLA Modules:
  0.0 558.2 jit_solution(2696833082540266306)
XLA Ops:
  6.5 6.7 %first_flip.1 = f32[4,2,64,1024]{3,2,1,0:T(8,128)} custom-call(s32[1]{0:T(128)} %bitcast.place_ref, f32[1,2,1024,1024]{3,2,1,0:T(8,128)} %refs_3_.7), custom_call_target="tpu_custom_call" | custom-call | bytes 4194304 | tf_op jit(solution)/shard_map/first_flip/pallas_call | solution.py:17
  13.2 5.2 all-to-all-start
  33.4 17.0 %collective-permute-done.15.refs_1_ = f32[2,32,1024]{2,1,0:T(8,128)S(1)} collective-permute-done((f32[2,32,1024]{2,1,0:T(8,128)S(1)}, f32[2,32,1024]{2,1,0:T(8,128)S(1)}, u32[]{:S(2)}, u32[]{:S(2)}) %collective-permute-start.15) | collective-permute-done | bytes 262176 | tf_op jit(solution)/shard_map/ppermute | solution.py:264
  50.4 5.8 %collective-permute-done.17.refs_3_ = f32[2,32,1024]{2,1,0:T(8,128)S(1)} collective-permute-done((f32[2,32,1024]{2,1,0:T(8,128)S(1)}, f32[2,32,1024]{2,1,0:T(8,128)S(1)}, u32[]{:S(2)}, u32[]{:S(2)}) %collective-permute-start.17) | collective-permute-done | bytes 262176 | tf_op jit(solution)/shard_map/ppermute | solution.py:264
  57.2 5.1 all-to-all-start.4
  65.8 22.1 %collective-permute-done.10.refs_2_ = f32[2,64,1024]{2,1,0:T(8,128)S(1)} collective-permute-done((f32[2,64,1024]{2,1,0:T(8,128)S(1)}, f32[2,64,1024]{2,1,0:T(8,128)S(1)}, u32[]{:S(2)}, u32[]{:S(2)}) %collective-permute-start.10) | collective-permute-done | bytes 524320 | tf_op jit(solution)/shard_map/ppermute | solution.py:264
  90.6 4.9 all-to-all-start.3
  99.9 8.7 %mask.1.refs_8_ = bf16[2,2,1024,1024]{3,2,1,0:T(8,128)(2,1)} custom-call(s32[2,2,8,8]{3,2,1,0:T(8,128)S(1)} %bitcast.37, bf16[1,2,2,1024,1024]{4,3,2,1,0:T(8,128)(2,1)} %integrals_ref.1), custom_call_target="tpu_custom_call" | custom-call | bytes 16777216 | tf_op jit(solution)/shard_map/mask/pallas_call | solution.py:17
  108.6 35.9 %all-to-all-done.3 = f32[8,64,1024]{2,1,0:T(8,128)S(1)} async-done(((f32[8,64,1024]{2,1,0:T(8,128)}), f32[8,64,1024]{2,1,0:T(8,128)S(1)}, u32[]{:S(2)}, u32[]{:S(2)}) %all-to-all-start.3) | async-done | bytes 2097184 | tf_op jit(solution)/shard_map/all_to_all | solution.py:258
  149.6 6.8 %product.7 = f32[4,2,32,1024]{3,2,1,0:T(8,128)} custom-call(s32[1]{0:T(128)} %bitcast.place_ref, f32[1,2,1024,1024]{3,2,1,0:T(8,128)} %refs_3_.7, f32[1,2,1024,1024]{3,2,1,0:T(8,128)} %refs_3_.7, f32[1,2,1024,1024]{3,2,1,0:T(8,128)} %refs_3_.7, f32[1,2,1024,1024]{3,2,1,0:T(8,128)} %refs_3_.7, f32[2,32,1024]{2,1,0:T(8,128)S(1)} %get-tuple-element.74.refs_4_, ...), custom_call_target="tpu_custom_call" | custom-call | flops 2147483648 | bytes 2097152 | tf_op jit(solution)/shard_map/product/pallas_call | solution.py:17
  161.8 16.9 %collective-permute-done.12.refs_5_ = f32[2,64,1024]{2,1,0:T(8,128)S(1)} collective-permute-done((f32[2,64,1024]{2,1,0:T(8,128)S(1)}, f32[2,64,1024]{2,1,0:T(8,128)S(1)}, u32[]{:S(2)}, u32[]{:S(2)}) %collective-permute-start.12) | collective-permute-done | bytes 524320 | tf_op jit(solution)/shard_map/ppermute | solution.py:264
  178.6 7.7 %collective-permute-done.13.refs_6_ = f32[2,64,1024]{2,1,0:T(8,128)S(1)} collective-permute-done((f32[2,64,1024]{2,1,0:T(8,128)S(1)}, f32[2,64,1024]{2,1,0:T(8,128)S(1)}, u32[]{:S(2)}, u32[]{:S(2)}) %collective-permute-start.13) | collective-permute-done | bytes 524320 | tf_op jit(solution)/shard_map/ppermute | solution.py:264
  186.3 5.9 %collective-permute-done.14.refs_7_ = f32[2,64,1024]{2,1,0:T(8,128)S(1)} collective-permute-done((f32[2,64,1024]{2,1,0:T(8,128)S(1)}, f32[2,64,1024]{2,1,0:T(8,128)S(1)}, u32[]{:S(2)}, u32[]{:S(2)}) %collective-permute-start.14) | collective-permute-done | bytes 524320 | tf_op jit(solution)/shard_map/ppermute | solution.py:264
  192.2 9.1 %product.6 = f32[4,2,64,1024]{3,2,1,0:T(8,128)} custom-call(s32[1]{0:T(128)} %bitcast.place_ref, f32[1,2,1024,1024]{3,2,1,0:T(8,128)} %refs_3_.7, f32[1,2,1024,1024]{3,2,1,0:T(8,128)} %refs_3_.7, f32[1,2,1024,1024]{3,2,1,0:T(8,128)} %refs_3_.7, f32[1,2,1024,1024]{3,2,1,0:T(8,128)} %refs_3_.7, f32[2,64,1024]{2,1,0:T(8,128)S(1)} %get-tuple-element.66.refs_4_, ...), custom_call_target="tpu_custom_call" | custom-call | flops 4294967296 | bytes 4194304 | tf_op jit(solution)/shard_map/product/pallas_call | solution.py:17
  204.9 28.4 %collective-permute-done.3.refs_1_ = f32[2,96,1024]{2,1,0:T(8,128)S(1)} collective-permute-done((f32[2,96,1024]{2,1,0:T(8,128)}, f32[2,96,1024]{2,1,0:T(8,128)S(1)}, u32[]{:S(2)}, u32[]{:S(2)}) %collective-permute-start.3) | collective-permute-done | bytes 786464 | tf_op jit(solution)/shard_map/ppermute | solution.py:264
  233.3 14.7 %collective-permute-done.4.refs_2_ = f32[2,96,1024]{2,1,0:T(8,128)S(1)} collective-permute-done((f32[2,96,1024]{2,1,0:T(8,128)}, f32[2,96,1024]{2,1,0:T(8,128)S(1)}, u32[]{:S(2)}, u32[]{:S(2)}) %collective-permute-start.4) | collective-permute-done | bytes 786464 | tf_op jit(solution)/shard_map/ppermute | solution.py:264
  259.6 14.6 %collective-permute-done.refs_5_ = f32[2,64,1024]{2,1,0:T(8,128)S(1)} collective-permute-done((f32[2,64,1024]{2,1,0:T(8,128)S(1)}, f32[2,64,1024]{2,1,0:T(8,128)S(1)}, u32[]{:S(2)}, u32[]{:S(2)}) %collective-permute-start) | collective-permute-done | bytes 524320 | tf_op jit(solution)/shard_map/ppermute | solution.py:264
  274.2 12.0 %collective-permute-done.2.refs_7_ = f32[2,64,1024]{2,1,0:T(8,128)S(1)} collective-permute-done((f32[2,64,1024]{2,1,0:T(8,128)S(1)}, f32[2,64,1024]{2,1,0:T(8,128)S(1)}, u32[]{:S(2)}, u32[]{:S(2)}) %collective-permute-start.2) | collective-permute-done | bytes 524320 | tf_op jit(solution)/shard_map/ppermute | solution.py:264
  286.2 9.1 %product.4 = f32[4,2,64,1024]{3,2,1,0:T(8,128)} custom-call(s32[1]{0:T(128)} %bitcast.place_ref, f32[1,2,1024,1024]{3,2,1,0:T(8,128)} %refs_3_.7, f32[1,2,1024,1024]{3,2,1,0:T(8,128)} %refs_3_.7, f32[1,2,1024,1024]{3,2,1,0:T(8,128)} %refs_3_.7, f32[1,2,1024,1024]{3,2,1,0:T(8,128)} %refs_3_.7, f32[2,64,1024]{2,1,0:T(8,128)S(1)} %get-tuple-element.50.refs_4_, ...), custom_call_target="tpu_custom_call" | custom-call | flops 4294967296 | bytes 4194304 | tf_op jit(solution)/shard_map/product/pallas_call | solution.py:17
  295.3 32.2 %all-to-all-done.2 = f32[8,96,1024]{2,1,0:T(8,128)} async-done(((f32[8,96,1024]{2,1,0:T(8,128)}), f32[8,96,1024]{2,1,0:T(8,128)}, u32[]{:S(2)}, u32[]{:S(2)}) %all-to-all-start.2) | async-done | bytes 3145760 | tf_op jit(solution)/shard_map/all_to_all | solution.py:258
  333.2 17.0 %collective-permute-done.6.refs_5_ = f32[2,96,1024]{2,1,0:T(8,128)S(1)} collective-permute-done((f32[2,96,1024]{2,1,0:T(8,128)S(1)}, f32[2,96,1024]{2,1,0:T(8,128)S(1)}, u32[]{:S(2)}, u32[]{:S(2)}) %collective-permute-start.6) | collective-permute-done | bytes 786464 | tf_op jit(solution)/shard_map/ppermute | solution.py:264
  350.2 16.1 %collective-permute-done.7.refs_6_ = f32[2,96,1024]{2,1,0:T(8,128)S(1)} collective-permute-done((f32[2,96,1024]{2,1,0:T(8,128)S(1)}, f32[2,96,1024]{2,1,0:T(8,128)S(1)}, u32[]{:S(2)}, u32[]{:S(2)}) %collective-permute-start.7) | collective-permute-done | bytes 786464 | tf_op jit(solution)/shard_map/ppermute | solution.py:264
  366.3 11.5 %product.5 = f32[4,2,96,1024]{3,2,1,0:T(8,128)} custom-call(s32[1]{0:T(128)} %bitcast.place_ref, f32[1,2,1024,1024]{3,2,1,0:T(8,128)} %refs_3_.7, f32[1,2,1024,1024]{3,2,1,0:T(8,128)} %refs_3_.7, f32[1,2,1024,1024]{3,2,1,0:T(8,128)} %refs_3_.7, f32[1,2,1024,1024]{3,2,1,0:T(8,128)} %refs_3_.7, f32[2,96,1024]{2,1,0:T(8,128)S(1)} %get-tuple-element.58.refs_4_, ...), custom_call_target="tpu_custom_call" | custom-call | flops 6442450944 | bytes 6291456 | tf_op jit(solution)/shard_map/product/pallas_call | solution.py:17
  395.6 5.7 %collective-permute-done.27 = f32[2,2,32,256]{3,2,1,0:T(8,128)S(1)} collective-permute-done((f32[2,2,32,256]{3,2,1,0:T(8,128)S(1)}, f32[2,2,32,256]{3,2,1,0:T(8,128)S(1)}, u32[]{:S(2)}, u32[]{:S(2)}) %collective-permute-start.27) | collective-permute-done | bytes 131104 | tf_op jit(solution)/shard_map/ppermute | solution.py:264
  408.5 4.9 all-to-all-start.9
  419.2 4.8 collective-permute-done.21
  429.7 5.1 all-to-all-start.5
  436.4 13.8 %all-to-all-done.5 = f32[8,2,32,256]{3,2,1,0:T(8,128)S(1)} async-done(((f32[8,2,32,256]{3,2,1,0:T(8,128)}), f32[8,2,32,256]{3,2,1,0:T(8,128)S(1)}, u32[]{:S(2)}, u32[]{:S(2)}) %all-to-all-start.5) | async-done | bytes 524320 | tf_op jit(solution)/shard_map/all_to_all | solution.py:258
  455.9 7.4 %all-to-all-done.12.refs_7_ = f32[8,2,16,256]{3,2,1,0:T(8,128)S(1)} async-done(((f32[8,2,16,256]{3,2,1,0:T(8,128)}), f32[8,2,16,256]{3,2,1,0:T(8,128)S(1)}, u32[]{:S(2)}, u32[]{:S(2)}) %all-to-all-start.12) | async-done | bytes 262176 | tf_op jit(solution)/shard_map/all_to_all | solution.py:258
  482.1 24.4 %all_to_all.65 = f32[8,2,48,256]{3,2,1,0:T(8,128)} all-to-all(f32[8,2,48,256]{3,2,1,0:T(8,128)S(1)} %pad_maximum_fusion), channel_id=1, replica_groups=mesh['ia'=8,'ka'=4] {'ia'}, dimensions={0} | all-to-all | bytes 1572864 | tf_op jit(solution)/shard_map/all_to_all | solution.py:258
  514.9 10.4 %all-to-all-done.6.refs_4_ = f32[8,2,32,256]{3,2,1,0:T(8,128)S(1)} async-done(((f32[8,2,32,256]{3,2,1,0:T(8,128)}), f32[8,2,32,256]{3,2,1,0:T(8,128)S(1)}, u32[]{:S(2)}, u32[]{:S(2)}) %all-to-all-start.6) | async-done | bytes 524320 | tf_op jit(solution)/shard_map/all_to_all | solution.py:258
  525.2 24.4 %all_to_all.66.refs_5_ = f32[8,2,48,256]{3,2,1,0:T(8,128)S(1)} all-to-all(f32[8,2,48,256]{3,2,1,0:T(8,128)} %broadcast_select_fusion), channel_id=1, replica_groups=mesh['ia'=8,'ka'=4] {'ia'}, dimensions={0} | all-to-all | bytes 1572864 | tf_op jit(solution)/shard_map/all_to_all | solution.py:258
  (152 shorter events, 130.7 us)
Async XLA Ops:
  13.2 44.0 %all-to-all-start = ((f32[4,2,64,1024]{3,2,1,0:T(8,128)}), f32[4,2,64,1024]{3,2,1,0:T(8,128)}, u32[]{:S(2)}, u32[]{:S(2)}) async-start(f32[4,2,64,1024]{3,2,1,0:T(8,128)} %first_flip.1), calls=%async_computation | async-start | bytes 4194304 | tf_op jit(solution)/shard_map/all_to_all | solution.py:258
  21.2 29.2 %collective-permute-start.15 = (f32[2,32,1024]{2,1,0:T(8,128)S(1)}, f32[2,32,1024]{2,1,0:T(8,128)S(1)}, u32[]{:S(2)}, u32[]{:S(2)}) collective-permute-start(f32[2,32,1024]{2,1,0:T(8,128)S(1)} %get-tuple-element.71), channel_id=1, source_target_pairs={{0,1},{1,0},{2,3},{3,2},{4,5},{5,4},{6,7},{7,6},{8,9},{9,8},{10,11... | collective-permute-start | bytes 786440 | tf_op jit(solution)/shard_map/ppermute | solution.py:264
  26.2 24.2 %collective-permute-start.16 = (f32[2,32,1024]{2,1,0:T(8,128)S(1)}, f32[2,32,1024]{2,1,0:T(8,128)S(1)}, u32[]{:S(2)}, u32[]{:S(2)}) collective-permute-start(f32[2,32,1024]{2,1,0:T(8,128)S(1)} %get-tuple-element.72), channel_id=1, source_target_pairs={{0,2},{1,3},{2,0},{3,1},{4,6},{5,7},{6,4},{7,5},{8,10},{9,11},{10,... | collective-permute-start | bytes 786440 | tf_op jit(solution)/shard_map/ppermute | solution.py:264
  30.6 25.6 %collective-permute-start.17 = (f32[2,32,1024]{2,1,0:T(8,128)S(1)}, f32[2,32,1024]{2,1,0:T(8,128)S(1)}, u32[]{:S(2)}, u32[]{:S(2)}) collective-permute-start(f32[2,32,1024]{2,1,0:T(8,128)S(1)} %get-tuple-element.73), channel_id=1, source_target_pairs={{0,3},{1,2},{2,1},{3,0},{4,7},{5,6},{6,5},{7,4},{8,11},{9,10},{10,... | collective-permute-start | bytes 786440 | tf_op jit(solution)/shard_map/ppermute | solution.py:264
  57.2 33.4 %all-to-all-start.4 = ((f32[8,32,1024]{2,1,0:T(8,128)}), f32[8,32,1024]{2,1,0:T(8,128)S(1)}, u32[]{:S(2)}, u32[]{:S(2)}) async-start(f32[8,32,1024]{2,1,0:T(8,128)} %bitcast.12), calls=%async_computation.4 | async-start | bytes 2097152 | tf_op jit(solution)/shard_map/all_to_all | solution.py:258
  62.4 25.6 %collective-permute-start.10 = (f32[2,64,1024]{2,1,0:T(8,128)S(1)}, f32[2,64,1024]{2,1,0:T(8,128)S(1)}, u32[]{:S(2)}, u32[]{:S(2)}) collective-permute-start(f32[2,64,1024]{2,1,0:T(8,128)S(1)} %get-tuple-element.64), channel_id=1, source_target_pairs={{0,2},{1,3},{2,0},{3,1},{4,6},{5,7},{6,4},{7,5},{8,10},{9,11},{10,... | collective-permute-start | bytes 1572872 | tf_op jit(solution)/shard_map/ppermute | solution.py:264
  62.9 25.0 %collective-permute-start.11 = (f32[2,64,1024]{2,1,0:T(8,128)S(1)}, f32[2,64,1024]{2,1,0:T(8,128)S(1)}, u32[]{:S(2)}, u32[]{:S(2)}) collective-permute-start(f32[2,64,1024]{2,1,0:T(8,128)S(1)} %get-tuple-element.65), channel_id=1, source_target_pairs={{0,3},{1,2},{2,1},{3,0},{4,7},{5,6},{6,5},{7,4},{8,11},{9,10},{10,... | collective-permute-start | bytes 1572872 | tf_op jit(solution)/shard_map/ppermute | solution.py:264
  64.4 24.8 %collective-permute-start.9 = (f32[2,64,1024]{2,1,0:T(8,128)S(1)}, f32[2,64,1024]{2,1,0:T(8,128)S(1)}, u32[]{:S(2)}, u32[]{:S(2)}) collective-permute-start(f32[2,64,1024]{2,1,0:T(8,128)S(1)} %get-tuple-element.63), channel_id=1, source_target_pairs={{0,1},{1,0},{2,3},{3,2},{4,5},{5,4},{6,7},{7,6},{8,9},{9,8},{10,11... | collective-permute-start | bytes 1572872 | tf_op jit(solution)/shard_map/ppermute | solution.py:264
  90.6 53.9 %all-to-all-start.3 = ((f32[8,64,1024]{2,1,0:T(8,128)}), f32[8,64,1024]{2,1,0:T(8,128)S(1)}, u32[]{:S(2)}, u32[]{:S(2)}) async-start(f32[8,64,1024]{2,1,0:T(8,128)} %bitcast.27), calls=%async_computation.3 | async-start | bytes 4194304 | tf_op jit(solution)/shard_map/all_to_all | solution.py:258
  96.4 53.1 %collective-permute-start.18 = (f32[2,32,1024]{2,1,0:T(8,128)}, f32[2,32,1024]{2,1,0:T(8,128)S(1)}, u32[]{:S(2)}, u32[]{:S(2)}) collective-permute-start(f32[2,32,1024]{2,1,0:T(8,128)} %get-tuple-element.75), channel_id=1, source_target_pairs={{0,1},{1,0},{2,3},{3,2},{4,5},{5,4},{6,7},{7,6},{8,9},{9,8},{10,11... | collective-permute-start | bytes 786440 | tf_op jit(solution)/shard_map/ppermute | solution.py:264
  97.0 52.6 %collective-permute-start.19 = (f32[2,32,1024]{2,1,0:T(8,128)}, f32[2,32,1024]{2,1,0:T(8,128)S(1)}, u32[]{:S(2)}, u32[]{:S(2)}) collective-permute-start(f32[2,32,1024]{2,1,0:T(8,128)} %get-tuple-element.76), channel_id=1, source_target_pairs={{0,2},{1,3},{2,0},{3,1},{4,6},{5,7},{6,4},{7,5},{8,10},{9,11},{10,... | collective-permute-start | bytes 786440 | tf_op jit(solution)/shard_map/ppermute | solution.py:264
  97.5 52.1 %collective-permute-start.20 = (f32[2,32,1024]{2,1,0:T(8,128)}, f32[2,32,1024]{2,1,0:T(8,128)S(1)}, u32[]{:S(2)}, u32[]{:S(2)}) collective-permute-start(f32[2,32,1024]{2,1,0:T(8,128)} %get-tuple-element.77), channel_id=1, source_target_pairs={{0,3},{1,2},{2,1},{3,0},{4,7},{5,6},{6,5},{7,4},{8,11},{9,10},{10,... | collective-permute-start | bytes 786440 | tf_op jit(solution)/shard_map/ppermute | solution.py:264
  145.9 105.5 %all-to-all-start.1 = ((f32[8,64,1024]{2,1,0:T(8,128)}), f32[8,64,1024]{2,1,0:T(8,128)S(1)}, u32[]{:S(2)}, u32[]{:S(2)}) async-start(f32[8,64,1024]{2,1,0:T(8,128)} %bitcast.1), calls=%async_computation.1 | async-start | bytes 4194304 | tf_op jit(solution)/shard_map/all_to_all | solution.py:258
  149.5 228.3 %reduce-scatter.19.cloned.1.call-start = ((), (), s32[]{:S(2)}) async-start(), calls=%async_computation.20 | async-start | bytes 1310720
  156.4 234.5 %reduce-scatter.17.cloned.1.call-start = ((), (), s32[]{:S(2)}) async-start(), calls=%async_computation.19 | async-start | bytes 2621440
  158.2 20.4 %collective-permute-start.12 = (f32[2,64,1024]{2,1,0:T(8,128)S(1)}, f32[2,64,1024]{2,1,0:T(8,128)S(1)}, u32[]{:S(2)}, u32[]{:S(2)}) collective-permute-start(f32[2,64,1024]{2,1,0:T(8,128)S(1)} %get-tuple-element.67), channel_id=1, source_target_pairs={{0,1},{1,0},{2,3},{3,2},{4,5},{5,4},{6,7},{7,6},{8,9},{9,8},{10,11... | collective-permute-start | bytes 1572872 | tf_op jit(solution)/shard_map/ppermute | solution.py:264
  158.8 27.5 %collective-permute-start.13 = (f32[2,64,1024]{2,1,0:T(8,128)S(1)}, f32[2,64,1024]{2,1,0:T(8,128)S(1)}, u32[]{:S(2)}, u32[]{:S(2)}) collective-permute-start(f32[2,64,1024]{2,1,0:T(8,128)S(1)} %get-tuple-element.68), channel_id=1, source_target_pairs={{0,2},{1,3},{2,0},{3,1},{4,6},{5,7},{6,4},{7,5},{8,10},{9,11},{10,... | collective-permute-start | bytes 1572872 | tf_op jit(solution)/shard_map/ppermute | solution.py:264
  159.3 32.9 %collective-permute-start.14 = (f32[2,64,1024]{2,1,0:T(8,128)S(1)}, f32[2,64,1024]{2,1,0:T(8,128)S(1)}, u32[]{:S(2)}, u32[]{:S(2)}) collective-permute-start(f32[2,64,1024]{2,1,0:T(8,128)S(1)} %get-tuple-element.69), channel_id=1, source_target_pairs={{0,3},{1,2},{2,1},{3,0},{4,7},{5,6},{6,5},{7,4},{8,11},{9,10},{10,... | collective-permute-start | bytes 1572872 | tf_op jit(solution)/shard_map/ppermute | solution.py:264
  201.4 32.0 %collective-permute-start.3 = (f32[2,96,1024]{2,1,0:T(8,128)}, f32[2,96,1024]{2,1,0:T(8,128)S(1)}, u32[]{:S(2)}, u32[]{:S(2)}) collective-permute-start(f32[2,96,1024]{2,1,0:T(8,128)} %copy-done.14), channel_id=1, source_target_pairs={{0,1},{1,0},{2,3},{3,2},{4,5},{5,4},{6,7},{7,6},{8,9},{9,8},{10,11... | collective-permute-start | bytes 2359304 | tf_op jit(solution)/shard_map/ppermute | solution.py:264
  202.1 45.9 %collective-permute-start.4 = (f32[2,96,1024]{2,1,0:T(8,128)}, f32[2,96,1024]{2,1,0:T(8,128)S(1)}, u32[]{:S(2)}, u32[]{:S(2)}) collective-permute-start(f32[2,96,1024]{2,1,0:T(8,128)} %copy-done.15), channel_id=1, source_target_pairs={{0,2},{1,3},{2,0},{3,1},{4,6},{5,7},{6,4},{7,5},{8,10},{9,11},{10,... | collective-permute-start | bytes 2359304 | tf_op jit(solution)/shard_map/ppermute | solution.py:264
  203.4 46.0 %collective-permute-start.5 = (f32[2,96,1024]{2,1,0:T(8,128)}, f32[2,96,1024]{2,1,0:T(8,128)S(1)}, u32[]{:S(2)}, u32[]{:S(2)}) collective-permute-start(f32[2,96,1024]{2,1,0:T(8,128)} %copy-done.16), channel_id=1, source_target_pairs={{0,3},{1,2},{2,1},{3,0},{4,7},{5,6},{6,5},{7,4},{8,11},{9,10},{10,... | collective-permute-start | bytes 2359304 | tf_op jit(solution)/shard_map/ppermute | solution.py:264
  251.4 76.2 %all-to-all-start.2 = ((f32[8,96,1024]{2,1,0:T(8,128)}), f32[8,96,1024]{2,1,0:T(8,128)}, u32[]{:S(2)}, u32[]{:S(2)}) async-start(f32[8,96,1024]{2,1,0:T(8,128)} %bitcast.38), calls=%async_computation.2 | async-start | bytes 6291456 | tf_op jit(solution)/shard_map/all_to_all | solution.py:258
  255.9 157.6 %reduce-scatter.13.cloned.1.call-start = ((), (), s32[]{:S(2)}) async-start(), calls=%async_computation.17 | async-start | bytes 2621440
  258.5 27.7 %collective-permute-start.2 = (f32[2,64,1024]{2,1,0:T(8,128)S(1)}, f32[2,64,1024]{2,1,0:T(8,128)S(1)}, u32[]{:S(2)}, u32[]{:S(2)}) collective-permute-start(f32[2,64,1024]{2,1,0:T(8,128)S(1)} %get-tuple-element.53), channel_id=1, source_target_pairs={{0,3},{1,2},{2,1},{3,0},{4,7},{5,6},{6,5},{7,4},{8,11},{9,10},{10,... | collective-permute-start | bytes 1572872 | tf_op jit(solution)/shard_map/ppermute | solution.py:264
  295.3 171.5 %reduce-scatter.15.cloned.1.call-start = ((), (), s32[]{:S(2)}) async-start(), calls=%async_computation.18 | async-start | bytes 3932160
  329.7 20.5 %collective-permute-start.6 = (f32[2,96,1024]{2,1,0:T(8,128)S(1)}, f32[2,96,1024]{2,1,0:T(8,128)S(1)}, u32[]{:S(2)}, u32[]{:S(2)}) collective-permute-start(f32[2,96,1024]{2,1,0:T(8,128)S(1)} %get-tuple-element.59), channel_id=1, source_target_pairs={{0,1},{1,0},{2,3},{3,2},{4,5},{5,4},{6,7},{7,6},{8,9},{9,8},{10,11... | collective-permute-start | bytes 2359304 | tf_op jit(solution)/shard_map/ppermute | solution.py:264
  330.6 35.7 %collective-permute-start.7 = (f32[2,96,1024]{2,1,0:T(8,128)S(1)}, f32[2,96,1024]{2,1,0:T(8,128)S(1)}, u32[]{:S(2)}, u32[]{:S(2)}) collective-permute-start(f32[2,96,1024]{2,1,0:T(8,128)S(1)} %get-tuple-element.60), channel_id=1, source_target_pairs={{0,2},{1,3},{2,0},{3,1},{4,6},{5,7},{6,4},{7,5},{8,10},{9,11},{10,... | collective-permute-start | bytes 2359304 | tf_op jit(solution)/shard_map/ppermute | solution.py:264
  332.1 34.2 %collective-permute-start.8 = (f32[2,96,1024]{2,1,0:T(8,128)S(1)}, f32[2,96,1024]{2,1,0:T(8,128)S(1)}, u32[]{:S(2)}, u32[]{:S(2)}) collective-permute-start(f32[2,96,1024]{2,1,0:T(8,128)S(1)} %get-tuple-element.61), channel_id=1, source_target_pairs={{0,3},{1,2},{2,1},{3,0},{4,7},{5,6},{6,5},{7,4},{8,11},{9,10},{10,... | collective-permute-start | bytes 2359304 | tf_op jit(solution)/shard_map/ppermute | solution.py:264
  387.5 21.0 %all-to-all-start.11 = ((f32[8,2,16,256]{3,2,1,0:T(8,128)}), f32[8,2,16,256]{3,2,1,0:T(8,128)S(1)}, u32[]{:S(2)}, u32[]{:S(2)}) async-start(f32[8,2,16,256]{3,2,1,0:T(8,128)} %pad_maximum_fusion.3), calls=%async_computation.11 | async-start | bytes 524288 | tf_op jit(solution)/shard_map/all_to_all | solution.py:258
  408.5 21.2 %all-to-all-start.9 = ((f32[8,2,32,256]{3,2,1,0:T(8,128)}), f32[8,2,32,256]{3,2,1,0:T(8,128)S(1)}, u32[]{:S(2)}, u32[]{:S(2)}) async-start(f32[8,2,32,256]{3,2,1,0:T(8,128)} %pad_maximum_fusion.2), calls=%async_computation.9 | async-start | bytes 1048576 | tf_op jit(solution)/shard_map/all_to_all | solution.py:258
  429.7 20.5 %all-to-all-start.5 = ((f32[8,2,32,256]{3,2,1,0:T(8,128)}), f32[8,2,32,256]{3,2,1,0:T(8,128)S(1)}, u32[]{:S(2)}, u32[]{:S(2)}) async-start(f32[8,2,32,256]{3,2,1,0:T(8,128)} %pad_maximum_fusion.1), calls=%async_computation.5 | async-start | bytes 1048576 | tf_op jit(solution)/shard_map/all_to_all | solution.py:258
  463.3 18.8 %all-to-all-start.10 = ((f32[8,2,32,256]{3,2,1,0:T(8,128)}), f32[8,2,32,256]{3,2,1,0:T(8,128)S(1)}, u32[]{:S(2)}, u32[]{:S(2)}) async-start(f32[8,2,32,256]{3,2,1,0:T(8,128)} %bitcast.21), calls=%async_computation.10 | async-start | bytes 1048576 | tf_op jit(solution)/shard_map/all_to_all | solution.py:258
  (34 other events, 438.7 us)
Sparse Core Ops, SparseCore 0:
  156.5 36.8 reduce-scatter.18
  201.5 66.1 reduce-scatter.16
  295.4 34.2 reduce-scatter.12
  377.9 53.4 reduce-scatter.14

commit v4 on v3

--- a/solution.py
+++ b/solution.py
@@ -7,7 +7,8 @@
 from jax.experimental.pallas import tpu as pltpu
 from jax.sharding import PartitionSpec as P
 
-CHUNKS = (2, 3, 2, 1)
+CHUNKS = (1, 2, 3, 2)
+GROUPS = ((0, 1), (2,), (3,))
 LANES = 128
 VMEM_BYTES = 48 * 1024 * 1024
 
@@ -53,41 +54,50 @@
     )
 
 
-def flip_kernel(spans, place_ref, blocks_ref, *pieces):
+def flip_kernel(spans, low, place_ref, blocks_ref, after_ref, *pieces):
     flipped = blocks_ref[0, 0].T
     for (start, rows), piece in zip(spans, pieces):
-        piece[0] = flipped[start : start + rows]
-
-
-def flip(place, amplitudes, sections, e, spans):
+        piece[0] = flipped[start - low : start - low + rows]
+
+
+def flip(place, amplitudes, sections, e, spans, after):
     pairs, virtuals = amplitudes.shape[1], amplitudes.shape[3]
     wide = virtuals // sections
-    return call(
-        functools.partial(flip_kernel, spans),
+    low = spans[0][0] // LANES * LANES
+    read = LANES if sum(spans[-1]) <= low + LANES else wide
+    low = low if read == LANES else 0
+    return call(
+        functools.partial(flip_kernel, spans, low),
         "flip",
         place,
-        [amplitudes],
-        [pl.BlockSpec((1, 1, virtuals, wide), lambda d, at: (0, d, 0, at[0] ^ e))],
+        [amplitudes, after],
+        [
+            pl.BlockSpec(
+                (1, 1, virtuals, read),
+                lambda d, at: (0, d, 0, (at[0] ^ e) * (wide // read) + low // read),
+            ),
+            pl.BlockSpec(memory_space=pl.ANY),
+        ],
         [pl.BlockSpec((1, rows, virtuals), lambda d, at: (d, 0, 0)) for _, rows in spans],
         [jax.ShapeDtypeStruct((pairs, rows, virtuals), jnp.float32) for _, rows in spans],
         (pairs,),
     )
 
 
-def gather_kernel(place_ref, *refs):
-    pieces, out_ref = refs[:-1], refs[-1]
+def gather_kernel(ordered, place_ref, *refs):
+    pieces, out_ref = refs[:-2], refs[-1]
     for e, piece in enumerate(pieces):
-        out_ref[place_ref[0] ^ e] = piece[...]
-
-
-def gather(place, pieces):
+        out_ref[place_ref[0] ^ e if ordered else e] = piece[...]
+
+
+def gather(place, pieces, after, ordered=True):
     shape = (len(pieces), *pieces[0].shape)
     return call(
-        gather_kernel,
+        functools.partial(gather_kernel, ordered),
         "gather",
         place,
-        pieces,
-        [whole(pieces[0].shape)] * len(pieces),
+        [*pieces, after],
+        [whole(pieces[0].shape)] * len(pieces) + [pl.BlockSpec(memory_space=pl.ANY)],
         whole(shape),
         jax.ShapeDtypeStruct(shape, jnp.float32),
         (1,),
@@ -192,53 +202,67 @@
     )
 
 
-def cut_kernel(place_ref, total_ref, *cut_refs):
-    parts, _, short, wide = cut_refs[0].shape
+def cut_kernel(chunks, place_ref, *refs):
+    total_refs, cut_refs = refs[:chunks], refs[chunks:]
+    parts, _, _, wide = cut_refs[0].shape
     for e, cut_ref in enumerate(cut_refs):
-        start = pl.multiple_of((place_ref[0] ^ e) * wide, wide)
-        for part in range(parts):
-            cut_ref[part] = total_ref[:, part * short : (part + 1) * short, pl.ds(start, wide)]
-
-
-def cut(place, total, sections, parts):
-    slots, rows, virtuals = total.shape
+        columns = pl.ds(pl.multiple_of((place_ref[0] ^ e) * wide, wide), wide)
+        at = 0
+        for total_ref in total_refs:
+            short = total_ref.shape[1] // parts
+            for part in range(parts):
+                cut_ref[part, :, at : at + short] = total_ref[
+                    :, part * short : (part + 1) * short, columns
+                ]
+            at += short
+
+
+def cut(place, totals, sections, parts):
+    slots, _, virtuals = totals[0].shape
+    rows = sum(total.shape[1] for total in totals)
     shape = (parts, slots, rows // parts, virtuals // sections)
     return call(
-        cut_kernel,
+        functools.partial(cut_kernel, len(totals)),
         "cut",
         place,
-        [total],
-        [whole(total.shape)],
+        totals,
+        [whole(total.shape) for total in totals],
         [whole(shape)] * sections,
         [jax.ShapeDtypeStruct(shape, jnp.float32)] * sections,
         (1,),
     )
 
 
-def finish_kernel(spans, place_ref, *refs):
+def finish_kernel(spans, groups, place_ref, *refs):
     chunks = len(spans)
-    own_refs, delivered_refs = refs[:chunks], refs[chunks : 2 * chunks]
-    out_ref, columns_ref = refs[2 * chunks :]
+    own_refs, delivered_refs = refs[:chunks], refs[chunks : chunks + len(groups)]
+    out_ref, columns_ref = refs[chunks + len(groups) :]
     wide = out_ref.shape[2]
     sections = columns_ref.shape[0] // wide
-    for (start, _), delivered_ref in zip(spans, delivered_refs):
-        pieces, _, short, _ = delivered_ref.shape
-        parts = pieces // sections
+    for group, delivered_ref in zip(groups, delivered_refs):
+        parts = delivered_ref.shape[0] // sections
         for e in range(sections):
-            base = (place_ref[0] ^ e) * wide + start
+            base = (place_ref[0] ^ e) * wide
             for part in range(parts):
-                spot = pl.multiple_of(base + part * short, 8)
-                columns_ref[pl.ds(spot, short)] = delivered_ref[e * parts + part, 0]
+                at = 0
+                for chunk in group:
+                    start, rows = spans[chunk]
+                    short = rows // parts
+                    spot = pl.multiple_of(base + start + part * short, 8)
+                    columns_ref[pl.ds(spot, short)] = delivered_ref[
+                        e * parts + part, 0, at : at + short
+                    ]
+                    at += short
     turned = columns_ref[...].T
     for (start, rows), own_ref in zip(spans, own_refs):
         out_ref[0, 0, start : start + rows] = own_ref[0] + turned[start : start + rows]
 
 
-def finish(place, spans, own, delivered):
+def finish(place, spans, groups, own, delivered):
     slots, _, virtuals = own[0].shape
     wide = delivered[0].shape[-1]
     return call(
-        functools.partial(finish_kernel, spans),
+        functools.partial(finish_kernel, spans, groups),
         "finish",
         place,
         list(own) + list(delivered),
@@ -278,27 +302,34 @@
     source_row = (pair_list * slots + partner_slot).reshape(-1)
 
     first = first_flip(place, amplitudes, sections, sizes[0])
-    flipped = [flip(place, amplitudes, sections, e, spans[1:]) for e in range(sections)]
+    second = [flip(place, amplitudes, sections, e, spans[1:2], first) for e in range(sections)]
+    across = [swap(first, "ka")]
+    later = [flip(place, amplitudes, sections, e, spans[2:], across[0]) for e in range(sections)]
+    flipped = [[*early, *late] for early, late in zip(second, later)]
     masked = mask_blocks(integrals, tile_mask)
-
-    own, delivered = [], []
+    own = []
     for at, (start, rows) in enumerate(spans):
-        short = rows // pairs
-        if at == 0:
-            across = swap(first, "ka")
-        else:
-            across = gather(place, spread([pieces[at - 1] for pieces in flipped]))
-        crossed = swap(across.reshape(occupied, rows, virtuals), "ia")
-        crossed = crossed.reshape(sections, pairs, rows, virtuals)
-        mirrored = spread(scatter(place, crossed))
-        partial_rows = product(place, amplitudes, mirrored, masked, start)
-        summed = lax.psum_scatter(partial_rows, "ka", scatter_dimension=0, tiled=False)
-        own.append(summed)
-        columns = jnp.concatenate(spread(cut(place, summed, sections, pairs)))
-        met = swap(columns, "ia").reshape(occupied * slots, short, wide)
-        routed = jnp.take(met, source_row, axis=0).reshape(occupied, slots, short, wide)
-        delivered.append(swap(routed, "ia"))
-    return finish(place, spans, own, delivered)
+        if at > 0:
+            met = spread([pieces[at - 1] for pieces in flipped])
+            across.append(gather(place, met, mirrored[-1] if at > 1 else across[0]))
+        if at > 0:
+            mirrored = spread(returned)
+            partial_rows = product(place, amplitudes, mirrored, masked, spans[at - 1][0])
+            own.append(lax.psum_scatter(partial_rows, "ka", scatter_dimension=0, tiled=False))
+        crossed = swap(across[at].reshape(occupied, rows, virtuals), "ia")
+        returned = scatter(place, crossed.reshape(sections, pairs, rows, virtuals))
+    partial_rows = product(place, amplitudes, spread(returned), masked, spans[-1][0])
+    own.append(lax.psum_scatter(partial_rows, "ka", scatter_dimension=0, tiled=False))
+
+    delivered = []
+    for group in GROUPS:
+        columns = spread(cut(place, [own[at] for at in group], sections, pairs))
+        columns = gather(place, columns, returned[0], ordered=False)
+        piece = columns.shape[-2:]
+        met = swap(columns.reshape(occupied, slots, *piece), "ia")
+        routed = jnp.take(met.reshape(occupied * slots, *piece), source_row, axis=0)
+        delivered.append(swap(routed.reshape(occupied, slots, *piece), "ia"))
+    return finish(place, spans, GROUPS, own, delivered)
 
 
 def solution(mesh):

time: 560 us -> 564 us (level)
  blocking collectives: 48.8 us -> 102 us
  waiting for transfers between devices: 317 us -> 275 us
  starting transfers between devices: 86.5 us -> 68.6 us
  Pallas kernels: 68.1 us -> 80.6 us
    all_to_all x2 -> x3, blocking collectives: 48.8 us -> 102 us  [swap(): return lax.all_to_all(array, axis, split_axis=0, concat_axis=0, tiled=True)]
    all_to_all x11 -> x8, waiting for transfers between devices: 101 us -> 78.9 us  [swap(): return lax.all_to_all(array, axis, split_axis=0, concat_axis=0, tiled=True)]
    ppermute x33 -> x30, waiting for transfers between devices: 216 us -> 196 us  [spread(): lax.ppermute(pieces[e], 'ka', [(q, q ^ e) for q in range(count)])]
    all_to_all x11 -> x8, starting transfers between devices: 47.1 us -> 33.5 us  [swap(): return lax.all_to_all(array, axis, split_axis=0, concat_axis=0, tiled=True)]
    pallas_call x22 -> x28, Pallas kernels: 68.1 us -> 80.6 us  [call(): pl.pallas_call(kernel, grid_spec=pltpu.PrefetchScalarGridSpec(num_scalar_...]
    unnamed x37 -> x55, local copies, waits for them, and re-layouts: 12.2 us -> 16.9 us
    ppermute x33 -> x30, starting transfers between devices: 39.2 us -> 34.9 us  [spread(): lax.ppermute(pieces[e], 'ka', [(q, q ^ e) for q in range(count)])]
  transfers between devices with their start and end apart: 48 -> 42, of which waited for: 32 -> 24; matrix products, arithmetic and copies ran while one was open for 2% -> 1% of each run, Pallas kernels for 11% -> 13%
where the time goes in v4:
time: 564 us; the launch traced here: 562 us
  waiting for transfers between devices  275 us (49%)
  blocking collectives  102 us (18%)
  Pallas kernels  80.6 us (14%)
  starting transfers between devices  68.6 us (12%)
  local copies, waits for them, and re-layouts  20.6 us (4%)
  between operations  13.5 us (2%)
    ppermute x30, waiting for transfers between devices, spread(): lax.ppermute(pieces[e], 'ka', [(q, q ^ e) for q in range(count)])  196 us
    all_to_all x3, blocking collectives, swap(): return lax.all_to_all(array, axis, split_axis=0, concat_axis=0, tiled=True)  102 us
    pallas_call x28, Pallas kernels, call(): pl.pallas_call(kernel, grid_spec=pltpu.PrefetchScalarGridSpec(num_scalar_...  80.6 us
    all_to_all x8, waiting for transfers between devices, swap(): return lax.all_to_all(array, axis, split_axis=0, concat_axis=0, tiled=True)  78.9 us
    ppermute x30, starting transfers between devices, spread(): lax.ppermute(pieces[e], 'ka', [(q, q ^ e) for q in range(count)])  34.9 us
    all_to_all x8, starting transfers between devices, swap(): return lax.all_to_all(array, axis, split_axis=0, concat_axis=0, tiled=True)  33.5 us
    unnamed x55, local copies, waits for them, and re-layouts  16.9 us
  transfers between devices with their start and end apart: 42, of which 24 were waited for; matrix products, arithmetic and copies ran while one was open for 1% of the time, Pallas kernels for 13%

profile of v4, /device:TPU:0, one launch (start us, length us, event | category | flops | bytes accessed | tf_op | source)
XLA Modules:
  0.0 561.8 jit_solution(13518896577958341331)
XLA Ops:
  6.5 6.4 %first_flip.1.after_ref = f32[4,2,32,1024]{3,2,1,0:T(8,128)} custom-call(s32[1]{0:T(128)} %bitcast.place_ref, f32[1,2,1024,1024]{3,2,1,0:T(8,128)} %refs_3_.7), custom_call_target="tpu_custom_call" | custom-call | bytes 2097152 | tf_op jit(solution)/shard_map/first_flip/pallas_call | solution.py:18
  13.0 5.2 all-to-all-start
  27.8 16.6 %collective-permute-done.3.refs_1_ = f32[2,64,1024]{2,1,0:T(8,128)S(1)} collective-permute-done((f32[2,64,1024]{2,1,0:T(8,128)S(1)}, f32[2,64,1024]{2,1,0:T(8,128)S(1)}, u32[]{:S(2)}, u32[]{:S(2)}) %collective-permute-start.3) | collective-permute-done | bytes 524320 | tf_op jit(solution)/shard_map/ppermute | solution.py:288
  44.4 11.3 %collective-permute-done.5.refs_3_ = f32[2,64,1024]{2,1,0:T(8,128)S(1)} collective-permute-done((f32[2,64,1024]{2,1,0:T(8,128)S(1)}, f32[2,64,1024]{2,1,0:T(8,128)S(1)}, u32[]{:S(2)}, u32[]{:S(2)}) %collective-permute-start.5) | collective-permute-done | bytes 524320 | tf_op jit(solution)/shard_map/ppermute | solution.py:288
  55.9 53.9 %all_to_all.55 = f32[8,64,1024]{2,1,0:T(8,128)S(1)} all-to-all(f32[8,64,1024]{2,1,0:T(8,128)S(1)} %bitcast.28), channel_id=1, replica_groups=mesh['ia'=8,'ka'=4] {'ia'}, dimensions={0} | all-to-all | bytes 4194304 | tf_op jit(solution)/shard_map/all_to_all | solution.py:282
  130.8 9.1 %all-to-all-done.1 = f32[8,32,1024]{2,1,0:T(8,128)S(1)} async-done(((f32[8,32,1024]{2,1,0:T(8,128)}), f32[8,32,1024]{2,1,0:T(8,128)S(1)}, u32[]{:S(2)}, u32[]{:S(2)}) %all-to-all-start.1) | async-done | bytes 1048608 | tf_op jit(solution)/shard_map/all_to_all | solution.py:282
  142.6 15.9 %collective-permute-done.16.refs_2_ = f32[2,64,1024]{2,1,0:T(8,128)} collective-permute-done((f32[2,64,1024]{2,1,0:T(8,128)}, f32[2,64,1024]{2,1,0:T(8,128)}, u32[]{:S(2)}, u32[]{:S(2)}) %collective-permute-start.16) | collective-permute-done | bytes 524320 | tf_op jit(solution)/shard_map/ppermute | solution.py:288
  160.0 8.7 %mask.1.refs_8_ = bf16[2,2,1024,1024]{3,2,1,0:T(8,128)(2,1)} custom-call(s32[2,2,8,8]{3,2,1,0:T(8,128)S(1)} %bitcast.38, bf16[1,2,2,1024,1024]{4,3,2,1,0:T(8,128)(2,1)} %integrals_ref.1), custom_call_target="tpu_custom_call" | custom-call | bytes 16777216 | tf_op jit(solution)/shard_map/mask/pallas_call | solution.py:18
  174.3 5.0 all-to-all-start.4
  183.7 6.2 %product.4 = f32[4,2,32,1024]{3,2,1,0:T(8,128)S(1)} custom-call(s32[1]{0:T(128)} %bitcast.place_ref, f32[1,2,1024,1024]{3,2,1,0:T(8,128)} %refs_3_.7, f32[1,2,1024,1024]{3,2,1,0:T(8,128)} %refs_3_.7, f32[1,2,1024,1024]{3,2,1,0:T(8,128)} %refs_3_.7, f32[1,2,1024,1024]{3,2,1,0:T(8,128)} %refs_3_.7, f32[2,32,1024]{2,1,0:T(8,128)S(1)} %copy-done.14, ...), custom_call_target="tpu_custom_call" | custom-call | flops 2147483648 | bytes 2097152 | tf_op jit(solution)/shard_map/product/pallas_call | solution.py:18
  193.0 18.1 %collective-permute-done.6.refs_5_ = f32[2,64,1024]{2,1,0:T(8,128)S(1)} collective-permute-done((f32[2,64,1024]{2,1,0:T(8,128)}, f32[2,64,1024]{2,1,0:T(8,128)S(1)}, u32[]{:S(2)}, u32[]{:S(2)}) %collective-permute-start.6) | collective-permute-done | bytes 524320 | tf_op jit(solution)/shard_map/ppermute | solution.py:288
  211.3 9.2 %product.5 = f32[4,2,64,1024]{3,2,1,0:T(8,128)} custom-call(s32[1]{0:T(128)} %bitcast.place_ref, f32[1,2,1024,1024]{3,2,1,0:T(8,128)} %refs_3_.7, f32[1,2,1024,1024]{3,2,1,0:T(8,128)} %refs_3_.7, f32[1,2,1024,1024]{3,2,1,0:T(8,128)} %refs_3_.7, f32[1,2,1024,1024]{3,2,1,0:T(8,128)} %refs_3_.7, f32[2,64,1024]{2,1,0:T(8,128)S(1)} %copy-done.12, ...), custom_call_target="tpu_custom_call" | custom-call | flops 4294967296 | bytes 4194304 | tf_op jit(solution)/shard_map/product/pallas_call | solution.py:18
  224.1 23.2 %collective-permute-done.9.refs_1_ = f32[2,96,1024]{2,1,0:T(8,128)S(1)} collective-permute-done((f32[2,96,1024]{2,1,0:T(8,128)}, f32[2,96,1024]{2,1,0:T(8,128)S(1)}, u32[]{:S(2)}, u32[]{:S(2)}) %collective-permute-start.9) | collective-permute-done | bytes 786464 | tf_op jit(solution)/shard_map/ppermute | solution.py:288
  247.4 6.0 %collective-permute-done.10.refs_2_ = f32[2,96,1024]{2,1,0:T(8,128)S(1)} collective-permute-done((f32[2,96,1024]{2,1,0:T(8,128)}, f32[2,96,1024]{2,1,0:T(8,128)S(1)}, u32[]{:S(2)}, u32[]{:S(2)}) %collective-permute-start.10) | collective-permute-done | bytes 786464 | tf_op jit(solution)/shard_map/ppermute | solution.py:288
  253.4 15.2 %collective-permute-done.11.refs_3_ = f32[2,96,1024]{2,1,0:T(8,128)S(1)} collective-permute-done((f32[2,96,1024]{2,1,0:T(8,128)}, f32[2,96,1024]{2,1,0:T(8,128)S(1)}, u32[]{:S(2)}, u32[]{:S(2)}) %collective-permute-start.11) | collective-permute-done | bytes 786464 | tf_op jit(solution)/shard_map/ppermute | solution.py:288
  271.6 4.5 all-to-all-start.3
  279.9 14.3 %collective-permute-done.18.refs_5_ = f32[2,64,1024]{2,1,0:T(8,128)S(1)} collective-permute-done((f32[2,64,1024]{2,1,0:T(8,128)S(1)}, f32[2,64,1024]{2,1,0:T(8,128)S(1)}, u32[]{:S(2)}, u32[]{:S(2)}) %collective-permute-start.18) | collective-permute-done | bytes 524320 | tf_op jit(solution)/shard_map/ppermute | solution.py:288
  294.2 11.9 %collective-permute-done.20.refs_7_ = f32[2,64,1024]{2,1,0:T(8,128)S(1)} collective-permute-done((f32[2,64,1024]{2,1,0:T(8,128)S(1)}, f32[2,64,1024]{2,1,0:T(8,128)S(1)}, u32[]{:S(2)}, u32[]{:S(2)}) %collective-permute-start.20) | collective-permute-done | bytes 524320 | tf_op jit(solution)/shard_map/ppermute | solution.py:288
  306.1 9.1 %product.7 = f32[4,2,64,1024]{3,2,1,0:T(8,128)} custom-call(s32[1]{0:T(128)} %bitcast.place_ref, f32[1,2,1024,1024]{3,2,1,0:T(8,128)} %refs_3_.7, f32[1,2,1024,1024]{3,2,1,0:T(8,128)} %refs_3_.7, f32[1,2,1024,1024]{3,2,1,0:T(8,128)} %refs_3_.7, f32[1,2,1024,1024]{3,2,1,0:T(8,128)} %refs_3_.7, f32[2,64,1024]{2,1,0:T(8,128)S(1)} %get-tuple-element.62.refs_4_, ...), custom_call_target="tpu_custom_call" | custom-call | flops 4294967296 | bytes 4194304 | tf_op jit(solution)/shard_map/product/pallas_call | solution.py:18
  315.3 32.3 %all-to-all-done.3 = f32[8,96,1024]{2,1,0:T(8,128)} async-done(((f32[8,96,1024]{2,1,0:T(8,128)}), f32[8,96,1024]{2,1,0:T(8,128)}, u32[]{:S(2)}, u32[]{:S(2)}) %all-to-all-start.3) | async-done | bytes 3145760 | tf_op jit(solution)/shard_map/all_to_all | solution.py:282
  353.4 17.0 %collective-permute-done.12.refs_5_ = f32[2,96,1024]{2,1,0:T(8,128)S(1)} collective-permute-done((f32[2,96,1024]{2,1,0:T(8,128)S(1)}, f32[2,96,1024]{2,1,0:T(8,128)S(1)}, u32[]{:S(2)}, u32[]{:S(2)}) %collective-permute-start.12) | collective-permute-done | bytes 786464 | tf_op jit(solution)/shard_map/ppermute | solution.py:288
  370.3 16.6 %collective-permute-done.13.refs_6_ = f32[2,96,1024]{2,1,0:T(8,128)S(1)} collective-permute-done((f32[2,96,1024]{2,1,0:T(8,128)S(1)}, f32[2,96,1024]{2,1,0:T(8,128)S(1)}, u32[]{:S(2)}, u32[]{:S(2)}) %collective-permute-start.13) | collective-permute-done | bytes 786464 | tf_op jit(solution)/shard_map/ppermute | solution.py:288
  386.9 11.5 %product.6 = f32[4,2,96,1024]{3,2,1,0:T(8,128)} custom-call(s32[1]{0:T(128)} %bitcast.place_ref, f32[1,2,1024,1024]{3,2,1,0:T(8,128)} %refs_3_.7, f32[1,2,1024,1024]{3,2,1,0:T(8,128)} %refs_3_.7, f32[1,2,1024,1024]{3,2,1,0:T(8,128)} %refs_3_.7, f32[1,2,1024,1024]{3,2,1,0:T(8,128)} %refs_3_.7, f32[2,96,1024]{2,1,0:T(8,128)S(1)} %get-tuple-element.54.refs_4_, ...), custom_call_target="tpu_custom_call" | custom-call | flops 6442450944 | bytes 6291456 | tf_op jit(solution)/shard_map/product/pallas_call | solution.py:18
  404.1 6.4 %collective-permute-done.21.refs_1_ = f32[2,2,48,256]{3,2,1,0:T(8,128)S(1)} collective-permute-done((f32[2,2,48,256]{3,2,1,0:T(8,128)S(1)}, f32[2,2,48,256]{3,2,1,0:T(8,128)S(1)}, u32[]{:S(2)}, u32[]{:S(2)}) %collective-permute-start.21) | collective-permute-done | bytes 196640 | tf_op jit(solution)/shard_map/ppermute | solution.py:288
  434.0 7.7 %all-to-all-done.5 = f32[8,2,48,256]{3,2,1,0:T(8,128)S(1)} async-done(((f32[8,2,48,256]{3,2,1,0:T(8,128)}), f32[8,2,48,256]{3,2,1,0:T(8,128)S(1)}, u32[]{:S(2)}, u32[]{:S(2)}) %all-to-all-start.5) | async-done | bytes 786464 | tf_op jit(solution)/shard_map/all_to_all | solution.py:282
  450.4 4.2 collective-permute-done.24.refs_1_
  454.6 5.4 collective-permute-done.25.refs_2_
  460.9 4.8 all-to-all-start.7
  468.2 18.4 %all-to-all-done.7 = f32[8,2,48,256]{3,2,1,0:T(8,128)S(1)} async-done(((f32[8,2,48,256]{3,2,1,0:T(8,128)}), f32[8,2,48,256]{3,2,1,0:T(8,128)S(1)}, u32[]{:S(2)}, u32[]{:S(2)}) %all-to-all-start.7) | async-done | bytes 786464 | tf_op jit(solution)/shard_map/all_to_all | solution.py:282
  494.0 11.4 %all-to-all-done.10.refs_6_ = f32[8,2,32,256]{3,2,1,0:T(8,128)S(1)} async-done(((f32[8,2,32,256]{3,2,1,0:T(8,128)}), f32[8,2,32,256]{3,2,1,0:T(8,128)S(1)}, u32[]{:S(2)}, u32[]{:S(2)}) %all-to-all-start.10) | async-done | bytes 524320 | tf_op jit(solution)/shard_map/all_to_all | solution.py:282
  505.4 24.4 %all_to_all.56.refs_4_ = f32[8,2,48,256]{3,2,1,0:T(8,128)S(1)} all-to-all(f32[8,2,48,256]{3,2,1,0:T(8,128)} %bitcast.43), channel_id=1, replica_groups=mesh['ia'=8,'ka'=4] {'ia'}, dimensions={0} | all-to-all | bytes 1572864 | tf_op jit(solution)/shard_map/all_to_all | solution.py:282
  529.8 23.4 %all_to_all.57.refs_5_ = f32[8,2,48,256]{3,2,1,0:T(8,128)S(1)} all-to-all(f32[8,2,48,256]{3,2,1,0:T(8,128)S(1)} %bitcast.42), channel_id=1, replica_groups=mesh['ia'=8,'ka'=4] {'ia'}, dimensions={0} | all-to-all | bytes 1572864 | tf_op jit(solution)/shard_map/all_to_all | solution.py:282
  (159 shorter events, 114.9 us)
Async XLA Ops:
  13.0 42.8 %all-to-all-start = ((f32[4,2,32,1024]{3,2,1,0:T(8,128)}), f32[4,2,32,1024]{3,2,1,0:T(8,128)}, u32[]{:S(2)}, u32[]{:S(2)}) async-start(f32[4,2,32,1024]{3,2,1,0:T(8,128)} %first_flip.1.after_ref), calls=%async_computation | async-start | bytes 2097152 | tf_op jit(solution)/shard_map/all_to_all | solution.py:282
  19.6 24.8 %collective-permute-start.3 = (f32[2,64,1024]{2,1,0:T(8,128)S(1)}, f32[2,64,1024]{2,1,0:T(8,128)S(1)}, u32[]{:S(2)}, u32[]{:S(2)}) collective-permute-start(f32[2,64,1024]{2,1,0:T(8,128)S(1)} %flip.9), channel_id=1, source_target_pairs={{0,1},{1,0},{2,3},{3,2},{4,5},{5,4},{6,7},{7,6},{8,9},{9,8},{10,11... | collective-permute-start | bytes 1572872 | tf_op jit(solution)/shard_map/ppermute | solution.py:288
  23.1 21.3 %collective-permute-start.4 = (f32[2,64,1024]{2,1,0:T(8,128)S(1)}, f32[2,64,1024]{2,1,0:T(8,128)S(1)}, u32[]{:S(2)}, u32[]{:S(2)}) collective-permute-start(f32[2,64,1024]{2,1,0:T(8,128)S(1)} %flip.10), channel_id=1, source_target_pairs={{0,2},{1,3},{2,0},{3,1},{4,6},{5,7},{6,4},{7,5},{8,10},{9,11},{10,... | collective-permute-start | bytes 1572872 | tf_op jit(solution)/shard_map/ppermute | solution.py:288
  26.2 29.5 %collective-permute-start.5 = (f32[2,64,1024]{2,1,0:T(8,128)S(1)}, f32[2,64,1024]{2,1,0:T(8,128)S(1)}, u32[]{:S(2)}, u32[]{:S(2)}) collective-permute-start(f32[2,64,1024]{2,1,0:T(8,128)S(1)} %flip.11), channel_id=1, source_target_pairs={{0,3},{1,2},{2,1},{3,0},{4,7},{5,6},{6,5},{7,4},{8,11},{9,10},{10,... | collective-permute-start | bytes 1572872 | tf_op jit(solution)/shard_map/ppermute | solution.py:288
  109.8 30.1 %all-to-all-start.1 = ((f32[8,32,1024]{2,1,0:T(8,128)}), f32[8,32,1024]{2,1,0:T(8,128)S(1)}, u32[]{:S(2)}, u32[]{:S(2)}) async-start(f32[8,32,1024]{2,1,0:T(8,128)} %bitcast.1), calls=%async_computation.1 | async-start | bytes 2097152 | tf_op jit(solution)/shard_map/all_to_all | solution.py:282
  116.9 25.2 %collective-permute-start.15 = (f32[2,64,1024]{2,1,0:T(8,128)}, f32[2,64,1024]{2,1,0:T(8,128)}, u32[]{:S(2)}, u32[]{:S(2)}) collective-permute-start(f32[2,64,1024]{2,1,0:T(8,128)} %get-tuple-element.59), channel_id=1, source_target_pairs={{0,1},{1,0},{2,3},{3,2},{4,5},{5,4},{6,7},{7,6},{8,9},{9,8},{10,11... | collective-permute-start | bytes 1572872 | tf_op jit(solution)/shard_map/ppermute | solution.py:288
  121.0 37.6 %collective-permute-start.16 = (f32[2,64,1024]{2,1,0:T(8,128)}, f32[2,64,1024]{2,1,0:T(8,128)}, u32[]{:S(2)}, u32[]{:S(2)}) collective-permute-start(f32[2,64,1024]{2,1,0:T(8,128)} %get-tuple-element.60), channel_id=1, source_target_pairs={{0,2},{1,3},{2,0},{3,1},{4,6},{5,7},{6,4},{7,5},{8,10},{9,11},{10,... | collective-permute-start | bytes 1572872 | tf_op jit(solution)/shard_map/ppermute | solution.py:288
  124.1 47.4 %collective-permute-start.17 = (f32[2,64,1024]{2,1,0:T(8,128)}, f32[2,64,1024]{2,1,0:T(8,128)}, u32[]{:S(2)}, u32[]{:S(2)}) collective-permute-start(f32[2,64,1024]{2,1,0:T(8,128)} %get-tuple-element.61), channel_id=1, source_target_pairs={{0,3},{1,2},{2,1},{3,0},{4,7},{5,6},{6,5},{7,4},{8,11},{9,10},{10,... | collective-permute-start | bytes 1572872 | tf_op jit(solution)/shard_map/ppermute | solution.py:288
  129.9 41.6 %collective-permute-start.8 = (f32[2,64,1024]{2,1,0:T(8,128)}, f32[2,64,1024]{2,1,0:T(8,128)S(1)}, u32[]{:S(2)}, u32[]{:S(2)}) collective-permute-start(f32[2,64,1024]{2,1,0:T(8,128)} %get-tuple-element.49), channel_id=1, source_target_pairs={{0,3},{1,2},{2,1},{3,0},{4,7},{5,6},{6,5},{7,4},{8,11},{9,10},{10,... | collective-permute-start | bytes 1572872 | tf_op jit(solution)/shard_map/ppermute | solution.py:288
  141.5 37.9 %collective-permute-start = (f32[2,32,1024]{2,1,0:T(8,128)}, f32[2,32,1024]{2,1,0:T(8,128)S(1)}, u32[]{:S(2)}, u32[]{:S(2)}) collective-permute-start(f32[2,32,1024]{2,1,0:T(8,128)} %get-tuple-element.43), channel_id=1, source_target_pairs={{0,1},{1,0},{2,3},{3,2},{4,5},{5,4},{6,7},{7,6},{8,9},{9,8},{10,11... | collective-permute-start | bytes 786440 | tf_op jit(solution)/shard_map/ppermute | solution.py:288
  142.1 38.0 %collective-permute-start.1 = (f32[2,32,1024]{2,1,0:T(8,128)}, f32[2,32,1024]{2,1,0:T(8,128)S(1)}, u32[]{:S(2)}, u32[]{:S(2)}) collective-permute-start(f32[2,32,1024]{2,1,0:T(8,128)} %get-tuple-element.44), channel_id=1, source_target_pairs={{0,2},{1,3},{2,0},{3,1},{4,6},{5,7},{6,4},{7,5},{8,10},{9,11},{10,... | collective-permute-start | bytes 786440 | tf_op jit(solution)/shard_map/ppermute | solution.py:288
  158.5 22.3 %collective-permute-start.2 = (f32[2,32,1024]{2,1,0:T(8,128)}, f32[2,32,1024]{2,1,0:T(8,128)S(1)}, u32[]{:S(2)}, u32[]{:S(2)}) collective-permute-start(f32[2,32,1024]{2,1,0:T(8,128)} %get-tuple-element.45), channel_id=1, source_target_pairs={{0,3},{1,2},{2,1},{3,0},{4,7},{5,6},{6,5},{7,4},{8,11},{9,10},{10,... | collective-permute-start | bytes 786440 | tf_op jit(solution)/shard_map/ppermute | solution.py:288
  174.3 97.3 %all-to-all-start.4 = ((f32[8,64,1024]{2,1,0:T(8,128)}), f32[8,64,1024]{2,1,0:T(8,128)S(1)}, u32[]{:S(2)}, u32[]{:S(2)}) async-start(f32[8,64,1024]{2,1,0:T(8,128)} %bitcast.12), calls=%async_computation.4 | async-start | bytes 4194304 | tf_op jit(solution)/shard_map/all_to_all | solution.py:282
  179.4 219.1 %reduce-scatter.13.cloned.1.call-start = ((), (), s32[]{:S(2)}) async-start(), calls=%async_computation.15 | async-start | bytes 1310720
  190.8 207.7 %reduce-scatter.15.cloned.1.call-start = ((), (), s32[]{:S(2)}) async-start(), calls=%async_computation.16 | async-start | bytes 2621440
  190.9 20.2 %collective-permute-start.6 = (f32[2,64,1024]{2,1,0:T(8,128)}, f32[2,64,1024]{2,1,0:T(8,128)S(1)}, u32[]{:S(2)}, u32[]{:S(2)}) collective-permute-start(f32[2,64,1024]{2,1,0:T(8,128)} %copy-done.24), channel_id=1, source_target_pairs={{0,1},{1,0},{2,3},{3,2},{4,5},{5,4},{6,7},{7,6},{8,9},{9,8},{10,11... | collective-permute-start | bytes 1572872 | tf_op jit(solution)/shard_map/ppermute | solution.py:288
  191.5 19.8 %collective-permute-start.7 = (f32[2,64,1024]{2,1,0:T(8,128)}, f32[2,64,1024]{2,1,0:T(8,128)S(1)}, u32[]{:S(2)}, u32[]{:S(2)}) collective-permute-start(f32[2,64,1024]{2,1,0:T(8,128)} %copy-done.23), channel_id=1, source_target_pairs={{0,2},{1,3},{2,0},{3,1},{4,6},{5,7},{6,4},{7,5},{8,10},{9,11},{10,... | collective-permute-start | bytes 1572872 | tf_op jit(solution)/shard_map/ppermute | solution.py:288
  220.6 26.8 %collective-permute-start.9 = (f32[2,96,1024]{2,1,0:T(8,128)}, f32[2,96,1024]{2,1,0:T(8,128)S(1)}, u32[]{:S(2)}, u32[]{:S(2)}) collective-permute-start(f32[2,96,1024]{2,1,0:T(8,128)} %copy-done.20), channel_id=1, source_target_pairs={{0,1},{1,0},{2,3},{3,2},{4,5},{5,4},{6,7},{7,6},{8,9},{9,8},{10,11... | collective-permute-start | bytes 2359304 | tf_op jit(solution)/shard_map/ppermute | solution.py:288
  222.1 31.3 %collective-permute-start.10 = (f32[2,96,1024]{2,1,0:T(8,128)}, f32[2,96,1024]{2,1,0:T(8,128)S(1)}, u32[]{:S(2)}, u32[]{:S(2)}) collective-permute-start(f32[2,96,1024]{2,1,0:T(8,128)} %copy-done.21), channel_id=1, source_target_pairs={{0,2},{1,3},{2,0},{3,1},{4,6},{5,7},{6,4},{7,5},{8,10},{9,11},{10,... | collective-permute-start | bytes 2359304 | tf_op jit(solution)/shard_map/ppermute | solution.py:288
  223.5 45.1 %collective-permute-start.11 = (f32[2,96,1024]{2,1,0:T(8,128)}, f32[2,96,1024]{2,1,0:T(8,128)S(1)}, u32[]{:S(2)}, u32[]{:S(2)}) collective-permute-start(f32[2,96,1024]{2,1,0:T(8,128)} %copy-done.22), channel_id=1, source_target_pairs={{0,3},{1,2},{2,1},{3,0},{4,7},{5,6},{6,5},{7,4},{8,11},{9,10},{10,... | collective-permute-start | bytes 2359304 | tf_op jit(solution)/shard_map/ppermute | solution.py:288
  271.6 76.0 %all-to-all-start.3 = ((f32[8,96,1024]{2,1,0:T(8,128)}), f32[8,96,1024]{2,1,0:T(8,128)}, u32[]{:S(2)}, u32[]{:S(2)}) async-start(f32[8,96,1024]{2,1,0:T(8,128)} %bitcast.39), calls=%async_computation.3 | async-start | bytes 6291456 | tf_op jit(solution)/shard_map/all_to_all | solution.py:282
  276.1 144.7 %reduce-scatter.19.cloned.1.call-start = ((), (), s32[]{:S(2)}) async-start(), calls=%async_computation.18 | async-start | bytes 2621440
  276.3 17.9 %collective-permute-start.18 = (f32[2,64,1024]{2,1,0:T(8,128)S(1)}, f32[2,64,1024]{2,1,0:T(8,128)S(1)}, u32[]{:S(2)}, u32[]{:S(2)}) collective-permute-start(f32[2,64,1024]{2,1,0:T(8,128)S(1)} %get-tuple-element.63), channel_id=1, source_target_pairs={{0,1},{1,0},{2,3},{3,2},{4,5},{5,4},{6,7},{7,6},{8,9},{9,8},{10,11... | collective-permute-start | bytes 1572872 | tf_op jit(solution)/shard_map/ppermute | solution.py:288
  277.8 28.4 %collective-permute-start.20 = (f32[2,64,1024]{2,1,0:T(8,128)S(1)}, f32[2,64,1024]{2,1,0:T(8,128)S(1)}, u32[]{:S(2)}, u32[]{:S(2)}) collective-permute-start(f32[2,64,1024]{2,1,0:T(8,128)S(1)} %get-tuple-element.65), channel_id=1, source_target_pairs={{0,3},{1,2},{2,1},{3,0},{4,7},{5,6},{6,5},{7,4},{8,11},{9,10},{10,... | collective-permute-start | bytes 1572872 | tf_op jit(solution)/shard_map/ppermute | solution.py:288
  315.3 130.0 %reduce-scatter.17.cloned.1.call-start = ((), (), s32[]{:S(2)}) async-start(), calls=%async_computation.17 | async-start | bytes 3932160
  349.8 20.5 %collective-permute-start.12 = (f32[2,96,1024]{2,1,0:T(8,128)S(1)}, f32[2,96,1024]{2,1,0:T(8,128)S(1)}, u32[]{:S(2)}, u32[]{:S(2)}) collective-permute-start(f32[2,96,1024]{2,1,0:T(8,128)S(1)} %get-tuple-element.55), channel_id=1, source_target_pairs={{0,1},{1,0},{2,3},{3,2},{4,5},{5,4},{6,7},{7,6},{8,9},{9,8},{10,11... | collective-permute-start | bytes 2359304 | tf_op jit(solution)/shard_map/ppermute | solution.py:288
  351.3 35.7 %collective-permute-start.13 = (f32[2,96,1024]{2,1,0:T(8,128)S(1)}, f32[2,96,1024]{2,1,0:T(8,128)S(1)}, u32[]{:S(2)}, u32[]{:S(2)}) collective-permute-start(f32[2,96,1024]{2,1,0:T(8,128)S(1)} %get-tuple-element.56), channel_id=1, source_target_pairs={{0,2},{1,3},{2,0},{3,1},{4,6},{5,7},{6,4},{7,5},{8,10},{9,11},{10,... | collective-permute-start | bytes 2359304 | tf_op jit(solution)/shard_map/ppermute | solution.py:288
  351.3 35.7 %collective-permute-start.14 = (f32[2,96,1024]{2,1,0:T(8,128)S(1)}, f32[2,96,1024]{2,1,0:T(8,128)S(1)}, u32[]{:S(2)}, u32[]{:S(2)}) collective-permute-start(f32[2,96,1024]{2,1,0:T(8,128)S(1)} %get-tuple-element.57), channel_id=1, source_target_pairs={{0,3},{1,2},{2,1},{3,0},{4,7},{5,6},{6,5},{7,4},{8,11},{9,10},{10,... | collective-permute-start | bytes 2359304 | tf_op jit(solution)/shard_map/ppermute | solution.py:288
  417.3 24.5 %all-to-all-start.5 = ((f32[8,2,48,256]{3,2,1,0:T(8,128)}), f32[8,2,48,256]{3,2,1,0:T(8,128)S(1)}, u32[]{:S(2)}, u32[]{:S(2)}) async-start(f32[8,2,48,256]{3,2,1,0:T(8,128)} %bitcast.15), calls=%async_computation.5 | async-start | bytes 1572864 | tf_op jit(solution)/shard_map/all_to_all | solution.py:282
  441.7 19.2 %all-to-all-start.9 = ((f32[8,2,32,256]{3,2,1,0:T(8,128)}), f32[8,2,32,256]{3,2,1,0:T(8,128)S(1)}, u32[]{:S(2)}, u32[]{:S(2)}) async-start(f32[8,2,32,256]{3,2,1,0:T(8,128)} %bitcast.21), calls=%async_computation.9 | async-start | bytes 1048576 | tf_op jit(solution)/shard_map/all_to_all | solution.py:282
  460.9 25.8 %all-to-all-start.7 = ((f32[8,2,48,256]{3,2,1,0:T(8,128)}), f32[8,2,48,256]{3,2,1,0:T(8,128)S(1)}, u32[]{:S(2)}, u32[]{:S(2)}) async-start(f32[8,2,48,256]{3,2,1,0:T(8,128)} %bitcast.18), calls=%async_computation.7 | async-start | bytes 1572864 | tf_op jit(solution)/shard_map/all_to_all | solution.py:282
  486.6 18.8 %all-to-all-start.10 = ((f32[8,2,32,256]{3,2,1,0:T(8,128)}), f32[8,2,32,256]{3,2,1,0:T(8,128)S(1)}, u32[]{:S(2)}, u32[]{:S(2)}) async-start(f32[8,2,32,256]{3,2,1,0:T(8,128)} %broadcast_select_fusion.2), calls=%async_computation.10 | async-start | bytes 1048576 | tf_op jit(solution)/shard_map/all_to_all | solution.py:282
  (37 other events, 446.1 us)
Sparse Core Ops, SparseCore 0:
  191.0 32.7 reduce-scatter.12
  227.0 60.3 reduce-scatter.14
  315.4 34.2 reduce-scatter.18
  398.6 46.1 reduce-scatter.16

commit v5 on v4

--- a/solution.py
+++ b/solution.py
@@ -7,8 +7,8 @@
 from jax.experimental.pallas import tpu as pltpu
 from jax.sharding import PartitionSpec as P
 
-CHUNKS = (1, 2, 3, 2)
-GROUPS = ((0, 1), (2,), (3,))
+CHUNKS = (4, 2, 2)
+GROUPS = ((0, 1), (2,))
 LANES = 128
 VMEM_BYTES = 48 * 1024 * 1024
 
@@ -35,52 +35,41 @@
     return pl.BlockSpec(shape, lambda *_: (0,) * len(shape))
 
 
-def first_flip_kernel(place_ref, blocks_ref, piece_ref):
-    piece_ref[0, 0] = blocks_ref[0, 0].T[: piece_ref.shape[2]]
-
-
-def first_flip(place, amplitudes, sections, rows):
-    pairs, virtuals = amplitudes.shape[1], amplitudes.shape[3]
-    steps = virtuals // sections // LANES
-    return call(
-        first_flip_kernel,
-        "first_flip",
-        place,
-        [amplitudes],
-        [pl.BlockSpec((1, 1, virtuals, LANES), lambda d, q, at: (0, d, 0, q * steps))],
-        pl.BlockSpec((1, 1, rows, virtuals), lambda d, q, at: (q, d, 0, 0)),
-        jax.ShapeDtypeStruct((sections, pairs, rows, virtuals), jnp.float32),
-        (pairs, sections),
-    )
-
-
-def flip_kernel(spans, low, place_ref, blocks_ref, after_ref, *pieces):
-    flipped = blocks_ref[0, 0].T
-    for (start, rows), piece in zip(spans, pieces):
-        piece[0] = flipped[start - low : start - low + rows]
-
-
-def flip(place, amplitudes, sections, e, spans, after):
+def flip_kernel(shift, place_ref, *refs):
+    half = len(refs) // 2
+    blocks, pieces = refs[:half], refs[half + 1 :]
+    for block, piece in zip(blocks, pieces):
+        piece[...] = block[0, 0].T[shift : shift + piece.shape[0]]
+
+
+def flip(place, amplitudes, sections, t, span, after):
     pairs, virtuals = amplitudes.shape[1], amplitudes.shape[3]
     wide = virtuals // sections
-    low = spans[0][0] // LANES * LANES
-    read = LANES if sum(spans[-1]) <= low + LANES else wide
+    start, rows = span
+    low = start // LANES * LANES
+    read = LANES if start + rows <= low + LANES else wide
     low = low if read == LANES else 0
     return call(
-        functools.partial(flip_kernel, spans, low),
+        functools.partial(flip_kernel, start - low),
         "flip",
         place,
-        [amplitudes, after],
+        [amplitudes] * pairs + [after],
         [
             pl.BlockSpec(
                 (1, 1, virtuals, read),
-                lambda d, at: (0, d, 0, (at[0] ^ e) * (wide // read) + low // read),
-            ),
-            pl.BlockSpec(memory_space=pl.ANY),
-        ],
-        [pl.BlockSpec((1, rows, virtuals), lambda d, at: (d, 0, 0)) for _, rows in spans],
-        [jax.ShapeDtypeStruct((pairs, rows, virtuals), jnp.float32) for _, rows in spans],
-        (pairs,),
+                lambda n, at, e=e: (
+                    0,
+                    at[2] ^ e,
+                    0,
+                    (at[1] ^ t) * (wide // read) + low // read,
+                ),
+            )
+            for e in range(pairs)
+        ]
+        + [pl.BlockSpec(memory_space=pl.ANY)],
+        [whole((rows, virtuals))] * pairs,
+        [jax.ShapeDtypeStruct((rows, virtuals), jnp.float32)] * pairs,
+        (1,),
     )
 
 
@@ -100,25 +89,6 @@
         [whole(pieces[0].shape)] * len(pieces) + [pl.BlockSpec(memory_space=pl.ANY)],
         whole(shape),
         jax.ShapeDtypeStruct(shape, jnp.float32),
-        (1,),
-    )
-
-
-def scatter_kernel(place_ref, stacked_ref, *pieces):
-    for e, piece in enumerate(pieces):
-        piece[...] = stacked_ref[place_ref[0] ^ e]
-
-
-def scatter(place, stacked):
-    count, shape = stacked.shape[0], stacked.shape[1:]
-    return call(
-        scatter_kernel,
-        "scatter",
-        place,
-        [stacked],
-        [whole(stacked.shape)],
-        [whole(shape)] * count,
-        [jax.ShapeDtypeStruct(shape, jnp.float32)] * count,
         (1,),
     )
 
@@ -149,51 +119,63 @@
     )
 
 
-def product_kernel(sections, place_ref, *refs):
-    own_refs, mirrored_refs, refs = refs[:sections], refs[sections : 2 * sections], refs[2 * sections :]
-    masked_ref, out_ref, split_ref = refs
-    pairs, rows, _ = mirrored_refs[0].shape
+def product_kernel(sections, pairs, place_ref, *refs):
+    count = sections * pairs
+    own_refs, mirrored_refs, refs = refs[:count], refs[count : 2 * count], refs[2 * count :]
+    masked_refs, out_ref, split_ref = refs[:pairs], refs[pairs + 1], refs[pairs + 2]
+    rows = mirrored_refs[0].shape[0]
     tall = sections * rows
 
     @pl.when((pl.program_id(0) == 0) & (pl.program_id(1) == 0))
     def _():
-        for e in range(sections):
-            for k in range(pairs):
-                mixed = 2.0 * own_refs[e][0, k] - mirrored_refs[e][k]
+        for t in range(sections):
+            for e in range(pairs):
+                at = t * pairs + e
+                mixed = 2.0 * own_refs[at][0, 0] - mirrored_refs[at][...]
                 high = mixed.astype(jnp.bfloat16)
                 low = (mixed - high.astype(jnp.float32)).astype(jnp.bfloat16)
-                split_ref[k, pl.ds(e * rows, rows)] = high
-                split_ref[k, pl.ds(tall + e * rows, rows)] = low
+                split_ref[e, pl.ds(t * rows, rows)] = high
+                split_ref[e, pl.ds(tall + t * rows, rows)] = low
 
     total = None
-    for k in range(pairs):
-        both = jnp.dot(split_ref[k], masked_ref[0, k], preferred_element_type=jnp.float32)
+    for e in range(pairs):
+        both = jnp.dot(split_ref[e], masked_refs[e][0, 0], preferred_element_type=jnp.float32)
         both = both[:tall] + both[tall:]
         total = both if total is None else total + both
-    for e in range(sections):
-        out_ref[place_ref[0] ^ e, 0] = total[e * rows : (e + 1) * rows]
-
-
-def product(place, own, mirrored, masked, start):
-    sections = len(mirrored)
-    pairs, rows, virtuals = mirrored[0].shape
+    for t in range(sections):
+        out_ref[place_ref[0] ^ t, 0] = total[t * rows : (t + 1) * rows]
+
+
+def product(place, own, mirrored, masked, start, after):
+    sections, pairs = len(mirrored), len(mirrored[0])
+    rows, virtuals = mirrored[0][0].shape
     slots = masked.shape[0]
     deep = virtuals // sections
     wide = min(virtuals, 512)
     return call(
-        functools.partial(product_kernel, sections),
+        functools.partial(product_kernel, sections, pairs),
         "product",
         place,
-        [own] * sections + list(mirrored) + [masked],
+        [own] * (sections * pairs) + sum(mirrored, []) + [masked] * pairs + [after],
         [
             pl.BlockSpec(
-                tuple(pl.Element(size) for size in (1, pairs, rows, virtuals)),
-                lambda s, n, at, e=e: (0, 0, pl.multiple_of((at[0] ^ e) * deep + start, 8), 0),
+                tuple(pl.Element(size) for size in (1, 1, rows, virtuals)),
+                lambda s, n, at, t=t, e=e: (
+                    0,
+                    at[2] ^ e,
+                    pl.multiple_of((at[0] ^ t) * deep + start, 8),
+                    0,
+                ),
             )
-            for e in range(sections)
+            for t in range(sections)
+            for e in range(pairs)
         ]
-        + [whole(mirrored[0].shape)] * sections
-        + [pl.BlockSpec((1, pairs, virtuals, wide), lambda s, n, at: (s, 0, 0, n))],
+        + [whole((rows, virtuals))] * (sections * pairs)
+        + [
+            pl.BlockSpec((1, 1, virtuals, wide), lambda s, n, at, e=e: (s, at[2] ^ e, 0, n))
+            for e in range(pairs)
+        ]
+        + [pl.BlockSpec(memory_space=pl.ANY)],
         pl.BlockSpec((sections, 1, rows, wide), lambda s, n, at: (0, s, 0, n)),
         jax.ShapeDtypeStruct((sections, slots, rows, virtuals), jnp.float32),
         (slots, virtuals // wide),
@@ -282,6 +264,17 @@
     return lax.all_to_all(array, axis, split_axis=0, concat_axis=0, tiled=True)
 
 
+def route(array, sections, pairs, move):
+    moves = []
+    for plane in range(sections):
+        for core in range(pairs):
+            for line in range(sections):
+                to_plane, to_core, to_line = move(plane, core, line)
+                source = (plane * pairs + core) * sections + line
+                moves.append((source, (to_plane * pairs + to_core) * sections + to_line))
+    return lax.ppermute(array, ("ia", "ka"), moves)
+
+
 def spread(pieces):
     count = len(pieces)
     return [pieces[0]] + [
@@ -295,38 +288,36 @@
     wide = virtuals // sections
     sizes = [wide * part // sum(CHUNKS) for part in CHUNKS]
     spans = [(sum(sizes[:at]), size) for at, size in enumerate(sizes)]
-    place = lax.axis_index("ka").astype(jnp.int32).reshape(1)
+    here, there = lax.axis_index("ka"), lax.axis_index("ia")
+    place = jnp.stack([here, there // pairs, there % pairs]).astype(jnp.int32)
 
     owners = jnp.arange(occupied, dtype=jnp.int32)
     partner_slot = jnp.where(pair_list[pair_list, 0] == owners[:, None], 0, 1).astype(jnp.int32)
     source_row = (pair_list * slots + partner_slot).reshape(-1)
 
-    first = first_flip(place, amplitudes, sections, sizes[0])
-    second = [flip(place, amplitudes, sections, e, spans[1:2], first) for e in range(sections)]
-    across = [swap(first, "ka")]
-    later = [flip(place, amplitudes, sections, e, spans[2:], across[0]) for e in range(sections)]
-    flipped = [[*early, *late] for early, late in zip(second, later)]
     masked = mask_blocks(integrals, tile_mask)
-    own = []
-    for at, (start, rows) in enumerate(spans):
-        if at > 0:
-            met = spread([pieces[at - 1] for pieces in flipped])
-            across.append(gather(place, met, mirrored[-1] if at > 1 else across[0]))
-        if at > 0:
-            mirrored = spread(returned)
-            partial_rows = product(place, amplitudes, mirrored, masked, spans[at - 1][0])
-            own.append(lax.psum_scatter(partial_rows, "ka", scatter_dimension=0, tiled=False))
-        crossed = swap(across[at].reshape(occupied, rows, virtuals), "ia")
-        returned = scatter(place, crossed.reshape(sections, pairs, rows, virtuals))
-    partial_rows = product(place, amplitudes, spread(returned), masked, spans[-1][0])
-    own.append(lax.psum_scatter(partial_rows, "ka", scatter_dimension=0, tiled=False))
-
-    delivered = []
+    own, after, partial_rows = [], place, masked
+    for start, rows in spans:
+        mirrored = []
+        for t in range(sections):
+            landed = []
+            pieces = flip(place, amplitudes, sections, t, (start, rows), after)
+            after = pieces[0]
+            for e, piece in enumerate(pieces):
+                piece = route(piece, sections, pairs, lambda a, c, q: (q, c ^ e, a ^ t))
+                landed.append(piece)
+                if t > 0:
+                    landed[-1] = route(piece, sections, pairs, lambda q, c, l: (q, c, l ^ t))
+            mirrored.append(landed)
+        partial_rows = product(place, amplitudes, mirrored, masked, start, partial_rows)
+        own.append(lax.psum_scatter(partial_rows, "ka", scatter_dimension=0, tiled=False))
+
+    delivered, after = [], partial_rows
     for group in GROUPS:
         columns = spread(cut(place, [own[at] for at in group], sections, pairs))
-        columns = gather(place, columns, returned[0], ordered=False)
+        columns = gather(place, columns, after, ordered=False)
         piece = columns.shape[-2:]
-        met = swap(columns.reshape(occupied, slots, *piece), "ia")
+        met = after = swap(columns.reshape(occupied, slots, *piece), "ia")
         routed = jnp.take(met.reshape(occupied * slots, *piece), source_row, axis=0)
         delivered.append(swap(routed.reshape(occupied, slots, *piece), "ia"))
     return finish(place, spans, GROUPS, own, delivered)

time: 564 us -> 877 us (1.55)
  starting transfers between devices: 68.6 us -> 436 us
  blocking collectives: 102 us -> 41.3 us
  waiting for transfers between devices: 275 us -> 299 us
  local copies, waits for them, and re-layouts: 20.6 us -> 6.71 us
    ppermute x0 -> x42, starting transfers between devices: none -> 418 us  [route(): return lax.ppermute(array, ('ia', 'ka'), moves)]
    ppermute x0 -> x42, waiting for transfers between devices: none -> 196 us  [route(): return lax.ppermute(array, ('ia', 'ka'), moves)]
    ppermute x30 -> x6, waiting for transfers between devices: 196 us -> 33.5 us  [spread(): lax.ppermute(pieces[e], 'ka', [(q, q ^ e) for q in range(count)])]
    all_to_all x3 -> x1, blocking collectives: 102 us -> 41.3 us  [swap(): return lax.all_to_all(array, axis, split_axis=0, concat_axis=0, tiled=True)]
    all_to_all x8 -> x3, waiting for transfers between devices: 78.9 us -> 42.6 us  [swap(): return lax.all_to_all(array, axis, split_axis=0, concat_axis=0, tiled=True)]
    ppermute x30 -> x6, starting transfers between devices: 34.9 us -> 7.11 us  [spread(): lax.ppermute(pieces[e], 'ka', [(q, q ^ e) for q in range(count)])]
    unnamed x8 -> x6, waiting for transfers between devices: 0.14 us -> 27.3 us
    all_to_all x8 -> x3, starting transfers between devices: 33.5 us -> 11.6 us  [swap(): return lax.all_to_all(array, axis, split_axis=0, concat_axis=0, tiled=True)]
  transfers between devices with their start and end apart: 42 -> 54, of which waited for: 24 -> 30; matrix products, arithmetic and copies ran while one was open for 1% -> 1% of each run, Pallas kernels for 13% -> 5%
where the time goes in v5:
time: 877 us; the launch traced here: 876 us
  starting transfers between devices  436 us (50%)
  waiting for transfers between devices  299 us (34%)
  Pallas kernels  74.9 us (9%)
  blocking collectives  41.3 us (5%)
  between operations  13.4 us (2%)
    ppermute x42, starting transfers between devices, route(): return lax.ppermute(array, ('ia', 'ka'), moves)  418 us
    ppermute x42, waiting for transfers between devices, route(): return lax.ppermute(array, ('ia', 'ka'), moves)  196 us
    pallas_call x21, Pallas kernels, call(): pl.pallas_call(kernel, grid_spec=pltpu.PrefetchScalarGridSpec(num_scalar_...  74.9 us
    all_to_all x3, waiting for transfers between devices, swap(): return lax.all_to_all(array, axis, split_axis=0, concat_axis=0, tiled=True)  42.6 us
    all_to_all x1, blocking collectives, swap(): return lax.all_to_all(array, axis, split_axis=0, concat_axis=0, tiled=True)  41.3 us
    ppermute x6, waiting for transfers between devices, spread(): lax.ppermute(pieces[e], 'ka', [(q, q ^ e) for q in range(count)])  33.5 us
    unnamed x6, waiting for transfers between devices  27.3 us
  transfers between devices with their start and end apart: 54, of which 30 were waited for; matrix products, arithmetic and copies ran while one was open for 1% of the time, Pallas kernels for 5%

profile of v5, /device:TPU:0, one launch (start us, length us, event | category | flops | bytes accessed | tf_op | source)
XLA Modules:
  0.0 875.9 jit_solution(16630146702399958236)
XLA Ops:
  35.7 28.2 %collective-permute-start.18 = (f32[64,1024]{1,0:T(8,128)S(1)}, f32[64,1024]{1,0:T(8,128)}, u32[]{:S(2)}, u32[]{:S(2)}) collective-permute-start(f32[64,1024]{1,0:T(8,128)S(1)} %get-tuple-element.48), channel_id=1, source_target_pairs={{0,5},{1,13},{2,21},{3,29},{4,1},{5,9},{6,17},{7,25},{8,4},{9,12},... | collective-permute-start | bytes 786440 | tf_op jit(solution)/shard_map/ppermute | solution.py:275
  64.6 9.7 %collective-permute-done.20 = f32[64,1024]{1,0:T(8,128)S(1)} collective-permute-done((f32[64,1024]{1,0:T(8,128)S(1)}, f32[64,1024]{1,0:T(8,128)S(1)}, u32[]{:S(2)}, u32[]{:S(2)}) %collective-permute-start.20) | collective-permute-done | bytes 262176 | tf_op jit(solution)/shard_map/ppermute | solution.py:275
  74.3 49.9 %collective-permute-start.10 = (f32[128,1024]{1,0:T(8,128)S(1)}, f32[128,1024]{1,0:T(8,128)S(1)}, u32[]{:S(2)}, u32[]{:S(2)}) collective-permute-start(f32[128,1024]{1,0:T(8,128)S(1)} %get-tuple-element.43.refs_2_), channel_id=1, source_target_pairs={{0,3},{1,11},{2,19},{3,27},{4,7},{5,15},{6,23},{7,31},{8,2},{9,10}... | collective-permute-start | bytes 1572872 | tf_op jit(solution)/shard_map/ppermute | solution.py:275
  124.2 41.6 %collective-permute-start.12 = (f32[128,1024]{1,0:T(8,128)S(1)}, f32[128,1024]{1,0:T(8,128)S(1)}, u32[]{:S(2)}, u32[]{:S(2)}) collective-permute-start(f32[128,1024]{1,0:T(8,128)S(1)} %get-tuple-element.44), channel_id=1, source_target_pairs={{0,7},{1,15},{2,23},{3,31},{4,3},{5,11},{6,19},{7,27},{8,6},{9,14}... | collective-permute-start | bytes 1572872 | tf_op jit(solution)/shard_map/ppermute | solution.py:275
  165.8 40.3 %collective-permute-done.16 = f32[64,1024]{1,0:T(8,128)S(1)} collective-permute-done((f32[64,1024]{1,0:T(8,128)S(1)}, f32[64,1024]{1,0:T(8,128)S(1)}, u32[]{:S(2)}, u32[]{:S(2)}) %collective-permute-start.16) | collective-permute-done | bytes 262176 | tf_op jit(solution)/shard_map/ppermute | solution.py:275
  209.9 10.2 %collective-permute-start.15 = (f32[64,1024]{1,0:T(8,128)S(1)}, f32[64,1024]{1,0:T(8,128)S(1)}, u32[]{:S(2)}, u32[]{:S(2)}) collective-permute-start(f32[64,1024]{1,0:T(8,128)S(1)} %get-tuple-element.46), channel_id=1, source_target_pairs={{0,4},{1,12},{2,20},{3,28},{4,0},{5,8},{6,16},{7,24},{8,5},{9,13},... | collective-permute-start | bytes 786440 | tf_op jit(solution)/shard_map/ppermute | solution.py:275
  221.3 144.5 %collective-permute-start.2 = (f32[128,1024]{1,0:T(8,128)S(1)}, f32[128,1024]{1,0:T(8,128)S(1)}, u32[]{:S(2)}, u32[]{:S(2)}) collective-permute-start(f32[128,1024]{1,0:T(8,128)S(1)} %get-tuple-element.39.refs_2_), channel_id=1, source_target_pairs={{0,1},{1,9},{2,17},{3,25},{4,5},{5,13},{6,21},{7,29},{8,0},{9,8},{... | collective-permute-start | bytes 1572872 | tf_op jit(solution)/shard_map/ppermute | solution.py:275
  368.0 21.2 %collective-permute-start.11 = (f32[128,1024]{1,0:T(8,128)S(1)}, f32[128,1024]{1,0:T(8,128)S(1)}, u32[]{:S(2)}, u32[]{:S(2)}) collective-permute-start(f32[128,1024]{1,0:T(8,128)S(1)} %collective-permute-done.10), channel_id=1, source_target_pairs={{0,3},{1,2},{2,1},{3,0},{4,7},{5,6},{6,5},{7,4},{8,11},{9,10},{10,... | collective-permute-start | bytes 1572872 | tf_op jit(solution)/shard_map/ppermute | solution.py:275
  389.2 10.8 %collective-permute-done.2 = f32[128,1024]{1,0:T(8,128)S(1)} collective-permute-done((f32[128,1024]{1,0:T(8,128)S(1)}, f32[128,1024]{1,0:T(8,128)S(1)}, u32[]{:S(2)}, u32[]{:S(2)}) %collective-permute-start.2) | collective-permute-done | bytes 524320 | tf_op jit(solution)/shard_map/ppermute | solution.py:275
  400.0 9.5 %collective-permute-done.4 = f32[128,1024]{1,0:T(8,128)S(1)} collective-permute-done((f32[128,1024]{1,0:T(8,128)S(1)}, f32[128,1024]{1,0:T(8,128)S(1)}, u32[]{:S(2)}, u32[]{:S(2)}) %collective-permute-start.4) | collective-permute-done | bytes 524320 | tf_op jit(solution)/shard_map/ppermute | solution.py:275
  414.3 34.2 %collective-permute-done.25.refs_14_ = f32[64,1024]{1,0:T(8,128)S(1)} collective-permute-done((f32[64,1024]{1,0:T(8,128)S(1)}, f32[64,1024]{1,0:T(8,128)S(1)}, u32[]{:S(2)}, u32[]{:S(2)}) %collective-permute-start.25) | collective-permute-done | bytes 262176 | tf_op jit(solution)/shard_map/ppermute | solution.py:275
  450.5 8.7 mask.1.refs_16_.refs_17_.refs_18_
  475.7 6.5 collective-permute-done.5.refs_11_
  484.7 15.0 %product.3.refs_18_ = f32[4,2,128,1024]{3,2,1,0:T(8,128)} custom-call(s32[3]{0:T(128)S(1)} %pad_add_fusion.place_ref.refs_2_, f32[1,2,1024,1024]{3,2,1,0:T(8,128)} %refs_7_.5, f32[1,2,1024,1024]{3,2,1,0:T(8,128)} %refs_7_.5, f32[1,2,1024,1024]{3,2,1,0:T(8,128)} %refs_7_.5, f32[1,2,1024,1024]{3,2,1,0:T(8,128)} %refs_7_.5, f32[1,2,1024,1024]{3,2,1,0:T(8,128)} %refs_7_.5, ...), custom_call_target="tpu_custom_call" | custom-call | flops 8589934592 | bytes 8388608 | tf_op jit(solution)/shard_map/product/pallas_call | solution.py:18
  499.7 9.7 %product.4.refs_18_ = f32[4,2,64,1024]{3,2,1,0:T(8,128)} custom-call(s32[3]{0:T(128)S(1)} %pad_add_fusion.place_ref.refs_2_, f32[1,2,1024,1024]{3,2,1,0:T(8,128)} %refs_7_.5, f32[1,2,1024,1024]{3,2,1,0:T(8,128)} %refs_7_.5, f32[1,2,1024,1024]{3,2,1,0:T(8,128)} %refs_7_.5, f32[1,2,1024,1024]{3,2,1,0:T(8,128)} %refs_7_.5, f32[1,2,1024,1024]{3,2,1,0:T(8,128)} %refs_7_.5, ...), custom_call_target="tpu_custom_call" | custom-call | flops 4294967296 | bytes 4194304 | tf_op jit(solution)/shard_map/product/pallas_call | solution.py:18
  531.0 38.1 %collective-permute-start.32 = (f32[64,1024]{1,0:T(8,128)S(1)}, f32[64,1024]{1,0:T(8,128)S(1)}, u32[]{:S(2)}, u32[]{:S(2)}) collective-permute-start(f32[64,1024]{1,0:T(8,128)S(1)} %get-tuple-element.56), channel_id=1, source_target_pairs={{0,5},{1,13},{2,21},{3,29},{4,1},{5,9},{6,17},{7,25},{8,4},{9,12},... | collective-permute-start | bytes 786440 | tf_op jit(solution)/shard_map/ppermute | solution.py:275
  570.0 9.4 %collective-permute-done.34 = f32[64,1024]{1,0:T(8,128)S(1)} collective-permute-done((f32[64,1024]{1,0:T(8,128)S(1)}, f32[64,1024]{1,0:T(8,128)S(1)}, u32[]{:S(2)}, u32[]{:S(2)}) %collective-permute-start.34) | collective-permute-done | bytes 262176 | tf_op jit(solution)/shard_map/ppermute | solution.py:275
  584.9 32.2 %collective-permute-start.39 = (f32[64,1024]{1,0:T(8,128)S(1)}, f32[64,1024]{1,0:T(8,128)S(1)}, u32[]{:S(2)}, u32[]{:S(2)}) collective-permute-start(f32[64,1024]{1,0:T(8,128)S(1)} %collective-permute-done.38), channel_id=1, source_target_pairs={{0,3},{1,2},{2,1},{3,0},{4,7},{5,6},{6,5},{7,4},{8,11},{9,10},{10,... | collective-permute-start | bytes 786440 | tf_op jit(solution)/shard_map/ppermute | solution.py:275
  617.1 16.3 %collective-permute-done.30 = f32[64,1024]{1,0:T(8,128)S(1)} collective-permute-done((f32[64,1024]{1,0:T(8,128)S(1)}, f32[64,1024]{1,0:T(8,128)S(1)}, u32[]{:S(2)}, u32[]{:S(2)}) %collective-permute-start.30) | collective-permute-done | bytes 262176 | tf_op jit(solution)/shard_map/ppermute | solution.py:275
  637.7 10.8 %collective-permute-start.31 = (f32[64,1024]{1,0:T(8,128)S(1)}, f32[64,1024]{1,0:T(8,128)S(1)}, u32[]{:S(2)}, u32[]{:S(2)}) collective-permute-start(f32[64,1024]{1,0:T(8,128)S(1)} %collective-permute-done.30), channel_id=1, source_target_pairs={{0,1},{1,0},{2,3},{3,2},{4,5},{5,4},{6,7},{7,6},{8,9},{9,8},{10,11... | collective-permute-start | bytes 786440 | tf_op jit(solution)/shard_map/ppermute | solution.py:275
  648.5 8.4 collective-permute-done.41.refs_15_
  657.0 8.3 collective-permute-done.37.refs_13_
  668.2 11.2 %collective-permute-done.33.refs_11_ = f32[64,1024]{1,0:T(8,128)S(1)} collective-permute-done((f32[64,1024]{1,0:T(8,128)S(1)}, f32[64,1024]{1,0:T(8,128)S(1)}, u32[]{:S(2)}, u32[]{:S(2)}) %collective-permute-start.33) | collective-permute-done | bytes 262176 | tf_op jit(solution)/shard_map/ppermute | solution.py:275
  679.4 9.7 %product.5.refs_4_ = f32[4,2,64,1024]{3,2,1,0:T(8,128)} custom-call(s32[3]{0:T(128)S(1)} %pad_add_fusion.place_ref.refs_2_, f32[1,2,1024,1024]{3,2,1,0:T(8,128)} %refs_7_.5, f32[1,2,1024,1024]{3,2,1,0:T(8,128)} %refs_7_.5, f32[1,2,1024,1024]{3,2,1,0:T(8,128)} %refs_7_.5, f32[1,2,1024,1024]{3,2,1,0:T(8,128)} %refs_7_.5, f32[1,2,1024,1024]{3,2,1,0:T(8,128)} %refs_7_.5, ...), custom_call_target="tpu_custom_call" | custom-call | flops 4294967296 | bytes 4194304 | tf_op jit(solution)/shard_map/product/pallas_call | solution.py:18
  689.2 17.4 %reduce-scatter.10.cloned.1.call-done = f32[1,2,128,1024]{3,2,1,0:T(8,128)} async-done(((f32[4,2,128,1024]{3,2,1,0:T(8,128)}), f32[1,2,128,1024]{3,2,1,0:T(8,128)}) %reduce-scatter.10.cloned.1.call-update) | async-done | bytes 1048592
  713.0 11.8 %collective-permute-done.42.refs_1_ = f32[2,2,96,256]{3,2,1,0:T(8,128)S(1)} collective-permute-done((f32[2,2,96,256]{3,2,1,0:T(8,128)S(1)}, f32[2,2,96,256]{3,2,1,0:T(8,128)S(1)}, u32[]{:S(2)}, u32[]{:S(2)}) %collective-permute-start.42) | collective-permute-done | bytes 393248 | tf_op jit(solution)/shard_map/ppermute | solution.py:281
  729.2 11.7 %collective-permute-done.44.refs_3_ = f32[2,2,96,256]{3,2,1,0:T(8,128)S(1)} collective-permute-done((f32[2,2,96,256]{3,2,1,0:T(8,128)S(1)}, f32[2,2,96,256]{3,2,1,0:T(8,128)S(1)}, u32[]{:S(2)}, u32[]{:S(2)}) %collective-permute-start.44) | collective-permute-done | bytes 393248 | tf_op jit(solution)/shard_map/ppermute | solution.py:281
  747.3 9.2 %reduce-scatter.14.cloned.1.call-done = f32[1,2,64,1024]{3,2,1,0:T(8,128)} async-done(((f32[4,2,64,1024]{3,2,1,0:T(8,128)}), f32[1,2,64,1024]{3,2,1,0:T(8,128)}) %reduce-scatter.14.cloned.1.call-update) | async-done | bytes 524304
  767.4 17.7 %all-to-all-done.refs_4_ = f32[8,2,96,256]{3,2,1,0:T(8,128)S(1)} async-done(((f32[8,2,96,256]{3,2,1,0:T(8,128)}), f32[8,2,96,256]{3,2,1,0:T(8,128)S(1)}, u32[]{:S(2)}, u32[]{:S(2)}) %all-to-all-start) | async-done | bytes 1572896 | tf_op jit(solution)/shard_map/all_to_all | solution.py:264
  791.0 14.2 %all-to-all-done.2 = f32[8,2,32,256]{3,2,1,0:T(8,128)S(1)} async-done(((f32[8,2,32,256]{3,2,1,0:T(8,128)}), f32[8,2,32,256]{3,2,1,0:T(8,128)S(1)}, u32[]{:S(2)}, u32[]{:S(2)}) %all-to-all-start.2) | async-done | bytes 524320 | tf_op jit(solution)/shard_map/all_to_all | solution.py:264
  814.8 10.7 %all-to-all-done.3.refs_4_ = f32[8,2,32,256]{3,2,1,0:T(8,128)S(1)} async-done(((f32[8,2,32,256]{3,2,1,0:T(8,128)}), f32[8,2,32,256]{3,2,1,0:T(8,128)S(1)}, u32[]{:S(2)}, u32[]{:S(2)}) %all-to-all-start.3) | async-done | bytes 524320 | tf_op jit(solution)/shard_map/all_to_all | solution.py:264
  825.5 41.3 %all_to_all.20.refs_3_ = f32[8,2,96,256]{3,2,1,0:T(8,128)S(1)} all-to-all(f32[8,2,96,256]{3,2,1,0:T(8,128)} %broadcast_select_fusion), channel_id=1, replica_groups=mesh['ia'=8,'ka'=4] {'ia'}, dimensions={0} | all-to-all | bytes 3145728 | tf_op jit(solution)/shard_map/all_to_all | solution.py:264
  (131 shorter events, 144.0 us)
Async XLA Ops:
  6.5 682.6 %reduce-scatter.12.cloned.1.call-start = ((), (), s32[]{:S(2)}) async-start(), calls=%async_computation.8 | async-start | bytes 2621440
  27.3 36.7 %collective-permute-start.26 = (f32[64,1024]{1,0:T(8,128)S(1)}, f32[64,1024]{1,0:T(8,128)S(1)}, u32[]{:S(2)}, u32[]{:S(2)}) collective-permute-start(f32[64,1024]{1,0:T(8,128)S(1)} %get-tuple-element.52), channel_id=1, source_target_pairs={{0,7},{1,15},{2,23},{3,31},{4,3},{5,11},{6,19},{7,27},{8,6},{9,14}... | collective-permute-start | bytes 786440 | tf_op jit(solution)/shard_map/ppermute | solution.py:275
  30.0 44.3 %collective-permute-start.20 = (f32[64,1024]{1,0:T(8,128)S(1)}, f32[64,1024]{1,0:T(8,128)S(1)}, u32[]{:S(2)}, u32[]{:S(2)}) collective-permute-start(f32[64,1024]{1,0:T(8,128)S(1)} %get-tuple-element.49.refs_2_), channel_id=1, source_target_pairs={{0,2},{1,10},{2,18},{3,26},{4,6},{5,14},{6,22},{7,30},{8,3},{9,11}... | collective-permute-start | bytes 786440 | tf_op jit(solution)/shard_map/ppermute | solution.py:275
  30.5 93.7 %collective-permute-start.22 = (f32[64,1024]{1,0:T(8,128)S(1)}, f32[64,1024]{1,0:T(8,128)S(1)}, u32[]{:S(2)}, u32[]{:S(2)}) collective-permute-start(f32[64,1024]{1,0:T(8,128)S(1)} %get-tuple-element.50), channel_id=1, source_target_pairs={{0,6},{1,14},{2,22},{3,30},{4,2},{5,10},{6,18},{7,26},{8,7},{9,15}... | collective-permute-start | bytes 786440 | tf_op jit(solution)/shard_map/ppermute | solution.py:275
  31.1 175.0 %collective-permute-start.16 = (f32[64,1024]{1,0:T(8,128)S(1)}, f32[64,1024]{1,0:T(8,128)S(1)}, u32[]{:S(2)}, u32[]{:S(2)}) collective-permute-start(f32[64,1024]{1,0:T(8,128)S(1)} %get-tuple-element.47.refs_2_), channel_id=1, source_target_pairs={{0,1},{1,9},{2,17},{3,25},{4,5},{5,13},{6,21},{7,29},{8,0},{9,8},{... | collective-permute-start | bytes 786440 | tf_op jit(solution)/shard_map/ppermute | solution.py:275
  35.7 174.1 %collective-permute-start.18 = (f32[64,1024]{1,0:T(8,128)S(1)}, f32[64,1024]{1,0:T(8,128)}, u32[]{:S(2)}, u32[]{:S(2)}) collective-permute-start(f32[64,1024]{1,0:T(8,128)S(1)} %get-tuple-element.48), channel_id=1, source_target_pairs={{0,5},{1,13},{2,21},{3,29},{4,1},{5,9},{6,17},{7,25},{8,4},{9,12},... | collective-permute-start | bytes 786440 | tf_op jit(solution)/shard_map/ppermute | solution.py:275
  63.9 156.2 %collective-permute-start.14 = (f32[64,1024]{1,0:T(8,128)S(1)}, f32[64,1024]{1,0:T(8,128)S(1)}, u32[]{:S(2)}, u32[]{:S(2)}) collective-permute-start(f32[64,1024]{1,0:T(8,128)S(1)} %get-tuple-element.45.refs_2_), channel_id=1, source_target_pairs={{0,0},{1,8},{2,16},{3,24},{4,4},{5,12},{6,20},{7,28},{8,1},{9,9},{... | collective-permute-start | bytes 786440 | tf_op jit(solution)/shard_map/ppermute | solution.py:275
  74.3 291.4 %collective-permute-start.10 = (f32[128,1024]{1,0:T(8,128)S(1)}, f32[128,1024]{1,0:T(8,128)S(1)}, u32[]{:S(2)}, u32[]{:S(2)}) collective-permute-start(f32[128,1024]{1,0:T(8,128)S(1)} %get-tuple-element.43.refs_2_), channel_id=1, source_target_pairs={{0,3},{1,11},{2,19},{3,27},{4,7},{5,15},{6,23},{7,31},{8,2},{9,10}... | collective-permute-start | bytes 1572872 | tf_op jit(solution)/shard_map/ppermute | solution.py:275
  124.2 242.9 %collective-permute-start.12 = (f32[128,1024]{1,0:T(8,128)S(1)}, f32[128,1024]{1,0:T(8,128)S(1)}, u32[]{:S(2)}, u32[]{:S(2)}) collective-permute-start(f32[128,1024]{1,0:T(8,128)S(1)} %get-tuple-element.44), channel_id=1, source_target_pairs={{0,7},{1,15},{2,23},{3,31},{4,3},{5,11},{6,19},{7,27},{8,6},{9,14}... | collective-permute-start | bytes 1572872 | tf_op jit(solution)/shard_map/ppermute | solution.py:275
  206.1 161.7 %collective-permute-start.6 = (f32[128,1024]{1,0:T(8,128)S(1)}, f32[128,1024]{1,0:T(8,128)S(1)}, u32[]{:S(2)}, u32[]{:S(2)}) collective-permute-start(f32[128,1024]{1,0:T(8,128)S(1)} %get-tuple-element.41.refs_2_), channel_id=1, source_target_pairs={{0,2},{1,10},{2,18},{3,26},{4,6},{5,14},{6,22},{7,30},{8,3},{9,11}... | collective-permute-start | bytes 1572872 | tf_op jit(solution)/shard_map/ppermute | solution.py:275
  220.1 147.9 %collective-permute-start.8 = (f32[128,1024]{1,0:T(8,128)S(1)}, f32[128,1024]{1,0:T(8,128)S(1)}, u32[]{:S(2)}, u32[]{:S(2)}) collective-permute-start(f32[128,1024]{1,0:T(8,128)S(1)} %get-tuple-element.42), channel_id=1, source_target_pairs={{0,6},{1,14},{2,22},{3,30},{4,2},{5,10},{6,18},{7,26},{8,7},{9,15}... | collective-permute-start | bytes 1572872 | tf_op jit(solution)/shard_map/ppermute | solution.py:275
  221.3 178.7 %collective-permute-start.2 = (f32[128,1024]{1,0:T(8,128)S(1)}, f32[128,1024]{1,0:T(8,128)S(1)}, u32[]{:S(2)}, u32[]{:S(2)}) collective-permute-start(f32[128,1024]{1,0:T(8,128)S(1)} %get-tuple-element.39.refs_2_), channel_id=1, source_target_pairs={{0,1},{1,9},{2,17},{3,25},{4,5},{5,13},{6,21},{7,29},{8,0},{9,8},{... | collective-permute-start | bytes 1572872 | tf_op jit(solution)/shard_map/ppermute | solution.py:275
  365.7 43.7 %collective-permute-start.4 = (f32[128,1024]{1,0:T(8,128)S(1)}, f32[128,1024]{1,0:T(8,128)S(1)}, u32[]{:S(2)}, u32[]{:S(2)}) collective-permute-start(f32[128,1024]{1,0:T(8,128)S(1)} %get-tuple-element.40), channel_id=1, source_target_pairs={{0,5},{1,13},{2,21},{3,29},{4,1},{5,9},{6,17},{7,25},{8,4},{9,12},... | collective-permute-start | bytes 1572872 | tf_op jit(solution)/shard_map/ppermute | solution.py:275
  367.2 42.3 %collective-permute-start = (f32[128,1024]{1,0:T(8,128)S(1)}, f32[128,1024]{1,0:T(8,128)S(1)}, u32[]{:S(2)}, u32[]{:S(2)}) collective-permute-start(f32[128,1024]{1,0:T(8,128)S(1)} %get-tuple-element.37.refs_2_), channel_id=1, source_target_pairs={{0,0},{1,8},{2,16},{3,24},{4,4},{5,12},{6,20},{7,28},{8,1},{9,9},{... | collective-permute-start | bytes 1572872 | tf_op jit(solution)/shard_map/ppermute | solution.py:275
  367.9 46.3 %collective-permute-start.1 = (f32[128,1024]{1,0:T(8,128)S(1)}, f32[128,1024]{1,0:T(8,128)S(1)}, u32[]{:S(2)}, u32[]{:S(2)}) collective-permute-start(f32[128,1024]{1,0:T(8,128)S(1)} %get-tuple-element.38), channel_id=1, source_target_pairs={{0,4},{1,12},{2,20},{3,28},{4,0},{5,8},{6,16},{7,24},{8,5},{9,13},... | collective-permute-start | bytes 1572872 | tf_op jit(solution)/shard_map/ppermute | solution.py:275
  368.0 80.4 %collective-permute-start.11 = (f32[128,1024]{1,0:T(8,128)S(1)}, f32[128,1024]{1,0:T(8,128)S(1)}, u32[]{:S(2)}, u32[]{:S(2)}) collective-permute-start(f32[128,1024]{1,0:T(8,128)S(1)} %collective-permute-done.10), channel_id=1, source_target_pairs={{0,3},{1,2},{2,1},{3,0},{4,7},{5,6},{6,5},{7,4},{8,11},{9,10},{10,... | collective-permute-start | bytes 1572872 | tf_op jit(solution)/shard_map/ppermute | solution.py:275
  400.0 48.5 %collective-permute-start.25 = (f32[64,1024]{1,0:T(8,128)S(1)}, f32[64,1024]{1,0:T(8,128)S(1)}, u32[]{:S(2)}, u32[]{:S(2)}) collective-permute-start(f32[64,1024]{1,0:T(8,128)S(1)} %collective-permute-done.24), channel_id=1, source_target_pairs={{0,3},{1,2},{2,1},{3,0},{4,7},{5,6},{6,5},{7,4},{8,11},{9,10},{10,... | collective-permute-start | bytes 786440 | tf_op jit(solution)/shard_map/ppermute | solution.py:275
  409.5 50.2 %collective-permute-start.13 = (f32[128,1024]{1,0:T(8,128)S(1)}, f32[128,1024]{1,0:T(8,128)S(1)}, u32[]{:S(2)}, u32[]{:S(2)}) collective-permute-start(f32[128,1024]{1,0:T(8,128)S(1)} %collective-permute-done.12), channel_id=1, source_target_pairs={{0,3},{1,2},{2,1},{3,0},{4,7},{5,6},{6,5},{7,4},{8,11},{9,10},{10,... | collective-permute-start | bytes 1572872 | tf_op jit(solution)/shard_map/ppermute | solution.py:275
  409.5 53.7 %collective-permute-start.7 = (f32[128,1024]{1,0:T(8,128)S(1)}, f32[128,1024]{1,0:T(8,128)S(1)}, u32[]{:S(2)}, u32[]{:S(2)}) collective-permute-start(f32[128,1024]{1,0:T(8,128)S(1)} %collective-permute-done.6), channel_id=1, source_target_pairs={{0,2},{1,3},{2,0},{3,1},{4,6},{5,7},{6,4},{7,5},{8,10},{9,11},{10,... | collective-permute-start | bytes 1572872 | tf_op jit(solution)/shard_map/ppermute | solution.py:275
  414.2 49.0 %collective-permute-start.9 = (f32[128,1024]{1,0:T(8,128)S(1)}, f32[128,1024]{1,0:T(8,128)S(1)}, u32[]{:S(2)}, u32[]{:S(2)}) collective-permute-start(f32[128,1024]{1,0:T(8,128)S(1)} %collective-permute-done.8), channel_id=1, source_target_pairs={{0,2},{1,3},{2,0},{3,1},{4,6},{5,7},{6,4},{7,5},{8,10},{9,11},{10,... | collective-permute-start | bytes 1572872 | tf_op jit(solution)/shard_map/ppermute | solution.py:275
  459.7 39.9 %collective-permute-start.27 = (f32[64,1024]{1,0:T(8,128)S(1)}, f32[64,1024]{1,0:T(8,128)S(1)}, u32[]{:S(2)}, u32[]{:S(2)}) collective-permute-start(f32[64,1024]{1,0:T(8,128)S(1)} %collective-permute-done.26), channel_id=1, source_target_pairs={{0,3},{1,2},{2,1},{3,0},{4,7},{5,6},{6,5},{7,4},{8,11},{9,10},{10,... | collective-permute-start | bytes 786440 | tf_op jit(solution)/shard_map/ppermute | solution.py:275
  509.4 197.2 %reduce-scatter.10.cloned.1.call-start = ((), (), s32[]{:S(2)}) async-start(), calls=%async_computation.7 | async-start | bytes 5242880
  510.1 246.4 %reduce-scatter.14.cloned.1.call-start = ((), (), s32[]{:S(2)}) async-start(), calls=%async_computation.9 | async-start | bytes 2621440
  518.6 50.5 %collective-permute-start.40 = (f32[64,1024]{1,0:T(8,128)S(1)}, f32[64,1024]{1,0:T(8,128)S(1)}, u32[]{:S(2)}, u32[]{:S(2)}) collective-permute-start(f32[64,1024]{1,0:T(8,128)S(1)} %get-tuple-element.60), channel_id=1, source_target_pairs={{0,7},{1,15},{2,23},{3,31},{4,3},{5,11},{6,19},{7,27},{8,6},{9,14}... | collective-permute-start | bytes 786440 | tf_op jit(solution)/shard_map/ppermute | solution.py:275
  523.2 56.2 %collective-permute-start.34 = (f32[64,1024]{1,0:T(8,128)S(1)}, f32[64,1024]{1,0:T(8,128)S(1)}, u32[]{:S(2)}, u32[]{:S(2)}) collective-permute-start(f32[64,1024]{1,0:T(8,128)S(1)} %get-tuple-element.57.refs_2_), channel_id=1, source_target_pairs={{0,2},{1,10},{2,18},{3,26},{4,6},{5,14},{6,22},{7,30},{8,3},{9,11}... | collective-permute-start | bytes 786440 | tf_op jit(solution)/shard_map/ppermute | solution.py:275
  523.2 61.7 %collective-permute-start.36 = (f32[64,1024]{1,0:T(8,128)S(1)}, f32[64,1024]{1,0:T(8,128)S(1)}, u32[]{:S(2)}, u32[]{:S(2)}) collective-permute-start(f32[64,1024]{1,0:T(8,128)S(1)} %get-tuple-element.58), channel_id=1, source_target_pairs={{0,6},{1,14},{2,22},{3,30},{4,2},{5,10},{6,18},{7,26},{8,7},{9,15}... | collective-permute-start | bytes 786440 | tf_op jit(solution)/shard_map/ppermute | solution.py:275
  523.2 110.2 %collective-permute-start.30 = (f32[64,1024]{1,0:T(8,128)S(1)}, f32[64,1024]{1,0:T(8,128)S(1)}, u32[]{:S(2)}, u32[]{:S(2)}) collective-permute-start(f32[64,1024]{1,0:T(8,128)S(1)} %get-tuple-element.55.refs_2_), channel_id=1, source_target_pairs={{0,1},{1,9},{2,17},{3,25},{4,5},{5,13},{6,21},{7,29},{8,0},{9,8},{... | collective-permute-start | bytes 786440 | tf_op jit(solution)/shard_map/ppermute | solution.py:275
  531.0 104.7 %collective-permute-start.32 = (f32[64,1024]{1,0:T(8,128)S(1)}, f32[64,1024]{1,0:T(8,128)S(1)}, u32[]{:S(2)}, u32[]{:S(2)}) collective-permute-start(f32[64,1024]{1,0:T(8,128)S(1)} %get-tuple-element.56), channel_id=1, source_target_pairs={{0,5},{1,13},{2,21},{3,29},{4,1},{5,9},{6,17},{7,25},{8,4},{9,12},... | collective-permute-start | bytes 786440 | tf_op jit(solution)/shard_map/ppermute | solution.py:275
  569.1 66.6 %collective-permute-start.28 = (f32[64,1024]{1,0:T(8,128)S(1)}, f32[64,1024]{1,0:T(8,128)S(1)}, u32[]{:S(2)}, u32[]{:S(2)}) collective-permute-start(f32[64,1024]{1,0:T(8,128)S(1)} %get-tuple-element.53.refs_2_), channel_id=1, source_target_pairs={{0,0},{1,8},{2,16},{3,24},{4,4},{5,12},{6,20},{7,28},{8,1},{9,9},{... | collective-permute-start | bytes 786440 | tf_op jit(solution)/shard_map/ppermute | solution.py:275
  579.4 58.3 %collective-permute-start.29 = (f32[64,1024]{1,0:T(8,128)S(1)}, f32[64,1024]{1,0:T(8,128)S(1)}, u32[]{:S(2)}, u32[]{:S(2)}) collective-permute-start(f32[64,1024]{1,0:T(8,128)S(1)} %get-tuple-element.54), channel_id=1, source_target_pairs={{0,4},{1,12},{2,20},{3,28},{4,0},{5,8},{6,16},{7,24},{8,5},{9,13},... | collective-permute-start | bytes 786440 | tf_op jit(solution)/shard_map/ppermute | solution.py:275
  584.9 63.6 %collective-permute-start.39 = (f32[64,1024]{1,0:T(8,128)S(1)}, f32[64,1024]{1,0:T(8,128)S(1)}, u32[]{:S(2)}, u32[]{:S(2)}) collective-permute-start(f32[64,1024]{1,0:T(8,128)S(1)} %collective-permute-done.38), channel_id=1, source_target_pairs={{0,3},{1,2},{2,1},{3,0},{4,7},{5,6},{6,5},{7,4},{8,11},{9,10},{10,... | collective-permute-start | bytes 786440 | tf_op jit(solution)/shard_map/ppermute | solution.py:275
  742.6 42.5 %all-to-all-start = ((f32[8,2,96,256]{3,2,1,0:T(8,128)}), f32[8,2,96,256]{3,2,1,0:T(8,128)S(1)}, u32[]{:S(2)}, u32[]{:S(2)}) async-start(f32[8,2,96,256]{3,2,1,0:T(8,128)} %bitcast.8), calls=%async_computation | async-start | bytes 3145728 | tf_op jit(solution)/shard_map/all_to_all | solution.py:264
  (30 other events, 1062.1 us)
Sparse Core Ops, SparseCore 0:
  509.5 99.3 reduce-scatter.11
  612.1 94.3 reduce-scatter.9
  709.5 46.9 reduce-scatter.13

commit v6 on v4

--- a/solution.py
+++ b/solution.py
@@ -7,8 +7,8 @@
 from jax.experimental.pallas import tpu as pltpu
 from jax.sharding import PartitionSpec as P
 
-CHUNKS = (1, 2, 3, 2)
-GROUPS = ((0, 1), (2,), (3,))
+CHUNKS = (3, 2, 2, 1)
+GROUPS = ((0,), (1,), (2, 3))
 LANES = 128
 VMEM_BYTES = 48 * 1024 * 1024
 
@@ -54,46 +54,63 @@
     )
 
 
-def flip_kernel(spans, low, place_ref, blocks_ref, after_ref, *pieces):
-    flipped = blocks_ref[0, 0].T
-    for (start, rows), piece in zip(spans, pieces):
-        piece[0] = flipped[start - low : start - low + rows]
-
-
-def flip(place, amplitudes, sections, e, spans, after):
+def flip_kernel(place_ref, blocks_ref, after_ref, piece_ref):
+    wide = blocks_ref.shape[-1]
+    piece_ref[0] = blocks_ref[0, 0].T[wide - piece_ref.shape[1] :]
+
+
+def flip(place, amplitudes, sections, e, rows, after):
     pairs, virtuals = amplitudes.shape[1], amplitudes.shape[3]
     wide = virtuals // sections
-    low = spans[0][0] // LANES * LANES
-    read = LANES if sum(spans[-1]) <= low + LANES else wide
-    low = low if read == LANES else 0
-    return call(
-        functools.partial(flip_kernel, spans, low),
+    return call(
+        flip_kernel,
         "flip",
         place,
         [amplitudes, after],
         [
-            pl.BlockSpec(
-                (1, 1, virtuals, read),
-                lambda d, at: (0, d, 0, (at[0] ^ e) * (wide // read) + low // read),
-            ),
+            pl.BlockSpec((1, 1, virtuals, wide), lambda d, at: (0, d, 0, at[0] ^ e)),
             pl.BlockSpec(memory_space=pl.ANY),
         ],
-        [pl.BlockSpec((1, rows, virtuals), lambda d, at: (d, 0, 0)) for _, rows in spans],
-        [jax.ShapeDtypeStruct((pairs, rows, virtuals), jnp.float32) for _, rows in spans],
+        pl.BlockSpec((1, rows, virtuals), lambda d, at: (d, 0, 0)),
+        jax.ShapeDtypeStruct((pairs, rows, virtuals), jnp.float32),
         (pairs,),
     )
 
 
-def gather_kernel(ordered, place_ref, *refs):
+def part_kernel(count, place_ref, *refs):
+    pieces, out_refs = refs[:count], refs[count:]
+    for e, piece in enumerate(pieces):
+        at = 0
+        for out_ref in out_refs:
+            rows = out_ref.shape[2]
+            out_ref[place_ref[0] ^ e, 0] = piece[0, at : at + rows]
+            at += rows
+
+
+def part(place, pieces, sizes):
+    count, (pairs, rows, virtuals) = len(pieces), pieces[0].shape
+    return call(
+        functools.partial(part_kernel, count),
+        "part",
+        place,
+        pieces,
+        [pl.BlockSpec((1, rows, virtuals), lambda d, at: (d, 0, 0))] * count,
+        [pl.BlockSpec((count, 1, size, virtuals), lambda d, at: (0, d, 0, 0)) for size in sizes],
+        [jax.ShapeDtypeStruct((count, pairs, size, virtuals), jnp.float32) for size in sizes],
+        (pairs,),
+    )
+
+
+def gather_kernel(place_ref, *refs):
     pieces, out_ref = refs[:-2], refs[-1]
     for e, piece in enumerate(pieces):
-        out_ref[place_ref[0] ^ e if ordered else e] = piece[...]
-
-
-def gather(place, pieces, after, ordered=True):
+        out_ref[e] = piece[...]
+
+
+def gather(place, pieces, after):
     shape = (len(pieces), *pieces[0].shape)
     return call(
-        functools.partial(gather_kernel, ordered),
+        gather_kernel,
         "gather",
         place,
         [*pieces, after],
@@ -104,19 +121,19 @@
     )
 
 
-def scatter_kernel(place_ref, stacked_ref, *pieces):
+def scatter_kernel(place_ref, stacked_ref, after_ref, *pieces):
     for e, piece in enumerate(pieces):
         piece[...] = stacked_ref[place_ref[0] ^ e]
 
 
-def scatter(place, stacked):
+def scatter(place, stacked, after):
     count, shape = stacked.shape[0], stacked.shape[1:]
     return call(
         scatter_kernel,
         "scatter",
         place,
-        [stacked],
-        [whole(stacked.shape)],
+        [stacked, after],
+        [whole(stacked.shape), pl.BlockSpec(memory_space=pl.ANY)],
         [whole(shape)] * count,
         [jax.ShapeDtypeStruct(shape, jnp.float32)] * count,
         (1,),
@@ -151,7 +168,7 @@
 
 def product_kernel(sections, place_ref, *refs):
     own_refs, mirrored_refs, refs = refs[:sections], refs[sections : 2 * sections], refs[2 * sections :]
-    masked_ref, out_ref, split_ref = refs
+    masked_ref, _, out_ref, split_ref = refs
     pairs, rows, _ = mirrored_refs[0].shape
     tall = sections * rows
 
@@ -174,7 +191,7 @@
         out_ref[place_ref[0] ^ e, 0] = total[e * rows : (e + 1) * rows]
 
 
-def product(place, own, mirrored, masked, start):
+def product(place, own, mirrored, masked, start, after):
     sections = len(mirrored)
     pairs, rows, virtuals = mirrored[0].shape
     slots = masked.shape[0]
@@ -184,7 +201,7 @@
         functools.partial(product_kernel, sections),
         "product",
         place,
-        [own] * sections + list(mirrored) + [masked],
+        [own] * sections + list(mirrored) + [masked, after],
         [
             pl.BlockSpec(
                 tuple(pl.Element(size) for size in (1, pairs, rows, virtuals)),
@@ -193,7 +210,10 @@
             for e in range(sections)
         ]
         + [whole(mirrored[0].shape)] * sections
-        + [pl.BlockSpec((1, pairs, virtuals, wide), lambda s, n, at: (s, 0, 0, n))],
+        + [
+            pl.BlockSpec((1, pairs, virtuals, wide), lambda s, n, at: (s, 0, 0, n)),
+            pl.BlockSpec(memory_space=pl.ANY),
+        ],
         pl.BlockSpec((sections, 1, rows, wide), lambda s, n, at: (0, s, 0, n)),
         jax.ShapeDtypeStruct((sections, slots, rows, virtuals), jnp.float32),
         (slots, virtuals // wide),
@@ -302,31 +322,25 @@
     source_row = (pair_list * slots + partner_slot).reshape(-1)
 
     first = first_flip(place, amplitudes, sections, sizes[0])
-    second = [flip(place, amplitudes, sections, e, spans[1:2], first) for e in range(sections)]
-    across = [swap(first, "ka")]
-    later = [flip(place, amplitudes, sections, e, spans[2:], across[0]) for e in range(sections)]
-    flipped = [[*early, *late] for early, late in zip(second, later)]
+    rest = [flip(place, amplitudes, sections, e, sum(sizes[1:]), first) for e in range(sections)]
+    across = [swap(first, "ka"), *part(place, spread(rest), sizes[1:])]
     masked = mask_blocks(integrals, tile_mask)
-    own = []
-    for at, (start, rows) in enumerate(spans):
-        if at > 0:
-            met = spread([pieces[at - 1] for pieces in flipped])
-            across.append(gather(place, met, mirrored[-1] if at > 1 else across[0]))
-        if at > 0:
-            mirrored = spread(returned)
-            partial_rows = product(place, amplitudes, mirrored, masked, spans[at - 1][0])
-            own.append(lax.psum_scatter(partial_rows, "ka", scatter_dimension=0, tiled=False))
-        crossed = swap(across[at].reshape(occupied, rows, virtuals), "ia")
-        returned = scatter(place, crossed.reshape(sections, pairs, rows, virtuals))
-    partial_rows = product(place, amplitudes, spread(returned), masked, spans[-1][0])
-    own.append(lax.psum_scatter(partial_rows, "ka", scatter_dimension=0, tiled=False))
-
-    delivered = []
+
+    own, returned, partial_rows = [], [place], masked
+    for (start, rows), sent in zip(spans, across):
+        crossed = swap(sent.reshape(occupied, rows, virtuals), "ia")
+        crossed = crossed.reshape(sections, pairs, rows, virtuals)
+        returned = scatter(place, crossed, returned[0])
+        mirrored = spread(returned)
+        partial_rows = product(place, amplitudes, mirrored, masked, start, partial_rows)
+        own.append(lax.psum_scatter(partial_rows, "ka", scatter_dimension=0, tiled=False))
+
+    delivered, after = [], returned[0]
     for group in GROUPS:
         columns = spread(cut(place, [own[at] for at in group], sections, pairs))
-        columns = gather(place, columns, returned[0], ordered=False)
+        columns = gather(place, columns, after)
         piece = columns.shape[-2:]
-        met = swap(columns.reshape(occupied, slots, *piece), "ia")
+        met = after = swap(columns.reshape(occupied, slots, *piece), "ia")
         routed = jnp.take(met.reshape(occupied * slots, *piece), source_row, axis=0)
         delivered.append(swap(routed.reshape(occupied, slots, *piece), "ia"))
     return finish(place, spans, GROUPS, own, delivered)

time: 564 us -> 598 us (1.060)
  blocking collectives: 102 us -> 219 us
  waiting for transfers between devices: 275 us -> 224 us
  starting transfers between devices: 68.6 us -> 51 us
  local copies, waits for them, and re-layouts: 20.6 us -> 12.4 us
  Pallas kernels: 80.6 us -> 73.9 us
    all_to_all x3 -> x5, blocking collectives: 102 us -> 219 us  [swap(): return lax.all_to_all(array, axis, split_axis=0, concat_axis=0, tiled=True)]
    ppermute x30 -> x24, waiting for transfers between devices: 196 us -> 130 us  [spread(): lax.ppermute(pieces[e], 'ka', [(q, q ^ e) for q in range(count)])]
    unnamed x8, waiting for transfers between devices: 0.14 us -> 24.1 us
    all_to_all x8 -> x6, starting transfers between devices: 33.5 us -> 23.7 us  [swap(): return lax.all_to_all(array, axis, split_axis=0, concat_axis=0, tiled=True)]
    all_to_all x8 -> x6, waiting for transfers between devices: 78.9 us -> 70.5 us  [swap(): return lax.all_to_all(array, axis, split_axis=0, concat_axis=0, tiled=True)]
    ppermute x30 -> x24, starting transfers between devices: 34.9 us -> 27.1 us  [spread(): lax.ppermute(pieces[e], 'ka', [(q, q ^ e) for q in range(count)])]
    unnamed x55 -> x37, local copies, waits for them, and re-layouts: 16.9 us -> 9.56 us
    pallas_call x28 -> x22, Pallas kernels: 80.6 us -> 73.9 us  [call(): pl.pallas_call(kernel, grid_spec=pltpu.PrefetchScalarGridSpec(num_scalar_...]
  transfers between devices with their start and end apart: 42 -> 34, of which waited for: 24 -> 24; matrix products, arithmetic and copies ran while one was open for 1% -> 1% of each run, Pallas kernels for 13% -> 11%
where the time goes in v6:
time: 598 us; the launch traced here: 596 us
  waiting for transfers between devices  224 us (37%)
  blocking collectives  219 us (37%)
  Pallas kernels  73.9 us (12%)
  starting transfers between devices  51 us (9%)
  between operations  13.4 us (2%)
  local copies, waits for them, and re-layouts  12.4 us (2%)
    all_to_all x5, blocking collectives, swap(): return lax.all_to_all(array, axis, split_axis=0, concat_axis=0, tiled=True)  219 us
    ppermute x24, waiting for transfers between devices, spread(): lax.ppermute(pieces[e], 'ka', [(q, q ^ e) for q in range(count)])  130 us
    pallas_call x22, Pallas kernels, call(): pl.pallas_call(kernel, grid_spec=pltpu.PrefetchScalarGridSpec(num_scalar_...  73.9 us
    all_to_all x6, waiting for transfers between devices, swap(): return lax.all_to_all(array, axis, split_axis=0, concat_axis=0, tiled=True)  70.5 us
    ppermute x24, starting transfers between devices, spread(): lax.ppermute(pieces[e], 'ka', [(q, q ^ e) for q in range(count)])  27.1 us
    unnamed x8, waiting for transfers between devices  24.1 us
    all_to_all x6, starting transfers between devices, swap(): return lax.all_to_all(array, axis, split_axis=0, concat_axis=0, tiled=True)  23.7 us
  transfers between devices with their start and end apart: 34, of which 24 were waited for; matrix products, arithmetic and copies ran while one was open for 1% of the time, Pallas kernels for 11%

profile of v6, /device:TPU:0, one launch (start us, length us, event | category | flops | bytes accessed | tf_op | source)
XLA Modules:
  0.0 596.1 jit_solution(7057099406727324796)
XLA Ops:
  6.5 5.3 first_flip.1.after_ref
  11.8 41.6 %all_to_all.55 = f32[4,2,96,1024]{3,2,1,0:T(8,128)S(1)} all-to-all(f32[4,2,96,1024]{3,2,1,0:T(8,128)S(1)} %first_flip.1.after_ref), channel_id=1, replica_groups=mesh['ia'=8,'ka'=4] {'ka'}, dimensions={0} | all-to-all | bytes 6291456 | tf_op jit(solution)/shard_map/all_to_all | solution.py:302
  53.4 76.3 %all_to_all.56 = f32[8,96,1024]{2,1,0:T(8,128)} all-to-all(f32[8,96,1024]{2,1,0:T(8,128)S(1)} %bitcast.42), channel_id=1, replica_groups=mesh['ia'=8,'ka'=4] {'ia'}, dimensions={0} | all-to-all | bytes 6291456 | tf_op jit(solution)/shard_map/all_to_all | solution.py:302
  145.1 7.2 %collective-permute-done.refs_5_ = f32[2,96,1024]{2,1,0:T(8,128)S(1)} collective-permute-done((f32[2,96,1024]{2,1,0:T(8,128)S(1)}, f32[2,96,1024]{2,1,0:T(8,128)S(1)}, u32[]{:S(2)}, u32[]{:S(2)}) %collective-permute-start) | collective-permute-done | bytes 786464 | tf_op jit(solution)/shard_map/ppermute | solution.py:308
  153.3 8.7 %mask.1.refs_8_.refs_9_ = bf16[2,2,1024,1024]{3,2,1,0:T(8,128)(2,1)} custom-call(s32[2,2,8,8]{3,2,1,0:T(8,128)S(1)} %bitcast.40, bf16[1,2,2,1024,1024]{4,3,2,1,0:T(8,128)(2,1)} %integrals_ref.1), custom_call_target="tpu_custom_call" | custom-call | bytes 16777216 | tf_op jit(solution)/shard_map/mask/pallas_call | solution.py:18
  162.0 8.2 %collective-permute-done.1.refs_6_ = f32[2,96,1024]{2,1,0:T(8,128)S(1)} collective-permute-done((f32[2,96,1024]{2,1,0:T(8,128)S(1)}, f32[2,96,1024]{2,1,0:T(8,128)S(1)}, u32[]{:S(2)}, u32[]{:S(2)}) %collective-permute-start.1) | collective-permute-done | bytes 786464 | tf_op jit(solution)/shard_map/ppermute | solution.py:308
  170.2 11.5 %product.4.refs_9_ = f32[4,2,96,1024]{3,2,1,0:T(8,128)} custom-call(s32[1]{0:T(128)} %bitcast.place_ref.after_ref, f32[1,2,1024,1024]{3,2,1,0:T(8,128)} %refs_3_.7, f32[1,2,1024,1024]{3,2,1,0:T(8,128)} %refs_3_.7, f32[1,2,1024,1024]{3,2,1,0:T(8,128)} %refs_3_.7, f32[1,2,1024,1024]{3,2,1,0:T(8,128)} %refs_3_.7, ...), custom_call_target="tpu_custom_call" | custom-call | flops 6442450944 | bytes 6291456 | tf_op jit(solution)/shard_map/product/pallas_call | solution.py:18
  183.6 22.9 %collective-permute-done.3.refs_1_ = f32[2,160,1024]{2,1,0:T(8,128)} collective-permute-done((f32[2,160,1024]{2,1,0:T(8,128)}, f32[2,160,1024]{2,1,0:T(8,128)}, u32[]{:S(2)}, u32[]{:S(2)}) %collective-permute-start.3) | collective-permute-done | bytes 1310752 | tf_op jit(solution)/shard_map/ppermute | solution.py:308
  209.6 31.7 %collective-permute-done.5.refs_3_ = f32[2,160,1024]{2,1,0:T(8,128)} collective-permute-done((f32[2,160,1024]{2,1,0:T(8,128)}, f32[2,160,1024]{2,1,0:T(8,128)}, u32[]{:S(2)}, u32[]{:S(2)}) %collective-permute-start.5) | collective-permute-done | bytes 1310752 | tf_op jit(solution)/shard_map/ppermute | solution.py:308
  244.9 53.4 %all_to_all.57 = f32[8,64,1024]{2,1,0:T(8,128)} all-to-all(f32[8,64,1024]{2,1,0:T(8,128)} %bitcast.47), channel_id=1, replica_groups=mesh['ia'=8,'ka'=4] {'ia'}, dimensions={0} | all-to-all | bytes 4194304 | tf_op jit(solution)/shard_map/all_to_all | solution.py:302
  298.4 3.7 all-to-all-start.3
  307.4 11.3 %collective-permute-done.6.refs_5_ = f32[2,64,1024]{2,1,0:T(8,128)S(1)} collective-permute-done((f32[2,64,1024]{2,1,0:T(8,128)S(1)}, f32[2,64,1024]{2,1,0:T(8,128)S(1)}, u32[]{:S(2)}, u32[]{:S(2)}) %collective-permute-start.6) | collective-permute-done | bytes 524320 | tf_op jit(solution)/shard_map/ppermute | solution.py:308
  318.7 10.0 %collective-permute-done.7.refs_6_ = f32[2,64,1024]{2,1,0:T(8,128)S(1)} collective-permute-done((f32[2,64,1024]{2,1,0:T(8,128)S(1)}, f32[2,64,1024]{2,1,0:T(8,128)S(1)}, u32[]{:S(2)}, u32[]{:S(2)}) %collective-permute-start.7) | collective-permute-done | bytes 524320 | tf_op jit(solution)/shard_map/ppermute | solution.py:308
  329.9 9.0 %product.5.refs_9_ = f32[4,2,64,1024]{3,2,1,0:T(8,128)} custom-call(s32[1]{0:T(128)} %bitcast.place_ref.after_ref, f32[1,2,1024,1024]{3,2,1,0:T(8,128)} %refs_3_.7, f32[1,2,1024,1024]{3,2,1,0:T(8,128)} %refs_3_.7, f32[1,2,1024,1024]{3,2,1,0:T(8,128)} %refs_3_.7, f32[1,2,1024,1024]{3,2,1,0:T(8,128)} %refs_3_.7, ...), custom_call_target="tpu_custom_call" | custom-call | flops 4294967296 | bytes 4194304 | tf_op jit(solution)/shard_map/product/pallas_call | solution.py:18
  339.8 11.3 %all-to-all-done.3 = f32[8,64,1024]{2,1,0:T(8,128)S(1)} async-done(((f32[8,64,1024]{2,1,0:T(8,128)}), f32[8,64,1024]{2,1,0:T(8,128)S(1)}, u32[]{:S(2)}, u32[]{:S(2)}) %all-to-all-start.3) | async-done | bytes 2097184 | tf_op jit(solution)/shard_map/all_to_all | solution.py:302
  361.3 19.8 %all-to-all-done.4 = f32[8,32,1024]{2,1,0:T(8,128)S(1)} async-done(((f32[8,32,1024]{2,1,0:T(8,128)}), f32[8,32,1024]{2,1,0:T(8,128)S(1)}, u32[]{:S(2)}, u32[]{:S(2)}) %all-to-all-start.4) | async-done | bytes 1048608 | tf_op jit(solution)/shard_map/all_to_all | solution.py:302
  386.5 3.8 collective-permute-done.11.refs_7_
  390.3 9.5 %product.6.refs_9_ = f32[4,2,64,1024]{3,2,1,0:T(8,128)} custom-call(s32[1]{0:T(128)} %bitcast.place_ref.after_ref, f32[1,2,1024,1024]{3,2,1,0:T(8,128)} %refs_3_.7, f32[1,2,1024,1024]{3,2,1,0:T(8,128)} %refs_3_.7, f32[1,2,1024,1024]{3,2,1,0:T(8,128)} %refs_3_.7, f32[1,2,1024,1024]{3,2,1,0:T(8,128)} %refs_3_.7, f32[2,64,1024]{2,1,0:T(8,128)S(1)} %copy-done.6, ...), custom_call_target="tpu_custom_call" | custom-call | flops 4294967296 | bytes 4194304 | tf_op jit(solution)/shard_map/product/pallas_call | solution.py:18
  400.9 6.8 %product.7 = f32[4,2,32,1024]{3,2,1,0:T(8,128)} custom-call(s32[1]{0:T(128)} %bitcast.place_ref.after_ref, f32[1,2,1024,1024]{3,2,1,0:T(8,128)} %refs_3_.7, f32[1,2,1024,1024]{3,2,1,0:T(8,128)} %refs_3_.7, f32[1,2,1024,1024]{3,2,1,0:T(8,128)} %refs_3_.7, f32[1,2,1024,1024]{3,2,1,0:T(8,128)} %refs_3_.7, f32[2,32,1024]{2,1,0:T(8,128)S(1)} %get-tuple-element.52.refs_4_, ...), custom_call_target="tpu_custom_call" | custom-call | flops 2147483648 | bytes 2097152 | tf_op jit(solution)/shard_map/product/pallas_call | solution.py:18
  413.1 4.7 collective-permute-done.15.refs_1_
  417.8 4.4 collective-permute-done.16.refs_2_
  426.6 4.9 all-to-all-start.5
  436.1 5.1 collective-permute-done.18.refs_1_
  444.3 8.2 %all-to-all-done.5.refs_4_ = f32[8,2,48,256]{3,2,1,0:T(8,128)S(1)} async-done(((f32[8,2,48,256]{3,2,1,0:T(8,128)}), f32[8,2,48,256]{3,2,1,0:T(8,128)S(1)}, u32[]{:S(2)}, u32[]{:S(2)}) %all-to-all-start.5) | async-done | bytes 786464 | tf_op jit(solution)/shard_map/all_to_all | solution.py:302
  456.8 23.5 %reduce-scatter.17.cloned.1.call-done = f32[1,2,64,1024]{3,2,1,0:T(8,128)} async-done(((f32[4,2,64,1024]{3,2,1,0:T(8,128)}), f32[1,2,64,1024]{3,2,1,0:T(8,128)}) %reduce-scatter.17.cloned.1.call-update) | async-done | bytes 524304
  485.9 4.3 collective-permute-done.21.refs_1_
  490.2 4.2 collective-permute-done.22.refs_2_
  495.4 4.6 all-to-all-start.9
  502.5 18.4 %all-to-all-done.9 = f32[8,2,48,256]{3,2,1,0:T(8,128)S(1)} async-done(((f32[8,2,48,256]{3,2,1,0:T(8,128)}), f32[8,2,48,256]{3,2,1,0:T(8,128)S(1)}, u32[]{:S(2)}, u32[]{:S(2)}) %all-to-all-start.9) | async-done | bytes 786464 | tf_op jit(solution)/shard_map/all_to_all | solution.py:302
  526.9 12.8 %all-to-all-done.8.refs_5_ = f32[8,2,32,256]{3,2,1,0:T(8,128)S(1)} async-done(((f32[8,2,32,256]{3,2,1,0:T(8,128)}), f32[8,2,32,256]{3,2,1,0:T(8,128)S(1)}, u32[]{:S(2)}, u32[]{:S(2)}) %all-to-all-start.8) | async-done | bytes 524320 | tf_op jit(solution)/shard_map/all_to_all | solution.py:302
  539.7 24.4 %all_to_all.58.refs_4_ = f32[8,2,48,256]{3,2,1,0:T(8,128)S(1)} all-to-all(f32[8,2,48,256]{3,2,1,0:T(8,128)} %bitcast.45), channel_id=1, replica_groups=mesh['ia'=8,'ka'=4] {'ia'}, dimensions={0} | all-to-all | bytes 1572864 | tf_op jit(solution)/shard_map/all_to_all | solution.py:302
  564.1 23.4 %all_to_all.59.refs_6_ = f32[8,2,48,256]{3,2,1,0:T(8,128)S(1)} all-to-all(f32[8,2,48,256]{3,2,1,0:T(8,128)S(1)} %bitcast.44), channel_id=1, replica_groups=mesh['ia'=8,'ka'=4] {'ia'}, dimensions={0} | all-to-all | bytes 1572864 | tf_op jit(solution)/shard_map/all_to_all | solution.py:302
  (121 shorter events, 87.7 us)
Async XLA Ops:
  6.5 401.8 %reduce-scatter.13.cloned.1.call-start = ((), (), s32[]{:S(2)}) async-start(), calls=%async_computation.15 | async-start | bytes 3932160
  131.8 20.5 %collective-permute-start = (f32[2,96,1024]{2,1,0:T(8,128)S(1)}, f32[2,96,1024]{2,1,0:T(8,128)S(1)}, u32[]{:S(2)}, u32[]{:S(2)}) collective-permute-start(f32[2,96,1024]{2,1,0:T(8,128)S(1)} %get-tuple-element.38), channel_id=1, source_target_pairs={{0,1},{1,0},{2,3},{3,2},{4,5},{5,4},{6,7},{7,6},{8,9},{9,8},{10,11... | collective-permute-start | bytes 2359304 | tf_op jit(solution)/shard_map/ppermute | solution.py:308
  132.8 37.3 %collective-permute-start.1 = (f32[2,96,1024]{2,1,0:T(8,128)S(1)}, f32[2,96,1024]{2,1,0:T(8,128)S(1)}, u32[]{:S(2)}, u32[]{:S(2)}) collective-permute-start(f32[2,96,1024]{2,1,0:T(8,128)S(1)} %get-tuple-element.39), channel_id=1, source_target_pairs={{0,2},{1,3},{2,0},{3,1},{4,6},{5,7},{6,4},{7,5},{8,10},{9,11},{10,... | collective-permute-start | bytes 2359304 | tf_op jit(solution)/shard_map/ppermute | solution.py:308
  133.4 36.8 %collective-permute-start.2 = (f32[2,96,1024]{2,1,0:T(8,128)S(1)}, f32[2,96,1024]{2,1,0:T(8,128)S(1)}, u32[]{:S(2)}, u32[]{:S(2)}) collective-permute-start(f32[2,96,1024]{2,1,0:T(8,128)S(1)} %get-tuple-element.40), channel_id=1, source_target_pairs={{0,3},{1,2},{2,1},{3,0},{4,7},{5,6},{6,5},{7,4},{8,11},{9,10},{10,... | collective-permute-start | bytes 2359304 | tf_op jit(solution)/shard_map/ppermute | solution.py:308
  138.1 68.4 %collective-permute-start.3 = (f32[2,160,1024]{2,1,0:T(8,128)}, f32[2,160,1024]{2,1,0:T(8,128)}, u32[]{:S(2)}, u32[]{:S(2)}) collective-permute-start(f32[2,160,1024]{2,1,0:T(8,128)} %flip.5), channel_id=1, source_target_pairs={{0,1},{1,0},{2,3},{3,2},{4,5},{5,4},{6,7},{7,6},{8,9},{9,8},{10,11... | collective-permute-start | bytes 3932168 | tf_op jit(solution)/shard_map/ppermute | solution.py:308
  141.8 67.7 %collective-permute-start.4 = (f32[2,160,1024]{2,1,0:T(8,128)}, f32[2,160,1024]{2,1,0:T(8,128)}, u32[]{:S(2)}, u32[]{:S(2)}) collective-permute-start(f32[2,160,1024]{2,1,0:T(8,128)} %flip.6), channel_id=1, source_target_pairs={{0,2},{1,3},{2,0},{3,1},{4,6},{5,7},{6,4},{7,5},{8,10},{9,11},{10,... | collective-permute-start | bytes 3932168 | tf_op jit(solution)/shard_map/ppermute | solution.py:308
  152.4 88.9 %collective-permute-start.5 = (f32[2,160,1024]{2,1,0:T(8,128)}, f32[2,160,1024]{2,1,0:T(8,128)}, u32[]{:S(2)}, u32[]{:S(2)}) collective-permute-start(f32[2,160,1024]{2,1,0:T(8,128)} %flip.7), channel_id=1, source_target_pairs={{0,3},{1,2},{2,1},{3,0},{4,7},{5,6},{6,5},{7,4},{8,11},{9,10},{10,... | collective-permute-start | bytes 3932168 | tf_op jit(solution)/shard_map/ppermute | solution.py:308
  298.4 52.7 %all-to-all-start.3 = ((f32[8,64,1024]{2,1,0:T(8,128)}), f32[8,64,1024]{2,1,0:T(8,128)S(1)}, u32[]{:S(2)}, u32[]{:S(2)}) async-start(f32[8,64,1024]{2,1,0:T(8,128)} %bitcast.46), calls=%async_computation.3 | async-start | bytes 4194304 | tf_op jit(solution)/shard_map/all_to_all | solution.py:302
  302.1 129.4 %reduce-scatter.15.cloned.1.call-start = ((), (), s32[]{:S(2)}) async-start(), calls=%async_computation.16 | async-start | bytes 2621440
  303.9 14.8 %collective-permute-start.6 = (f32[2,64,1024]{2,1,0:T(8,128)S(1)}, f32[2,64,1024]{2,1,0:T(8,128)S(1)}, u32[]{:S(2)}, u32[]{:S(2)}) collective-permute-start(f32[2,64,1024]{2,1,0:T(8,128)S(1)} %get-tuple-element.43), channel_id=1, source_target_pairs={{0,1},{1,0},{2,3},{3,2},{4,5},{5,4},{6,7},{7,6},{8,9},{9,8},{10,11... | collective-permute-start | bytes 1572872 | tf_op jit(solution)/shard_map/ppermute | solution.py:308
  304.6 24.1 %collective-permute-start.7 = (f32[2,64,1024]{2,1,0:T(8,128)S(1)}, f32[2,64,1024]{2,1,0:T(8,128)S(1)}, u32[]{:S(2)}, u32[]{:S(2)}) collective-permute-start(f32[2,64,1024]{2,1,0:T(8,128)S(1)} %get-tuple-element.44), channel_id=1, source_target_pairs={{0,2},{1,3},{2,0},{3,1},{4,6},{5,7},{6,4},{7,5},{8,10},{9,11},{10,... | collective-permute-start | bytes 1572872 | tf_op jit(solution)/shard_map/ppermute | solution.py:308
  306.0 23.9 %collective-permute-start.8 = (f32[2,64,1024]{2,1,0:T(8,128)S(1)}, f32[2,64,1024]{2,1,0:T(8,128)S(1)}, u32[]{:S(2)}, u32[]{:S(2)}) collective-permute-start(f32[2,64,1024]{2,1,0:T(8,128)S(1)} %get-tuple-element.45), channel_id=1, source_target_pairs={{0,3},{1,2},{2,1},{3,0},{4,7},{5,6},{6,5},{7,4},{8,11},{9,10},{10,... | collective-permute-start | bytes 1572872 | tf_op jit(solution)/shard_map/ppermute | solution.py:308
  351.1 30.1 %all-to-all-start.4 = ((f32[8,32,1024]{2,1,0:T(8,128)}), f32[8,32,1024]{2,1,0:T(8,128)S(1)}, u32[]{:S(2)}, u32[]{:S(2)}) async-start(f32[8,32,1024]{2,1,0:T(8,128)} %bitcast.37), calls=%async_computation.4 | async-start | bytes 2097152 | tf_op jit(solution)/shard_map/all_to_all | solution.py:302
  354.7 102.1 %reduce-scatter.19.cloned.1.call-start = ((), (), s32[]{:S(2)}) async-start(), calls=%async_computation.18 | async-start | bytes 1310720
  357.8 27.2 %collective-permute-start.9 = (f32[2,64,1024]{2,1,0:T(8,128)}, f32[2,64,1024]{2,1,0:T(8,128)}, u32[]{:S(2)}, u32[]{:S(2)}) collective-permute-start(f32[2,64,1024]{2,1,0:T(8,128)} %get-tuple-element.48), channel_id=1, source_target_pairs={{0,1},{1,0},{2,3},{3,2},{4,5},{5,4},{6,7},{7,6},{8,9},{9,8},{10,11... | collective-permute-start | bytes 1572872 | tf_op jit(solution)/shard_map/ppermute | solution.py:308
  358.5 28.0 %collective-permute-start.10 = (f32[2,64,1024]{2,1,0:T(8,128)}, f32[2,64,1024]{2,1,0:T(8,128)}, u32[]{:S(2)}, u32[]{:S(2)}) collective-permute-start(f32[2,64,1024]{2,1,0:T(8,128)} %get-tuple-element.49), channel_id=1, source_target_pairs={{0,2},{1,3},{2,0},{3,1},{4,6},{5,7},{6,4},{7,5},{8,10},{9,11},{10,... | collective-permute-start | bytes 1572872 | tf_op jit(solution)/shard_map/ppermute | solution.py:308
  359.9 30.4 %collective-permute-start.11 = (f32[2,64,1024]{2,1,0:T(8,128)}, f32[2,64,1024]{2,1,0:T(8,128)}, u32[]{:S(2)}, u32[]{:S(2)}) collective-permute-start(f32[2,64,1024]{2,1,0:T(8,128)} %get-tuple-element.50), channel_id=1, source_target_pairs={{0,3},{1,2},{2,1},{3,0},{4,7},{5,6},{6,5},{7,4},{8,11},{9,10},{10,... | collective-permute-start | bytes 1572872 | tf_op jit(solution)/shard_map/ppermute | solution.py:308
  383.0 16.9 %collective-permute-start.12 = (f32[2,32,1024]{2,1,0:T(8,128)}, f32[2,32,1024]{2,1,0:T(8,128)S(1)}, u32[]{:S(2)}, u32[]{:S(2)}) collective-permute-start(f32[2,32,1024]{2,1,0:T(8,128)} %get-tuple-element.53), channel_id=1, source_target_pairs={{0,1},{1,0},{2,3},{3,2},{4,5},{5,4},{6,7},{7,6},{8,9},{9,8},{10,11... | collective-permute-start | bytes 786440 | tf_op jit(solution)/shard_map/ppermute | solution.py:308
  383.6 16.3 %collective-permute-start.13 = (f32[2,32,1024]{2,1,0:T(8,128)S(1)}, f32[2,32,1024]{2,1,0:T(8,128)S(1)}, u32[]{:S(2)}, u32[]{:S(2)}) collective-permute-start(f32[2,32,1024]{2,1,0:T(8,128)S(1)} %get-tuple-element.54), channel_id=1, source_target_pairs={{0,2},{1,3},{2,0},{3,1},{4,6},{5,7},{6,4},{7,5},{8,10},{9,11},{10,... | collective-permute-start | bytes 786440 | tf_op jit(solution)/shard_map/ppermute | solution.py:308
  385.0 15.9 %collective-permute-start.14 = (f32[2,32,1024]{2,1,0:T(8,128)S(1)}, f32[2,32,1024]{2,1,0:T(8,128)S(1)}, u32[]{:S(2)}, u32[]{:S(2)}) collective-permute-start(f32[2,32,1024]{2,1,0:T(8,128)S(1)} %get-tuple-element.55), channel_id=1, source_target_pairs={{0,3},{1,2},{2,1},{3,0},{4,7},{5,6},{6,5},{7,4},{8,11},{9,10},{10,... | collective-permute-start | bytes 786440 | tf_op jit(solution)/shard_map/ppermute | solution.py:308
  407.7 72.6 %reduce-scatter.17.cloned.1.call-start = ((), (), s32[]{:S(2)}) async-start(), calls=%async_computation.17 | async-start | bytes 2621440
  409.5 8.3 %collective-permute-start.15 = (f32[2,2,48,256]{3,2,1,0:T(8,128)S(1)}, f32[2,2,48,256]{3,2,1,0:T(8,128)S(1)}, u32[]{:S(2)}, u32[]{:S(2)}) collective-permute-start(f32[2,2,48,256]{3,2,1,0:T(8,128)S(1)} %get-tuple-element.57), channel_id=1, source_target_pairs={{0,1},{1,0},{2,3},{3,2},{4,5},{5,4},{6,7},{7,6},{8,9},{9,8},{10,11... | collective-permute-start | bytes 589832 | tf_op jit(solution)/shard_map/ppermute | solution.py:308
  410.8 11.4 %collective-permute-start.16 = (f32[2,2,48,256]{3,2,1,0:T(8,128)S(1)}, f32[2,2,48,256]{3,2,1,0:T(8,128)S(1)}, u32[]{:S(2)}, u32[]{:S(2)}) collective-permute-start(f32[2,2,48,256]{3,2,1,0:T(8,128)S(1)} %get-tuple-element.58), channel_id=1, source_target_pairs={{0,2},{1,3},{2,0},{3,1},{4,6},{5,7},{6,4},{7,5},{8,10},{9,11},{10,... | collective-permute-start | bytes 589832 | tf_op jit(solution)/shard_map/ppermute | solution.py:308
  411.9 13.8 %collective-permute-start.17 = (f32[2,2,48,256]{3,2,1,0:T(8,128)S(1)}, f32[2,2,48,256]{3,2,1,0:T(8,128)S(1)}, u32[]{:S(2)}, u32[]{:S(2)}) collective-permute-start(f32[2,2,48,256]{3,2,1,0:T(8,128)S(1)} %get-tuple-element.59), channel_id=1, source_target_pairs={{0,3},{1,2},{2,1},{3,0},{4,7},{5,6},{6,5},{7,4},{8,11},{9,10},{10,... | collective-permute-start | bytes 589832 | tf_op jit(solution)/shard_map/ppermute | solution.py:308
  426.6 25.8 %all-to-all-start.5 = ((f32[8,2,48,256]{3,2,1,0:T(8,128)}), f32[8,2,48,256]{3,2,1,0:T(8,128)S(1)}, u32[]{:S(2)}, u32[]{:S(2)}) async-start(f32[8,2,48,256]{3,2,1,0:T(8,128)} %bitcast.15), calls=%async_computation.5 | async-start | bytes 1572864 | tf_op jit(solution)/shard_map/all_to_all | solution.py:302
  432.6 8.7 %collective-permute-start.18 = (f32[2,2,32,256]{3,2,1,0:T(8,128)S(1)}, f32[2,2,32,256]{3,2,1,0:T(8,128)S(1)}, u32[]{:S(2)}, u32[]{:S(2)}) collective-permute-start(f32[2,2,32,256]{3,2,1,0:T(8,128)S(1)} %get-tuple-element.61), channel_id=1, source_target_pairs={{0,1},{1,0},{2,3},{3,2},{4,5},{5,4},{6,7},{7,6},{8,9},{9,8},{10,11... | collective-permute-start | bytes 393224 | tf_op jit(solution)/shard_map/ppermute | solution.py:308
  434.6 9.7 %collective-permute-start.20 = (f32[2,2,32,256]{3,2,1,0:T(8,128)S(1)}, f32[2,2,32,256]{3,2,1,0:T(8,128)S(1)}, u32[]{:S(2)}, u32[]{:S(2)}) collective-permute-start(f32[2,2,32,256]{3,2,1,0:T(8,128)S(1)} %get-tuple-element.63), channel_id=1, source_target_pairs={{0,3},{1,2},{2,1},{3,0},{4,7},{5,6},{6,5},{7,4},{8,11},{9,10},{10,... | collective-permute-start | bytes 393224 | tf_op jit(solution)/shard_map/ppermute | solution.py:308
  453.3 41.1 %all-to-all-start.7 = ((f32[8,2,32,256]{3,2,1,0:T(8,128)}), f32[8,2,32,256]{3,2,1,0:T(8,128)S(1)}, u32[]{:S(2)}, u32[]{:S(2)}) async-start(f32[8,2,32,256]{3,2,1,0:T(8,128)} %bitcast.18), calls=%async_computation.7 | async-start | bytes 1048576 | tf_op jit(solution)/shard_map/all_to_all | solution.py:302
  483.8 10.6 %collective-permute-start.22 = (f32[2,2,48,256]{3,2,1,0:T(8,128)S(1)}, f32[2,2,48,256]{3,2,1,0:T(8,128)S(1)}, u32[]{:S(2)}, u32[]{:S(2)}) collective-permute-start(f32[2,2,48,256]{3,2,1,0:T(8,128)S(1)} %get-tuple-element.66), channel_id=1, source_target_pairs={{0,2},{1,3},{2,0},{3,1},{4,6},{5,7},{6,4},{7,5},{8,10},{9,11},{10,... | collective-permute-start | bytes 589832 | tf_op jit(solution)/shard_map/ppermute | solution.py:308
  484.4 10.0 %collective-permute-start.23 = (f32[2,2,48,256]{3,2,1,0:T(8,128)S(1)}, f32[2,2,48,256]{3,2,1,0:T(8,128)S(1)}, u32[]{:S(2)}, u32[]{:S(2)}) collective-permute-start(f32[2,2,48,256]{3,2,1,0:T(8,128)S(1)} %get-tuple-element.67), channel_id=1, source_target_pairs={{0,3},{1,2},{2,1},{3,0},{4,7},{5,6},{6,5},{7,4},{8,11},{9,10},{10,... | collective-permute-start | bytes 589832 | tf_op jit(solution)/shard_map/ppermute | solution.py:308
  495.4 25.6 %all-to-all-start.9 = ((f32[8,2,48,256]{3,2,1,0:T(8,128)}), f32[8,2,48,256]{3,2,1,0:T(8,128)S(1)}, u32[]{:S(2)}, u32[]{:S(2)}) async-start(f32[8,2,48,256]{3,2,1,0:T(8,128)} %bitcast.22), calls=%async_computation.9 | async-start | bytes 1572864 | tf_op jit(solution)/shard_map/all_to_all | solution.py:302
  520.9 18.8 %all-to-all-start.8 = ((f32[8,2,32,256]{3,2,1,0:T(8,128)}), f32[8,2,32,256]{3,2,1,0:T(8,128)S(1)}, u32[]{:S(2)}, u32[]{:S(2)}) async-start(f32[8,2,32,256]{3,2,1,0:T(8,128)} %broadcast_select_fusion.2), calls=%async_computation.8 | async-start | bytes 1048576 | tf_op jit(solution)/shard_map/all_to_all | solution.py:302
  (20 other events, 392.3 us)
Sparse Core Ops, SparseCore 0:
  181.8 76.5 reduce-scatter.12
  339.9 48.4 reduce-scatter.14
  407.8 34.4 reduce-scatter.18
  445.1 35.1 reduce-scatter.16

commit v7 on v6

--- a/solution.py
+++ b/solution.py
@@ -140,7 +140,7 @@
     )
 
 
-def mask_kernel(tiles, mask_ref, integrals_ref, masked_ref):
+def mask_kernel(tiles, mask_ref, integrals_ref, after_ref, masked_ref):
     side = integrals_ref.shape[-1] // tiles
     slot, pair = pl.program_id(0), pl.program_id(1)
     for r in range(tiles):
@@ -151,15 +151,18 @@
             masked_ref[0, 0, spot[0], spot[1]] = jnp.where(keep, tile, jnp.zeros_like(tile))
 
 
-def mask_blocks(integrals, tile_mask):
+def mask_blocks(integrals, tile_mask, after):
     _, slots, pairs, virtuals, _ = integrals.shape
     out_shape = jax.ShapeDtypeStruct((slots, pairs, virtuals, virtuals), jnp.bfloat16)
     return call(
         functools.partial(mask_kernel, tile_mask.shape[-1]),
         "mask",
         tile_mask[0],
-        [integrals],
-        [pl.BlockSpec((1, 1, 1, virtuals, virtuals), lambda s, k, mask: (0, s, k, 0, 0))],
+        [integrals, after],
+        [
+            pl.BlockSpec((1, 1, 1, virtuals, virtuals), lambda s, k, mask: (0, s, k, 0, 0)),
+            pl.BlockSpec(memory_space=pl.ANY),
+        ],
         pl.BlockSpec((1, 1, virtuals, virtuals), lambda s, k, mask: (s, k, 0, 0)),
         out_shape,
         (slots, pairs),
@@ -324,25 +327,33 @@
     first = first_flip(place, amplitudes, sections, sizes[0])
     rest = [flip(place, amplitudes, sections, e, sum(sizes[1:]), first) for e in range(sections)]
     across = [swap(first, "ka"), *part(place, spread(rest), sizes[1:])]
-    masked = mask_blocks(integrals, tile_mask)
-
-    own, returned, partial_rows = [], [place], masked
-    for (start, rows), sent in zip(spans, across):
+    masked = mask_blocks(integrals, tile_mask, across[1])
+
+    own, delivered, after, partial_rows = [], [], across[1], masked
+
+    def send(group, after):
+        columns = spread(cut(place, [own[at] for at in group], sections, pairs))
+        return gather(place, columns, after)
+
+    def deliver(columns):
+        piece = columns.shape[-2:]
+        met = swap(columns.reshape(occupied, slots, *piece), "ia")
+        routed = jnp.take(met.reshape(occupied * slots, *piece), source_row, axis=0)
+        return swap(routed.reshape(occupied, slots, *piece), "ia")
+
+    for at, ((start, rows), sent) in enumerate(zip(spans, across)):
         crossed = swap(sent.reshape(occupied, rows, virtuals), "ia")
-        crossed = crossed.reshape(sections, pairs, rows, virtuals)
-        returned = scatter(place, crossed, returned[0])
+        if at == len(spans) - 1:
+            after = leading = send(GROUPS[0], after)
+        returned = scatter(place, crossed.reshape(sections, pairs, rows, virtuals), after)
+        after = returned[0]
         mirrored = spread(returned)
         partial_rows = product(place, amplitudes, mirrored, masked, start, partial_rows)
         own.append(lax.psum_scatter(partial_rows, "ka", scatter_dimension=0, tiled=False))
 
-    delivered, after = [], returned[0]
-    for group in GROUPS:
-        columns = spread(cut(place, [own[at] for at in group], sections, pairs))
-        columns = gather(place, columns, after)
-        piece = columns.shape[-2:]
-        met = after = swap(columns.reshape(occupied, slots, *piece), "ia")
-        routed = jnp.take(met.reshape(occupied * slots, *piece), source_row, axis=0)
-        delivered.append(swap(routed.reshape(occupied, slots, *piece), "ia"))
+    delivered.append(deliver(leading))
+    for group in GROUPS[1:]:
+        delivered.append(deliver(send(group, delivered[-1])))
     return finish(place, spans, GROUPS, own, delivered)
 
 

time: 598 us -> 529 us (0.88)
  blocking collectives: 219 us -> 142 us
  waiting for transfers between devices: 224 us -> 230 us
    all_to_all x5 -> x4, blocking collectives: 219 us -> 142 us  [swap(): return lax.all_to_all(array, axis, split_axis=0, concat_axis=0, tiled=True)]
    ppermute x24, waiting for transfers between devices: 130 us -> 154 us  [spread(): lax.ppermute(pieces[e], 'ka', [(q, q ^ e) for q in range(count)])]
    unnamed x8, waiting for transfers between devices: 24.1 us -> 0.13 us
    all_to_all x6 -> x7, waiting for transfers between devices: 70.5 us -> 75.4 us  [swap(): return lax.all_to_all(array, axis, split_axis=0, concat_axis=0, tiled=True)]
    all_to_all x6 -> x7, starting transfers between devices: 23.7 us -> 27.2 us  [swap(): return lax.all_to_all(array, axis, split_axis=0, concat_axis=0, tiled=True)]
  transfers between devices with their start and end apart: 34 -> 35, of which waited for: 24 -> 20; matrix products, arithmetic and copies ran while one was open for 1% -> 1% of each run, Pallas kernels for 11% -> 9%
where the time goes in v7:
time: 529 us; the launch traced here: 527 us
  waiting for transfers between devices  230 us (43%)
  blocking collectives  142 us (27%)
  Pallas kernels  70.8 us (13%)
  starting transfers between devices  55.8 us (11%)
  between operations  13.4 us (3%)
  local copies, waits for them, and re-layouts  11.9 us (2%)
    ppermute x24, waiting for transfers between devices, spread(): lax.ppermute(pieces[e], 'ka', [(q, q ^ e) for q in range(count)])  154 us
    all_to_all x4, blocking collectives, swap(): return lax.all_to_all(array, axis, split_axis=0, concat_axis=0, tiled=True)  142 us
    all_to_all x7, waiting for transfers between devices, swap(): return lax.all_to_all(array, axis, split_axis=0, concat_axis=0, tiled=True)  75.4 us
    pallas_call x22, Pallas kernels, call(): pl.pallas_call(kernel, grid_spec=pltpu.PrefetchScalarGridSpec(num_scalar_...  70.8 us
    ppermute x24, starting transfers between devices, spread(): lax.ppermute(pieces[e], 'ka', [(q, q ^ e) for q in range(count)])  28.5 us
    all_to_all x7, starting transfers between devices, swap(): return lax.all_to_all(array, axis, split_axis=0, concat_axis=0, tiled=True)  27.2 us
  transfers between devices with their start and end apart: 35, of which 20 were waited for; matrix products, arithmetic and copies ran while one was open for 1% of the time, Pallas kernels for 9%

profile of v7, /device:TPU:0, one launch (start us, length us, event | category | flops | bytes accessed | tf_op | source)
XLA Modules:
  0.0 527.1 jit_solution(1109197817534397798)
XLA Ops:
  6.5 5.3 %first_flip.1.after_ref = f32[4,2,96,1024]{3,2,1,0:T(8,128)S(1)} custom-call(s32[1]{0:T(128)} %bitcast.place_ref, f32[1,2,1024,1024]{3,2,1,0:T(8,128)} %refs_3_.7), custom_call_target="tpu_custom_call" | custom-call | bytes 6291456 | tf_op jit(solution)/shard_map/first_flip/pallas_call | solution.py:18
  11.8 41.7 %all_to_all.55 = f32[4,2,96,1024]{3,2,1,0:T(8,128)} all-to-all(f32[4,2,96,1024]{3,2,1,0:T(8,128)S(1)} %first_flip.1.after_ref), channel_id=1, replica_groups=mesh['ia'=8,'ka'=4] {'ka'}, dimensions={0} | all-to-all | bytes 6291456 | tf_op jit(solution)/shard_map/all_to_all | solution.py:305
  53.5 4.9 all-to-all-start.1
  69.9 22.1 %collective-permute-done.refs_1_ = f32[2,160,1024]{2,1,0:T(8,128)S(1)} collective-permute-done((f32[2,160,1024]{2,1,0:T(8,128)S(1)}, f32[2,160,1024]{2,1,0:T(8,128)S(1)}, u32[]{:S(2)}, u32[]{:S(2)}) %collective-permute-start) | collective-permute-done | bytes 1310752 | tf_op jit(solution)/shard_map/ppermute | solution.py:311
  92.0 30.3 %collective-permute-done.1.refs_2_ = f32[2,160,1024]{2,1,0:T(8,128)S(1)} collective-permute-done((f32[2,160,1024]{2,1,0:T(8,128)S(1)}, f32[2,160,1024]{2,1,0:T(8,128)S(1)}, u32[]{:S(2)}, u32[]{:S(2)}) %collective-permute-start.1) | collective-permute-done | bytes 1310752 | tf_op jit(solution)/shard_map/ppermute | solution.py:311
  123.4 3.6 part.1
  137.4 8.7 %mask.1.refs_8_.refs_9_ = bf16[2,2,1024,1024]{3,2,1,0:T(8,128)(2,1)} custom-call(s32[2,2,8,8]{3,2,1,0:T(8,128)S(1)} %bitcast.39, bf16[1,2,2,1024,1024]{4,3,2,1,0:T(8,128)(2,1)} %integrals_ref.1, f32[4,2,64,1024]{3,2,1,0:T(8,128)S(1)} %copy-done.1), custom_call_target="tpu_custom_call" | custom-call | bytes 16777216 | tf_op jit(solution)/shard_map/mask/pallas_call | solution.py:18
  146.1 8.3 %collective-permute-done.3.refs_5_ = f32[2,96,1024]{2,1,0:T(8,128)S(1)} collective-permute-done((f32[2,96,1024]{2,1,0:T(8,128)S(1)}, f32[2,96,1024]{2,1,0:T(8,128)S(1)}, u32[]{:S(2)}, u32[]{:S(2)}) %collective-permute-start.3) | collective-permute-done | bytes 786464 | tf_op jit(solution)/shard_map/ppermute | solution.py:311
  154.4 16.1 %collective-permute-done.4.refs_6_ = f32[2,96,1024]{2,1,0:T(8,128)S(1)} collective-permute-done((f32[2,96,1024]{2,1,0:T(8,128)S(1)}, f32[2,96,1024]{2,1,0:T(8,128)S(1)}, u32[]{:S(2)}, u32[]{:S(2)}) %collective-permute-start.4) | collective-permute-done | bytes 786464 | tf_op jit(solution)/shard_map/ppermute | solution.py:311
  170.5 11.4 %product.4.refs_9_ = f32[4,2,96,1024]{3,2,1,0:T(8,128)} custom-call(s32[1]{0:T(128)} %bitcast.place_ref, f32[1,2,1024,1024]{3,2,1,0:T(8,128)} %refs_3_.7, f32[1,2,1024,1024]{3,2,1,0:T(8,128)} %refs_3_.7, f32[1,2,1024,1024]{3,2,1,0:T(8,128)} %refs_3_.7, f32[1,2,1024,1024]{3,2,1,0:T(8,128)} %refs_3_.7, f32[2,96,1024]{2,1,0:T(8,128)S(1)} %get-tuple-element.38.refs_4_.after_ref, ...), custom_call_target="tpu_custom_call" | custom-call | flops 6442450944 | bytes 6291456 | tf_op jit(solution)/shard_map/product/pallas_call | solution.py:18
  181.9 51.8 %all_to_all.56 = f32[8,64,1024]{2,1,0:T(8,128)S(1)} all-to-all(f32[8,64,1024]{2,1,0:T(8,128)S(1)} %bitcast.26), channel_id=1, replica_groups=mesh['ia'=8,'ka'=4] {'ia'}, dimensions={0} | all-to-all | bytes 4194304 | tf_op jit(solution)/shard_map/all_to_all | solution.py:305
  238.5 3.6 all-to-all-start.3
  242.2 7.9 %collective-permute-done.6.refs_5_ = f32[2,64,1024]{2,1,0:T(8,128)S(1)} collective-permute-done((f32[2,64,1024]{2,1,0:T(8,128)}, f32[2,64,1024]{2,1,0:T(8,128)S(1)}, u32[]{:S(2)}, u32[]{:S(2)}) %collective-permute-start.6) | collective-permute-done | bytes 524320 | tf_op jit(solution)/shard_map/ppermute | solution.py:311
  250.1 10.6 %collective-permute-done.7.refs_6_ = f32[2,64,1024]{2,1,0:T(8,128)} collective-permute-done((f32[2,64,1024]{2,1,0:T(8,128)}, f32[2,64,1024]{2,1,0:T(8,128)}, u32[]{:S(2)}, u32[]{:S(2)}) %collective-permute-start.7) | collective-permute-done | bytes 524320 | tf_op jit(solution)/shard_map/ppermute | solution.py:311
  260.7 9.4 %product.5.refs_9_ = f32[4,2,64,1024]{3,2,1,0:T(8,128)} custom-call(s32[1]{0:T(128)} %bitcast.place_ref, f32[1,2,1024,1024]{3,2,1,0:T(8,128)} %refs_3_.7, f32[1,2,1024,1024]{3,2,1,0:T(8,128)} %refs_3_.7, f32[1,2,1024,1024]{3,2,1,0:T(8,128)} %refs_3_.7, f32[1,2,1024,1024]{3,2,1,0:T(8,128)} %refs_3_.7, f32[2,64,1024]{2,1,0:T(8,128)S(1)} %get-tuple-element.42.refs_4_.after_ref, ...), custom_call_target="tpu_custom_call" | custom-call | flops 4294967296 | bytes 4194304 | tf_op jit(solution)/shard_map/product/pallas_call | solution.py:18
  270.1 21.0 %all-to-all-done.3 = f32[8,64,1024]{2,1,0:T(8,128)S(1)} async-done(((f32[8,64,1024]{2,1,0:T(8,128)}), f32[8,64,1024]{2,1,0:T(8,128)S(1)}, u32[]{:S(2)}, u32[]{:S(2)}) %all-to-all-start.3) | async-done | bytes 2097184 | tf_op jit(solution)/shard_map/all_to_all | solution.py:305
  299.2 28.0 %collective-permute-done.12.refs_1_ = f32[2,2,48,256]{3,2,1,0:T(8,128)S(1)} collective-permute-done((f32[2,2,48,256]{3,2,1,0:T(8,128)S(1)}, f32[2,2,48,256]{3,2,1,0:T(8,128)S(1)}, u32[]{:S(2)}, u32[]{:S(2)}) %collective-permute-start.12) | collective-permute-done | bytes 196640 | tf_op jit(solution)/shard_map/ppermute | solution.py:311
  328.7 5.1 collective-permute-done.14.refs_3_
  338.4 9.1 %product.6.refs_9_ = f32[4,2,64,1024]{3,2,1,0:T(8,128)} custom-call(s32[1]{0:T(128)} %bitcast.place_ref, f32[1,2,1024,1024]{3,2,1,0:T(8,128)} %refs_3_.7, f32[1,2,1024,1024]{3,2,1,0:T(8,128)} %refs_3_.7, f32[1,2,1024,1024]{3,2,1,0:T(8,128)} %refs_3_.7, f32[1,2,1024,1024]{3,2,1,0:T(8,128)} %refs_3_.7, f32[2,64,1024]{2,1,0:T(8,128)S(1)} %get-tuple-element.47.refs_4_, ...), custom_call_target="tpu_custom_call" | custom-call | flops 4294967296 | bytes 4194304 | tf_op jit(solution)/shard_map/product/pallas_call | solution.py:18
  347.5 11.7 %all-to-all-done.5 = f32[8,2,48,256]{3,2,1,0:T(8,128)S(1)} async-done(((f32[8,2,48,256]{3,2,1,0:T(8,128)}), f32[8,2,48,256]{3,2,1,0:T(8,128)S(1)}, u32[]{:S(2)}, u32[]{:S(2)}) %all-to-all-start.5) | async-done | bytes 786464 | tf_op jit(solution)/shard_map/all_to_all | solution.py:305
  359.2 3.6 all-to-all-start.4
  365.5 23.8 %all-to-all-done.4 = f32[8,32,1024]{2,1,0:T(8,128)S(1)} async-done(((f32[8,32,1024]{2,1,0:T(8,128)}), f32[8,32,1024]{2,1,0:T(8,128)S(1)}, u32[]{:S(2)}, u32[]{:S(2)}) %all-to-all-start.4) | async-done | bytes 1048608 | tf_op jit(solution)/shard_map/all_to_all | solution.py:305
  389.3 3.5 all-to-all-start.6
  396.5 5.6 %collective-permute-done.15.refs_5_ = f32[2,32,1024]{2,1,0:T(8,128)S(1)} collective-permute-done((f32[2,32,1024]{2,1,0:T(8,128)S(1)}, f32[2,32,1024]{2,1,0:T(8,128)S(1)}, u32[]{:S(2)}, u32[]{:S(2)}) %collective-permute-start.15) | collective-permute-done | bytes 262176 | tf_op jit(solution)/shard_map/ppermute | solution.py:311
  402.1 5.9 %collective-permute-done.16.refs_6_ = f32[2,32,1024]{2,1,0:T(8,128)S(1)} collective-permute-done((f32[2,32,1024]{2,1,0:T(8,128)S(1)}, f32[2,32,1024]{2,1,0:T(8,128)S(1)}, u32[]{:S(2)}, u32[]{:S(2)}) %collective-permute-start.16) | collective-permute-done | bytes 262176 | tf_op jit(solution)/shard_map/ppermute | solution.py:311
  408.1 6.8 %product.7 = f32[4,2,32,1024]{3,2,1,0:T(8,128)} custom-call(s32[1]{0:T(128)} %bitcast.place_ref, f32[1,2,1024,1024]{3,2,1,0:T(8,128)} %refs_3_.7, f32[1,2,1024,1024]{3,2,1,0:T(8,128)} %refs_3_.7, f32[1,2,1024,1024]{3,2,1,0:T(8,128)} %refs_3_.7, f32[1,2,1024,1024]{3,2,1,0:T(8,128)} %refs_3_.7, f32[2,32,1024]{2,1,0:T(8,128)S(1)} %get-tuple-element.56.refs_4_, ...), custom_call_target="tpu_custom_call" | custom-call | flops 2147483648 | bytes 2097152 | tf_op jit(solution)/shard_map/product/pallas_call | solution.py:18
  425.9 4.6 all-to-all-start.7
  430.6 15.3 %all-to-all-done.7 = f32[8,2,32,256]{3,2,1,0:T(8,128)S(1)} async-done(((f32[8,2,32,256]{3,2,1,0:T(8,128)}), f32[8,2,32,256]{3,2,1,0:T(8,128)S(1)}, u32[]{:S(2)}, u32[]{:S(2)}) %all-to-all-start.7) | async-done | bytes 524320 | tf_op jit(solution)/shard_map/all_to_all | solution.py:305
  456.5 4.2 collective-permute-done.21.refs_1_
  460.7 4.7 collective-permute-done.22.refs_2_
  466.1 25.0 %all_to_all.57 = f32[8,2,48,256]{3,2,1,0:T(8,128)} all-to-all(f32[8,2,48,256]{3,2,1,0:T(8,128)S(1)} %bitcast.32), channel_id=1, replica_groups=mesh['ia'=8,'ka'=4] {'ia'}, dimensions={0} | all-to-all | bytes 1572864 | tf_op jit(solution)/shard_map/all_to_all | solution.py:305
  495.2 23.4 %all_to_all.58.refs_6_ = f32[8,2,48,256]{3,2,1,0:T(8,128)S(1)} all-to-all(f32[8,2,48,256]{3,2,1,0:T(8,128)S(1)} %bitcast.43), channel_id=1, replica_groups=mesh['ia'=8,'ka'=4] {'ia'}, dimensions={0} | all-to-all | bytes 1572864 | tf_op jit(solution)/shard_map/all_to_all | solution.py:305
  (113 shorter events, 76.7 us)
Async XLA Ops:
  53.5 76.5 %all-to-all-start.1 = ((f32[8,96,1024]{2,1,0:T(8,128)}), f32[8,96,1024]{2,1,0:T(8,128)}, u32[]{:S(2)}, u32[]{:S(2)}) async-start(f32[8,96,1024]{2,1,0:T(8,128)} %bitcast.40), calls=%async_computation.1 | async-start | bytes 6291456 | tf_op jit(solution)/shard_map/all_to_all | solution.py:305
  58.4 237.5 %reduce-scatter.13.cloned.1.call-start = ((), (), s32[]{:S(2)}) async-start(), calls=%async_computation.15 | async-start | bytes 3932160
  60.4 31.6 %collective-permute-start = (f32[2,160,1024]{2,1,0:T(8,128)S(1)}, f32[2,160,1024]{2,1,0:T(8,128)S(1)}, u32[]{:S(2)}, u32[]{:S(2)}) collective-permute-start(f32[2,160,1024]{2,1,0:T(8,128)S(1)} %flip.5), channel_id=1, source_target_pairs={{0,1},{1,0},{2,3},{3,2},{4,5},{5,4},{6,7},{7,6},{8,9},{9,8},{10,11... | collective-permute-start | bytes 3932168 | tf_op jit(solution)/shard_map/ppermute | solution.py:311
  63.3 59.0 %collective-permute-start.1 = (f32[2,160,1024]{2,1,0:T(8,128)S(1)}, f32[2,160,1024]{2,1,0:T(8,128)S(1)}, u32[]{:S(2)}, u32[]{:S(2)}) collective-permute-start(f32[2,160,1024]{2,1,0:T(8,128)S(1)} %flip.6), channel_id=1, source_target_pairs={{0,2},{1,3},{2,0},{3,1},{4,6},{5,7},{6,4},{7,5},{8,10},{9,11},{10,... | collective-permute-start | bytes 3932168 | tf_op jit(solution)/shard_map/ppermute | solution.py:311
  65.9 56.5 %collective-permute-start.2 = (f32[2,160,1024]{2,1,0:T(8,128)S(1)}, f32[2,160,1024]{2,1,0:T(8,128)S(1)}, u32[]{:S(2)}, u32[]{:S(2)}) collective-permute-start(f32[2,160,1024]{2,1,0:T(8,128)S(1)} %flip.7), channel_id=1, source_target_pairs={{0,3},{1,2},{2,1},{3,0},{4,7},{5,6},{6,5},{7,4},{8,11},{9,10},{10,... | collective-permute-start | bytes 3932168 | tf_op jit(solution)/shard_map/ppermute | solution.py:311
  133.9 20.5 %collective-permute-start.3 = (f32[2,96,1024]{2,1,0:T(8,128)S(1)}, f32[2,96,1024]{2,1,0:T(8,128)S(1)}, u32[]{:S(2)}, u32[]{:S(2)}) collective-permute-start(f32[2,96,1024]{2,1,0:T(8,128)S(1)} %get-tuple-element.39), channel_id=1, source_target_pairs={{0,1},{1,0},{2,3},{3,2},{4,5},{5,4},{6,7},{7,6},{8,9},{9,8},{10,11... | collective-permute-start | bytes 2359304 | tf_op jit(solution)/shard_map/ppermute | solution.py:311
  134.9 35.7 %collective-permute-start.4 = (f32[2,96,1024]{2,1,0:T(8,128)S(1)}, f32[2,96,1024]{2,1,0:T(8,128)S(1)}, u32[]{:S(2)}, u32[]{:S(2)}) collective-permute-start(f32[2,96,1024]{2,1,0:T(8,128)S(1)} %get-tuple-element.40), channel_id=1, source_target_pairs={{0,2},{1,3},{2,0},{3,1},{4,6},{5,7},{6,4},{7,5},{8,10},{9,11},{10,... | collective-permute-start | bytes 2359304 | tf_op jit(solution)/shard_map/ppermute | solution.py:311
  135.4 35.1 %collective-permute-start.5 = (f32[2,96,1024]{2,1,0:T(8,128)S(1)}, f32[2,96,1024]{2,1,0:T(8,128)S(1)}, u32[]{:S(2)}, u32[]{:S(2)}) collective-permute-start(f32[2,96,1024]{2,1,0:T(8,128)S(1)} %get-tuple-element.41), channel_id=1, source_target_pairs={{0,3},{1,2},{2,1},{3,0},{4,7},{5,6},{6,5},{7,4},{8,11},{9,10},{10,... | collective-permute-start | bytes 2359304 | tf_op jit(solution)/shard_map/ppermute | solution.py:311
  235.0 15.1 %collective-permute-start.6 = (f32[2,64,1024]{2,1,0:T(8,128)}, f32[2,64,1024]{2,1,0:T(8,128)S(1)}, u32[]{:S(2)}, u32[]{:S(2)}) collective-permute-start(f32[2,64,1024]{2,1,0:T(8,128)} %get-tuple-element.43), channel_id=1, source_target_pairs={{0,1},{1,0},{2,3},{3,2},{4,5},{5,4},{6,7},{7,6},{8,9},{9,8},{10,11... | collective-permute-start | bytes 1572872 | tf_op jit(solution)/shard_map/ppermute | solution.py:311
  236.1 24.6 %collective-permute-start.7 = (f32[2,64,1024]{2,1,0:T(8,128)}, f32[2,64,1024]{2,1,0:T(8,128)}, u32[]{:S(2)}, u32[]{:S(2)}) collective-permute-start(f32[2,64,1024]{2,1,0:T(8,128)} %get-tuple-element.44), channel_id=1, source_target_pairs={{0,2},{1,3},{2,0},{3,1},{4,6},{5,7},{6,4},{7,5},{8,10},{9,11},{10,... | collective-permute-start | bytes 1572872 | tf_op jit(solution)/shard_map/ppermute | solution.py:311
  237.1 23.7 %collective-permute-start.8 = (f32[2,64,1024]{2,1,0:T(8,128)}, f32[2,64,1024]{2,1,0:T(8,128)}, u32[]{:S(2)}, u32[]{:S(2)}) collective-permute-start(f32[2,64,1024]{2,1,0:T(8,128)} %get-tuple-element.45), channel_id=1, source_target_pairs={{0,3},{1,2},{2,1},{3,0},{4,7},{5,6},{6,5},{7,4},{8,11},{9,10},{10,... | collective-permute-start | bytes 1572872 | tf_op jit(solution)/shard_map/ppermute | solution.py:311
  238.5 52.6 %all-to-all-start.3 = ((f32[8,64,1024]{2,1,0:T(8,128)}), f32[8,64,1024]{2,1,0:T(8,128)S(1)}, u32[]{:S(2)}, u32[]{:S(2)}) async-start(f32[8,64,1024]{2,1,0:T(8,128)} %bitcast.44), calls=%async_computation.3 | async-start | bytes 4194304 | tf_op jit(solution)/shard_map/all_to_all | solution.py:305
  242.1 172.8 %reduce-scatter.15.cloned.1.call-start = ((), (), s32[]{:S(2)}) async-start(), calls=%async_computation.16 | async-start | bytes 2621440
  292.4 45.9 %collective-permute-start.9 = (f32[2,64,1024]{2,1,0:T(8,128)}, f32[2,64,1024]{2,1,0:T(8,128)S(1)}, u32[]{:S(2)}, u32[]{:S(2)}) collective-permute-start(f32[2,64,1024]{2,1,0:T(8,128)} %get-tuple-element.48), channel_id=1, source_target_pairs={{0,1},{1,0},{2,3},{3,2},{4,5},{5,4},{6,7},{7,6},{8,9},{9,8},{10,11... | collective-permute-start | bytes 1572872 | tf_op jit(solution)/shard_map/ppermute | solution.py:311
  293.5 44.8 %collective-permute-start.10 = (f32[2,64,1024]{2,1,0:T(8,128)}, f32[2,64,1024]{2,1,0:T(8,128)S(1)}, u32[]{:S(2)}, u32[]{:S(2)}) collective-permute-start(f32[2,64,1024]{2,1,0:T(8,128)} %get-tuple-element.49), channel_id=1, source_target_pairs={{0,2},{1,3},{2,0},{3,1},{4,6},{5,7},{6,4},{7,5},{8,10},{9,11},{10,... | collective-permute-start | bytes 1572872 | tf_op jit(solution)/shard_map/ppermute | solution.py:311
  294.5 43.9 %collective-permute-start.11 = (f32[2,64,1024]{2,1,0:T(8,128)}, f32[2,64,1024]{2,1,0:T(8,128)S(1)}, u32[]{:S(2)}, u32[]{:S(2)}) collective-permute-start(f32[2,64,1024]{2,1,0:T(8,128)} %get-tuple-element.50), channel_id=1, source_target_pairs={{0,3},{1,2},{2,1},{3,0},{4,7},{5,6},{6,5},{7,4},{8,11},{9,10},{10,... | collective-permute-start | bytes 1572872 | tf_op jit(solution)/shard_map/ppermute | solution.py:311
  297.1 30.1 %collective-permute-start.12 = (f32[2,2,48,256]{3,2,1,0:T(8,128)S(1)}, f32[2,2,48,256]{3,2,1,0:T(8,128)S(1)}, u32[]{:S(2)}, u32[]{:S(2)}) collective-permute-start(f32[2,2,48,256]{3,2,1,0:T(8,128)S(1)} %get-tuple-element.53), channel_id=1, source_target_pairs={{0,1},{1,0},{2,3},{3,2},{4,5},{5,4},{6,7},{7,6},{8,9},{9,8},{10,11... | collective-permute-start | bytes 589832 | tf_op jit(solution)/shard_map/ppermute | solution.py:311
  298.3 30.4 %collective-permute-start.13 = (f32[2,2,48,256]{3,2,1,0:T(8,128)S(1)}, f32[2,2,48,256]{3,2,1,0:T(8,128)S(1)}, u32[]{:S(2)}, u32[]{:S(2)}) collective-permute-start(f32[2,2,48,256]{3,2,1,0:T(8,128)S(1)} %get-tuple-element.54), channel_id=1, source_target_pairs={{0,2},{1,3},{2,0},{3,1},{4,6},{5,7},{6,4},{7,5},{8,10},{9,11},{10,... | collective-permute-start | bytes 589832 | tf_op jit(solution)/shard_map/ppermute | solution.py:311
  334.7 24.4 %all-to-all-start.5 = ((f32[8,2,48,256]{3,2,1,0:T(8,128)}), f32[8,2,48,256]{3,2,1,0:T(8,128)S(1)}, u32[]{:S(2)}, u32[]{:S(2)}) async-start(f32[8,2,48,256]{3,2,1,0:T(8,128)} %bitcast.15), calls=%async_computation.5 | async-start | bytes 1572864 | tf_op jit(solution)/shard_map/all_to_all | solution.py:305
  338.3 112.5 %reduce-scatter.17.cloned.1.call-start = ((), (), s32[]{:S(2)}) async-start(), calls=%async_computation.17 | async-start | bytes 2621440
  359.2 30.1 %all-to-all-start.4 = ((f32[8,32,1024]{2,1,0:T(8,128)}), f32[8,32,1024]{2,1,0:T(8,128)S(1)}, u32[]{:S(2)}, u32[]{:S(2)}) async-start(f32[8,32,1024]{2,1,0:T(8,128)} %bitcast.12), calls=%async_computation.4 | async-start | bytes 2097152 | tf_op jit(solution)/shard_map/all_to_all | solution.py:305
  389.3 35.8 %all-to-all-start.6 = ((f32[8,2,48,256]{3,2,1,0:T(8,128)}), f32[8,2,48,256]{3,2,1,0:T(8,128)S(1)}, u32[]{:S(2)}, u32[]{:S(2)}) async-start(f32[8,2,48,256]{3,2,1,0:T(8,128)} %bitcast.17), calls=%async_computation.6 | async-start | bytes 1572864 | tf_op jit(solution)/shard_map/all_to_all | solution.py:305
  392.8 58.0 %reduce-scatter.19.cloned.1.call-start = ((), (), s32[]{:S(2)}) async-start(), calls=%async_computation.18 | async-start | bytes 1310720
  392.9 9.2 %collective-permute-start.15 = (f32[2,32,1024]{2,1,0:T(8,128)S(1)}, f32[2,32,1024]{2,1,0:T(8,128)S(1)}, u32[]{:S(2)}, u32[]{:S(2)}) collective-permute-start(f32[2,32,1024]{2,1,0:T(8,128)S(1)} %get-tuple-element.57), channel_id=1, source_target_pairs={{0,1},{1,0},{2,3},{3,2},{4,5},{5,4},{6,7},{7,6},{8,9},{9,8},{10,11... | collective-permute-start | bytes 786440 | tf_op jit(solution)/shard_map/ppermute | solution.py:311
  394.2 13.9 %collective-permute-start.16 = (f32[2,32,1024]{2,1,0:T(8,128)S(1)}, f32[2,32,1024]{2,1,0:T(8,128)S(1)}, u32[]{:S(2)}, u32[]{:S(2)}) collective-permute-start(f32[2,32,1024]{2,1,0:T(8,128)S(1)} %get-tuple-element.58), channel_id=1, source_target_pairs={{0,2},{1,3},{2,0},{3,1},{4,6},{5,7},{6,4},{7,5},{8,10},{9,11},{10,... | collective-permute-start | bytes 786440 | tf_op jit(solution)/shard_map/ppermute | solution.py:311
  395.0 13.0 %collective-permute-start.17 = (f32[2,32,1024]{2,1,0:T(8,128)S(1)}, f32[2,32,1024]{2,1,0:T(8,128)S(1)}, u32[]{:S(2)}, u32[]{:S(2)}) collective-permute-start(f32[2,32,1024]{2,1,0:T(8,128)S(1)} %get-tuple-element.59), channel_id=1, source_target_pairs={{0,3},{1,2},{2,1},{3,0},{4,7},{5,6},{6,5},{7,4},{8,11},{9,10},{10,... | collective-permute-start | bytes 786440 | tf_op jit(solution)/shard_map/ppermute | solution.py:311
  416.9 8.1 %collective-permute-start.19 = (f32[2,2,32,256]{3,2,1,0:T(8,128)S(1)}, f32[2,2,32,256]{3,2,1,0:T(8,128)S(1)}, u32[]{:S(2)}, u32[]{:S(2)}) collective-permute-start(f32[2,2,32,256]{3,2,1,0:T(8,128)S(1)} %get-tuple-element.62), channel_id=1, source_target_pairs={{0,2},{1,3},{2,0},{3,1},{4,6},{5,7},{6,4},{7,5},{8,10},{9,11},{10,... | collective-permute-start | bytes 393224 | tf_op jit(solution)/shard_map/ppermute | solution.py:311
  425.9 19.9 %all-to-all-start.7 = ((f32[8,2,32,256]{3,2,1,0:T(8,128)}), f32[8,2,32,256]{3,2,1,0:T(8,128)S(1)}, u32[]{:S(2)}, u32[]{:S(2)}) async-start(f32[8,2,32,256]{3,2,1,0:T(8,128)} %bitcast.18), calls=%async_computation.7 | async-start | bytes 1048576 | tf_op jit(solution)/shard_map/all_to_all | solution.py:305
  447.3 18.8 %all-to-all-start.8 = ((f32[8,2,32,256]{3,2,1,0:T(8,128)}), f32[8,2,32,256]{3,2,1,0:T(8,128)S(1)}, u32[]{:S(2)}, u32[]{:S(2)}) async-start(f32[8,2,32,256]{3,2,1,0:T(8,128)} %broadcast_select_fusion.2), calls=%async_computation.8 | async-start | bytes 1048576 | tf_op jit(solution)/shard_map/all_to_all | solution.py:305
  452.9 7.8 %collective-permute-start.21 = (f32[2,2,48,256]{3,2,1,0:T(8,128)S(1)}, f32[2,2,48,256]{3,2,1,0:T(8,128)S(1)}, u32[]{:S(2)}, u32[]{:S(2)}) collective-permute-start(f32[2,2,48,256]{3,2,1,0:T(8,128)S(1)} %get-tuple-element.65), channel_id=1, source_target_pairs={{0,1},{1,0},{2,3},{3,2},{4,5},{5,4},{6,7},{7,6},{8,9},{9,8},{10,11... | collective-permute-start | bytes 589832 | tf_op jit(solution)/shard_map/ppermute | solution.py:311
  454.3 11.1 %collective-permute-start.22 = (f32[2,2,48,256]{3,2,1,0:T(8,128)S(1)}, f32[2,2,48,256]{3,2,1,0:T(8,128)S(1)}, u32[]{:S(2)}, u32[]{:S(2)}) collective-permute-start(f32[2,2,48,256]{3,2,1,0:T(8,128)S(1)} %get-tuple-element.66), channel_id=1, source_target_pairs={{0,2},{1,3},{2,0},{3,1},{4,6},{5,7},{6,4},{7,5},{8,10},{9,11},{10,... | collective-permute-start | bytes 589832 | tf_op jit(solution)/shard_map/ppermute | solution.py:311
  455.4 10.0 %collective-permute-start.23 = (f32[2,2,48,256]{3,2,1,0:T(8,128)S(1)}, f32[2,2,48,256]{3,2,1,0:T(8,128)S(1)}, u32[]{:S(2)}, u32[]{:S(2)}) collective-permute-start(f32[2,2,48,256]{3,2,1,0:T(8,128)S(1)} %get-tuple-element.67), channel_id=1, source_target_pairs={{0,3},{1,2},{2,1},{3,0},{4,7},{5,6},{6,5},{7,4},{8,11},{9,10},{10,... | collective-permute-start | bytes 589832 | tf_op jit(solution)/shard_map/ppermute | solution.py:311
  (16 other events, 163.6 us)
Sparse Core Ops, SparseCore 0:
  182.1 42.3 reduce-scatter.12
  270.2 39.0 reduce-scatter.14
  347.6 35.5 reduce-scatter.16
  415.0 28.1 reduce-scatter.18

commit v8 on v7

--- a/solution.py
+++ b/solution.py
@@ -7,8 +7,9 @@
 from jax.experimental.pallas import tpu as pltpu
 from jax.sharding import PartitionSpec as P
 
-CHUNKS = (3, 2, 2, 1)
-GROUPS = ((0,), (1,), (2, 3))
+CHUNKS = (2, 3, 2, 1)
+SETS = ((0,), (1,), (2, 3))
+GROUPS = ((0,), (1, 2, 3))
 LANES = 128
 VMEM_BYTES = 48 * 1024 * 1024
 
@@ -54,16 +55,15 @@
     )
 
 
-def flip_kernel(place_ref, blocks_ref, after_ref, piece_ref):
-    wide = blocks_ref.shape[-1]
-    piece_ref[0] = blocks_ref[0, 0].T[wide - piece_ref.shape[1] :]
-
-
-def flip(place, amplitudes, sections, e, rows, after):
+def flip_kernel(start, place_ref, blocks_ref, after_ref, piece_ref):
+    piece_ref[0] = blocks_ref[0, 0].T[start : start + piece_ref.shape[1]]
+
+
+def flip(place, amplitudes, sections, e, start, rows, after):
     pairs, virtuals = amplitudes.shape[1], amplitudes.shape[3]
     wide = virtuals // sections
     return call(
-        flip_kernel,
+        functools.partial(flip_kernel, start),
         "flip",
         place,
         [amplitudes, after],
@@ -78,7 +78,7 @@
 
 
 def part_kernel(count, place_ref, *refs):
-    pieces, out_refs = refs[:count], refs[count:]
+    pieces, out_refs = refs[:count], refs[count + 1 :]
     for e, piece in enumerate(pieces):
         at = 0
         for out_ref in out_refs:
@@ -87,14 +87,15 @@
             at += rows
 
 
-def part(place, pieces, sizes):
+def part(place, pieces, sizes, after):
     count, (pairs, rows, virtuals) = len(pieces), pieces[0].shape
     return call(
         functools.partial(part_kernel, count),
         "part",
         place,
-        pieces,
-        [pl.BlockSpec((1, rows, virtuals), lambda d, at: (d, 0, 0))] * count,
+        [*pieces, after],
+        [pl.BlockSpec((1, rows, virtuals), lambda d, at: (d, 0, 0))] * count
+        + [pl.BlockSpec(memory_space=pl.ANY)],
         [pl.BlockSpec((count, 1, size, virtuals), lambda d, at: (0, d, 0, 0)) for size in sizes],
         [jax.ShapeDtypeStruct((count, pairs, size, virtuals), jnp.float32) for size in sizes],
         (pairs,),
@@ -171,7 +172,7 @@
 
 def product_kernel(sections, place_ref, *refs):
     own_refs, mirrored_refs, refs = refs[:sections], refs[sections : 2 * sections], refs[2 * sections :]
-    masked_ref, _, out_ref, split_ref = refs
+    masked_ref, out_refs, split_ref = refs[0], refs[2:-1], refs[-1]
     pairs, rows, _ = mirrored_refs[0].shape
     tall = sections * rows
 
@@ -190,8 +191,8 @@
         both = jnp.dot(split_ref[k], masked_ref[0, k], preferred_element_type=jnp.float32)
         both = both[:tall] + both[tall:]
         total = both if total is None else total + both
-    for e in range(sections):
-        out_ref[place_ref[0] ^ e, 0] = total[e * rows : (e + 1) * rows]
+    for e, out_ref in enumerate(out_refs):
+        out_ref[0] = total[e * rows : (e + 1) * rows]
 
 
 def product(place, own, mirrored, masked, start, after):
@@ -217,11 +218,30 @@
             pl.BlockSpec((1, pairs, virtuals, wide), lambda s, n, at: (s, 0, 0, n)),
             pl.BlockSpec(memory_space=pl.ANY),
         ],
-        pl.BlockSpec((sections, 1, rows, wide), lambda s, n, at: (0, s, 0, n)),
-        jax.ShapeDtypeStruct((sections, slots, rows, virtuals), jnp.float32),
+        [pl.BlockSpec((1, rows, wide), lambda s, n, at: (s, 0, n))] * sections,
+        [jax.ShapeDtypeStruct((slots, rows, virtuals), jnp.float32)] * sections,
         (slots, virtuals // wide),
         scratch=[pltpu.VMEM((pairs, 2 * sections * rows, virtuals), jnp.bfloat16)],
         flops=4 * sections * rows * pairs * virtuals * virtuals * slots,
+    )
+
+
+def add_kernel(place_ref, *refs):
+    refs[-1][...] = sum((part[...] for part in refs[1:-1]), refs[0][...])
+
+
+def add(place, parts):
+    slots, rows, virtuals = parts[0].shape
+    block = pl.BlockSpec((1, rows, virtuals), lambda s, at: (s, 0, 0))
+    return call(
+        add_kernel,
+        "add",
+        place,
+        parts,
+        [block] * len(parts),
+        block,
+        jax.ShapeDtypeStruct(parts[0].shape, jnp.float32),
+        (slots,),
     )
 
 
@@ -324,13 +344,6 @@
     partner_slot = jnp.where(pair_list[pair_list, 0] == owners[:, None], 0, 1).astype(jnp.int32)
     source_row = (pair_list * slots + partner_slot).reshape(-1)
 
-    first = first_flip(place, amplitudes, sections, sizes[0])
-    rest = [flip(place, amplitudes, sections, e, sum(sizes[1:]), first) for e in range(sections)]
-    across = [swap(first, "ka"), *part(place, spread(rest), sizes[1:])]
-    masked = mask_blocks(integrals, tile_mask, across[1])
-
-    own, delivered, after, partial_rows = [], [], across[1], masked
-
     def send(group, after):
         columns = spread(cut(place, [own[at] for at in group], sections, pairs))
         return gather(place, columns, after)
@@ -341,15 +354,30 @@
         routed = jnp.take(met.reshape(occupied * slots, *piece), source_row, axis=0)
         return swap(routed.reshape(occupied, slots, *piece), "ia")
 
+    first = first_flip(place, amplitudes, sections, sizes[0])
+    masked = mask_blocks(integrals, tile_mask, first)
+    across = [swap(first, "ka")]
+    tokens = [first, *across]
+    for chunks, after in zip(SETS[1:], tokens):
+        rows = [sizes[at] for at in chunks]
+        pieces = [
+            flip(place, amplitudes, sections, e, spans[chunks[0]][0], sum(rows), after)
+            for e in range(sections)
+        ]
+        across += part(place, spread(pieces), rows, masked)
+    ready = [across[chunks[0]] for chunks in SETS[1:]]
+
+    own, delivered, partial_rows = [], [], [masked]
     for at, ((start, rows), sent) in enumerate(zip(spans, across)):
         crossed = swap(sent.reshape(occupied, rows, virtuals), "ia")
+        after = ready[at] if at < len(ready) else crossed
         if at == len(spans) - 1:
-            after = leading = send(GROUPS[0], after)
+            after = leading = send(GROUPS[0], crossed)
         returned = scatter(place, crossed.reshape(sections, pairs, rows, virtuals), after)
-        after = returned[0]
-        mirrored = spread(returned)
-        partial_rows = product(place, amplitudes, mirrored, masked, start, partial_rows)
-        own.append(lax.psum_scatter(partial_rows, "ka", scatter_dimension=0, tiled=False))
+        partial_rows = product(
+            place, amplitudes, spread(returned), masked, start, partial_rows[0]
+        )
+        own.append(add(place, spread(partial_rows)))
 
     delivered.append(deliver(leading))
     for group in GROUPS[1:]:

time: 529 us -> 539 us (1.019)
  blocking collectives: 142 us -> 112 us
  Pallas kernels: 70.8 us -> 86.8 us
  between operations: 13.4 us -> 0.37 us
  starting transfers between devices: 55.8 us -> 68.4 us
  local copies, waits for them, and re-layouts: 11.9 us -> 24.5 us
  waiting for transfers between devices: 230 us -> 241 us
    all_to_all x4 -> x3, blocking collectives: 142 us -> 112 us  [swap(): return lax.all_to_all(array, axis, split_axis=0, concat_axis=0, tiled=True)]
    pallas_call x22 -> x29, Pallas kernels: 70.8 us -> 86.8 us  [call(): pl.pallas_call(kernel, grid_spec=pltpu.PrefetchScalarGridSpec(num_scalar_...]
    ppermute x24 -> x36, starting transfers between devices: 28.5 us -> 41.3 us  [spread(): lax.ppermute(pieces[e], 'ka', [(q, q ^ e) for q in range(count)])]
    unnamed x27 -> x71, local copies, waits for them, and re-layouts: 6.95 us -> 17.9 us
    ppermute x24 -> x36, waiting for transfers between devices: 154 us -> 165 us  [spread(): lax.ppermute(pieces[e], 'ka', [(q, q ^ e) for q in range(count)])]
    all_to_all x7 -> x6, waiting for transfers between devices: 75.4 us -> 75.8 us  [swap(): return lax.all_to_all(array, axis, split_axis=0, concat_axis=0, tiled=True)]
    all_to_all x7 -> x6, starting transfers between devices: 27.2 us -> 27.1 us  [swap(): return lax.all_to_all(array, axis, split_axis=0, concat_axis=0, tiled=True)]
  transfers between devices with their start and end apart: 35 -> 42, of which waited for: 20 -> 16; matrix products, arithmetic and copies ran while one was open for 1% -> 1% of each run, Pallas kernels for 9% -> 15%
where the time goes in v8:
time: 539 us; the launch traced here: 537 us
  waiting for transfers between devices  241 us (45%)
  blocking collectives  112 us (21%)
  Pallas kernels  86.8 us (16%)
  starting transfers between devices  68.4 us (13%)
  local copies, waits for them, and re-layouts  24.5 us (5%)
    ppermute x36, waiting for transfers between devices, spread(): lax.ppermute(pieces[e], 'ka', [(q, q ^ e) for q in range(count)])  165 us
    all_to_all x3, blocking collectives, swap(): return lax.all_to_all(array, axis, split_axis=0, concat_axis=0, tiled=True)  112 us
    pallas_call x29, Pallas kernels, call(): pl.pallas_call(kernel, grid_spec=pltpu.PrefetchScalarGridSpec(num_scalar_...  86.8 us
    all_to_all x6, waiting for transfers between devices, swap(): return lax.all_to_all(array, axis, split_axis=0, concat_axis=0, tiled=True)  75.8 us
    ppermute x36, starting transfers between devices, spread(): lax.ppermute(pieces[e], 'ka', [(q, q ^ e) for q in range(count)])  41.3 us
    all_to_all x6, starting transfers between devices, swap(): return lax.all_to_all(array, axis, split_axis=0, concat_axis=0, tiled=True)  27.1 us
    unnamed x71, local copies, waits for them, and re-layouts  17.9 us
  transfers between devices with their start and end apart: 42, of which 16 were waited for; matrix products, arithmetic and copies ran while one was open for 1% of the time, Pallas kernels for 15%

profile of v8, /device:TPU:0, one launch (start us, length us, event | category | flops | bytes accessed | tf_op | source)
XLA Modules:
  0.0 536.8 jit_solution(13679011149129082857)
XLA Ops:
  0.0 5.3 first_flip.1.after_ref
  5.3 30.4 %all_to_all.45.after_ref = f32[4,2,64,1024]{3,2,1,0:T(8,128)} all-to-all(f32[4,2,64,1024]{3,2,1,0:T(8,128)S(1)} %first_flip.1.after_ref), channel_id=1, replica_groups=mesh['ia'=8,'ka'=4] {'ka'}, dimensions={0} | all-to-all | bytes 4194304 | tf_op jit(solution)/shard_map/all_to_all | solution.py:325
  35.7 4.9 all-to-all-start.1
  51.2 8.7 %mask.1.refs_4_.refs_8_.refs_9_ = bf16[2,2,1024,1024]{3,2,1,0:T(8,128)(2,1)} custom-call(s32[2,2,8,8]{3,2,1,0:T(8,128)S(1)} %bitcast.22, bf16[1,2,2,1024,1024]{4,3,2,1,0:T(8,128)(2,1)} %integrals_ref.1, f32[4,2,64,1024]{3,2,1,0:T(8,128)S(1)} %first_flip.1.after_ref), custom_call_target="tpu_custom_call" | custom-call | bytes 16777216 | tf_op jit(solution)/shard_map/mask/pallas_call | solution.py:19
  64.4 19.0 %collective-permute-done.10.refs_2_ = f32[2,96,1024]{2,1,0:T(8,128)S(1)} collective-permute-done((f32[2,96,1024]{2,1,0:T(8,128)S(1)}, f32[2,96,1024]{2,1,0:T(8,128)S(1)}, u32[]{:S(2)}, u32[]{:S(2)}) %collective-permute-start.10) | collective-permute-done | bytes 786464 | tf_op jit(solution)/shard_map/ppermute | solution.py:331
  85.1 4.6 all-to-all-done.1
  89.8 4.4 all-to-all-start.3
  105.5 11.0 %collective-permute-done.refs_1_ = f32[2,96,1024]{2,1,0:T(8,128)S(1)} collective-permute-done((f32[2,96,1024]{2,1,0:T(8,128)S(1)}, f32[2,96,1024]{2,1,0:T(8,128)S(1)}, u32[]{:S(2)}, u32[]{:S(2)}) %collective-permute-start) | collective-permute-done | bytes 786464 | tf_op jit(solution)/shard_map/ppermute | solution.py:331
  116.5 18.9 %collective-permute-done.1.refs_2_ = f32[2,96,1024]{2,1,0:T(8,128)S(1)} collective-permute-done((f32[2,96,1024]{2,1,0:T(8,128)S(1)}, f32[2,96,1024]{2,1,0:T(8,128)S(1)}, u32[]{:S(2)}, u32[]{:S(2)}) %collective-permute-start.1) | collective-permute-done | bytes 786464 | tf_op jit(solution)/shard_map/ppermute | solution.py:331
  137.2 6.0 %all-to-all-done.3.after_ref = f32[8,64,1024]{2,1,0:T(8,128)} async-done(((f32[8,64,1024]{2,1,0:T(8,128)}), f32[8,64,1024]{2,1,0:T(8,128)}, u32[]{:S(2)}, u32[]{:S(2)}) %all-to-all-start.3) | async-done | bytes 2097184 | tf_op jit(solution)/shard_map/all_to_all | solution.py:325
  143.2 4.5 all-to-all-start.2
  147.7 2.9 scatter.4
  154.1 65.1 %all-to-all-done.2 = f32[8,96,1024]{2,1,0:T(8,128)} async-done(((f32[8,96,1024]{2,1,0:T(8,128)}), f32[8,96,1024]{2,1,0:T(8,128)}, u32[]{:S(2)}, u32[]{:S(2)}) %all-to-all-start.2) | async-done | bytes 3145760 | tf_op jit(solution)/shard_map/all_to_all | solution.py:325
  219.2 3.6 all-to-all-start.4
  224.7 8.4 %product.4 = (f32[2,64,1024]{2,1,0:T(8,128)S(1)}, f32[2,64,1024]{2,1,0:T(8,128)S(1)}, f32[2,64,1024]{2,1,0:T(8,128)S(1)}, f32[2,64,1024]{2,1,0:T(8,128)S(1)}) custom-call(s32[1]{0:T(128)} %bitcast.place_ref, f32[1,2,1024,1024]{3,2,1,0:T(8,128)} %refs_3_.7, f32[1,2,1024,1024]{3,2,1,0:T(8,128)} %refs_3_.7, f32[1,2,1024,1024]{3,2,1,0:T(8,128)} %refs_3_.7, ...), custom_call_target="tpu_custom_call" | custom-call | flops 4294967296 | bytes 4194304 | tf_op jit(solution)/shard_map/product/pallas_call | solution.py:19
  236.6 3.5 scatter.5
  242.5 5.4 %collective-permute-done.6.refs_1_ = f32[2,64,1024]{2,1,0:T(8,128)S(1)} collective-permute-done((f32[2,64,1024]{2,1,0:T(8,128)S(1)}, f32[2,64,1024]{2,1,0:T(8,128)S(1)}, u32[]{:S(2)}, u32[]{:S(2)}) %collective-permute-start.6) | collective-permute-done | bytes 524320 | tf_op jit(solution)/shard_map/ppermute | solution.py:331
  248.8 11.3 %collective-permute-done.7.refs_2_ = f32[2,64,1024]{2,1,0:T(8,128)S(1)} collective-permute-done((f32[2,64,1024]{2,1,0:T(8,128)S(1)}, f32[2,64,1024]{2,1,0:T(8,128)S(1)}, u32[]{:S(2)}, u32[]{:S(2)}) %collective-permute-start.7) | collective-permute-done | bytes 524320 | tf_op jit(solution)/shard_map/ppermute | solution.py:331
  263.1 32.1 %collective-permute-done.24.refs_1_ = f32[2,2,32,256]{3,2,1,0:T(8,128)S(1)} collective-permute-done((f32[2,2,32,256]{3,2,1,0:T(8,128)S(1)}, f32[2,2,32,256]{3,2,1,0:T(8,128)S(1)}, u32[]{:S(2)}, u32[]{:S(2)}) %collective-permute-start.24) | collective-permute-done | bytes 131104 | tf_op jit(solution)/shard_map/ppermute | solution.py:331
  297.0 2.9 scatter.6
  306.3 4.8 all-to-all-start.5
  317.8 11.3 %product.5 = (f32[2,96,1024]{2,1,0:T(8,128)S(1)}, f32[2,96,1024]{2,1,0:T(8,128)S(1)}, f32[2,96,1024]{2,1,0:T(8,128)S(1)}, f32[2,96,1024]{2,1,0:T(8,128)S(1)}) custom-call(s32[1]{0:T(128)} %bitcast.place_ref, f32[1,2,1024,1024]{3,2,1,0:T(8,128)} %refs_3_.7, f32[1,2,1024,1024]{3,2,1,0:T(8,128)} %refs_3_.7, f32[1,2,1024,1024]{3,2,1,0:T(8,128)} %refs_3_.7, ...), custom_call_target="tpu_custom_call" | custom-call | flops 6442450944 | bytes 6291456 | tf_op jit(solution)/shard_map/product/pallas_call | solution.py:19
  331.1 9.2 %product.6 = (f32[2,64,1024]{2,1,0:T(8,128)S(1)}, f32[2,64,1024]{2,1,0:T(8,128)}, f32[2,64,1024]{2,1,0:T(8,128)S(1)}, f32[2,64,1024]{2,1,0:T(8,128)S(1)}) custom-call(s32[1]{0:T(128)} %bitcast.place_ref, f32[1,2,1024,1024]{3,2,1,0:T(8,128)} %refs_3_.7, f32[1,2,1024,1024]{3,2,1,0:T(8,128)} %refs_3_.7, f32[1,2,1024,1024]{3,2,1,0:T(8,128)} %refs_3_.7, ...), custom_call_target="tpu_custom_call" | custom-call | flops 4294967296 | bytes 4194304 | tf_op jit(solution)/shard_map/product/pallas_call | solution.py:19
  341.7 6.8 %product.7 = (f32[2,32,1024]{2,1,0:T(8,128)S(1)}, f32[2,32,1024]{2,1,0:T(8,128)}, f32[2,32,1024]{2,1,0:T(8,128)}, f32[2,32,1024]{2,1,0:T(8,128)S(1)}) custom-call(s32[1]{0:T(128)} %bitcast.place_ref, f32[1,2,1024,1024]{3,2,1,0:T(8,128)} %refs_3_.7, f32[1,2,1024,1024]{3,2,1,0:T(8,128)} %refs_3_.7, f32[1,2,1024,1024]{3,2,1,0:T(8,128)} %refs_3_.7, ...), custom_call_target="tpu_custom_call" | custom-call | flops 2147483648 | bytes 2097152 | tf_op jit(solution)/shard_map/product/pallas_call | solution.py:19
  353.5 7.5 %collective-permute-done.30.refs_1_ = f32[2,32,1024]{2,1,0:T(8,128)S(1)} collective-permute-done((f32[2,32,1024]{2,1,0:T(8,128)}, f32[2,32,1024]{2,1,0:T(8,128)S(1)}, u32[]{:S(2)}, u32[]{:S(2)}) %collective-permute-start.30) | collective-permute-done | bytes 262176 | tf_op jit(solution)/shard_map/ppermute | solution.py:331
  372.8 5.1 all-to-all-start.6
  381.8 39.9 %collective-permute-done.22.refs_2_ = f32[2,64,1024]{2,1,0:T(8,128)S(1)} collective-permute-done((f32[2,64,1024]{2,1,0:T(8,128)}, f32[2,64,1024]{2,1,0:T(8,128)S(1)}, u32[]{:S(2)}, u32[]{:S(2)}) %collective-permute-start.22) | collective-permute-done | bytes 524320 | tf_op jit(solution)/shard_map/ppermute | solution.py:331
  431.0 8.8 %collective-permute-done.33.refs_1_ = f32[2,2,96,256]{3,2,1,0:T(8,128)S(1)} collective-permute-done((f32[2,2,96,256]{3,2,1,0:T(8,128)}, f32[2,2,96,256]{3,2,1,0:T(8,128)S(1)}, u32[]{:S(2)}, u32[]{:S(2)}) %collective-permute-start.33) | collective-permute-done | bytes 393248 | tf_op jit(solution)/shard_map/ppermute | solution.py:331
  440.1 7.0 %collective-permute-done.35.refs_3_ = f32[2,2,96,256]{3,2,1,0:T(8,128)} collective-permute-done((f32[2,2,96,256]{3,2,1,0:T(8,128)}, f32[2,2,96,256]{3,2,1,0:T(8,128)}, u32[]{:S(2)}, u32[]{:S(2)}) %collective-permute-start.35) | collective-permute-done | bytes 393248 | tf_op jit(solution)/shard_map/ppermute | solution.py:331
  448.3 41.4 %all_to_all.46 = f32[8,2,96,256]{3,2,1,0:T(8,128)} all-to-all(f32[8,2,96,256]{3,2,1,0:T(8,128)S(1)} %bitcast.21), channel_id=1, replica_groups=mesh['ia'=8,'ka'=4] {'ia'}, dimensions={0} | all-to-all | bytes 3145728 | tf_op jit(solution)/shard_map/all_to_all | solution.py:325
  489.7 3.2 gather_fusion.2
  494.5 40.3 %all_to_all.47.refs_5_ = f32[8,2,96,256]{3,2,1,0:T(8,128)S(1)} all-to-all(f32[8,2,96,256]{3,2,1,0:T(8,128)S(1)} %broadcast_select_fusion), channel_id=1, replica_groups=mesh['ia'=8,'ka'=4] {'ia'}, dimensions={0} | all-to-all | bytes 3145728 | tf_op jit(solution)/shard_map/all_to_all | solution.py:325
  (167 shorter events, 98.5 us)
Async XLA Ops:
  35.7 54.1 %all-to-all-start.1 = ((f32[8,64,1024]{2,1,0:T(8,128)}), f32[8,64,1024]{2,1,0:T(8,128)}, u32[]{:S(2)}, u32[]{:S(2)}) async-start(f32[8,64,1024]{2,1,0:T(8,128)} %bitcast.18), calls=%async_computation.1 | async-start | bytes 4194304 | tf_op jit(solution)/shard_map/all_to_all | solution.py:325
  44.0 20.4 %collective-permute-start.9 = (f32[2,96,1024]{2,1,0:T(8,128)S(1)}, f32[2,96,1024]{2,1,0:T(8,128)S(1)}, u32[]{:S(2)}, u32[]{:S(2)}) collective-permute-start(f32[2,96,1024]{2,1,0:T(8,128)S(1)} %flip.13), channel_id=1, source_target_pairs={{0,1},{1,0},{2,3},{3,2},{4,5},{5,4},{6,7},{7,6},{8,9},{9,8},{10,11... | collective-permute-start | bytes 2359304 | tf_op jit(solution)/shard_map/ppermute | solution.py:331
  46.8 36.6 %collective-permute-start.10 = (f32[2,96,1024]{2,1,0:T(8,128)S(1)}, f32[2,96,1024]{2,1,0:T(8,128)S(1)}, u32[]{:S(2)}, u32[]{:S(2)}) collective-permute-start(f32[2,96,1024]{2,1,0:T(8,128)S(1)} %flip.14), channel_id=1, source_target_pairs={{0,2},{1,3},{2,0},{3,1},{4,6},{5,7},{6,4},{7,5},{8,10},{9,11},{10,... | collective-permute-start | bytes 2359304 | tf_op jit(solution)/shard_map/ppermute | solution.py:331
  49.2 34.2 %collective-permute-start.11 = (f32[2,96,1024]{2,1,0:T(8,128)S(1)}, f32[2,96,1024]{2,1,0:T(8,128)S(1)}, u32[]{:S(2)}, u32[]{:S(2)}) collective-permute-start(f32[2,96,1024]{2,1,0:T(8,128)S(1)} %flip.15), channel_id=1, source_target_pairs={{0,3},{1,2},{2,1},{3,0},{4,7},{5,6},{6,5},{7,4},{8,11},{9,10},{10,... | collective-permute-start | bytes 2359304 | tf_op jit(solution)/shard_map/ppermute | solution.py:331
  89.8 53.4 %all-to-all-start.3 = ((f32[8,64,1024]{2,1,0:T(8,128)}), f32[8,64,1024]{2,1,0:T(8,128)}, u32[]{:S(2)}, u32[]{:S(2)}) async-start(f32[8,64,1024]{2,1,0:T(8,128)} %bitcast.20), calls=%async_computation.3 | async-start | bytes 4194304 | tf_op jit(solution)/shard_map/all_to_all | solution.py:325
  96.1 20.4 %collective-permute-start = (f32[2,96,1024]{2,1,0:T(8,128)S(1)}, f32[2,96,1024]{2,1,0:T(8,128)S(1)}, u32[]{:S(2)}, u32[]{:S(2)}) collective-permute-start(f32[2,96,1024]{2,1,0:T(8,128)S(1)} %flip.9), channel_id=1, source_target_pairs={{0,1},{1,0},{2,3},{3,2},{4,5},{5,4},{6,7},{7,6},{8,9},{9,8},{10,11... | collective-permute-start | bytes 2359304 | tf_op jit(solution)/shard_map/ppermute | solution.py:331
  99.0 36.4 %collective-permute-start.1 = (f32[2,96,1024]{2,1,0:T(8,128)S(1)}, f32[2,96,1024]{2,1,0:T(8,128)S(1)}, u32[]{:S(2)}, u32[]{:S(2)}) collective-permute-start(f32[2,96,1024]{2,1,0:T(8,128)S(1)} %flip.10), channel_id=1, source_target_pairs={{0,2},{1,3},{2,0},{3,1},{4,6},{5,7},{6,4},{7,5},{8,10},{9,11},{10,... | collective-permute-start | bytes 2359304 | tf_op jit(solution)/shard_map/ppermute | solution.py:331
  101.5 33.9 %collective-permute-start.2 = (f32[2,96,1024]{2,1,0:T(8,128)S(1)}, f32[2,96,1024]{2,1,0:T(8,128)S(1)}, u32[]{:S(2)}, u32[]{:S(2)}) collective-permute-start(f32[2,96,1024]{2,1,0:T(8,128)S(1)} %flip.11), channel_id=1, source_target_pairs={{0,3},{1,2},{2,1},{3,0},{4,7},{5,6},{6,5},{7,4},{8,11},{9,10},{10,... | collective-permute-start | bytes 2359304 | tf_op jit(solution)/shard_map/ppermute | solution.py:331
  143.2 76.0 %all-to-all-start.2 = ((f32[8,96,1024]{2,1,0:T(8,128)}), f32[8,96,1024]{2,1,0:T(8,128)}, u32[]{:S(2)}, u32[]{:S(2)}) async-start(f32[8,96,1024]{2,1,0:T(8,128)} %bitcast.23), calls=%async_computation.2 | async-start | bytes 6291456 | tf_op jit(solution)/shard_map/all_to_all | solution.py:325
  150.5 72.2 %collective-permute-start.3 = (f32[2,64,1024]{2,1,0:T(8,128)}, f32[2,64,1024]{2,1,0:T(8,128)S(1)}, u32[]{:S(2)}, u32[]{:S(2)}) collective-permute-start(f32[2,64,1024]{2,1,0:T(8,128)} %get-tuple-element.48), channel_id=1, source_target_pairs={{0,1},{1,0},{2,3},{3,2},{4,5},{5,4},{6,7},{7,6},{8,9},{9,8},{10,11... | collective-permute-start | bytes 1572872 | tf_op jit(solution)/shard_map/ppermute | solution.py:331
  151.5 71.3 %collective-permute-start.4 = (f32[2,64,1024]{2,1,0:T(8,128)}, f32[2,64,1024]{2,1,0:T(8,128)S(1)}, u32[]{:S(2)}, u32[]{:S(2)}) collective-permute-start(f32[2,64,1024]{2,1,0:T(8,128)} %get-tuple-element.49), channel_id=1, source_target_pairs={{0,2},{1,3},{2,0},{3,1},{4,6},{5,7},{6,4},{7,5},{8,10},{9,11},{10,... | collective-permute-start | bytes 1572872 | tf_op jit(solution)/shard_map/ppermute | solution.py:331
  152.0 70.7 %collective-permute-start.5 = (f32[2,64,1024]{2,1,0:T(8,128)}, f32[2,64,1024]{2,1,0:T(8,128)S(1)}, u32[]{:S(2)}, u32[]{:S(2)}) collective-permute-start(f32[2,64,1024]{2,1,0:T(8,128)} %get-tuple-element.50), channel_id=1, source_target_pairs={{0,3},{1,2},{2,1},{3,0},{4,7},{5,6},{6,5},{7,4},{8,11},{9,10},{10,... | collective-permute-start | bytes 1572872 | tf_op jit(solution)/shard_map/ppermute | solution.py:331
  219.2 84.0 %all-to-all-start.4 = ((f32[8,32,1024]{2,1,0:T(8,128)}), f32[8,32,1024]{2,1,0:T(8,128)S(1)}, u32[]{:S(2)}, u32[]{:S(2)}) async-start(f32[8,32,1024]{2,1,0:T(8,128)} %bitcast.8), calls=%async_computation.4 | async-start | bytes 2097152 | tf_op jit(solution)/shard_map/all_to_all | solution.py:325
  234.1 26.0 %collective-permute-start.7 = (f32[2,64,1024]{2,1,0:T(8,128)S(1)}, f32[2,64,1024]{2,1,0:T(8,128)S(1)}, u32[]{:S(2)}, u32[]{:S(2)}) collective-permute-start(f32[2,64,1024]{2,1,0:T(8,128)S(1)} %get-tuple-element.53), channel_id=1, source_target_pairs={{0,2},{1,3},{2,0},{3,1},{4,6},{5,7},{6,4},{7,5},{8,10},{9,11},{10,... | collective-permute-start | bytes 1572872 | tf_op jit(solution)/shard_map/ppermute | solution.py:331
  234.6 25.5 %collective-permute-start.8 = (f32[2,64,1024]{2,1,0:T(8,128)S(1)}, f32[2,64,1024]{2,1,0:T(8,128)S(1)}, u32[]{:S(2)}, u32[]{:S(2)}) collective-permute-start(f32[2,64,1024]{2,1,0:T(8,128)S(1)} %get-tuple-element.54), channel_id=1, source_target_pairs={{0,3},{1,2},{2,1},{3,0},{4,7},{5,6},{6,5},{7,4},{8,11},{9,10},{10,... | collective-permute-start | bytes 1572872 | tf_op jit(solution)/shard_map/ppermute | solution.py:331
  241.0 70.1 %collective-permute-start.12 = (f32[2,96,1024]{2,1,0:T(8,128)}, f32[2,96,1024]{2,1,0:T(8,128)S(1)}, u32[]{:S(2)}, u32[]{:S(2)}) collective-permute-start(f32[2,96,1024]{2,1,0:T(8,128)} %get-tuple-element.57), channel_id=1, source_target_pairs={{0,1},{1,0},{2,3},{3,2},{4,5},{5,4},{6,7},{7,6},{8,9},{9,8},{10,11... | collective-permute-start | bytes 2359304 | tf_op jit(solution)/shard_map/ppermute | solution.py:331
  241.9 71.0 %collective-permute-start.13 = (f32[2,96,1024]{2,1,0:T(8,128)}, f32[2,96,1024]{2,1,0:T(8,128)}, u32[]{:S(2)}, u32[]{:S(2)}) collective-permute-start(f32[2,96,1024]{2,1,0:T(8,128)} %get-tuple-element.58), channel_id=1, source_target_pairs={{0,2},{1,3},{2,0},{3,1},{4,6},{5,7},{6,4},{7,5},{8,10},{9,11},{10,... | collective-permute-start | bytes 2359304 | tf_op jit(solution)/shard_map/ppermute | solution.py:331
  247.9 66.5 %collective-permute-start.14 = (f32[2,96,1024]{2,1,0:T(8,128)}, f32[2,96,1024]{2,1,0:T(8,128)}, u32[]{:S(2)}, u32[]{:S(2)}) collective-permute-start(f32[2,96,1024]{2,1,0:T(8,128)} %get-tuple-element.59), channel_id=1, source_target_pairs={{0,3},{1,2},{2,1},{3,0},{4,7},{5,6},{6,5},{7,4},{8,11},{9,10},{10,... | collective-permute-start | bytes 2359304 | tf_op jit(solution)/shard_map/ppermute | solution.py:331
  261.0 34.2 %collective-permute-start.24 = (f32[2,2,32,256]{3,2,1,0:T(8,128)S(1)}, f32[2,2,32,256]{3,2,1,0:T(8,128)S(1)}, u32[]{:S(2)}, u32[]{:S(2)}) collective-permute-start(f32[2,2,32,256]{3,2,1,0:T(8,128)S(1)} %get-tuple-element.74), channel_id=1, source_target_pairs={{0,1},{1,0},{2,3},{3,2},{4,5},{5,4},{6,7},{7,6},{8,9},{9,8},{10,11... | collective-permute-start | bytes 393224 | tf_op jit(solution)/shard_map/ppermute | solution.py:331
  262.2 38.5 %collective-permute-start.25 = (f32[2,2,32,256]{3,2,1,0:T(8,128)}, f32[2,2,32,256]{3,2,1,0:T(8,128)S(1)}, u32[]{:S(2)}, u32[]{:S(2)}) collective-permute-start(f32[2,2,32,256]{3,2,1,0:T(8,128)} %get-tuple-element.75), channel_id=1, source_target_pairs={{0,2},{1,3},{2,0},{3,1},{4,6},{5,7},{6,4},{7,5},{8,10},{9,11},{10,... | collective-permute-start | bytes 393224 | tf_op jit(solution)/shard_map/ppermute | solution.py:331
  300.6 29.4 %collective-permute-start.18 = (f32[2,64,1024]{2,1,0:T(8,128)}, f32[2,64,1024]{2,1,0:T(8,128)}, u32[]{:S(2)}, u32[]{:S(2)}) collective-permute-start(f32[2,64,1024]{2,1,0:T(8,128)} %get-tuple-element.65), channel_id=1, source_target_pairs={{0,1},{1,0},{2,3},{3,2},{4,5},{5,4},{6,7},{7,6},{8,9},{9,8},{10,11... | collective-permute-start | bytes 1572872 | tf_op jit(solution)/shard_map/ppermute | solution.py:331
  302.1 28.9 %collective-permute-start.19 = (f32[2,64,1024]{2,1,0:T(8,128)}, f32[2,64,1024]{2,1,0:T(8,128)}, u32[]{:S(2)}, u32[]{:S(2)}) collective-permute-start(f32[2,64,1024]{2,1,0:T(8,128)} %get-tuple-element.66), channel_id=1, source_target_pairs={{0,2},{1,3},{2,0},{3,1},{4,6},{5,7},{6,4},{7,5},{8,10},{9,11},{10,... | collective-permute-start | bytes 1572872 | tf_op jit(solution)/shard_map/ppermute | solution.py:331
  306.3 57.6 %all-to-all-start.5 = ((f32[8,2,32,256]{3,2,1,0:T(8,128)}), f32[8,2,32,256]{3,2,1,0:T(8,128)}, u32[]{:S(2)}, u32[]{:S(2)}) async-start(f32[8,2,32,256]{3,2,1,0:T(8,128)} %bitcast.10), calls=%async_computation.5 | async-start | bytes 1048576 | tf_op jit(solution)/shard_map/all_to_all | solution.py:325
  312.9 28.8 %collective-permute-start.27 = (f32[2,32,1024]{2,1,0:T(8,128)}, f32[2,32,1024]{2,1,0:T(8,128)S(1)}, u32[]{:S(2)}, u32[]{:S(2)}) collective-permute-start(f32[2,32,1024]{2,1,0:T(8,128)} %get-tuple-element.78), channel_id=1, source_target_pairs={{0,1},{1,0},{2,3},{3,2},{4,5},{5,4},{6,7},{7,6},{8,9},{9,8},{10,11... | collective-permute-start | bytes 786440 | tf_op jit(solution)/shard_map/ppermute | solution.py:331
  314.4 27.3 %collective-permute-start.28 = (f32[2,32,1024]{2,1,0:T(8,128)}, f32[2,32,1024]{2,1,0:T(8,128)S(1)}, u32[]{:S(2)}, u32[]{:S(2)}) collective-permute-start(f32[2,32,1024]{2,1,0:T(8,128)} %get-tuple-element.79), channel_id=1, source_target_pairs={{0,2},{1,3},{2,0},{3,1},{4,6},{5,7},{6,4},{7,5},{8,10},{9,11},{10,... | collective-permute-start | bytes 786440 | tf_op jit(solution)/shard_map/ppermute | solution.py:331
  340.3 28.6 %collective-permute-start.21 = (f32[2,64,1024]{2,1,0:T(8,128)}, f32[2,64,1024]{2,1,0:T(8,128)S(1)}, u32[]{:S(2)}, u32[]{:S(2)}) collective-permute-start(f32[2,64,1024]{2,1,0:T(8,128)} %get-tuple-element.69), channel_id=1, source_target_pairs={{0,1},{1,0},{2,3},{3,2},{4,5},{5,4},{6,7},{7,6},{8,9},{9,8},{10,11... | collective-permute-start | bytes 1572872 | tf_op jit(solution)/shard_map/ppermute | solution.py:331
  352.9 71.8 %collective-permute-start.15 = (f32[2,96,1024]{2,1,0:T(8,128)}, f32[2,96,1024]{2,1,0:T(8,128)}, u32[]{:S(2)}, u32[]{:S(2)}) collective-permute-start(f32[2,96,1024]{2,1,0:T(8,128)} %copy-done.28), channel_id=1, source_target_pairs={{0,1},{1,0},{2,3},{3,2},{4,5},{5,4},{6,7},{7,6},{8,9},{9,8},{10,11... | collective-permute-start | bytes 2359304 | tf_op jit(solution)/shard_map/ppermute | solution.py:331
  361.0 63.6 %collective-permute-start.16 = (f32[2,96,1024]{2,1,0:T(8,128)}, f32[2,96,1024]{2,1,0:T(8,128)}, u32[]{:S(2)}, u32[]{:S(2)}) collective-permute-start(f32[2,96,1024]{2,1,0:T(8,128)} %copy-done.27), channel_id=1, source_target_pairs={{0,2},{1,3},{2,0},{3,1},{4,6},{5,7},{6,4},{7,5},{8,10},{9,11},{10,... | collective-permute-start | bytes 2359304 | tf_op jit(solution)/shard_map/ppermute | solution.py:331
  362.4 62.2 %collective-permute-start.17 = (f32[2,96,1024]{2,1,0:T(8,128)}, f32[2,96,1024]{2,1,0:T(8,128)}, u32[]{:S(2)}, u32[]{:S(2)}) collective-permute-start(f32[2,96,1024]{2,1,0:T(8,128)} %copy-done.26), channel_id=1, source_target_pairs={{0,3},{1,2},{2,1},{3,0},{4,7},{5,6},{6,5},{7,4},{8,11},{9,10},{10,... | collective-permute-start | bytes 2359304 | tf_op jit(solution)/shard_map/ppermute | solution.py:331
  368.2 53.5 %collective-permute-start.22 = (f32[2,64,1024]{2,1,0:T(8,128)}, f32[2,64,1024]{2,1,0:T(8,128)S(1)}, u32[]{:S(2)}, u32[]{:S(2)}) collective-permute-start(f32[2,64,1024]{2,1,0:T(8,128)} %copy-done.30), channel_id=1, source_target_pairs={{0,2},{1,3},{2,0},{3,1},{4,6},{5,7},{6,4},{7,5},{8,10},{9,11},{10,... | collective-permute-start | bytes 1572872 | tf_op jit(solution)/shard_map/ppermute | solution.py:331
  368.9 53.6 %collective-permute-start.23 = (f32[2,64,1024]{2,1,0:T(8,128)}, f32[2,64,1024]{2,1,0:T(8,128)}, u32[]{:S(2)}, u32[]{:S(2)}) collective-permute-start(f32[2,64,1024]{2,1,0:T(8,128)} %copy-done.29), channel_id=1, source_target_pairs={{0,3},{1,2},{2,1},{3,0},{4,7},{5,6},{6,5},{7,4},{8,11},{9,10},{10,... | collective-permute-start | bytes 1572872 | tf_op jit(solution)/shard_map/ppermute | solution.py:331
  372.8 58.2 %all-to-all-start.6 = ((f32[8,2,32,256]{3,2,1,0:T(8,128)}), f32[8,2,32,256]{3,2,1,0:T(8,128)S(1)}, u32[]{:S(2)}, u32[]{:S(2)}) async-start(f32[8,2,32,256]{3,2,1,0:T(8,128)} %broadcast_select_fusion.1), calls=%async_computation.6 | async-start | bytes 1048576 | tf_op jit(solution)/shard_map/all_to_all | solution.py:325
  (45 other events, 324.3 us)

commit v9 on v8

--- a/solution.py
+++ b/solution.py
@@ -9,19 +9,26 @@
 
 CHUNKS = (2, 3, 2, 1)
 SETS = ((0,), (1,), (2, 3))
-GROUPS = ((0,), (1, 2, 3))
+GROUPS = ((0,), (1,), (2, 3))
 LANES = 128
 VMEM_BYTES = 48 * 1024 * 1024
 
 
-def call(kernel, name, scalars, operands, in_specs, out_specs, out_shape, grid, scratch=(), flops=0):
+def call(
+    kernel, name, scalars, operands, in_specs, out_specs, out_shape, grid, scratch=(), flops=0, after=()
+):
     moved = sum(x.size * x.dtype.itemsize for x in jax.tree.leaves(out_shape)) * 2
+    reads = 1 + len(operands)
+
+    def trimmed(*refs):
+        kernel(*refs[:reads], *refs[reads + len(after) :])
+
     return pl.pallas_call(
-        kernel,
+        trimmed,
         grid_spec=pltpu.PrefetchScalarGridSpec(
             num_scalar_prefetch=1,
             grid=grid,
-            in_specs=in_specs,
+            in_specs=list(in_specs) + [pl.BlockSpec(memory_space=pl.ANY)] * len(after),
             out_specs=out_specs,
             scratch_shapes=list(scratch),
         ),
@@ -29,7 +36,7 @@
         compiler_params=pltpu.CompilerParams(vmem_limit_bytes=VMEM_BYTES),
         cost_estimate=pl.CostEstimate(flops=flops, bytes_accessed=moved, transcendentals=0),
         name=name,
-    )(scalars, *operands)
+    )(scalars, *operands, *after)
 
 
 def whole(shape):
@@ -55,7 +62,7 @@
     )
 
 
-def flip_kernel(start, place_ref, blocks_ref, after_ref, piece_ref):
+def flip_kernel(start, place_ref, blocks_ref, piece_ref):
     piece_ref[0] = blocks_ref[0, 0].T[start : start + piece_ref.shape[1]]
 
 
@@ -66,44 +73,38 @@
         functools.partial(flip_kernel, start),
         "flip",
         place,
-        [amplitudes, after],
-        [
-            pl.BlockSpec((1, 1, virtuals, wide), lambda d, at: (0, d, 0, at[0] ^ e)),
-            pl.BlockSpec(memory_space=pl.ANY),
-        ],
+        [amplitudes],
+        [pl.BlockSpec((1, 1, virtuals, wide), lambda d, at: (0, d, 0, at[0] ^ e))],
         pl.BlockSpec((1, rows, virtuals), lambda d, at: (d, 0, 0)),
         jax.ShapeDtypeStruct((pairs, rows, virtuals), jnp.float32),
         (pairs,),
-    )
-
-
-def part_kernel(count, place_ref, *refs):
-    pieces, out_refs = refs[:count], refs[count + 1 :]
+        after=after,
+    )
+
+
+def part_kernel(start, place_ref, *refs):
+    pieces, out_ref = refs[:-1], refs[-1]
     for e, piece in enumerate(pieces):
-        at = 0
-        for out_ref in out_refs:
-            rows = out_ref.shape[2]
-            out_ref[place_ref[0] ^ e, 0] = piece[0, at : at + rows]
-            at += rows
-
-
-def part(place, pieces, sizes, after):
+        out_ref[place_ref[0] ^ e, 0] = piece[0, start : start + out_ref.shape[2]]
+
+
+def part(place, pieces, start, size, after):
     count, (pairs, rows, virtuals) = len(pieces), pieces[0].shape
     return call(
-        functools.partial(part_kernel, count),
+        functools.partial(part_kernel, start),
         "part",
         place,
-        [*pieces, after],
-        [pl.BlockSpec((1, rows, virtuals), lambda d, at: (d, 0, 0))] * count
-        + [pl.BlockSpec(memory_space=pl.ANY)],
-        [pl.BlockSpec((count, 1, size, virtuals), lambda d, at: (0, d, 0, 0)) for size in sizes],
-        [jax.ShapeDtypeStruct((count, pairs, size, virtuals), jnp.float32) for size in sizes],
+        pieces,
+        [pl.BlockSpec((1, rows, virtuals), lambda d, at: (d, 0, 0))] * count,
+        pl.BlockSpec((count, 1, size, virtuals), lambda d, at: (0, d, 0, 0)),
+        jax.ShapeDtypeStruct((count, pairs, size, virtuals), jnp.float32),
         (pairs,),
+        after=after,
     )
 
 
 def gather_kernel(place_ref, *refs):
-    pieces, out_ref = refs[:-2], refs[-1]
+    pieces, out_ref = refs[:-1], refs[-1]
     for e, piece in enumerate(pieces):
         out_ref[e] = piece[...]
 
@@ -114,15 +115,16 @@
         gather_kernel,
         "gather",
         place,
-        [*pieces, after],
-        [whole(pieces[0].shape)] * len(pieces) + [pl.BlockSpec(memory_space=pl.ANY)],
+        pieces,
+        [whole(pieces[0].shape)] * len(pieces),
         whole(shape),
         jax.ShapeDtypeStruct(shape, jnp.float32),
         (1,),
-    )
-
-
-def scatter_kernel(place_ref, stacked_ref, after_ref, *pieces):
+        after=after,
+    )
+
+
+def scatter_kernel(place_ref, stacked_ref, *pieces):
     for e, piece in enumerate(pieces):
         piece[...] = stacked_ref[place_ref[0] ^ e]
 
@@ -133,15 +135,16 @@
         scatter_kernel,
         "scatter",
         place,
-        [stacked, after],
-        [whole(stacked.shape), pl.BlockSpec(memory_space=pl.ANY)],
+        [stacked],
+        [whole(stacked.shape)],
         [whole(shape)] * count,
         [jax.ShapeDtypeStruct(shape, jnp.float32)] * count,
         (1,),
-    )
-
-
-def mask_kernel(tiles, mask_ref, integrals_ref, after_ref, masked_ref):
+        after=after,
+    )
+
+
+def mask_kernel(tiles, mask_ref, integrals_ref, masked_ref):
     side = integrals_ref.shape[-1] // tiles
     slot, pair = pl.program_id(0), pl.program_id(1)
     for r in range(tiles):
@@ -159,20 +162,18 @@
         functools.partial(mask_kernel, tile_mask.shape[-1]),
         "mask",
         tile_mask[0],
-        [integrals, after],
-        [
-            pl.BlockSpec((1, 1, 1, virtuals, virtuals), lambda s, k, mask: (0, s, k, 0, 0)),
-            pl.BlockSpec(memory_space=pl.ANY),
-        ],
+        [integrals],
+        [pl.BlockSpec((1, 1, 1, virtuals, virtuals), lambda s, k, mask: (0, s, k, 0, 0))],
         pl.BlockSpec((1, 1, virtuals, virtuals), lambda s, k, mask: (s, k, 0, 0)),
         out_shape,
         (slots, pairs),
+        after=after,
     )
 
 
 def product_kernel(sections, place_ref, *refs):
     own_refs, mirrored_refs, refs = refs[:sections], refs[sections : 2 * sections], refs[2 * sections :]
-    masked_ref, out_refs, split_ref = refs[0], refs[2:-1], refs[-1]
+    masked_ref, out_refs, split_ref = refs[0], refs[1:-1], refs[-1]
     pairs, rows, _ = mirrored_refs[0].shape
     tall = sections * rows
 
@@ -205,7 +206,7 @@
         functools.partial(product_kernel, sections),
         "product",
         place,
-        [own] * sections + list(mirrored) + [masked, after],
+        [own] * sections + list(mirrored) + [masked],
         [
             pl.BlockSpec(
                 tuple(pl.Element(size) for size in (1, pairs, rows, virtuals)),
@@ -214,15 +215,13 @@
             for e in range(sections)
         ]
         + [whole(mirrored[0].shape)] * sections
-        + [
-            pl.BlockSpec((1, pairs, virtuals, wide), lambda s, n, at: (s, 0, 0, n)),
-            pl.BlockSpec(memory_space=pl.ANY),
-        ],
+        + [pl.BlockSpec((1, pairs, virtuals, wide), lambda s, n, at: (s, 0, 0, n))],
         [pl.BlockSpec((1, rows, wide), lambda s, n, at: (s, 0, n))] * sections,
         [jax.ShapeDtypeStruct((slots, rows, virtuals), jnp.float32)] * sections,
         (slots, virtuals // wide),
         scratch=[pltpu.VMEM((pairs, 2 * sections * rows, virtuals), jnp.bfloat16)],
         flops=4 * sections * rows * pairs * virtuals * virtuals * slots,
+        after=after,
     )
 
 
@@ -344,9 +343,25 @@
     partner_slot = jnp.where(pair_list[pair_list, 0] == owners[:, None], 0, 1).astype(jnp.int32)
     source_row = (pair_list * slots + partner_slot).reshape(-1)
 
-    def send(group, after):
-        columns = spread(cut(place, [own[at] for at in group], sections, pairs))
-        return gather(place, columns, after)
+    def fetch(chunks, after):
+        start, rows = spans[chunks[0]][0], sum(sizes[at] for at in chunks)
+        pieces = [flip(place, amplitudes, sections, e, start, rows, after) for e in range(sections)]
+        pieces = spread(pieces)
+        return [
+            functools.partial(part, place, pieces, spans[at][0] - start, sizes[at]) for at in chunks
+        ]
+
+    def hop(at):
+        crossed = swap(across[at].reshape(occupied, sizes[at], virtuals), "ia")
+        return crossed.reshape(sections, pairs, sizes[at], virtuals)
+
+    def multiply(at, returned, after):
+        start = spans[at][0]
+        return product(place, amplitudes, spread(returned), masked, start, after)
+
+    def send(group):
+        columns = cut(place, [own[at] for at in group], sections, pairs)
+        return columns[0], lambda after: gather(place, spread(columns), after)
 
     def deliver(columns):
         piece = columns.shape[-2:]
@@ -355,33 +370,34 @@
         return swap(routed.reshape(occupied, slots, *piece), "ia")
 
     first = first_flip(place, amplitudes, sections, sizes[0])
-    masked = mask_blocks(integrals, tile_mask, first)
+    masked = mask_blocks(integrals, tile_mask, [first])
     across = [swap(first, "ka")]
-    tokens = [first, *across]
-    for chunks, after in zip(SETS[1:], tokens):
-        rows = [sizes[at] for at in chunks]
-        pieces = [
-            flip(place, amplitudes, sections, e, spans[chunks[0]][0], sum(rows), after)
-            for e in range(sections)
-        ]
-        across += part(place, spread(pieces), rows, masked)
-    ready = [across[chunks[0]] for chunks in SETS[1:]]
-
-    own, delivered, partial_rows = [], [], [masked]
-    for at, ((start, rows), sent) in enumerate(zip(spans, across)):
-        crossed = swap(sent.reshape(occupied, rows, virtuals), "ia")
-        after = ready[at] if at < len(ready) else crossed
+    (second,) = fetch(SETS[1], [first])
+    across.append(second([masked]))
+    waiting = fetch(SETS[2], [across[1]])
+    own, delivered = [], []
+    after = [across[1]]
+    for at in range(len(spans)):
+        crossed = hop(at)
         if at == len(spans) - 1:
-            after = leading = send(GROUPS[0], crossed)
-        returned = scatter(place, crossed.reshape(sections, pairs, rows, virtuals), after)
-        partial_rows = product(
-            place, amplitudes, spread(returned), masked, start, partial_rows[0]
-        )
+            leading = columns([crossed])
+            after = [*after, leading]
+        returned = scatter(place, crossed, after)
+        begun = []
+        if at == 1:
+            token, columns = send(GROUPS[0])
+            begun = [token]
+        partial_rows = multiply(at, returned, begun)
+        after = [partial_rows[0]]
+        if waiting:
+            across.append(waiting.pop(0)(after))
+            after = [across[-1]]
         own.append(add(place, spread(partial_rows)))
 
     delivered.append(deliver(leading))
     for group in GROUPS[1:]:
-        delivered.append(deliver(send(group, delivered[-1])))
+        _, columns = send(group)
+        delivered.append(deliver(columns([delivered[-1]])))
     return finish(place, spans, GROUPS, own, delivered)
 
 

time: 539 us -> 527 us (0.978)
  waiting for transfers between devices: 241 us -> 256 us
  blocking collectives: 112 us -> 97.9 us
  Pallas kernels: 86.8 us -> 77.9 us
  local copies, waits for them, and re-layouts: 24.5 us -> 17 us
    ppermute x36 -> x39, waiting for transfers between devices: 165 us -> 199 us  [spread(): lax.ppermute(pieces[e], 'ka', [(q, q ^ e) for q in range(count)])]
    all_to_all x6 -> x7, waiting for transfers between devices: 75.8 us -> 57.1 us  [swap(): return lax.all_to_all(array, axis, split_axis=0, concat_axis=0, tiled=True)]
    all_to_all x3 -> x4, blocking collectives: 112 us -> 97.9 us  [swap(): return lax.all_to_all(array, axis, split_axis=0, concat_axis=0, tiled=True)]
    pallas_call x29 -> x32, Pallas kernels: 86.8 us -> 77.9 us  [call(): pl.pallas_call(trimmed, grid_spec=pltpu.PrefetchScalarGridSpec(num_scalar...]
    unnamed x71 -> x69, local copies, waits for them, and re-layouts: 17.9 us -> 10.9 us
    ppermute x36 -> x39, starting transfers between devices: 41.3 us -> 44.9 us  [spread(): lax.ppermute(pieces[e], 'ka', [(q, q ^ e) for q in range(count)])]
    all_to_all x6 -> x7, starting transfers between devices: 27.1 us -> 28.3 us  [swap(): return lax.all_to_all(array, axis, split_axis=0, concat_axis=0, tiled=True)]
  transfers between devices with their start and end apart: 42 -> 46, of which waited for: 16 -> 29; matrix products, arithmetic and copies ran while one was open for 1% -> 1% of each run, Pallas kernels for 15% -> 11%
where the time goes in v9:
time: 527 us; the launch traced here: 525 us
  waiting for transfers between devices  256 us (49%)
  blocking collectives  97.9 us (19%)
  Pallas kernels  77.9 us (15%)
  starting transfers between devices  73.2 us (14%)
  local copies, waits for them, and re-layouts  17 us (3%)
    ppermute x39, waiting for transfers between devices, spread(): lax.ppermute(pieces[e], 'ka', [(q, q ^ e) for q in range(count)])  199 us
    all_to_all x4, blocking collectives, swap(): return lax.all_to_all(array, axis, split_axis=0, concat_axis=0, tiled=True)  97.9 us
    pallas_call x32, Pallas kernels, call(): pl.pallas_call(trimmed, grid_spec=pltpu.PrefetchScalarGridSpec(num_scalar...  77.9 us
    all_to_all x7, waiting for transfers between devices, swap(): return lax.all_to_all(array, axis, split_axis=0, concat_axis=0, tiled=True)  57.1 us
    ppermute x39, starting transfers between devices, spread(): lax.ppermute(pieces[e], 'ka', [(q, q ^ e) for q in range(count)])  44.9 us
    all_to_all x7, starting transfers between devices, swap(): return lax.all_to_all(array, axis, split_axis=0, concat_axis=0, tiled=True)  28.3 us
    unnamed x69, local copies, waits for them, and re-layouts  10.9 us
  transfers between devices with their start and end apart: 46, of which 29 were waited for; matrix products, arithmetic and copies ran while one was open for 1% of the time, Pallas kernels for 11%

profile of v9, /device:TPU:0, one launch (start us, length us, event | category | flops | bytes accessed | tf_op | source)
XLA Modules:
  0.0 525.2 jit_solution(10060346184743022271)
XLA Ops:
  0.0 5.3 %first_flip.1.refs_2_ = f32[4,2,64,1024]{3,2,1,0:T(8,128)S(1)} custom-call(s32[1]{0:T(128)} %bitcast.refs_0_, f32[1,2,1024,1024]{3,2,1,0:T(8,128)} %refs_4_.7), custom_call_target="tpu_custom_call" | custom-call | bytes 4194304 | tf_op jit(solution)/shard_map/first_flip/pallas_call | solution.py:26
  5.3 30.4 %all_to_all.55 = f32[4,2,64,1024]{3,2,1,0:T(8,128)} all-to-all(f32[4,2,64,1024]{3,2,1,0:T(8,128)S(1)} %first_flip.1.refs_2_), channel_id=1, replica_groups=mesh['ia'=8,'ka'=4] {'ka'}, dimensions={0} | all-to-all | bytes 4194304 | tf_op jit(solution)/shard_map/all_to_all | solution.py:324
  35.7 4.9 all-to-all-start.1
  52.0 8.7 %mask.1.refs_5_.refs_9_ = bf16[2,2,1024,1024]{3,2,1,0:T(8,128)(2,1)} custom-call(s32[2,2,8,8]{3,2,1,0:T(8,128)S(1)} %bitcast.27, bf16[1,2,2,1024,1024]{4,3,2,1,0:T(8,128)(2,1)} %refs_1_.19, f32[4,2,64,1024]{3,2,1,0:T(8,128)S(1)} %first_flip.1.refs_2_), custom_call_target="tpu_custom_call" | custom-call | bytes 16777216 | tf_op jit(solution)/shard_map/mask/pallas_call | solution.py:26
  62.9 19.1 %collective-permute-done.1.refs_3_ = f32[2,96,1024]{2,1,0:T(8,128)S(1)} collective-permute-done((f32[2,96,1024]{2,1,0:T(8,128)S(1)}, f32[2,96,1024]{2,1,0:T(8,128)S(1)}, u32[]{:S(2)}, u32[]{:S(2)}) %collective-permute-start.1) | collective-permute-done | bytes 786464 | tf_op jit(solution)/shard_map/ppermute | solution.py:330
  83.8 5.9 %all-to-all-done.1 = f32[8,64,1024]{2,1,0:T(8,128)} async-done(((f32[8,64,1024]{2,1,0:T(8,128)}), f32[8,64,1024]{2,1,0:T(8,128)}, u32[]{:S(2)}, u32[]{:S(2)}) %all-to-all-start.1) | async-done | bytes 2097184 | tf_op jit(solution)/shard_map/all_to_all | solution.py:324
  89.8 4.5 all-to-all-start.2
  106.6 4.3 collective-permute-done.3.refs_6_
  111.9 11.3 %collective-permute-done.4.refs_7_ = f32[2,64,1024]{2,1,0:T(8,128)S(1)} collective-permute-done((f32[2,64,1024]{2,1,0:T(8,128)S(1)}, f32[2,64,1024]{2,1,0:T(8,128)S(1)}, u32[]{:S(2)}, u32[]{:S(2)}) %collective-permute-start.4) | collective-permute-done | bytes 524320 | tf_op jit(solution)/shard_map/ppermute | solution.py:330
  123.2 8.8 %product.4 = (f32[2,64,1024]{2,1,0:T(8,128)S(1)}, f32[2,64,1024]{2,1,0:T(8,128)}, f32[2,64,1024]{2,1,0:T(8,128)S(1)}, f32[2,64,1024]{2,1,0:T(8,128)S(1)}) custom-call(s32[1]{0:T(128)} %bitcast.refs_0_, f32[1,2,1024,1024]{3,2,1,0:T(8,128)} %refs_4_.7, f32[1,2,1024,1024]{3,2,1,0:T(8,128)} %refs_4_.7, f32[1,2,1024,1024]{3,2,1,0:T(8,128)} %refs_4_.7, ...), custom_call_target="tpu_custom_call" | custom-call | flops 4294967296 | bytes 4194304 | tf_op jit(solution)/shard_map/product/pallas_call | solution.py:26
  134.9 4.2 collective-permute-done.9.refs_2_
  139.1 16.5 %collective-permute-done.10.refs_3_ = f32[2,96,1024]{2,1,0:T(8,128)S(1)} collective-permute-done((f32[2,96,1024]{2,1,0:T(8,128)S(1)}, f32[2,96,1024]{2,1,0:T(8,128)S(1)}, u32[]{:S(2)}, u32[]{:S(2)}) %collective-permute-start.10) | collective-permute-done | bytes 786464 | tf_op jit(solution)/shard_map/ppermute | solution.py:330
  161.3 4.5 all-to-all-done.2
  174.0 53.2 %collective-permute-done.7.refs_3_ = f32[2,64,1024]{2,1,0:T(8,128)S(1)} collective-permute-done((f32[2,64,1024]{2,1,0:T(8,128)S(1)}, f32[2,64,1024]{2,1,0:T(8,128)S(1)}, u32[]{:S(2)}, u32[]{:S(2)}) %collective-permute-start.7) | collective-permute-done | bytes 524320 | tf_op jit(solution)/shard_map/ppermute | solution.py:330
  229.3 11.3 %product.5 = (f32[2,96,1024]{2,1,0:T(8,128)S(1)}, f32[2,96,1024]{2,1,0:T(8,128)S(1)}, f32[2,96,1024]{2,1,0:T(8,128)S(1)}, f32[2,96,1024]{2,1,0:T(8,128)S(1)}) custom-call(s32[1]{0:T(128)} %bitcast.refs_0_, f32[1,2,1024,1024]{3,2,1,0:T(8,128)} %refs_4_.7, f32[1,2,1024,1024]{3,2,1,0:T(8,128)} %refs_4_.7, f32[1,2,1024,1024]{3,2,1,0:T(8,128)} %refs_4_.7, ...), custom_call_target="tpu_custom_call" | custom-call | flops 6442450944 | bytes 6291456 | tf_op jit(solution)/shard_map/product/pallas_call | solution.py:26
  256.3 17.1 %all-to-all-done.4 = f32[8,32,1024]{2,1,0:T(8,128)S(1)} async-done(((f32[8,32,1024]{2,1,0:T(8,128)}), f32[8,32,1024]{2,1,0:T(8,128)S(1)}, u32[]{:S(2)}, u32[]{:S(2)}) %all-to-all-start.4) | async-done | bytes 1048608 | tf_op jit(solution)/shard_map/all_to_all | solution.py:324
  278.8 14.2 %all-to-all-done.5 = f32[8,2,32,256]{3,2,1,0:T(8,128)S(1)} async-done(((f32[8,2,32,256]{3,2,1,0:T(8,128)}), f32[8,2,32,256]{3,2,1,0:T(8,128)S(1)}, u32[]{:S(2)}, u32[]{:S(2)}) %all-to-all-start.5) | async-done | bytes 524320 | tf_op jit(solution)/shard_map/all_to_all | solution.py:324
  293.7 18.4 %all_to_all.56.refs_5_ = f32[8,2,32,256]{3,2,1,0:T(8,128)} all-to-all(f32[8,2,32,256]{3,2,1,0:T(8,128)S(1)} %broadcast_select_fusion.2), channel_id=1, replica_groups=mesh['ia'=8,'ka'=4] {'ia'}, dimensions={0} | all-to-all | bytes 1048576 | tf_op jit(solution)/shard_map/all_to_all | solution.py:324
  319.3 17.1 %collective-permute-done.15.refs_2_ = f32[2,96,1024]{2,1,0:T(8,128)S(1)} collective-permute-done((f32[2,96,1024]{2,1,0:T(8,128)}, f32[2,96,1024]{2,1,0:T(8,128)S(1)}, u32[]{:S(2)}, u32[]{:S(2)}) %collective-permute-start.15) | collective-permute-done | bytes 786464 | tf_op jit(solution)/shard_map/ppermute | solution.py:330
  336.4 17.1 %collective-permute-done.16.refs_3_ = f32[2,96,1024]{2,1,0:T(8,128)S(1)} collective-permute-done((f32[2,96,1024]{2,1,0:T(8,128)}, f32[2,96,1024]{2,1,0:T(8,128)S(1)}, u32[]{:S(2)}, u32[]{:S(2)}) %collective-permute-start.16) | collective-permute-done | bytes 786464 | tf_op jit(solution)/shard_map/ppermute | solution.py:330
  358.5 4.1 collective-permute-done.33.refs_2_
  367.0 4.6 all-to-all-start.7
  377.2 15.4 %all-to-all-done.7 = f32[8,2,48,256]{3,2,1,0:T(8,128)} async-done(((f32[8,2,48,256]{3,2,1,0:T(8,128)}), f32[8,2,48,256]{3,2,1,0:T(8,128)}, u32[]{:S(2)}, u32[]{:S(2)}) %all-to-all-start.7) | async-done | bytes 786464 | tf_op jit(solution)/shard_map/all_to_all | solution.py:324
  402.2 8.4 %product.6 = (f32[2,64,1024]{2,1,0:T(8,128)S(1)}, f32[2,64,1024]{2,1,0:T(8,128)S(1)}, f32[2,64,1024]{2,1,0:T(8,128)S(1)}, f32[2,64,1024]{2,1,0:T(8,128)S(1)}) custom-call(s32[1]{0:T(128)} %bitcast.refs_0_, f32[1,2,1024,1024]{3,2,1,0:T(8,128)} %refs_4_.7, f32[1,2,1024,1024]{3,2,1,0:T(8,128)} %refs_4_.7, f32[1,2,1024,1024]{3,2,1,0:T(8,128)} %refs_4_.7, ...), custom_call_target="tpu_custom_call" | custom-call | flops 4294967296 | bytes 4194304 | tf_op jit(solution)/shard_map/product/pallas_call | solution.py:26
  416.2 3.8 collective-permute-done.27.refs_6_
  422.0 15.2 %collective-permute-done.29.refs_8_ = f32[2,32,1024]{2,1,0:T(8,128)S(1)} collective-permute-done((f32[2,32,1024]{2,1,0:T(8,128)S(1)}, f32[2,32,1024]{2,1,0:T(8,128)S(1)}, u32[]{:S(2)}, u32[]{:S(2)}) %collective-permute-start.29) | collective-permute-done | bytes 262176 | tf_op jit(solution)/shard_map/ppermute | solution.py:330
  437.3 6.2 %product.7 = (f32[2,32,1024]{2,1,0:T(8,128)S(1)}, f32[2,32,1024]{2,1,0:T(8,128)S(1)}, f32[2,32,1024]{2,1,0:T(8,128)S(1)}, f32[2,32,1024]{2,1,0:T(8,128)S(1)}) custom-call(s32[1]{0:T(128)} %bitcast.refs_0_, f32[1,2,1024,1024]{3,2,1,0:T(8,128)} %refs_4_.7, f32[1,2,1024,1024]{3,2,1,0:T(8,128)} %refs_4_.7, f32[1,2,1024,1024]{3,2,1,0:T(8,128)} %refs_4_.7, ...), custom_call_target="tpu_custom_call" | custom-call | flops 2147483648 | bytes 2097152 | tf_op jit(solution)/shard_map/product/pallas_call | solution.py:26
  448.6 5.1 collective-permute-done.30.refs_2_
  453.8 5.0 collective-permute-done.31.refs_3_
  462.5 4.3 collective-permute-done.36.refs_2_
  470.1 25.7 %all_to_all.57 = f32[8,2,48,256]{3,2,1,0:T(8,128)} all-to-all(f32[8,2,48,256]{3,2,1,0:T(8,128)S(1)} %bitcast.25), channel_id=1, replica_groups=mesh['ia'=8,'ka'=4] {'ia'}, dimensions={0} | all-to-all | bytes 1572864 | tf_op jit(solution)/shard_map/all_to_all | solution.py:324
  499.8 23.4 %all_to_all.58.refs_7_ = f32[8,2,48,256]{3,2,1,0:T(8,128)S(1)} all-to-all(f32[8,2,48,256]{3,2,1,0:T(8,128)S(1)} %bitcast.31), channel_id=1, replica_groups=mesh['ia'=8,'ka'=4] {'ia'}, dimensions={0} | all-to-all | bytes 1572864 | tf_op jit(solution)/shard_map/all_to_all | solution.py:324
  (183 shorter events, 126.6 us)
Async XLA Ops:
  35.7 54.1 %all-to-all-start.1 = ((f32[8,64,1024]{2,1,0:T(8,128)}), f32[8,64,1024]{2,1,0:T(8,128)}, u32[]{:S(2)}, u32[]{:S(2)}) async-start(f32[8,64,1024]{2,1,0:T(8,128)} %bitcast.28), calls=%async_computation.1 | async-start | bytes 4194304 | tf_op jit(solution)/shard_map/all_to_all | solution.py:324
  42.5 20.4 %collective-permute-start = (f32[2,96,1024]{2,1,0:T(8,128)S(1)}, f32[2,96,1024]{2,1,0:T(8,128)S(1)}, u32[]{:S(2)}, u32[]{:S(2)}) collective-permute-start(f32[2,96,1024]{2,1,0:T(8,128)S(1)} %flip.9), channel_id=1, source_target_pairs={{0,1},{1,0},{2,3},{3,2},{4,5},{5,4},{6,7},{7,6},{8,9},{9,8},{10,11... | collective-permute-start | bytes 2359304 | tf_op jit(solution)/shard_map/ppermute | solution.py:330
  45.5 36.6 %collective-permute-start.1 = (f32[2,96,1024]{2,1,0:T(8,128)S(1)}, f32[2,96,1024]{2,1,0:T(8,128)S(1)}, u32[]{:S(2)}, u32[]{:S(2)}) collective-permute-start(f32[2,96,1024]{2,1,0:T(8,128)S(1)} %flip.10), channel_id=1, source_target_pairs={{0,2},{1,3},{2,0},{3,1},{4,6},{5,7},{6,4},{7,5},{8,10},{9,11},{10,... | collective-permute-start | bytes 2359304 | tf_op jit(solution)/shard_map/ppermute | solution.py:330
  48.0 34.0 %collective-permute-start.2 = (f32[2,96,1024]{2,1,0:T(8,128)S(1)}, f32[2,96,1024]{2,1,0:T(8,128)S(1)}, u32[]{:S(2)}, u32[]{:S(2)}) collective-permute-start(f32[2,96,1024]{2,1,0:T(8,128)S(1)} %flip.11), channel_id=1, source_target_pairs={{0,3},{1,2},{2,1},{3,0},{4,7},{5,6},{6,5},{7,4},{8,11},{9,10},{10,... | collective-permute-start | bytes 2359304 | tf_op jit(solution)/shard_map/ppermute | solution.py:330
  89.8 76.0 %all-to-all-start.2 = ((f32[8,96,1024]{2,1,0:T(8,128)}), f32[8,96,1024]{2,1,0:T(8,128)}, u32[]{:S(2)}, u32[]{:S(2)}) async-start(f32[8,96,1024]{2,1,0:T(8,128)} %bitcast.21), calls=%async_computation.2 | async-start | bytes 6291456 | tf_op jit(solution)/shard_map/all_to_all | solution.py:324
  96.2 14.8 %collective-permute-start.3 = (f32[2,64,1024]{2,1,0:T(8,128)S(1)}, f32[2,64,1024]{2,1,0:T(8,128)S(1)}, u32[]{:S(2)}, u32[]{:S(2)}) collective-permute-start(f32[2,64,1024]{2,1,0:T(8,128)S(1)} %get-tuple-element.51), channel_id=1, source_target_pairs={{0,1},{1,0},{2,3},{3,2},{4,5},{5,4},{6,7},{7,6},{8,9},{9,8},{10,11... | collective-permute-start | bytes 1572872 | tf_op jit(solution)/shard_map/ppermute | solution.py:330
  97.1 26.0 %collective-permute-start.4 = (f32[2,64,1024]{2,1,0:T(8,128)S(1)}, f32[2,64,1024]{2,1,0:T(8,128)S(1)}, u32[]{:S(2)}, u32[]{:S(2)}) collective-permute-start(f32[2,64,1024]{2,1,0:T(8,128)S(1)} %get-tuple-element.52), channel_id=1, source_target_pairs={{0,2},{1,3},{2,0},{3,1},{4,6},{5,7},{6,4},{7,5},{8,10},{9,11},{10,... | collective-permute-start | bytes 1572872 | tf_op jit(solution)/shard_map/ppermute | solution.py:330
  97.7 25.5 %collective-permute-start.5 = (f32[2,64,1024]{2,1,0:T(8,128)S(1)}, f32[2,64,1024]{2,1,0:T(8,128)S(1)}, u32[]{:S(2)}, u32[]{:S(2)}) collective-permute-start(f32[2,64,1024]{2,1,0:T(8,128)S(1)} %get-tuple-element.53), channel_id=1, source_target_pairs={{0,3},{1,2},{2,1},{3,0},{4,7},{5,6},{6,5},{7,4},{8,11},{9,10},{10,... | collective-permute-start | bytes 1572872 | tf_op jit(solution)/shard_map/ppermute | solution.py:330
  105.1 34.0 %collective-permute-start.9 = (f32[2,96,1024]{2,1,0:T(8,128)S(1)}, f32[2,96,1024]{2,1,0:T(8,128)S(1)}, u32[]{:S(2)}, u32[]{:S(2)}) collective-permute-start(f32[2,96,1024]{2,1,0:T(8,128)S(1)} %flip.13), channel_id=1, source_target_pairs={{0,1},{1,0},{2,3},{3,2},{4,5},{5,4},{6,7},{7,6},{8,9},{9,8},{10,11... | collective-permute-start | bytes 2359304 | tf_op jit(solution)/shard_map/ppermute | solution.py:330
  106.1 49.6 %collective-permute-start.10 = (f32[2,96,1024]{2,1,0:T(8,128)S(1)}, f32[2,96,1024]{2,1,0:T(8,128)S(1)}, u32[]{:S(2)}, u32[]{:S(2)}) collective-permute-start(f32[2,96,1024]{2,1,0:T(8,128)S(1)} %flip.14), channel_id=1, source_target_pairs={{0,2},{1,3},{2,0},{3,1},{4,6},{5,7},{6,4},{7,5},{8,10},{9,11},{10,... | collective-permute-start | bytes 2359304 | tf_op jit(solution)/shard_map/ppermute | solution.py:330
  111.0 45.4 %collective-permute-start.11 = (f32[2,96,1024]{2,1,0:T(8,128)S(1)}, f32[2,96,1024]{2,1,0:T(8,128)S(1)}, u32[]{:S(2)}, u32[]{:S(2)}) collective-permute-start(f32[2,96,1024]{2,1,0:T(8,128)S(1)} %flip.15), channel_id=1, source_target_pairs={{0,3},{1,2},{2,1},{3,0},{4,7},{5,6},{6,5},{7,4},{8,11},{9,10},{10,... | collective-permute-start | bytes 2359304 | tf_op jit(solution)/shard_map/ppermute | solution.py:330
  132.0 40.5 %collective-permute-start.6 = (f32[2,64,1024]{2,1,0:T(8,128)}, f32[2,64,1024]{2,1,0:T(8,128)}, u32[]{:S(2)}, u32[]{:S(2)}) collective-permute-start(f32[2,64,1024]{2,1,0:T(8,128)} %get-tuple-element.55), channel_id=1, source_target_pairs={{0,1},{1,0},{2,3},{3,2},{4,5},{5,4},{6,7},{7,6},{8,9},{9,8},{10,11... | collective-permute-start | bytes 1572872 | tf_op jit(solution)/shard_map/ppermute | solution.py:330
  168.0 60.3 %collective-permute-start.12 = (f32[2,96,1024]{2,1,0:T(8,128)S(1)}, f32[2,96,1024]{2,1,0:T(8,128)S(1)}, u32[]{:S(2)}, u32[]{:S(2)}) collective-permute-start(f32[2,96,1024]{2,1,0:T(8,128)S(1)} %get-tuple-element.59), channel_id=1, source_target_pairs={{0,1},{1,0},{2,3},{3,2},{4,5},{5,4},{6,7},{7,6},{8,9},{9,8},{10,11... | collective-permute-start | bytes 2359304 | tf_op jit(solution)/shard_map/ppermute | solution.py:330
  169.0 59.3 %collective-permute-start.13 = (f32[2,96,1024]{2,1,0:T(8,128)S(1)}, f32[2,96,1024]{2,1,0:T(8,128)S(1)}, u32[]{:S(2)}, u32[]{:S(2)}) collective-permute-start(f32[2,96,1024]{2,1,0:T(8,128)S(1)} %get-tuple-element.60), channel_id=1, source_target_pairs={{0,2},{1,3},{2,0},{3,1},{4,6},{5,7},{6,4},{7,5},{8,10},{9,11},{10,... | collective-permute-start | bytes 2359304 | tf_op jit(solution)/shard_map/ppermute | solution.py:330
  169.6 58.8 %collective-permute-start.14 = (f32[2,96,1024]{2,1,0:T(8,128)S(1)}, f32[2,96,1024]{2,1,0:T(8,128)S(1)}, u32[]{:S(2)}, u32[]{:S(2)}) collective-permute-start(f32[2,96,1024]{2,1,0:T(8,128)S(1)} %get-tuple-element.61), channel_id=1, source_target_pairs={{0,3},{1,2},{2,1},{3,0},{4,7},{5,6},{6,5},{7,4},{8,11},{9,10},{10,... | collective-permute-start | bytes 2359304 | tf_op jit(solution)/shard_map/ppermute | solution.py:330
  171.6 55.6 %collective-permute-start.7 = (f32[2,64,1024]{2,1,0:T(8,128)S(1)}, f32[2,64,1024]{2,1,0:T(8,128)S(1)}, u32[]{:S(2)}, u32[]{:S(2)}) collective-permute-start(f32[2,64,1024]{2,1,0:T(8,128)S(1)} %copy-done.31), channel_id=1, source_target_pairs={{0,2},{1,3},{2,0},{3,1},{4,6},{5,7},{6,4},{7,5},{8,10},{9,11},{10,... | collective-permute-start | bytes 1572872 | tf_op jit(solution)/shard_map/ppermute | solution.py:330
  172.5 54.6 %collective-permute-start.8 = (f32[2,64,1024]{2,1,0:T(8,128)S(1)}, f32[2,64,1024]{2,1,0:T(8,128)S(1)}, u32[]{:S(2)}, u32[]{:S(2)}) collective-permute-start(f32[2,64,1024]{2,1,0:T(8,128)S(1)} %copy-done.29), channel_id=1, source_target_pairs={{0,3},{1,2},{2,1},{3,0},{4,7},{5,6},{6,5},{7,4},{8,11},{9,10},{10,... | collective-permute-start | bytes 1572872 | tf_op jit(solution)/shard_map/ppermute | solution.py:330
  243.3 30.1 %all-to-all-start.4 = ((f32[8,32,1024]{2,1,0:T(8,128)}), f32[8,32,1024]{2,1,0:T(8,128)S(1)}, u32[]{:S(2)}, u32[]{:S(2)}) async-start(f32[8,32,1024]{2,1,0:T(8,128)} %bitcast.8), calls=%async_computation.4 | async-start | bytes 2097152 | tf_op jit(solution)/shard_map/all_to_all | solution.py:324
  274.3 18.8 %all-to-all-start.5 = ((f32[8,2,32,256]{3,2,1,0:T(8,128)}), f32[8,2,32,256]{3,2,1,0:T(8,128)S(1)}, u32[]{:S(2)}, u32[]{:S(2)}) async-start(f32[8,2,32,256]{3,2,1,0:T(8,128)} %bitcast.10), calls=%async_computation.5 | async-start | bytes 1048576 | tf_op jit(solution)/shard_map/all_to_all | solution.py:324
  312.2 54.8 %all-to-all-start.3 = ((f32[8,64,1024]{2,1,0:T(8,128)}), f32[8,64,1024]{2,1,0:T(8,128)S(1)}, u32[]{:S(2)}, u32[]{:S(2)}) async-start(f32[8,64,1024]{2,1,0:T(8,128)} %bitcast.6), calls=%async_computation.3 | async-start | bytes 4194304 | tf_op jit(solution)/shard_map/all_to_all | solution.py:324
  315.8 20.6 %collective-permute-start.15 = (f32[2,96,1024]{2,1,0:T(8,128)}, f32[2,96,1024]{2,1,0:T(8,128)S(1)}, u32[]{:S(2)}, u32[]{:S(2)}) collective-permute-start(f32[2,96,1024]{2,1,0:T(8,128)} %copy-done.27), channel_id=1, source_target_pairs={{0,1},{1,0},{2,3},{3,2},{4,5},{5,4},{6,7},{7,6},{8,9},{9,8},{10,11... | collective-permute-start | bytes 2359304 | tf_op jit(solution)/shard_map/ppermute | solution.py:330
  317.0 36.6 %collective-permute-start.16 = (f32[2,96,1024]{2,1,0:T(8,128)}, f32[2,96,1024]{2,1,0:T(8,128)S(1)}, u32[]{:S(2)}, u32[]{:S(2)}) collective-permute-start(f32[2,96,1024]{2,1,0:T(8,128)} %copy-done.26), channel_id=1, source_target_pairs={{0,2},{1,3},{2,0},{3,1},{4,6},{5,7},{6,4},{7,5},{8,10},{9,11},{10,... | collective-permute-start | bytes 2359304 | tf_op jit(solution)/shard_map/ppermute | solution.py:330
  317.9 35.7 %collective-permute-start.17 = (f32[2,96,1024]{2,1,0:T(8,128)}, f32[2,96,1024]{2,1,0:T(8,128)S(1)}, u32[]{:S(2)}, u32[]{:S(2)}) collective-permute-start(f32[2,96,1024]{2,1,0:T(8,128)} %copy-done.25), channel_id=1, source_target_pairs={{0,3},{1,2},{2,1},{3,0},{4,7},{5,6},{6,5},{7,4},{8,11},{9,10},{10,... | collective-permute-start | bytes 2359304 | tf_op jit(solution)/shard_map/ppermute | solution.py:330
  367.0 25.6 %all-to-all-start.7 = ((f32[8,2,48,256]{3,2,1,0:T(8,128)}), f32[8,2,48,256]{3,2,1,0:T(8,128)}, u32[]{:S(2)}, u32[]{:S(2)}) async-start(f32[8,2,48,256]{3,2,1,0:T(8,128)} %bitcast.26), calls=%async_computation.7 | async-start | bytes 1572864 | tf_op jit(solution)/shard_map/all_to_all | solution.py:324
  373.7 25.5 %collective-permute-start.18 = (f32[2,64,1024]{2,1,0:T(8,128)}, f32[2,64,1024]{2,1,0:T(8,128)S(1)}, u32[]{:S(2)}, u32[]{:S(2)}) collective-permute-start(f32[2,64,1024]{2,1,0:T(8,128)} %get-tuple-element.68), channel_id=1, source_target_pairs={{0,1},{1,0},{2,3},{3,2},{4,5},{5,4},{6,7},{7,6},{8,9},{9,8},{10,11... | collective-permute-start | bytes 1572872 | tf_op jit(solution)/shard_map/ppermute | solution.py:330
  374.9 25.5 %collective-permute-start.19 = (f32[2,64,1024]{2,1,0:T(8,128)}, f32[2,64,1024]{2,1,0:T(8,128)S(1)}, u32[]{:S(2)}, u32[]{:S(2)}) collective-permute-start(f32[2,64,1024]{2,1,0:T(8,128)} %get-tuple-element.69), channel_id=1, source_target_pairs={{0,2},{1,3},{2,0},{3,1},{4,6},{5,7},{6,4},{7,5},{8,10},{9,11},{10,... | collective-permute-start | bytes 1572872 | tf_op jit(solution)/shard_map/ppermute | solution.py:330
  375.7 25.5 %collective-permute-start.20 = (f32[2,64,1024]{2,1,0:T(8,128)}, f32[2,64,1024]{2,1,0:T(8,128)}, u32[]{:S(2)}, u32[]{:S(2)}) collective-permute-start(f32[2,64,1024]{2,1,0:T(8,128)} %get-tuple-element.70), channel_id=1, source_target_pairs={{0,3},{1,2},{2,1},{3,0},{4,7},{5,6},{6,5},{7,4},{8,11},{9,10},{10,... | collective-permute-start | bytes 1572872 | tf_op jit(solution)/shard_map/ppermute | solution.py:330
  395.4 74.6 %all-to-all-start.8 = ((f32[8,2,48,256]{3,2,1,0:T(8,128)}), f32[8,2,48,256]{3,2,1,0:T(8,128)S(1)}, u32[]{:S(2)}, u32[]{:S(2)}) async-start(f32[8,2,48,256]{3,2,1,0:T(8,128)} %bitcast.29), calls=%async_computation.8 | async-start | bytes 1572864 | tf_op jit(solution)/shard_map/all_to_all | solution.py:324
  411.6 33.9 %collective-permute-start.21 = (f32[2,64,1024]{2,1,0:T(8,128)S(1)}, f32[2,64,1024]{2,1,0:T(8,128)S(1)}, u32[]{:S(2)}, u32[]{:S(2)}) collective-permute-start(f32[2,64,1024]{2,1,0:T(8,128)S(1)} %get-tuple-element.72), channel_id=1, source_target_pairs={{0,1},{1,0},{2,3},{3,2},{4,5},{5,4},{6,7},{7,6},{8,9},{9,8},{10,11... | collective-permute-start | bytes 1572872 | tf_op jit(solution)/shard_map/ppermute | solution.py:330
  413.6 23.6 %collective-permute-start.29 = (f32[2,32,1024]{2,1,0:T(8,128)S(1)}, f32[2,32,1024]{2,1,0:T(8,128)S(1)}, u32[]{:S(2)}, u32[]{:S(2)}) collective-permute-start(f32[2,32,1024]{2,1,0:T(8,128)S(1)} %get-tuple-element.81), channel_id=1, source_target_pairs={{0,3},{1,2},{2,1},{3,0},{4,7},{5,6},{6,5},{7,4},{8,11},{9,10},{10,... | collective-permute-start | bytes 786440 | tf_op jit(solution)/shard_map/ppermute | solution.py:330
  415.1 33.2 %collective-permute-start.22 = (f32[2,64,1024]{2,1,0:T(8,128)S(1)}, f32[2,64,1024]{2,1,0:T(8,128)S(1)}, u32[]{:S(2)}, u32[]{:S(2)}) collective-permute-start(f32[2,64,1024]{2,1,0:T(8,128)S(1)} %get-tuple-element.73), channel_id=1, source_target_pairs={{0,2},{1,3},{2,0},{3,1},{4,6},{5,7},{6,4},{7,5},{8,10},{9,11},{10,... | collective-permute-start | bytes 1572872 | tf_op jit(solution)/shard_map/ppermute | solution.py:330
  420.0 28.4 %collective-permute-start.23 = (f32[2,64,1024]{2,1,0:T(8,128)S(1)}, f32[2,64,1024]{2,1,0:T(8,128)S(1)}, u32[]{:S(2)}, u32[]{:S(2)}) collective-permute-start(f32[2,64,1024]{2,1,0:T(8,128)S(1)} %get-tuple-element.74), channel_id=1, source_target_pairs={{0,3},{1,2},{2,1},{3,0},{4,7},{5,6},{6,5},{7,4},{8,11},{9,10},{10,... | collective-permute-start | bytes 1572872 | tf_op jit(solution)/shard_map/ppermute | solution.py:330
  (48 other events, 491.1 us)

commit v10 on v9

--- a/solution.py
+++ b/solution.py
@@ -229,7 +229,7 @@
     refs[-1][...] = sum((part[...] for part in refs[1:-1]), refs[0][...])
 
 
-def add(place, parts):
+def add(place, parts, after):
     slots, rows, virtuals = parts[0].shape
     block = pl.BlockSpec((1, rows, virtuals), lambda s, at: (s, 0, 0))
     return call(
@@ -241,6 +241,7 @@
         block,
         jax.ShapeDtypeStruct(parts[0].shape, jnp.float32),
         (slots,),
+        after=after,
     )
 
 
@@ -355,17 +356,22 @@
         crossed = swap(across[at].reshape(occupied, sizes[at], virtuals), "ia")
         return crossed.reshape(sections, pairs, sizes[at], virtuals)
 
-    def multiply(at, returned, after):
-        start = spans[at][0]
-        return product(place, amplitudes, spread(returned), masked, start, after)
+    def turn(at, crossed, after):
+        pieces = scatter(place, crossed, after)
+        return pieces[0], spread(pieces)
+
+    def multiply(at, mirrored, after):
+        parts = product(place, amplitudes, mirrored, masked, spans[at][0], after)
+        return parts[0], spread(parts)
 
     def send(group):
-        columns = cut(place, [own[at] for at in group], sections, pairs)
-        return columns[0], lambda after: gather(place, spread(columns), after)
-
-    def deliver(columns):
-        piece = columns.shape[-2:]
-        met = swap(columns.reshape(occupied, slots, *piece), "ia")
+        return spread(cut(place, [own[at] for at in group], sections, pairs))
+
+    def meet(columns):
+        return swap(columns.reshape(occupied, slots, *columns.shape[-2:]), "ia")
+
+    def deliver(met):
+        piece = met.shape[-2:]
         routed = jnp.take(met.reshape(occupied * slots, *piece), source_row, axis=0)
         return swap(routed.reshape(occupied, slots, *piece), "ia")
 
@@ -375,29 +381,27 @@
     (second,) = fetch(SETS[1], [first])
     across.append(second([masked]))
     waiting = fetch(SETS[2], [across[1]])
-    own, delivered = [], []
-    after = [across[1]]
-    for at in range(len(spans)):
-        crossed = hop(at)
-        if at == len(spans) - 1:
-            leading = columns([crossed])
-            after = [*after, leading]
-        returned = scatter(place, crossed, after)
-        begun = []
-        if at == 1:
-            token, columns = send(GROUPS[0])
-            begun = [token]
-        partial_rows = multiply(at, returned, begun)
-        after = [partial_rows[0]]
-        if waiting:
-            across.append(waiting.pop(0)(after))
-            after = [across[-1]]
-        own.append(add(place, spread(partial_rows)))
-
-    delivered.append(deliver(leading))
+    turned, mirrored = turn(0, hop(0), [across[1]])
+    begun, parts = multiply(0, mirrored, [])
+    across.append(waiting[0]([begun]))
+    turned, mirrored = turn(1, hop(1), [across[2]])
+    turned, later = turn(2, hop(2), [turned])
+    across.append(waiting[1]([turned]))
+    own = [add(place, parts, [turned])]
+    begun, parts = multiply(1, mirrored, [turned])
+    crossed = hop(3)
+    leading = gather(place, send(GROUPS[0]), [crossed])
+    turned, mirrored = turn(3, crossed, [begun, leading])
+    own.append(add(place, parts, []))
+    met = meet(leading)
+    begun, parts = multiply(2, later, [turned, met])
+    own.append(add(place, parts, []))
+    _, parts = multiply(3, mirrored, [begun])
+    own.append(add(place, parts, []))
+
+    delivered = [deliver(met)]
     for group in GROUPS[1:]:
-        _, columns = send(group)
-        delivered.append(deliver(columns([delivered[-1]])))
+        delivered.append(deliver(meet(gather(place, send(group), [delivered[-1]]))))
     return finish(place, spans, GROUPS, own, delivered)
 
 

time: 527 us -> 529 us (level)
  blocking collectives: 97.9 us -> 79.3 us
  local copies, waits for them, and re-layouts: 17 us -> 26.5 us
  starting transfers between devices: 73.2 us -> 79 us
    all_to_all x4 -> x3, blocking collectives: 97.9 us -> 79.3 us  [swap(): return lax.all_to_all(array, axis, split_axis=0, concat_axis=0, tiled=True)]
    all_to_all x7 -> x8, waiting for transfers between devices: 57.1 us -> 71.4 us  [swap(): return lax.all_to_all(array, axis, split_axis=0, concat_axis=0, tiled=True)]
    ppermute x39, waiting for transfers between devices: 199 us -> 185 us  [spread(): lax.ppermute(pieces[e], 'ka', [(q, q ^ e) for q in range(count)])]
    unnamed x69 -> x71, local copies, waits for them, and re-layouts: 10.9 us -> 20.7 us
    all_to_all x7 -> x8, starting transfers between devices: 28.3 us -> 34.7 us  [swap(): return lax.all_to_all(array, axis, split_axis=0, concat_axis=0, tiled=True)]
  transfers between devices with their start and end apart: 46 -> 47, of which waited for: 29 -> 22; matrix products, arithmetic and copies ran while one was open for 1% -> 1% of each run, Pallas kernels for 11% -> 13%
where the time goes in v10:
time: 529 us; the launch traced here: 527 us
  waiting for transfers between devices  257 us (49%)
  Pallas kernels  80.5 us (15%)
  blocking collectives  79.3 us (15%)
  starting transfers between devices  79 us (15%)
  local copies, waits for them, and re-layouts  26.5 us (5%)
    ppermute x39, waiting for transfers between devices, spread(): lax.ppermute(pieces[e], 'ka', [(q, q ^ e) for q in range(count)])  185 us
    pallas_call x32, Pallas kernels, call(): pl.pallas_call(trimmed, grid_spec=pltpu.PrefetchScalarGridSpec(num_scalar...  80.5 us
    all_to_all x3, blocking collectives, swap(): return lax.all_to_all(array, axis, split_axis=0, concat_axis=0, tiled=True)  79.3 us
    all_to_all x8, waiting for transfers between devices, swap(): return lax.all_to_all(array, axis, split_axis=0, concat_axis=0, tiled=True)  71.4 us
    ppermute x39, starting transfers between devices, spread(): lax.ppermute(pieces[e], 'ka', [(q, q ^ e) for q in range(count)])  44.3 us
    all_to_all x8, starting transfers between devices, swap(): return lax.all_to_all(array, axis, split_axis=0, concat_axis=0, tiled=True)  34.7 us
    unnamed x71, local copies, waits for them, and re-layouts  20.7 us
  transfers between devices with their start and end apart: 47, of which 22 were waited for; matrix products, arithmetic and copies ran while one was open for 1% of the time, Pallas kernels for 13%

profile of v10, /device:TPU:0, one launch (start us, length us, event | category | flops | bytes accessed | tf_op | source)
XLA Modules:
  0.0 526.9 jit_solution(12278205290479286691)
XLA Ops:
  0.0 5.3 first_flip.1.refs_2_
  5.3 30.4 %all_to_all.55 = f32[4,2,64,1024]{3,2,1,0:T(8,128)} all-to-all(f32[4,2,64,1024]{3,2,1,0:T(8,128)S(1)} %first_flip.1.refs_2_), channel_id=1, replica_groups=mesh['ia'=8,'ka'=4] {'ka'}, dimensions={0} | all-to-all | bytes 4194304 | tf_op jit(solution)/shard_map/all_to_all | solution.py:325
  35.7 4.9 all-to-all-start.1
  52.0 8.7 %mask.1.refs_5_.refs_9_ = bf16[2,2,1024,1024]{3,2,1,0:T(8,128)(2,1)} custom-call(s32[2,2,8,8]{3,2,1,0:T(8,128)S(1)} %bitcast.27, bf16[1,2,2,1024,1024]{4,3,2,1,0:T(8,128)(2,1)} %refs_1_.19, f32[4,2,64,1024]{3,2,1,0:T(8,128)S(1)} %first_flip.1.refs_2_), custom_call_target="tpu_custom_call" | custom-call | bytes 16777216 | tf_op jit(solution)/shard_map/mask/pallas_call | solution.py:26
  62.9 19.1 %collective-permute-done.1.refs_3_ = f32[2,96,1024]{2,1,0:T(8,128)S(1)} collective-permute-done((f32[2,96,1024]{2,1,0:T(8,128)S(1)}, f32[2,96,1024]{2,1,0:T(8,128)S(1)}, u32[]{:S(2)}, u32[]{:S(2)}) %collective-permute-start.1) | collective-permute-done | bytes 786464 | tf_op jit(solution)/shard_map/ppermute | solution.py:331
  83.8 5.9 %all-to-all-done.1 = f32[8,64,1024]{2,1,0:T(8,128)} async-done(((f32[8,64,1024]{2,1,0:T(8,128)}), f32[8,64,1024]{2,1,0:T(8,128)}, u32[]{:S(2)}, u32[]{:S(2)}) %all-to-all-start.1) | async-done | bytes 2097184 | tf_op jit(solution)/shard_map/all_to_all | solution.py:325
  89.8 4.5 all-to-all-start.3
  113.7 26.3 %collective-permute-done.4.refs_7_ = f32[2,64,1024]{2,1,0:T(8,128)S(1)} collective-permute-done((f32[2,64,1024]{2,1,0:T(8,128)S(1)}, f32[2,64,1024]{2,1,0:T(8,128)S(1)}, u32[]{:S(2)}, u32[]{:S(2)}) %collective-permute-start.4) | collective-permute-done | bytes 524320 | tf_op jit(solution)/shard_map/ppermute | solution.py:331
  140.0 8.8 %product.4 = (f32[2,64,1024]{2,1,0:T(8,128)S(1)}, f32[2,64,1024]{2,1,0:T(8,128)}, f32[2,64,1024]{2,1,0:T(8,128)S(1)}, f32[2,64,1024]{2,1,0:T(8,128)S(1)}) custom-call(s32[1]{0:T(128)} %bitcast.refs_0_, f32[1,2,1024,1024]{3,2,1,0:T(8,128)} %refs_4_.7, f32[1,2,1024,1024]{3,2,1,0:T(8,128)} %refs_4_.7, f32[1,2,1024,1024]{3,2,1,0:T(8,128)} %refs_4_.7, ...), custom_call_target="tpu_custom_call" | custom-call | flops 4294967296 | bytes 4194304 | tf_op jit(solution)/shard_map/product/pallas_call | solution.py:26
  150.4 5.6 %collective-permute-done.10.refs_3_ = f32[2,96,1024]{2,1,0:T(8,128)S(1)} collective-permute-done((f32[2,96,1024]{2,1,0:T(8,128)S(1)}, f32[2,96,1024]{2,1,0:T(8,128)S(1)}, u32[]{:S(2)}, u32[]{:S(2)}) %collective-permute-start.10) | collective-permute-done | bytes 786464 | tf_op jit(solution)/shard_map/ppermute | solution.py:331
  160.9 4.9 all-to-all-done.3
  175.1 43.2 %all-to-all-done.2 = f32[8,64,1024]{2,1,0:T(8,128)S(1)} async-done(((f32[8,64,1024]{2,1,0:T(8,128)}), f32[8,64,1024]{2,1,0:T(8,128)S(1)}, u32[]{:S(2)}, u32[]{:S(2)}) %all-to-all-start.2) | async-done | bytes 2097184 | tf_op jit(solution)/shard_map/all_to_all | solution.py:325
  225.6 3.7 all-to-all-start.4
  234.4 10.0 %collective-permute-done.6.refs_2_ = f32[2,64,1024]{2,1,0:T(8,128)S(1)} collective-permute-done((f32[2,64,1024]{2,1,0:T(8,128)}, f32[2,64,1024]{2,1,0:T(8,128)S(1)}, u32[]{:S(2)}, u32[]{:S(2)}) %collective-permute-start.6) | collective-permute-done | bytes 524320 | tf_op jit(solution)/shard_map/ppermute | solution.py:331
  245.4 11.2 %collective-permute-done.7.refs_3_ = f32[2,64,1024]{2,1,0:T(8,128)S(1)} collective-permute-done((f32[2,64,1024]{2,1,0:T(8,128)}, f32[2,64,1024]{2,1,0:T(8,128)S(1)}, u32[]{:S(2)}, u32[]{:S(2)}) %collective-permute-start.7) | collective-permute-done | bytes 524320 | tf_op jit(solution)/shard_map/ppermute | solution.py:331
  261.4 30.2 %collective-permute-done.21.refs_2_ = f32[2,2,32,256]{3,2,1,0:T(8,128)S(1)} collective-permute-done((f32[2,2,32,256]{3,2,1,0:T(8,128)S(1)}, f32[2,2,32,256]{3,2,1,0:T(8,128)S(1)}, u32[]{:S(2)}, u32[]{:S(2)}) %collective-permute-start.21) | collective-permute-done | bytes 131104 | tf_op jit(solution)/shard_map/ppermute | solution.py:331
  292.6 4.9 collective-permute-done.23.refs_4_
  298.3 4.8 all-to-all-start.5
  303.2 12.1 %product.5 = (f32[2,96,1024]{2,1,0:T(8,128)S(1)}, f32[2,96,1024]{2,1,0:T(8,128)}, f32[2,96,1024]{2,1,0:T(8,128)}, f32[2,96,1024]{2,1,0:T(8,128)}) custom-call(s32[1]{0:T(128)} %bitcast.refs_0_, f32[1,2,1024,1024]{3,2,1,0:T(8,128)} %refs_4_.7, f32[1,2,1024,1024]{3,2,1,0:T(8,128)} %refs_4_.7, f32[1,2,1024,1024]{3,2,1,0:T(8,128)} %refs_4_.7, ...), custom_call_target="tpu_custom_call" | custom-call | flops 6442450944 | bytes 6291456 | tf_op jit(solution)/shard_map/product/pallas_call | solution.py:26
  321.2 5.1 all-to-all-start.6
  326.3 10.5 %collective-permute-done.15.refs_2_ = f32[2,96,1024]{2,1,0:T(8,128)S(1)} collective-permute-done((f32[2,96,1024]{2,1,0:T(8,128)}, f32[2,96,1024]{2,1,0:T(8,128)S(1)}, u32[]{:S(2)}, u32[]{:S(2)}) %collective-permute-start.15) | collective-permute-done | bytes 786464 | tf_op jit(solution)/shard_map/ppermute | solution.py:331
  337.6 16.3 %collective-permute-done.16.refs_3_ = f32[2,96,1024]{2,1,0:T(8,128)} collective-permute-done((f32[2,96,1024]{2,1,0:T(8,128)}, f32[2,96,1024]{2,1,0:T(8,128)}, u32[]{:S(2)}, u32[]{:S(2)}) %collective-permute-start.16) | collective-permute-done | bytes 786464 | tf_op jit(solution)/shard_map/ppermute | solution.py:331
  361.3 4.3 collective-permute-done.33.refs_2_
  370.0 4.5 all-to-all-start.7
  378.1 17.3 %all-to-all-done.7 = f32[8,2,48,256]{3,2,1,0:T(8,128)S(1)} async-done(((f32[8,2,48,256]{3,2,1,0:T(8,128)}), f32[8,2,48,256]{3,2,1,0:T(8,128)S(1)}, u32[]{:S(2)}, u32[]{:S(2)}) %all-to-all-start.7) | async-done | bytes 786464 | tf_op jit(solution)/shard_map/all_to_all | solution.py:325
  399.1 3.7 all-to-all-start.8
  407.6 8.7 %product.6 = (f32[2,64,1024]{2,1,0:T(8,128)S(1)}, f32[2,64,1024]{2,1,0:T(8,128)S(1)}, f32[2,64,1024]{2,1,0:T(8,128)S(1)}, f32[2,64,1024]{2,1,0:T(8,128)S(1)}) custom-call(s32[1]{0:T(128)} %bitcast.refs_0_, f32[1,2,1024,1024]{3,2,1,0:T(8,128)} %refs_4_.7, f32[1,2,1024,1024]{3,2,1,0:T(8,128)} %refs_4_.7, f32[1,2,1024,1024]{3,2,1,0:T(8,128)} %refs_4_.7, ...), custom_call_target="tpu_custom_call" | custom-call | flops 4294967296 | bytes 4194304 | tf_op jit(solution)/shard_map/product/pallas_call | solution.py:26
  418.7 6.1 %product.7 = (f32[2,32,1024]{2,1,0:T(8,128)S(1)}, f32[2,32,1024]{2,1,0:T(8,128)S(1)}, f32[2,32,1024]{2,1,0:T(8,128)S(1)}, f32[2,32,1024]{2,1,0:T(8,128)S(1)}) custom-call(s32[1]{0:T(128)} %bitcast.refs_0_, f32[1,2,1024,1024]{3,2,1,0:T(8,128)} %refs_4_.7, f32[1,2,1024,1024]{3,2,1,0:T(8,128)} %refs_4_.7, f32[1,2,1024,1024]{3,2,1,0:T(8,128)} %refs_4_.7, ...), custom_call_target="tpu_custom_call" | custom-call | flops 2147483648 | bytes 2097152 | tf_op jit(solution)/shard_map/product/pallas_call | solution.py:26
  430.4 3.7 collective-permute-done.30.refs_2_
  435.6 26.2 %collective-permute-done.31.refs_3_ = f32[2,32,1024]{2,1,0:T(8,128)S(1)} collective-permute-done((f32[2,32,1024]{2,1,0:T(8,128)S(1)}, f32[2,32,1024]{2,1,0:T(8,128)S(1)}, u32[]{:S(2)}, u32[]{:S(2)}) %collective-permute-start.31) | collective-permute-done | bytes 262176 | tf_op jit(solution)/shard_map/ppermute | solution.py:331
  471.3 25.5 %all_to_all.56 = f32[8,2,48,256]{3,2,1,0:T(8,128)} all-to-all(f32[8,2,48,256]{3,2,1,0:T(8,128)S(1)} %bitcast.26), channel_id=1, replica_groups=mesh['ia'=8,'ka'=4] {'ia'}, dimensions={0} | all-to-all | bytes 1572864 | tf_op jit(solution)/shard_map/all_to_all | solution.py:325
  500.8 23.4 %all_to_all.57.refs_7_ = f32[8,2,48,256]{3,2,1,0:T(8,128)S(1)} all-to-all(f32[8,2,48,256]{3,2,1,0:T(8,128)S(1)} %bitcast.32), channel_id=1, replica_groups=mesh['ia'=8,'ka'=4] {'ia'}, dimensions={0} | all-to-all | bytes 1572864 | tf_op jit(solution)/shard_map/all_to_all | solution.py:325
  (186 shorter events, 126.4 us)
Async XLA Ops:
  35.7 54.1 %all-to-all-start.1 = ((f32[8,64,1024]{2,1,0:T(8,128)}), f32[8,64,1024]{2,1,0:T(8,128)}, u32[]{:S(2)}, u32[]{:S(2)}) async-start(f32[8,64,1024]{2,1,0:T(8,128)} %bitcast.28), calls=%async_computation.1 | async-start | bytes 4194304 | tf_op jit(solution)/shard_map/all_to_all | solution.py:325
  45.5 36.6 %collective-permute-start.1 = (f32[2,96,1024]{2,1,0:T(8,128)S(1)}, f32[2,96,1024]{2,1,0:T(8,128)S(1)}, u32[]{:S(2)}, u32[]{:S(2)}) collective-permute-start(f32[2,96,1024]{2,1,0:T(8,128)S(1)} %flip.10), channel_id=1, source_target_pairs={{0,2},{1,3},{2,0},{3,1},{4,6},{5,7},{6,4},{7,5},{8,10},{9,11},{10,... | collective-permute-start | bytes 2359304 | tf_op jit(solution)/shard_map/ppermute | solution.py:331
  48.0 34.0 %collective-permute-start.2 = (f32[2,96,1024]{2,1,0:T(8,128)S(1)}, f32[2,96,1024]{2,1,0:T(8,128)S(1)}, u32[]{:S(2)}, u32[]{:S(2)}) collective-permute-start(f32[2,96,1024]{2,1,0:T(8,128)S(1)} %flip.11), channel_id=1, source_target_pairs={{0,3},{1,2},{2,1},{3,0},{4,7},{5,6},{6,5},{7,4},{8,11},{9,10},{10,... | collective-permute-start | bytes 2359304 | tf_op jit(solution)/shard_map/ppermute | solution.py:331
  89.8 76.0 %all-to-all-start.3 = ((f32[8,96,1024]{2,1,0:T(8,128)}), f32[8,96,1024]{2,1,0:T(8,128)}, u32[]{:S(2)}, u32[]{:S(2)}) async-start(f32[8,96,1024]{2,1,0:T(8,128)} %bitcast.21), calls=%async_computation.3 | async-start | bytes 6291456 | tf_op jit(solution)/shard_map/all_to_all | solution.py:325
  97.1 42.9 %collective-permute-start.4 = (f32[2,64,1024]{2,1,0:T(8,128)S(1)}, f32[2,64,1024]{2,1,0:T(8,128)S(1)}, u32[]{:S(2)}, u32[]{:S(2)}) collective-permute-start(f32[2,64,1024]{2,1,0:T(8,128)S(1)} %get-tuple-element.52), channel_id=1, source_target_pairs={{0,2},{1,3},{2,0},{3,1},{4,6},{5,7},{6,4},{7,5},{8,10},{9,11},{10,... | collective-permute-start | bytes 1572872 | tf_op jit(solution)/shard_map/ppermute | solution.py:331
  97.7 42.3 %collective-permute-start.5 = (f32[2,64,1024]{2,1,0:T(8,128)S(1)}, f32[2,64,1024]{2,1,0:T(8,128)S(1)}, u32[]{:S(2)}, u32[]{:S(2)}) collective-permute-start(f32[2,64,1024]{2,1,0:T(8,128)S(1)} %get-tuple-element.53), channel_id=1, source_target_pairs={{0,3},{1,2},{2,1},{3,0},{4,7},{5,6},{6,5},{7,4},{8,11},{9,10},{10,... | collective-permute-start | bytes 1572872 | tf_op jit(solution)/shard_map/ppermute | solution.py:331
  105.1 50.9 %collective-permute-start.10 = (f32[2,96,1024]{2,1,0:T(8,128)S(1)}, f32[2,96,1024]{2,1,0:T(8,128)S(1)}, u32[]{:S(2)}, u32[]{:S(2)}) collective-permute-start(f32[2,96,1024]{2,1,0:T(8,128)S(1)} %flip.14), channel_id=1, source_target_pairs={{0,2},{1,3},{2,0},{3,1},{4,6},{5,7},{6,4},{7,5},{8,10},{9,11},{10,... | collective-permute-start | bytes 2359304 | tf_op jit(solution)/shard_map/ppermute | solution.py:331
  106.1 49.9 %collective-permute-start.11 = (f32[2,96,1024]{2,1,0:T(8,128)S(1)}, f32[2,96,1024]{2,1,0:T(8,128)S(1)}, u32[]{:S(2)}, u32[]{:S(2)}) collective-permute-start(f32[2,96,1024]{2,1,0:T(8,128)S(1)} %flip.15), channel_id=1, source_target_pairs={{0,3},{1,2},{2,1},{3,0},{4,7},{5,6},{6,5},{7,4},{8,11},{9,10},{10,... | collective-permute-start | bytes 2359304 | tf_op jit(solution)/shard_map/ppermute | solution.py:331
  111.0 45.0 %collective-permute-start.9 = (f32[2,96,1024]{2,1,0:T(8,128)S(1)}, f32[2,96,1024]{2,1,0:T(8,128)S(1)}, u32[]{:S(2)}, u32[]{:S(2)}) collective-permute-start(f32[2,96,1024]{2,1,0:T(8,128)S(1)} %flip.13), channel_id=1, source_target_pairs={{0,1},{1,0},{2,3},{3,2},{4,5},{5,4},{6,7},{7,6},{8,9},{9,8},{10,11... | collective-permute-start | bytes 2359304 | tf_op jit(solution)/shard_map/ppermute | solution.py:331
  165.8 52.6 %all-to-all-start.2 = ((f32[8,64,1024]{2,1,0:T(8,128)}), f32[8,64,1024]{2,1,0:T(8,128)S(1)}, u32[]{:S(2)}, u32[]{:S(2)}) async-start(f32[8,64,1024]{2,1,0:T(8,128)} %bitcast.4), calls=%async_computation.2 | async-start | bytes 4194304 | tf_op jit(solution)/shard_map/all_to_all | solution.py:325
  225.6 71.9 %all-to-all-start.4 = ((f32[8,32,1024]{2,1,0:T(8,128)}), f32[8,32,1024]{2,1,0:T(8,128)S(1)}, u32[]{:S(2)}, u32[]{:S(2)}) async-start(f32[8,32,1024]{2,1,0:T(8,128)} %bitcast.8), calls=%async_computation.4 | async-start | bytes 2097152 | tf_op jit(solution)/shard_map/all_to_all | solution.py:325
  230.3 26.2 %collective-permute-start.7 = (f32[2,64,1024]{2,1,0:T(8,128)}, f32[2,64,1024]{2,1,0:T(8,128)S(1)}, u32[]{:S(2)}, u32[]{:S(2)}) collective-permute-start(f32[2,64,1024]{2,1,0:T(8,128)} %copy-done.33), channel_id=1, source_target_pairs={{0,2},{1,3},{2,0},{3,1},{4,6},{5,7},{6,4},{7,5},{8,10},{9,11},{10,... | collective-permute-start | bytes 1572872 | tf_op jit(solution)/shard_map/ppermute | solution.py:331
  230.9 25.7 %collective-permute-start.8 = (f32[2,64,1024]{2,1,0:T(8,128)}, f32[2,64,1024]{2,1,0:T(8,128)}, u32[]{:S(2)}, u32[]{:S(2)}) collective-permute-start(f32[2,64,1024]{2,1,0:T(8,128)} %copy-done.32), channel_id=1, source_target_pairs={{0,3},{1,2},{2,1},{3,0},{4,7},{5,6},{6,5},{7,4},{8,11},{9,10},{10,... | collective-permute-start | bytes 1572872 | tf_op jit(solution)/shard_map/ppermute | solution.py:331
  232.9 70.2 %collective-permute-start.12 = (f32[2,96,1024]{2,1,0:T(8,128)}, f32[2,96,1024]{2,1,0:T(8,128)}, u32[]{:S(2)}, u32[]{:S(2)}) collective-permute-start(f32[2,96,1024]{2,1,0:T(8,128)} %copy-done.28), channel_id=1, source_target_pairs={{0,1},{1,0},{2,3},{3,2},{4,5},{5,4},{6,7},{7,6},{8,9},{9,8},{10,11... | collective-permute-start | bytes 2359304 | tf_op jit(solution)/shard_map/ppermute | solution.py:331
  233.8 69.3 %collective-permute-start.13 = (f32[2,96,1024]{2,1,0:T(8,128)}, f32[2,96,1024]{2,1,0:T(8,128)}, u32[]{:S(2)}, u32[]{:S(2)}) collective-permute-start(f32[2,96,1024]{2,1,0:T(8,128)} %copy-done.27), channel_id=1, source_target_pairs={{0,2},{1,3},{2,0},{3,1},{4,6},{5,7},{6,4},{7,5},{8,10},{9,11},{10,... | collective-permute-start | bytes 2359304 | tf_op jit(solution)/shard_map/ppermute | solution.py:331
  244.4 58.8 %collective-permute-start.14 = (f32[2,96,1024]{2,1,0:T(8,128)}, f32[2,96,1024]{2,1,0:T(8,128)}, u32[]{:S(2)}, u32[]{:S(2)}) collective-permute-start(f32[2,96,1024]{2,1,0:T(8,128)} %copy-done.26), channel_id=1, source_target_pairs={{0,3},{1,2},{2,1},{3,0},{4,7},{5,6},{6,5},{7,4},{8,11},{9,10},{10,... | collective-permute-start | bytes 2359304 | tf_op jit(solution)/shard_map/ppermute | solution.py:331
  258.5 33.1 %collective-permute-start.21 = (f32[2,2,32,256]{3,2,1,0:T(8,128)S(1)}, f32[2,2,32,256]{3,2,1,0:T(8,128)S(1)}, u32[]{:S(2)}, u32[]{:S(2)}) collective-permute-start(f32[2,2,32,256]{3,2,1,0:T(8,128)S(1)} %get-tuple-element.71), channel_id=1, source_target_pairs={{0,1},{1,0},{2,3},{3,2},{4,5},{5,4},{6,7},{7,6},{8,9},{9,8},{10,11... | collective-permute-start | bytes 393224 | tf_op jit(solution)/shard_map/ppermute | solution.py:331
  260.5 32.2 %collective-permute-start.22 = (f32[2,2,32,256]{3,2,1,0:T(8,128)S(1)}, f32[2,2,32,256]{3,2,1,0:T(8,128)S(1)}, u32[]{:S(2)}, u32[]{:S(2)}) collective-permute-start(f32[2,2,32,256]{3,2,1,0:T(8,128)S(1)} %get-tuple-element.72), channel_id=1, source_target_pairs={{0,2},{1,3},{2,0},{3,1},{4,6},{5,7},{6,4},{7,5},{8,10},{9,11},{10,... | collective-permute-start | bytes 393224 | tf_op jit(solution)/shard_map/ppermute | solution.py:331
  298.3 21.4 %all-to-all-start.5 = ((f32[8,2,32,256]{3,2,1,0:T(8,128)}), f32[8,2,32,256]{3,2,1,0:T(8,128)S(1)}, u32[]{:S(2)}, u32[]{:S(2)}) async-start(f32[8,2,32,256]{3,2,1,0:T(8,128)} %bitcast.10), calls=%async_computation.5 | async-start | bytes 1048576 | tf_op jit(solution)/shard_map/all_to_all | solution.py:325
  317.1 36.8 %collective-permute-start.16 = (f32[2,96,1024]{2,1,0:T(8,128)}, f32[2,96,1024]{2,1,0:T(8,128)}, u32[]{:S(2)}, u32[]{:S(2)}) collective-permute-start(f32[2,96,1024]{2,1,0:T(8,128)} %get-tuple-element.65), channel_id=1, source_target_pairs={{0,2},{1,3},{2,0},{3,1},{4,6},{5,7},{6,4},{7,5},{8,10},{9,11},{10,... | collective-permute-start | bytes 2359304 | tf_op jit(solution)/shard_map/ppermute | solution.py:331
  317.7 36.3 %collective-permute-start.17 = (f32[2,96,1024]{2,1,0:T(8,128)}, f32[2,96,1024]{2,1,0:T(8,128)}, u32[]{:S(2)}, u32[]{:S(2)}) collective-permute-start(f32[2,96,1024]{2,1,0:T(8,128)} %get-tuple-element.66), channel_id=1, source_target_pairs={{0,3},{1,2},{2,1},{3,0},{4,7},{5,6},{6,5},{7,4},{8,11},{9,10},{10,... | collective-permute-start | bytes 2359304 | tf_op jit(solution)/shard_map/ppermute | solution.py:331
  321.2 47.9 %all-to-all-start.6 = ((f32[8,2,32,256]{3,2,1,0:T(8,128)}), f32[8,2,32,256]{3,2,1,0:T(8,128)}, u32[]{:S(2)}, u32[]{:S(2)}) async-start(f32[8,2,32,256]{3,2,1,0:T(8,128)} %broadcast_select_fusion.2), calls=%async_computation.6 | async-start | bytes 1048576 | tf_op jit(solution)/shard_map/all_to_all | solution.py:325
  370.0 25.5 %all-to-all-start.7 = ((f32[8,2,48,256]{3,2,1,0:T(8,128)}), f32[8,2,48,256]{3,2,1,0:T(8,128)S(1)}, u32[]{:S(2)}, u32[]{:S(2)}) async-start(f32[8,2,48,256]{3,2,1,0:T(8,128)} %bitcast.14), calls=%async_computation.7 | async-start | bytes 1572864 | tf_op jit(solution)/shard_map/all_to_all | solution.py:325
  374.6 31.4 %collective-permute-start.18 = (f32[2,64,1024]{2,1,0:T(8,128)}, f32[2,64,1024]{2,1,0:T(8,128)}, u32[]{:S(2)}, u32[]{:S(2)}) collective-permute-start(f32[2,64,1024]{2,1,0:T(8,128)} %copy-done.31), channel_id=1, source_target_pairs={{0,1},{1,0},{2,3},{3,2},{4,5},{5,4},{6,7},{7,6},{8,9},{9,8},{10,11... | collective-permute-start | bytes 1572872 | tf_op jit(solution)/shard_map/ppermute | solution.py:331
  375.5 32.1 %collective-permute-start.19 = (f32[2,64,1024]{2,1,0:T(8,128)}, f32[2,64,1024]{2,1,0:T(8,128)}, u32[]{:S(2)}, u32[]{:S(2)}) collective-permute-start(f32[2,64,1024]{2,1,0:T(8,128)} %copy-done.30), channel_id=1, source_target_pairs={{0,2},{1,3},{2,0},{3,1},{4,6},{5,7},{6,4},{7,5},{8,10},{9,11},{10,... | collective-permute-start | bytes 1572872 | tf_op jit(solution)/shard_map/ppermute | solution.py:331
  376.6 31.0 %collective-permute-start.20 = (f32[2,64,1024]{2,1,0:T(8,128)}, f32[2,64,1024]{2,1,0:T(8,128)}, u32[]{:S(2)}, u32[]{:S(2)}) collective-permute-start(f32[2,64,1024]{2,1,0:T(8,128)} %copy-done.29), channel_id=1, source_target_pairs={{0,3},{1,2},{2,1},{3,0},{4,7},{5,6},{6,5},{7,4},{8,11},{9,10},{10,... | collective-permute-start | bytes 1572872 | tf_op jit(solution)/shard_map/ppermute | solution.py:331
  399.1 72.2 %all-to-all-start.8 = ((f32[8,2,48,256]{3,2,1,0:T(8,128)}), f32[8,2,48,256]{3,2,1,0:T(8,128)S(1)}, u32[]{:S(2)}, u32[]{:S(2)}) async-start(f32[8,2,48,256]{3,2,1,0:T(8,128)} %bitcast.29), calls=%async_computation.8 | async-start | bytes 1572864 | tf_op jit(solution)/shard_map/all_to_all | solution.py:325
  426.1 35.8 %collective-permute-start.24 = (f32[2,64,1024]{2,1,0:T(8,128)S(1)}, f32[2,64,1024]{2,1,0:T(8,128)S(1)}, u32[]{:S(2)}, u32[]{:S(2)}) collective-permute-start(f32[2,64,1024]{2,1,0:T(8,128)S(1)} %get-tuple-element.76), channel_id=1, source_target_pairs={{0,1},{1,0},{2,3},{3,2},{4,5},{5,4},{6,7},{7,6},{8,9},{9,8},{10,11... | collective-permute-start | bytes 1572872 | tf_op jit(solution)/shard_map/ppermute | solution.py:331
  427.0 35.0 %collective-permute-start.25 = (f32[2,64,1024]{2,1,0:T(8,128)S(1)}, f32[2,64,1024]{2,1,0:T(8,128)S(1)}, u32[]{:S(2)}, u32[]{:S(2)}) collective-permute-start(f32[2,64,1024]{2,1,0:T(8,128)S(1)} %get-tuple-element.77), channel_id=1, source_target_pairs={{0,2},{1,3},{2,0},{3,1},{4,6},{5,7},{6,4},{7,5},{8,10},{9,11},{10,... | collective-permute-start | bytes 1572872 | tf_op jit(solution)/shard_map/ppermute | solution.py:331
  428.0 33.9 %collective-permute-start.26 = (f32[2,64,1024]{2,1,0:T(8,128)S(1)}, f32[2,64,1024]{2,1,0:T(8,128)S(1)}, u32[]{:S(2)}, u32[]{:S(2)}) collective-permute-start(f32[2,64,1024]{2,1,0:T(8,128)S(1)} %get-tuple-element.78), channel_id=1, source_target_pairs={{0,3},{1,2},{2,1},{3,0},{4,7},{5,6},{6,5},{7,4},{8,11},{9,10},{10,... | collective-permute-start | bytes 1572872 | tf_op jit(solution)/shard_map/ppermute | solution.py:331
  429.6 32.3 %collective-permute-start.31 = (f32[2,32,1024]{2,1,0:T(8,128)S(1)}, f32[2,32,1024]{2,1,0:T(8,128)S(1)}, u32[]{:S(2)}, u32[]{:S(2)}) collective-permute-start(f32[2,32,1024]{2,1,0:T(8,128)S(1)} %get-tuple-element.84), channel_id=1, source_target_pairs={{0,2},{1,3},{2,0},{3,1},{4,6},{5,7},{6,4},{7,5},{8,10},{9,11},{10,... | collective-permute-start | bytes 786440 | tf_op jit(solution)/shard_map/ppermute | solution.py:331
  434.2 27.7 %collective-permute-start.32 = (f32[2,32,1024]{2,1,0:T(8,128)S(1)}, f32[2,32,1024]{2,1,0:T(8,128)S(1)}, u32[]{:S(2)}, u32[]{:S(2)}) collective-permute-start(f32[2,32,1024]{2,1,0:T(8,128)S(1)} %get-tuple-element.85), channel_id=1, source_target_pairs={{0,3},{1,2},{2,1},{3,0},{4,7},{5,6},{6,5},{7,4},{8,11},{9,10},{10,... | collective-permute-start | bytes 786440 | tf_op jit(solution)/shard_map/ppermute | solution.py:331
  (50 other events, 474.0 us)

commit v11 on v10

--- a/solution.py
+++ b/solution.py
@@ -273,6 +273,25 @@
         [whole(shape)] * sections,
         [jax.ShapeDtypeStruct(shape, jnp.float32)] * sections,
         (1,),
+    )
+
+
+def hold_kernel(index_ref, out_ref):
+    for at in range(out_ref.shape[0]):
+        out_ref[at] = index_ref[at]
+
+
+def hold(index, after):
+    return call(
+        hold_kernel,
+        "hold",
+        index,
+        [],
+        [],
+        pl.BlockSpec(memory_space=pltpu.SMEM),
+        jax.ShapeDtypeStruct(index.shape, index.dtype),
+        (1,),
+        after=after,
     )
 
 
@@ -370,9 +389,10 @@
     def meet(columns):
         return swap(columns.reshape(occupied, slots, *columns.shape[-2:]), "ia")
 
-    def deliver(met):
+    def deliver(met, after):
         piece = met.shape[-2:]
-        routed = jnp.take(met.reshape(occupied * slots, *piece), source_row, axis=0)
+        rows = hold(source_row, after)
+        routed = jnp.take(met.reshape(occupied * slots, *piece), rows, axis=0)
         return swap(routed.reshape(occupied, slots, *piece), "ia")
 
     first = first_flip(place, amplitudes, sections, sizes[0])
@@ -384,24 +404,25 @@
     turned, mirrored = turn(0, hop(0), [across[1]])
     begun, parts = multiply(0, mirrored, [])
     across.append(waiting[0]([begun]))
+    own = [add(place, parts, [])]
     turned, mirrored = turn(1, hop(1), [across[2]])
     turned, later = turn(2, hop(2), [turned])
-    across.append(waiting[1]([turned]))
-    own = [add(place, parts, [turned])]
-    begun, parts = multiply(1, mirrored, [turned])
+    across.append(waiting[1]([turned, own[0]]))
+    begun, parts = multiply(1, mirrored, [])
+    own.append(add(place, parts, []))
     crossed = hop(3)
-    leading = gather(place, send(GROUPS[0]), [crossed])
-    turned, mirrored = turn(3, crossed, [begun, leading])
+    leading = gather(place, send(GROUPS[0]), [crossed, begun])
+    turned, mirrored = turn(3, crossed, [leading])
+    begun, parts = multiply(2, later, [turned])
     own.append(add(place, parts, []))
-    met = meet(leading)
-    begun, parts = multiply(2, later, [turned, met])
+    delivered = [deliver(meet(leading), [begun])]
+    begun, parts = multiply(3, mirrored, delivered)
     own.append(add(place, parts, []))
-    _, parts = multiply(3, mirrored, [begun])
-    own.append(add(place, parts, []))
-
-    delivered = [deliver(met)]
+    after = [begun]
     for group in GROUPS[1:]:
-        delivered.append(deliver(meet(gather(place, send(group), [delivered[-1]]))))
+        met = meet(gather(place, send(group), [delivered[-1], *after]))
+        delivered.append(deliver(met, []))
+        after = []
     return finish(place, spans, GROUPS, own, delivered)
 
 

time: 529 us -> 522 us (0.987)
  waiting for transfers between devices: 257 us -> 241 us
  local copies, waits for them, and re-layouts: 26.5 us -> 34.9 us
    all_to_all x8, waiting for transfers between devices: 71.4 us -> 52.2 us  [swap(): return lax.all_to_all(array, axis, split_axis=0, concat_axis=0, tiled=True)]
    unnamed x71 -> x109, local copies, waits for them, and re-layouts: 20.7 us -> 28 us
    pallas_call x32 -> x34, Pallas kernels: 80.5 us -> 83.5 us  [call(): pl.pallas_call(trimmed, grid_spec=pltpu.PrefetchScalarGridSpec(num_scalar...]
  transfers between devices with their start and end apart: 47 -> 47, of which waited for: 22 -> 22; matrix products, arithmetic and copies ran while one was open for 1% -> 1% of each run, Pallas kernels for 13% -> 14%
where the time goes in v11:
time: 522 us; the launch traced here: 520 us
  waiting for transfers between devices  241 us (46%)
  Pallas kernels  83.5 us (16%)
  blocking collectives  79.3 us (15%)
  starting transfers between devices  77.2 us (15%)
  local copies, waits for them, and re-layouts  34.9 us (7%)
    ppermute x39, waiting for transfers between devices, spread(): lax.ppermute(pieces[e], 'ka', [(q, q ^ e) for q in range(count)])  189 us
    pallas_call x34, Pallas kernels, call(): pl.pallas_call(trimmed, grid_spec=pltpu.PrefetchScalarGridSpec(num_scalar...  83.5 us
    all_to_all x3, blocking collectives, swap(): return lax.all_to_all(array, axis, split_axis=0, concat_axis=0, tiled=True)  79.3 us
    all_to_all x8, waiting for transfers between devices, swap(): return lax.all_to_all(array, axis, split_axis=0, concat_axis=0, tiled=True)  52.2 us
    ppermute x39, starting transfers between devices, spread(): lax.ppermute(pieces[e], 'ka', [(q, q ^ e) for q in range(count)])  43.8 us
    all_to_all x8, starting transfers between devices, swap(): return lax.all_to_all(array, axis, split_axis=0, concat_axis=0, tiled=True)  33.3 us
    unnamed x109, local copies, waits for them, and re-layouts  28 us
  transfers between devices with their start and end apart: 47, of which 22 were waited for; matrix products, arithmetic and copies ran while one was open for 1% of the time, Pallas kernels for 14%

profile of v11, /device:TPU:0, one launch (start us, length us, event | category | flops | bytes accessed | tf_op | source)
XLA Modules:
  0.0 520.4 jit_solution(17114834773062900790)
XLA Ops:
  0.0 5.3 %first_flip.1.refs_2_ = f32[4,2,64,1024]{3,2,1,0:T(8,128)S(1)} custom-call(s32[1]{0:T(128)} %bitcast.refs_0_, f32[1,2,1024,1024]{3,2,1,0:T(8,128)} %refs_4_.7), custom_call_target="tpu_custom_call" | custom-call | bytes 4194304 | tf_op jit(solution)/shard_map/first_flip/pallas_call | solution.py:26
  5.3 30.4 %all_to_all.55 = f32[4,2,64,1024]{3,2,1,0:T(8,128)} all-to-all(f32[4,2,64,1024]{3,2,1,0:T(8,128)S(1)} %first_flip.1.refs_2_), channel_id=1, replica_groups=mesh['ia'=8,'ka'=4] {'ka'}, dimensions={0} | all-to-all | bytes 4194304 | tf_op jit(solution)/shard_map/all_to_all | solution.py:344
  35.7 4.9 all-to-all-start.1
  52.0 8.7 %mask.1.refs_5_.refs_9_ = bf16[2,2,1024,1024]{3,2,1,0:T(8,128)(2,1)} custom-call(s32[2,2,8,8]{3,2,1,0:T(8,128)S(1)} %bitcast.24, bf16[1,2,2,1024,1024]{4,3,2,1,0:T(8,128)(2,1)} %refs_1_.19, f32[4,2,64,1024]{3,2,1,0:T(8,128)S(1)} %first_flip.1.refs_2_), custom_call_target="tpu_custom_call" | custom-call | bytes 16777216 | tf_op jit(solution)/shard_map/mask/pallas_call | solution.py:26
  62.9 19.1 %collective-permute-done.1.refs_3_ = f32[2,96,1024]{2,1,0:T(8,128)S(1)} collective-permute-done((f32[2,96,1024]{2,1,0:T(8,128)S(1)}, f32[2,96,1024]{2,1,0:T(8,128)S(1)}, u32[]{:S(2)}, u32[]{:S(2)}) %collective-permute-start.1) | collective-permute-done | bytes 786464 | tf_op jit(solution)/shard_map/ppermute | solution.py:350
  83.8 6.0 %all-to-all-done.1 = f32[8,64,1024]{2,1,0:T(8,128)} async-done(((f32[8,64,1024]{2,1,0:T(8,128)}), f32[8,64,1024]{2,1,0:T(8,128)}, u32[]{:S(2)}, u32[]{:S(2)}) %all-to-all-start.1) | async-done | bytes 2097184 | tf_op jit(solution)/shard_map/all_to_all | solution.py:344
  89.8 4.5 all-to-all-start.2
  106.6 4.3 collective-permute-done.3.refs_6_
  113.7 9.5 %collective-permute-done.4.refs_7_ = f32[2,64,1024]{2,1,0:T(8,128)S(1)} collective-permute-done((f32[2,64,1024]{2,1,0:T(8,128)S(1)}, f32[2,64,1024]{2,1,0:T(8,128)S(1)}, u32[]{:S(2)}, u32[]{:S(2)}) %collective-permute-start.4) | collective-permute-done | bytes 524320 | tf_op jit(solution)/shard_map/ppermute | solution.py:350
  123.2 8.2 %product.4 = (f32[2,64,1024]{2,1,0:T(8,128)S(1)}, f32[2,64,1024]{2,1,0:T(8,128)S(1)}, f32[2,64,1024]{2,1,0:T(8,128)S(1)}, f32[2,64,1024]{2,1,0:T(8,128)S(1)}) custom-call(s32[1]{0:T(128)} %bitcast.refs_0_, f32[1,2,1024,1024]{3,2,1,0:T(8,128)} %refs_4_.7, f32[1,2,1024,1024]{3,2,1,0:T(8,128)} %refs_4_.7, f32[1,2,1024,1024]{3,2,1,0:T(8,128)} %refs_4_.7, ...), custom_call_target="tpu_custom_call" | custom-call | flops 4294967296 | bytes 4194304 | tf_op jit(solution)/shard_map/product/pallas_call | solution.py:26
  133.0 6.1 %collective-permute-done.9.refs_2_ = f32[2,96,1024]{2,1,0:T(8,128)S(1)} collective-permute-done((f32[2,96,1024]{2,1,0:T(8,128)S(1)}, f32[2,96,1024]{2,1,0:T(8,128)S(1)}, u32[]{:S(2)}, u32[]{:S(2)}) %collective-permute-start.9) | collective-permute-done | bytes 786464 | tf_op jit(solution)/shard_map/ppermute | solution.py:350
  139.1 16.9 %collective-permute-done.10.refs_3_ = f32[2,96,1024]{2,1,0:T(8,128)S(1)} collective-permute-done((f32[2,96,1024]{2,1,0:T(8,128)S(1)}, f32[2,96,1024]{2,1,0:T(8,128)S(1)}, u32[]{:S(2)}, u32[]{:S(2)}) %collective-permute-start.10) | collective-permute-done | bytes 786464 | tf_op jit(solution)/shard_map/ppermute | solution.py:350
  160.0 5.7 %all-to-all-done.2 = f32[8,96,1024]{2,1,0:T(8,128)} async-done(((f32[8,96,1024]{2,1,0:T(8,128)}), f32[8,96,1024]{2,1,0:T(8,128)}, u32[]{:S(2)}, u32[]{:S(2)}) %all-to-all-start.2) | async-done | bytes 3145760 | tf_op jit(solution)/shard_map/all_to_all | solution.py:344
  172.9 11.5 %collective-permute-done.6.refs_2_ = f32[2,64,1024]{2,1,0:T(8,128)S(1)} collective-permute-done((f32[2,64,1024]{2,1,0:T(8,128)}, f32[2,64,1024]{2,1,0:T(8,128)S(1)}, u32[]{:S(2)}, u32[]{:S(2)}) %collective-permute-start.6) | collective-permute-done | bytes 524320 | tf_op jit(solution)/shard_map/ppermute | solution.py:350
  184.4 11.3 %collective-permute-done.7.refs_3_ = f32[2,64,1024]{2,1,0:T(8,128)S(1)} collective-permute-done((f32[2,64,1024]{2,1,0:T(8,128)}, f32[2,64,1024]{2,1,0:T(8,128)S(1)}, u32[]{:S(2)}, u32[]{:S(2)}) %collective-permute-start.7) | collective-permute-done | bytes 524320 | tf_op jit(solution)/shard_map/ppermute | solution.py:350
  200.2 18.2 %all-to-all-done.3 = f32[8,64,1024]{2,1,0:T(8,128)S(1)} async-done(((f32[8,64,1024]{2,1,0:T(8,128)}), f32[8,64,1024]{2,1,0:T(8,128)S(1)}, u32[]{:S(2)}, u32[]{:S(2)}) %all-to-all-start.3) | async-done | bytes 2097184 | tf_op jit(solution)/shard_map/all_to_all | solution.py:344
  235.0 31.7 %collective-permute-done.21.refs_2_ = f32[2,2,32,256]{3,2,1,0:T(8,128)S(1)} collective-permute-done((f32[2,2,32,256]{3,2,1,0:T(8,128)}, f32[2,2,32,256]{3,2,1,0:T(8,128)S(1)}, u32[]{:S(2)}, u32[]{:S(2)}) %collective-permute-start.21) | collective-permute-done | bytes 131104 | tf_op jit(solution)/shard_map/ppermute | solution.py:350
  273.1 11.8 %product.5 = (f32[2,96,1024]{2,1,0:T(8,128)S(1)}, f32[2,96,1024]{2,1,0:T(8,128)}, f32[2,96,1024]{2,1,0:T(8,128)}, f32[2,96,1024]{2,1,0:T(8,128)}) custom-call(s32[1]{0:T(128)} %bitcast.refs_0_, f32[1,2,1024,1024]{3,2,1,0:T(8,128)} %refs_4_.7, f32[1,2,1024,1024]{3,2,1,0:T(8,128)} %refs_4_.7, f32[1,2,1024,1024]{3,2,1,0:T(8,128)} %refs_4_.7, ...), custom_call_target="tpu_custom_call" | custom-call | flops 6442450944 | bytes 6291456 | tf_op jit(solution)/shard_map/product/pallas_call | solution.py:26
  289.8 4.8 all-to-all-start.5
  296.7 8.7 %product.6 = (f32[2,64,1024]{2,1,0:T(8,128)S(1)}, f32[2,64,1024]{2,1,0:T(8,128)S(1)}, f32[2,64,1024]{2,1,0:T(8,128)S(1)}, f32[2,64,1024]{2,1,0:T(8,128)S(1)}) custom-call(s32[1]{0:T(128)} %bitcast.refs_0_, f32[1,2,1024,1024]{3,2,1,0:T(8,128)} %refs_4_.7, f32[1,2,1024,1024]{3,2,1,0:T(8,128)} %refs_4_.7, f32[1,2,1024,1024]{3,2,1,0:T(8,128)} %refs_4_.7, ...), custom_call_target="tpu_custom_call" | custom-call | flops 4294967296 | bytes 4194304 | tf_op jit(solution)/shard_map/product/pallas_call | solution.py:26
  311.4 3.7 all-to-all-start.6
  320.7 37.5 %collective-permute-done.16.refs_3_ = f32[2,96,1024]{2,1,0:T(8,128)S(1)} collective-permute-done((f32[2,96,1024]{2,1,0:T(8,128)}, f32[2,96,1024]{2,1,0:T(8,128)S(1)}, u32[]{:S(2)}, u32[]{:S(2)}) %collective-permute-start.16) | collective-permute-done | bytes 786464 | tf_op jit(solution)/shard_map/ppermute | solution.py:350
  367.2 6.1 %product.7 = (f32[2,32,1024]{2,1,0:T(8,128)S(1)}, f32[2,32,1024]{2,1,0:T(8,128)S(1)}, f32[2,32,1024]{2,1,0:T(8,128)S(1)}, f32[2,32,1024]{2,1,0:T(8,128)S(1)}) custom-call(s32[1]{0:T(128)} %bitcast.refs_0_, f32[1,2,1024,1024]{3,2,1,0:T(8,128)} %refs_4_.7, f32[1,2,1024,1024]{3,2,1,0:T(8,128)} %refs_4_.7, f32[1,2,1024,1024]{3,2,1,0:T(8,128)} %refs_4_.7, ...), custom_call_target="tpu_custom_call" | custom-call | flops 2147483648 | bytes 2097152 | tf_op jit(solution)/shard_map/product/pallas_call | solution.py:26
  375.1 4.8 all-to-all-start.7
  381.0 19.8 %all-to-all-done.7 = f32[8,2,48,256]{3,2,1,0:T(8,128)S(1)} async-done(((f32[8,2,48,256]{3,2,1,0:T(8,128)}), f32[8,2,48,256]{3,2,1,0:T(8,128)S(1)}, u32[]{:S(2)}, u32[]{:S(2)}) %all-to-all-start.7) | async-done | bytes 786464 | tf_op jit(solution)/shard_map/all_to_all | solution.py:344
  415.7 9.4 %collective-permute-done.24.refs_2_ = f32[2,64,1024]{2,1,0:T(8,128)S(1)} collective-permute-done((f32[2,64,1024]{2,1,0:T(8,128)}, f32[2,64,1024]{2,1,0:T(8,128)S(1)}, u32[]{:S(2)}, u32[]{:S(2)}) %collective-permute-start.24) | collective-permute-done | bytes 524320 | tf_op jit(solution)/shard_map/ppermute | solution.py:350
  426.6 10.4 %collective-permute-done.25.refs_3_ = f32[2,64,1024]{2,1,0:T(8,128)S(1)} collective-permute-done((f32[2,64,1024]{2,1,0:T(8,128)}, f32[2,64,1024]{2,1,0:T(8,128)S(1)}, u32[]{:S(2)}, u32[]{:S(2)}) %collective-permute-start.25) | collective-permute-done | bytes 524320 | tf_op jit(solution)/shard_map/ppermute | solution.py:350
  438.1 3.9 collective-permute-done.30.refs_2_
  442.0 5.6 %collective-permute-done.32.refs_4_ = f32[2,32,1024]{2,1,0:T(8,128)S(1)} collective-permute-done((f32[2,32,1024]{2,1,0:T(8,128)S(1)}, f32[2,32,1024]{2,1,0:T(8,128)S(1)}, u32[]{:S(2)}, u32[]{:S(2)}) %collective-permute-start.32) | collective-permute-done | bytes 262176 | tf_op jit(solution)/shard_map/ppermute | solution.py:350
  452.9 4.3 collective-permute-done.36.refs_2_
  465.7 25.4 %all_to_all.56 = f32[8,2,48,256]{3,2,1,0:T(8,128)} all-to-all(f32[8,2,48,256]{3,2,1,0:T(8,128)S(1)} %bitcast.23), channel_id=1, replica_groups=mesh['ia'=8,'ka'=4] {'ia'}, dimensions={0} | all-to-all | bytes 1572864 | tf_op jit(solution)/shard_map/all_to_all | solution.py:344
  495.0 23.4 %all_to_all.57.refs_7_ = f32[8,2,48,256]{3,2,1,0:T(8,128)S(1)} all-to-all(f32[8,2,48,256]{3,2,1,0:T(8,128)S(1)} %bitcast.29), channel_id=1, replica_groups=mesh['ia'=8,'ka'=4] {'ia'}, dimensions={0} | all-to-all | bytes 1572864 | tf_op jit(solution)/shard_map/all_to_all | solution.py:344
  (227 shorter events, 137.8 us)
Async XLA Ops:
  35.7 54.1 %all-to-all-start.1 = ((f32[8,64,1024]{2,1,0:T(8,128)}), f32[8,64,1024]{2,1,0:T(8,128)}, u32[]{:S(2)}, u32[]{:S(2)}) async-start(f32[8,64,1024]{2,1,0:T(8,128)} %bitcast.25), calls=%async_computation.1 | async-start | bytes 4194304 | tf_op jit(solution)/shard_map/all_to_all | solution.py:344
  45.5 36.6 %collective-permute-start.1 = (f32[2,96,1024]{2,1,0:T(8,128)S(1)}, f32[2,96,1024]{2,1,0:T(8,128)S(1)}, u32[]{:S(2)}, u32[]{:S(2)}) collective-permute-start(f32[2,96,1024]{2,1,0:T(8,128)S(1)} %flip.10), channel_id=1, source_target_pairs={{0,2},{1,3},{2,0},{3,1},{4,6},{5,7},{6,4},{7,5},{8,10},{9,11},{10,... | collective-permute-start | bytes 2359304 | tf_op jit(solution)/shard_map/ppermute | solution.py:350
  48.0 34.0 %collective-permute-start.2 = (f32[2,96,1024]{2,1,0:T(8,128)S(1)}, f32[2,96,1024]{2,1,0:T(8,128)S(1)}, u32[]{:S(2)}, u32[]{:S(2)}) collective-permute-start(f32[2,96,1024]{2,1,0:T(8,128)S(1)} %flip.11), channel_id=1, source_target_pairs={{0,3},{1,2},{2,1},{3,0},{4,7},{5,6},{6,5},{7,4},{8,11},{9,10},{10,... | collective-permute-start | bytes 2359304 | tf_op jit(solution)/shard_map/ppermute | solution.py:350
  89.8 76.0 %all-to-all-start.2 = ((f32[8,96,1024]{2,1,0:T(8,128)}), f32[8,96,1024]{2,1,0:T(8,128)}, u32[]{:S(2)}, u32[]{:S(2)}) async-start(f32[8,96,1024]{2,1,0:T(8,128)} %bitcast.19), calls=%async_computation.2 | async-start | bytes 6291456 | tf_op jit(solution)/shard_map/all_to_all | solution.py:344
  97.1 26.0 %collective-permute-start.4 = (f32[2,64,1024]{2,1,0:T(8,128)S(1)}, f32[2,64,1024]{2,1,0:T(8,128)S(1)}, u32[]{:S(2)}, u32[]{:S(2)}) collective-permute-start(f32[2,64,1024]{2,1,0:T(8,128)S(1)} %get-tuple-element.52), channel_id=1, source_target_pairs={{0,2},{1,3},{2,0},{3,1},{4,6},{5,7},{6,4},{7,5},{8,10},{9,11},{10,... | collective-permute-start | bytes 1572872 | tf_op jit(solution)/shard_map/ppermute | solution.py:350
  97.7 25.5 %collective-permute-start.5 = (f32[2,64,1024]{2,1,0:T(8,128)S(1)}, f32[2,64,1024]{2,1,0:T(8,128)S(1)}, u32[]{:S(2)}, u32[]{:S(2)}) collective-permute-start(f32[2,64,1024]{2,1,0:T(8,128)S(1)} %get-tuple-element.53), channel_id=1, source_target_pairs={{0,3},{1,2},{2,1},{3,0},{4,7},{5,6},{6,5},{7,4},{8,11},{9,10},{10,... | collective-permute-start | bytes 1572872 | tf_op jit(solution)/shard_map/ppermute | solution.py:350
  105.1 34.0 %collective-permute-start.9 = (f32[2,96,1024]{2,1,0:T(8,128)S(1)}, f32[2,96,1024]{2,1,0:T(8,128)S(1)}, u32[]{:S(2)}, u32[]{:S(2)}) collective-permute-start(f32[2,96,1024]{2,1,0:T(8,128)S(1)} %flip.13), channel_id=1, source_target_pairs={{0,1},{1,0},{2,3},{3,2},{4,5},{5,4},{6,7},{7,6},{8,9},{9,8},{10,11... | collective-permute-start | bytes 2359304 | tf_op jit(solution)/shard_map/ppermute | solution.py:350
  106.1 49.9 %collective-permute-start.10 = (f32[2,96,1024]{2,1,0:T(8,128)S(1)}, f32[2,96,1024]{2,1,0:T(8,128)S(1)}, u32[]{:S(2)}, u32[]{:S(2)}) collective-permute-start(f32[2,96,1024]{2,1,0:T(8,128)S(1)} %flip.14), channel_id=1, source_target_pairs={{0,2},{1,3},{2,0},{3,1},{4,6},{5,7},{6,4},{7,5},{8,10},{9,11},{10,... | collective-permute-start | bytes 2359304 | tf_op jit(solution)/shard_map/ppermute | solution.py:350
  111.0 45.0 %collective-permute-start.11 = (f32[2,96,1024]{2,1,0:T(8,128)S(1)}, f32[2,96,1024]{2,1,0:T(8,128)S(1)}, u32[]{:S(2)}, u32[]{:S(2)}) collective-permute-start(f32[2,96,1024]{2,1,0:T(8,128)S(1)} %flip.15), channel_id=1, source_target_pairs={{0,3},{1,2},{2,1},{3,0},{4,7},{5,6},{6,5},{7,4},{8,11},{9,10},{10,... | collective-permute-start | bytes 2359304 | tf_op jit(solution)/shard_map/ppermute | solution.py:350
  165.8 52.6 %all-to-all-start.3 = ((f32[8,64,1024]{2,1,0:T(8,128)}), f32[8,64,1024]{2,1,0:T(8,128)S(1)}, u32[]{:S(2)}, u32[]{:S(2)}) async-start(f32[8,64,1024]{2,1,0:T(8,128)} %bitcast.6), calls=%async_computation.3 | async-start | bytes 4194304 | tf_op jit(solution)/shard_map/all_to_all | solution.py:344
  170.4 25.3 %collective-permute-start.7 = (f32[2,64,1024]{2,1,0:T(8,128)}, f32[2,64,1024]{2,1,0:T(8,128)S(1)}, u32[]{:S(2)}, u32[]{:S(2)}) collective-permute-start(f32[2,64,1024]{2,1,0:T(8,128)} %copy-done.44), channel_id=1, source_target_pairs={{0,2},{1,3},{2,0},{3,1},{4,6},{5,7},{6,4},{7,5},{8,10},{9,11},{10,... | collective-permute-start | bytes 1572872 | tf_op jit(solution)/shard_map/ppermute | solution.py:350
  170.9 24.8 %collective-permute-start.8 = (f32[2,64,1024]{2,1,0:T(8,128)S(1)}, f32[2,64,1024]{2,1,0:T(8,128)S(1)}, u32[]{:S(2)}, u32[]{:S(2)}) collective-permute-start(f32[2,64,1024]{2,1,0:T(8,128)S(1)} %get-tuple-element.57), channel_id=1, source_target_pairs={{0,3},{1,2},{2,1},{3,0},{4,7},{5,6},{6,5},{7,4},{8,11},{9,10},{10,... | collective-permute-start | bytes 1572872 | tf_op jit(solution)/shard_map/ppermute | solution.py:350
  223.3 63.8 %all-to-all-start.4 = ((f32[8,32,1024]{2,1,0:T(8,128)}), f32[8,32,1024]{2,1,0:T(8,128)S(1)}, u32[]{:S(2)}, u32[]{:S(2)}) async-start(f32[8,32,1024]{2,1,0:T(8,128)} %bitcast.8), calls=%async_computation.4 | async-start | bytes 2097152 | tf_op jit(solution)/shard_map/all_to_all | solution.py:344
  226.9 40.7 %collective-permute-start.12 = (f32[2,96,1024]{2,1,0:T(8,128)}, f32[2,96,1024]{2,1,0:T(8,128)S(1)}, u32[]{:S(2)}, u32[]{:S(2)}) collective-permute-start(f32[2,96,1024]{2,1,0:T(8,128)} %get-tuple-element.59), channel_id=1, source_target_pairs={{0,1},{1,0},{2,3},{3,2},{4,5},{5,4},{6,7},{7,6},{8,9},{9,8},{10,11... | collective-permute-start | bytes 2359304 | tf_op jit(solution)/shard_map/ppermute | solution.py:350
  227.9 42.1 %collective-permute-start.13 = (f32[2,96,1024]{2,1,0:T(8,128)}, f32[2,96,1024]{2,1,0:T(8,128)}, u32[]{:S(2)}, u32[]{:S(2)}) collective-permute-start(f32[2,96,1024]{2,1,0:T(8,128)} %get-tuple-element.60), channel_id=1, source_target_pairs={{0,2},{1,3},{2,0},{3,1},{4,6},{5,7},{6,4},{7,5},{8,10},{9,11},{10,... | collective-permute-start | bytes 2359304 | tf_op jit(solution)/shard_map/ppermute | solution.py:350
  228.4 42.6 %collective-permute-start.14 = (f32[2,96,1024]{2,1,0:T(8,128)}, f32[2,96,1024]{2,1,0:T(8,128)}, u32[]{:S(2)}, u32[]{:S(2)}) collective-permute-start(f32[2,96,1024]{2,1,0:T(8,128)} %get-tuple-element.61), channel_id=1, source_target_pairs={{0,3},{1,2},{2,1},{3,0},{4,7},{5,6},{6,5},{7,4},{8,11},{9,10},{10,... | collective-permute-start | bytes 2359304 | tf_op jit(solution)/shard_map/ppermute | solution.py:350
  233.4 33.3 %collective-permute-start.21 = (f32[2,2,32,256]{3,2,1,0:T(8,128)}, f32[2,2,32,256]{3,2,1,0:T(8,128)S(1)}, u32[]{:S(2)}, u32[]{:S(2)}) collective-permute-start(f32[2,2,32,256]{3,2,1,0:T(8,128)} %get-tuple-element.71), channel_id=1, source_target_pairs={{0,1},{1,0},{2,3},{3,2},{4,5},{5,4},{6,7},{7,6},{8,9},{9,8},{10,11... | collective-permute-start | bytes 393224 | tf_op jit(solution)/shard_map/ppermute | solution.py:350
  234.4 50.6 %collective-permute-start.22 = (f32[2,2,32,256]{3,2,1,0:T(8,128)}, f32[2,2,32,256]{3,2,1,0:T(8,128)S(1)}, u32[]{:S(2)}, u32[]{:S(2)}) collective-permute-start(f32[2,2,32,256]{3,2,1,0:T(8,128)} %copy-done.51), channel_id=1, source_target_pairs={{0,2},{1,3},{2,0},{3,1},{4,6},{5,7},{6,4},{7,5},{8,10},{9,11},{10,... | collective-permute-start | bytes 393224 | tf_op jit(solution)/shard_map/ppermute | solution.py:350
  268.5 26.1 %collective-permute-start.18 = (f32[2,64,1024]{2,1,0:T(8,128)}, f32[2,64,1024]{2,1,0:T(8,128)}, u32[]{:S(2)}, u32[]{:S(2)}) collective-permute-start(f32[2,64,1024]{2,1,0:T(8,128)} %copy-done.43), channel_id=1, source_target_pairs={{0,1},{1,0},{2,3},{3,2},{4,5},{5,4},{6,7},{7,6},{8,9},{9,8},{10,11... | collective-permute-start | bytes 1572872 | tf_op jit(solution)/shard_map/ppermute | solution.py:350
  271.1 25.6 %collective-permute-start.20 = (f32[2,64,1024]{2,1,0:T(8,128)}, f32[2,64,1024]{2,1,0:T(8,128)}, u32[]{:S(2)}, u32[]{:S(2)}) collective-permute-start(f32[2,64,1024]{2,1,0:T(8,128)} %copy-done.41), channel_id=1, source_target_pairs={{0,3},{1,2},{2,1},{3,0},{4,7},{5,6},{6,5},{7,4},{8,11},{9,10},{10,... | collective-permute-start | bytes 1572872 | tf_op jit(solution)/shard_map/ppermute | solution.py:350
  285.0 34.8 %collective-permute-start.15 = (f32[2,96,1024]{2,1,0:T(8,128)}, f32[2,96,1024]{2,1,0:T(8,128)}, u32[]{:S(2)}, u32[]{:S(2)}) collective-permute-start(f32[2,96,1024]{2,1,0:T(8,128)} %get-tuple-element.63), channel_id=1, source_target_pairs={{0,1},{1,0},{2,3},{3,2},{4,5},{5,4},{6,7},{7,6},{8,9},{9,8},{10,11... | collective-permute-start | bytes 2359304 | tf_op jit(solution)/shard_map/ppermute | solution.py:350
  311.4 53.8 %all-to-all-start.6 = ((f32[8,2,32,256]{3,2,1,0:T(8,128)}), f32[8,2,32,256]{3,2,1,0:T(8,128)S(1)}, u32[]{:S(2)}, u32[]{:S(2)}) async-start(f32[8,2,32,256]{3,2,1,0:T(8,128)} %broadcast_select_fusion.2), calls=%async_computation.6 | async-start | bytes 1048576 | tf_op jit(solution)/shard_map/all_to_all | solution.py:344
  315.1 43.1 %collective-permute-start.16 = (f32[2,96,1024]{2,1,0:T(8,128)}, f32[2,96,1024]{2,1,0:T(8,128)S(1)}, u32[]{:S(2)}, u32[]{:S(2)}) collective-permute-start(f32[2,96,1024]{2,1,0:T(8,128)} %get-tuple-element.64), channel_id=1, source_target_pairs={{0,2},{1,3},{2,0},{3,1},{4,6},{5,7},{6,4},{7,5},{8,10},{9,11},{10,... | collective-permute-start | bytes 2359304 | tf_op jit(solution)/shard_map/ppermute | solution.py:350
  316.3 42.0 %collective-permute-start.17 = (f32[2,96,1024]{2,1,0:T(8,128)}, f32[2,96,1024]{2,1,0:T(8,128)S(1)}, u32[]{:S(2)}, u32[]{:S(2)}) collective-permute-start(f32[2,96,1024]{2,1,0:T(8,128)} %get-tuple-element.65), channel_id=1, source_target_pairs={{0,3},{1,2},{2,1},{3,0},{4,7},{5,6},{6,5},{7,4},{8,11},{9,10},{10,... | collective-permute-start | bytes 2359304 | tf_op jit(solution)/shard_map/ppermute | solution.py:350
  317.2 45.2 %collective-permute-start.27 = (f32[2,32,1024]{2,1,0:T(8,128)}, f32[2,32,1024]{2,1,0:T(8,128)S(1)}, u32[]{:S(2)}, u32[]{:S(2)}) collective-permute-start(f32[2,32,1024]{2,1,0:T(8,128)} %get-tuple-element.79), channel_id=1, source_target_pairs={{0,1},{1,0},{2,3},{3,2},{4,5},{5,4},{6,7},{7,6},{8,9},{9,8},{10,11... | collective-permute-start | bytes 786440 | tf_op jit(solution)/shard_map/ppermute | solution.py:350
  318.7 45.2 %collective-permute-start.28 = (f32[2,32,1024]{2,1,0:T(8,128)}, f32[2,32,1024]{2,1,0:T(8,128)S(1)}, u32[]{:S(2)}, u32[]{:S(2)}) collective-permute-start(f32[2,32,1024]{2,1,0:T(8,128)} %get-tuple-element.80), channel_id=1, source_target_pairs={{0,2},{1,3},{2,0},{3,1},{4,6},{5,7},{6,4},{7,5},{8,10},{9,11},{10,... | collective-permute-start | bytes 786440 | tf_op jit(solution)/shard_map/ppermute | solution.py:350
  319.8 44.8 %collective-permute-start.29 = (f32[2,32,1024]{2,1,0:T(8,128)}, f32[2,32,1024]{2,1,0:T(8,128)S(1)}, u32[]{:S(2)}, u32[]{:S(2)}) collective-permute-start(f32[2,32,1024]{2,1,0:T(8,128)} %get-tuple-element.81), channel_id=1, source_target_pairs={{0,3},{1,2},{2,1},{3,0},{4,7},{5,6},{6,5},{7,4},{8,11},{9,10},{10,... | collective-permute-start | bytes 786440 | tf_op jit(solution)/shard_map/ppermute | solution.py:350
  375.1 25.8 %all-to-all-start.7 = ((f32[8,2,48,256]{3,2,1,0:T(8,128)}), f32[8,2,48,256]{3,2,1,0:T(8,128)S(1)}, u32[]{:S(2)}, u32[]{:S(2)}) async-start(f32[8,2,48,256]{3,2,1,0:T(8,128)} %bitcast.13), calls=%async_computation.7 | async-start | bytes 1572864 | tf_op jit(solution)/shard_map/all_to_all | solution.py:344
  406.5 55.4 %all-to-all-start.8 = ((f32[8,2,48,256]{3,2,1,0:T(8,128)}), f32[8,2,48,256]{3,2,1,0:T(8,128)S(1)}, u32[]{:S(2)}, u32[]{:S(2)}) async-start(f32[8,2,48,256]{3,2,1,0:T(8,128)} %bitcast.26), calls=%async_computation.8 | async-start | bytes 1572864 | tf_op jit(solution)/shard_map/all_to_all | solution.py:344
  410.7 26.2 %collective-permute-start.25 = (f32[2,64,1024]{2,1,0:T(8,128)}, f32[2,64,1024]{2,1,0:T(8,128)S(1)}, u32[]{:S(2)}, u32[]{:S(2)}) collective-permute-start(f32[2,64,1024]{2,1,0:T(8,128)} %copy-done.39), channel_id=1, source_target_pairs={{0,2},{1,3},{2,0},{3,1},{4,6},{5,7},{6,4},{7,5},{8,10},{9,11},{10,... | collective-permute-start | bytes 1572872 | tf_op jit(solution)/shard_map/ppermute | solution.py:350
  413.7 28.4 %collective-permute-start.30 = (f32[2,32,1024]{2,1,0:T(8,128)}, f32[2,32,1024]{2,1,0:T(8,128)S(1)}, u32[]{:S(2)}, u32[]{:S(2)}) collective-permute-start(f32[2,32,1024]{2,1,0:T(8,128)} %copy-done.49), channel_id=1, source_target_pairs={{0,1},{1,0},{2,3},{3,2},{4,5},{5,4},{6,7},{7,6},{8,9},{9,8},{10,11... | collective-permute-start | bytes 786440 | tf_op jit(solution)/shard_map/ppermute | solution.py:350
  414.2 27.8 %collective-permute-start.31 = (f32[2,32,1024]{2,1,0:T(8,128)}, f32[2,32,1024]{2,1,0:T(8,128)S(1)}, u32[]{:S(2)}, u32[]{:S(2)}) collective-permute-start(f32[2,32,1024]{2,1,0:T(8,128)} %copy-done.48), channel_id=1, source_target_pairs={{0,2},{1,3},{2,0},{3,1},{4,6},{5,7},{6,4},{7,5},{8,10},{9,11},{10,... | collective-permute-start | bytes 786440 | tf_op jit(solution)/shard_map/ppermute | solution.py:350
  (69 other events, 543.8 us)

commit v12 on v11

--- a/solution.py
+++ b/solution.py
@@ -10,6 +10,7 @@
 CHUNKS = (2, 3, 2, 1)
 SETS = ((0,), (1,), (2, 3))
 GROUPS = ((0,), (1,), (2, 3))
+SCATTERED = (0, 1)
 LANES = 128
 VMEM_BYTES = 48 * 1024 * 1024
 
@@ -192,16 +193,26 @@
         both = jnp.dot(split_ref[k], masked_ref[0, k], preferred_element_type=jnp.float32)
         both = both[:tall] + both[tall:]
         total = both if total is None else total + both
-    for e, out_ref in enumerate(out_refs):
-        out_ref[0] = total[e * rows : (e + 1) * rows]
-
-
-def product(place, own, mirrored, masked, start, after):
+    for e in range(sections):
+        part = total[e * rows : (e + 1) * rows]
+        if len(out_refs) == 1:
+            out_refs[0][place_ref[0] ^ e, 0] = part
+        else:
+            out_refs[e][0] = part
+
+
+def product(place, own, mirrored, masked, start, after, stacked):
     sections = len(mirrored)
     pairs, rows, virtuals = mirrored[0].shape
     slots = masked.shape[0]
     deep = virtuals // sections
     wide = min(virtuals, 512)
+    if stacked:
+        blocks = [pl.BlockSpec((sections, 1, rows, wide), lambda s, n, at: (0, s, 0, n))]
+        shapes = [jax.ShapeDtypeStruct((sections, slots, rows, virtuals), jnp.float32)]
+    else:
+        blocks = [pl.BlockSpec((1, rows, wide), lambda s, n, at: (s, 0, n))] * sections
+        shapes = [jax.ShapeDtypeStruct((slots, rows, virtuals), jnp.float32)] * sections
     return call(
         functools.partial(product_kernel, sections),
         "product",
@@ -216,8 +227,8 @@
         ]
         + [whole(mirrored[0].shape)] * sections
         + [pl.BlockSpec((1, pairs, virtuals, wide), lambda s, n, at: (s, 0, 0, n))],
-        [pl.BlockSpec((1, rows, wide), lambda s, n, at: (s, 0, n))] * sections,
-        [jax.ShapeDtypeStruct((slots, rows, virtuals), jnp.float32)] * sections,
+        blocks,
+        shapes,
         (slots, virtuals // wide),
         scratch=[pltpu.VMEM((pairs, 2 * sections * rows, virtuals), jnp.bfloat16)],
         flops=4 * sections * rows * pairs * virtuals * virtuals * slots,
@@ -380,8 +391,11 @@
         return pieces[0], spread(pieces)
 
     def multiply(at, mirrored, after):
-        parts = product(place, amplitudes, mirrored, masked, spans[at][0], after)
-        return parts[0], spread(parts)
+        stacked = at in SCATTERED
+        parts = product(place, amplitudes, mirrored, masked, spans[at][0], after, stacked)
+        if stacked:
+            return parts[0], lax.psum_scatter(parts[0], "ka", scatter_dimension=0, tiled=False)
+        return parts[0], add(place, spread(parts), [])
 
     def send(group):
         return spread(cut(place, [own[at] for at in group], sections, pairs))
@@ -401,23 +415,20 @@
     (second,) = fetch(SETS[1], [first])
     across.append(second([masked]))
     waiting = fetch(SETS[2], [across[1]])
+    own = [None] * len(spans)
     turned, mirrored = turn(0, hop(0), [across[1]])
-    begun, parts = multiply(0, mirrored, [])
+    begun, own[0] = multiply(0, mirrored, [])
     across.append(waiting[0]([begun]))
-    own = [add(place, parts, [])]
     turned, mirrored = turn(1, hop(1), [across[2]])
     turned, later = turn(2, hop(2), [turned])
     across.append(waiting[1]([turned, own[0]]))
-    begun, parts = multiply(1, mirrored, [])
-    own.append(add(place, parts, []))
+    begun, own[1] = multiply(1, mirrored, [])
     crossed = hop(3)
     leading = gather(place, send(GROUPS[0]), [crossed, begun])
     turned, mirrored = turn(3, crossed, [leading])
-    begun, parts = multiply(2, later, [turned])
-    own.append(add(place, parts, []))
+    begun, own[2] = multiply(2, later, [turned])
     delivered = [deliver(meet(leading), [begun])]
-    begun, parts = multiply(3, mirrored, delivered)
-    own.append(add(place, parts, []))
+    begun, own[3] = multiply(3, mirrored, delivered)
     after = [begun]
     for group in GROUPS[1:]:
         met = meet(gather(place, send(group), [delivered[-1], *after]))

time: 522 us -> 518 us (level)
  local copies, waits for them, and re-layouts: 34.9 us -> 21.5 us
  between operations: 0.54 us -> 13.8 us
    all_to_all x8, waiting for transfers between devices: 52.2 us -> 38.7 us  [swap(): return lax.all_to_all(array, axis, split_axis=0, concat_axis=0, tiled=True)]
    unnamed x109 -> x63, local copies, waits for them, and re-layouts: 28 us -> 15.7 us
    ppermute x39 -> x33, waiting for transfers between devices: 189 us -> 199 us  [spread(): lax.ppermute(pieces[e], 'ka', [(q, q ^ e) for q in range(count)])]
    ppermute x39 -> x33, starting transfers between devices: 43.8 us -> 38.9 us  [spread(): lax.ppermute(pieces[e], 'ka', [(q, q ^ e) for q in range(count)])]
    pallas_call x34 -> x32, Pallas kernels: 83.5 us -> 85.7 us  [call(): pl.pallas_call(trimmed, grid_spec=pltpu.PrefetchScalarGridSpec(num_scalar...]
  transfers between devices with their start and end apart: 47 -> 43, of which waited for: 22 -> 26; matrix products, arithmetic and copies ran while one was open for 1% -> 1% of each run, Pallas kernels for 14% -> 15%
where the time goes in v12:
time: 518 us; the launch traced here: 516 us
  waiting for transfers between devices  238 us (46%)
  Pallas kernels  85.7 us (17%)
  blocking collectives  79.3 us (15%)
  starting transfers between devices  73.7 us (14%)
  local copies, waits for them, and re-layouts  21.5 us (4%)
  between operations  13.8 us (3%)
    ppermute x33, waiting for transfers between devices, spread(): lax.ppermute(pieces[e], 'ka', [(q, q ^ e) for q in range(count)])  199 us
    pallas_call x32, Pallas kernels, call(): pl.pallas_call(trimmed, grid_spec=pltpu.PrefetchScalarGridSpec(num_scalar...  85.7 us
    all_to_all x3, blocking collectives, swap(): return lax.all_to_all(array, axis, split_axis=0, concat_axis=0, tiled=True)  79.3 us
    ppermute x33, starting transfers between devices, spread(): lax.ppermute(pieces[e], 'ka', [(q, q ^ e) for q in range(count)])  38.9 us
    all_to_all x8, waiting for transfers between devices, swap(): return lax.all_to_all(array, axis, split_axis=0, concat_axis=0, tiled=True)  38.7 us
    all_to_all x8, starting transfers between devices, swap(): return lax.all_to_all(array, axis, split_axis=0, concat_axis=0, tiled=True)  34.7 us
    unnamed x63, local copies, waits for them, and re-layouts  15.7 us
  transfers between devices with their start and end apart: 43, of which 26 were waited for; matrix products, arithmetic and copies ran while one was open for 1% of the time, Pallas kernels for 15%

profile of v12, /device:TPU:0, one launch (start us, length us, event | category | flops | bytes accessed | tf_op | source)
XLA Modules:
  0.0 515.8 jit_solution(15541102061873719797)
XLA Ops:
  6.5 5.3 %first_flip.1.refs_2_ = f32[4,2,64,1024]{3,2,1,0:T(8,128)S(1)} custom-call(s32[1]{0:T(128)} %bitcast.refs_0_, f32[1,2,1024,1024]{3,2,1,0:T(8,128)} %refs_4_.7), custom_call_target="tpu_custom_call" | custom-call | bytes 4194304 | tf_op jit(solution)/shard_map/first_flip/pallas_call | solution.py:27
  11.8 30.4 %all_to_all.55 = f32[4,2,64,1024]{3,2,1,0:T(8,128)} all-to-all(f32[4,2,64,1024]{3,2,1,0:T(8,128)S(1)} %first_flip.1.refs_2_), channel_id=1, replica_groups=mesh['ia'=8,'ka'=4] {'ka'}, dimensions={0} | all-to-all | bytes 4194304 | tf_op jit(solution)/shard_map/all_to_all | solution.py:355
  42.2 4.9 all-to-all-start.1
  58.5 8.7 %mask.1.refs_5_.refs_9_ = bf16[2,2,1024,1024]{3,2,1,0:T(8,128)(2,1)} custom-call(s32[2,2,8,8]{3,2,1,0:T(8,128)S(1)} %bitcast.31, bf16[1,2,2,1024,1024]{4,3,2,1,0:T(8,128)(2,1)} %refs_1_.19, f32[4,2,64,1024]{3,2,1,0:T(8,128)S(1)} %first_flip.1.refs_2_), custom_call_target="tpu_custom_call" | custom-call | bytes 16777216 | tf_op jit(solution)/shard_map/mask/pallas_call | solution.py:27
  69.5 19.1 %collective-permute-done.1.refs_3_ = f32[2,96,1024]{2,1,0:T(8,128)S(1)} collective-permute-done((f32[2,96,1024]{2,1,0:T(8,128)S(1)}, f32[2,96,1024]{2,1,0:T(8,128)S(1)}, u32[]{:S(2)}, u32[]{:S(2)}) %collective-permute-start.1) | collective-permute-done | bytes 786464 | tf_op jit(solution)/shard_map/ppermute | solution.py:361
  90.3 6.0 %all-to-all-done.1 = f32[8,64,1024]{2,1,0:T(8,128)} async-done(((f32[8,64,1024]{2,1,0:T(8,128)}), f32[8,64,1024]{2,1,0:T(8,128)}, u32[]{:S(2)}, u32[]{:S(2)}) %all-to-all-start.1) | async-done | bytes 2097184 | tf_op jit(solution)/shard_map/all_to_all | solution.py:355
  96.3 4.5 all-to-all-start.2
  106.1 11.3 %collective-permute-done.3.refs_6_ = f32[2,64,1024]{2,1,0:T(8,128)S(1)} collective-permute-done((f32[2,64,1024]{2,1,0:T(8,128)S(1)}, f32[2,64,1024]{2,1,0:T(8,128)S(1)}, u32[]{:S(2)}, u32[]{:S(2)}) %collective-permute-start.3) | collective-permute-done | bytes 524320 | tf_op jit(solution)/shard_map/ppermute | solution.py:361
  117.4 11.3 %collective-permute-done.4.refs_7_ = f32[2,64,1024]{2,1,0:T(8,128)S(1)} collective-permute-done((f32[2,64,1024]{2,1,0:T(8,128)S(1)}, f32[2,64,1024]{2,1,0:T(8,128)S(1)}, u32[]{:S(2)}, u32[]{:S(2)}) %collective-permute-start.4) | collective-permute-done | bytes 524320 | tf_op jit(solution)/shard_map/ppermute | solution.py:361
  128.7 8.4 %product.4.refs_5_ = f32[4,2,64,1024]{3,2,1,0:T(8,128)S(1)} custom-call(s32[1]{0:T(128)} %bitcast.refs_0_, f32[1,2,1024,1024]{3,2,1,0:T(8,128)} %refs_4_.7, f32[1,2,1024,1024]{3,2,1,0:T(8,128)} %refs_4_.7, f32[1,2,1024,1024]{3,2,1,0:T(8,128)} %refs_4_.7, f32[1,2,1024,1024]{3,2,1,0:T(8,128)} %refs_4_.7, f32[2,64,1024]{2,1,0:T(8,128)S(1)} %get-tuple-element.42.refs_5_, ...), custom_call_target="tpu_custom_call" | custom-call | flops 4294967296 | bytes 4194304 | tf_op jit(solution)/shard_map/product/pallas_call | solution.py:27
  149.1 26.3 %collective-permute-done.6.refs_2_ = f32[2,96,1024]{2,1,0:T(8,128)S(1)} collective-permute-done((f32[2,96,1024]{2,1,0:T(8,128)S(1)}, f32[2,96,1024]{2,1,0:T(8,128)S(1)}, u32[]{:S(2)}, u32[]{:S(2)}) %collective-permute-start.6) | collective-permute-done | bytes 786464 | tf_op jit(solution)/shard_map/ppermute | solution.py:361
  177.7 19.1 %collective-permute-done.8.refs_4_ = f32[2,96,1024]{2,1,0:T(8,128)S(1)} collective-permute-done((f32[2,96,1024]{2,1,0:T(8,128)S(1)}, f32[2,96,1024]{2,1,0:T(8,128)S(1)}, u32[]{:S(2)}, u32[]{:S(2)}) %collective-permute-start.8) | collective-permute-done | bytes 786464 | tf_op jit(solution)/shard_map/ppermute | solution.py:361
  208.8 4.7 all-to-all-start.3
  213.5 12.6 %collective-permute-done.9.refs_6_ = f32[2,96,1024]{2,1,0:T(8,128)} collective-permute-done((f32[2,96,1024]{2,1,0:T(8,128)}, f32[2,96,1024]{2,1,0:T(8,128)}, u32[]{:S(2)}, u32[]{:S(2)}) %collective-permute-start.9) | collective-permute-done | bytes 786464 | tf_op jit(solution)/shard_map/ppermute | solution.py:361
  226.1 15.0 %collective-permute-done.10.refs_7_ = f32[2,96,1024]{2,1,0:T(8,128)} collective-permute-done((f32[2,96,1024]{2,1,0:T(8,128)}, f32[2,96,1024]{2,1,0:T(8,128)}, u32[]{:S(2)}, u32[]{:S(2)}) %collective-permute-start.10) | collective-permute-done | bytes 786464 | tf_op jit(solution)/shard_map/ppermute | solution.py:361
  241.1 12.1 %product.5.refs_6_ = f32[4,2,96,1024]{3,2,1,0:T(8,128)} custom-call(s32[1]{0:T(128)} %bitcast.refs_0_, f32[1,2,1024,1024]{3,2,1,0:T(8,128)} %refs_4_.7, f32[1,2,1024,1024]{3,2,1,0:T(8,128)} %refs_4_.7, f32[1,2,1024,1024]{3,2,1,0:T(8,128)} %refs_4_.7, f32[1,2,1024,1024]{3,2,1,0:T(8,128)} %refs_4_.7, f32[2,96,1024]{2,1,0:T(8,128)S(1)} %get-tuple-element.46.refs_5_.refs_2_, ...), custom_call_target="tpu_custom_call" | custom-call | flops 6442450944 | bytes 6291456 | tf_op jit(solution)/shard_map/product/pallas_call | solution.py:27
  253.3 9.2 %all-to-all-done.3 = f32[8,64,1024]{2,1,0:T(8,128)S(1)} async-done(((f32[8,64,1024]{2,1,0:T(8,128)}), f32[8,64,1024]{2,1,0:T(8,128)S(1)}, u32[]{:S(2)}, u32[]{:S(2)}) %all-to-all-start.3) | async-done | bytes 2097184 | tf_op jit(solution)/shard_map/all_to_all | solution.py:355
  270.7 4.4 all-to-all-start.4
  283.1 29.6 %collective-permute-done.15.refs_2_ = f32[2,2,32,256]{3,2,1,0:T(8,128)S(1)} collective-permute-done((f32[2,2,32,256]{3,2,1,0:T(8,128)}, f32[2,2,32,256]{3,2,1,0:T(8,128)S(1)}, u32[]{:S(2)}, u32[]{:S(2)}) %collective-permute-start.15) | collective-permute-done | bytes 131104 | tf_op jit(solution)/shard_map/ppermute | solution.py:361
  314.2 5.1 collective-permute-done.17.refs_4_
  322.5 4.5 all-to-all-start.5
  327.0 8.7 %product.6 = (f32[2,64,1024]{2,1,0:T(8,128)S(1)}, f32[2,64,1024]{2,1,0:T(8,128)S(1)}, f32[2,64,1024]{2,1,0:T(8,128)S(1)}, f32[2,64,1024]{2,1,0:T(8,128)S(1)}) custom-call(s32[1]{0:T(128)} %bitcast.refs_0_, f32[1,2,1024,1024]{3,2,1,0:T(8,128)} %refs_4_.7, f32[1,2,1024,1024]{3,2,1,0:T(8,128)} %refs_4_.7, f32[1,2,1024,1024]{3,2,1,0:T(8,128)} %refs_4_.7, ...), custom_call_target="tpu_custom_call" | custom-call | flops 4294967296 | bytes 4194304 | tf_op jit(solution)/shard_map/product/pallas_call | solution.py:27
  363.3 6.7 %product.7 = (f32[2,32,1024]{2,1,0:T(8,128)S(1)}, f32[2,32,1024]{2,1,0:T(8,128)}, f32[2,32,1024]{2,1,0:T(8,128)}, f32[2,32,1024]{2,1,0:T(8,128)S(1)}) custom-call(s32[1]{0:T(128)} %bitcast.refs_0_, f32[1,2,1024,1024]{3,2,1,0:T(8,128)} %refs_4_.7, f32[1,2,1024,1024]{3,2,1,0:T(8,128)} %refs_4_.7, f32[1,2,1024,1024]{3,2,1,0:T(8,128)} %refs_4_.7, ...), custom_call_target="tpu_custom_call" | custom-call | flops 2147483648 | bytes 2097152 | tf_op jit(solution)/shard_map/product/pallas_call | solution.py:27
  372.1 4.8 all-to-all-start.7
  378.0 19.8 %all-to-all-done.7 = f32[8,2,48,256]{3,2,1,0:T(8,128)S(1)} async-done(((f32[8,2,48,256]{3,2,1,0:T(8,128)}), f32[8,2,48,256]{3,2,1,0:T(8,128)S(1)}, u32[]{:S(2)}, u32[]{:S(2)}) %all-to-all-start.7) | async-done | bytes 786464 | tf_op jit(solution)/shard_map/all_to_all | solution.py:355
  410.7 9.2 %collective-permute-done.18.refs_2_ = f32[2,64,1024]{2,1,0:T(8,128)S(1)} collective-permute-done((f32[2,64,1024]{2,1,0:T(8,128)}, f32[2,64,1024]{2,1,0:T(8,128)S(1)}, u32[]{:S(2)}, u32[]{:S(2)}) %collective-permute-start.18) | collective-permute-done | bytes 524320 | tf_op jit(solution)/shard_map/ppermute | solution.py:361
  421.6 10.1 %collective-permute-done.19.refs_3_ = f32[2,64,1024]{2,1,0:T(8,128)S(1)} collective-permute-done((f32[2,64,1024]{2,1,0:T(8,128)S(1)}, f32[2,64,1024]{2,1,0:T(8,128)S(1)}, u32[]{:S(2)}, u32[]{:S(2)}) %collective-permute-start.19) | collective-permute-done | bytes 524320 | tf_op jit(solution)/shard_map/ppermute | solution.py:361
  431.9 5.0 collective-permute-done.24.refs_2_
  437.0 5.0 collective-permute-done.26.refs_4_
  445.8 4.3 collective-permute-done.30.refs_2_
  454.1 25.4 %all_to_all.56 = f32[8,2,48,256]{3,2,1,0:T(8,128)} all-to-all(f32[8,2,48,256]{3,2,1,0:T(8,128)S(1)} %bitcast.28), channel_id=1, replica_groups=mesh['ia'=8,'ka'=4] {'ia'}, dimensions={0} | all-to-all | bytes 1572864 | tf_op jit(solution)/shard_map/all_to_all | solution.py:355
  483.5 23.4 %all_to_all.57.refs_7_ = f32[8,2,48,256]{3,2,1,0:T(8,128)S(1)} all-to-all(f32[8,2,48,256]{3,2,1,0:T(8,128)S(1)} %bitcast.36), channel_id=1, replica_groups=mesh['ia'=8,'ka'=4] {'ia'}, dimensions={0} | all-to-all | bytes 1572864 | tf_op jit(solution)/shard_map/all_to_all | solution.py:355
  (173 shorter events, 127.0 us)
Async XLA Ops:
  42.2 54.1 %all-to-all-start.1 = ((f32[8,64,1024]{2,1,0:T(8,128)}), f32[8,64,1024]{2,1,0:T(8,128)}, u32[]{:S(2)}, u32[]{:S(2)}) async-start(f32[8,64,1024]{2,1,0:T(8,128)} %bitcast.32), calls=%async_computation.1 | async-start | bytes 4194304 | tf_op jit(solution)/shard_map/all_to_all | solution.py:355
  49.1 20.4 %collective-permute-start = (f32[2,96,1024]{2,1,0:T(8,128)S(1)}, f32[2,96,1024]{2,1,0:T(8,128)S(1)}, u32[]{:S(2)}, u32[]{:S(2)}) collective-permute-start(f32[2,96,1024]{2,1,0:T(8,128)S(1)} %flip.9), channel_id=1, source_target_pairs={{0,1},{1,0},{2,3},{3,2},{4,5},{5,4},{6,7},{7,6},{8,9},{9,8},{10,11... | collective-permute-start | bytes 2359304 | tf_op jit(solution)/shard_map/ppermute | solution.py:361
  51.9 36.6 %collective-permute-start.1 = (f32[2,96,1024]{2,1,0:T(8,128)S(1)}, f32[2,96,1024]{2,1,0:T(8,128)S(1)}, u32[]{:S(2)}, u32[]{:S(2)}) collective-permute-start(f32[2,96,1024]{2,1,0:T(8,128)S(1)} %flip.10), channel_id=1, source_target_pairs={{0,2},{1,3},{2,0},{3,1},{4,6},{5,7},{6,4},{7,5},{8,10},{9,11},{10,... | collective-permute-start | bytes 2359304 | tf_op jit(solution)/shard_map/ppermute | solution.py:361
  54.5 34.0 %collective-permute-start.2 = (f32[2,96,1024]{2,1,0:T(8,128)S(1)}, f32[2,96,1024]{2,1,0:T(8,128)S(1)}, u32[]{:S(2)}, u32[]{:S(2)}) collective-permute-start(f32[2,96,1024]{2,1,0:T(8,128)S(1)} %flip.11), channel_id=1, source_target_pairs={{0,3},{1,2},{2,1},{3,0},{4,7},{5,6},{6,5},{7,4},{8,11},{9,10},{10,... | collective-permute-start | bytes 2359304 | tf_op jit(solution)/shard_map/ppermute | solution.py:361
  96.3 105.5 %all-to-all-start.2 = ((f32[8,96,1024]{2,1,0:T(8,128)}), f32[8,96,1024]{2,1,0:T(8,128)}, u32[]{:S(2)}, u32[]{:S(2)}) async-start(f32[8,96,1024]{2,1,0:T(8,128)} %bitcast.22), calls=%async_computation.2 | async-start | bytes 6291456 | tf_op jit(solution)/shard_map/all_to_all | solution.py:355
  100.8 164.1 %reduce-scatter.7.cloned.1.call-start = ((), (), s32[]{:S(2)}) async-start(), calls=%async_computation.13 | async-start | bytes 2621440
  103.5 25.1 %collective-permute-start.4 = (f32[2,64,1024]{2,1,0:T(8,128)S(1)}, f32[2,64,1024]{2,1,0:T(8,128)S(1)}, u32[]{:S(2)}, u32[]{:S(2)}) collective-permute-start(f32[2,64,1024]{2,1,0:T(8,128)S(1)} %get-tuple-element.44), channel_id=1, source_target_pairs={{0,2},{1,3},{2,0},{3,1},{4,6},{5,7},{6,4},{7,5},{8,10},{9,11},{10,... | collective-permute-start | bytes 1572872 | tf_op jit(solution)/shard_map/ppermute | solution.py:361
  104.1 24.6 %collective-permute-start.5 = (f32[2,64,1024]{2,1,0:T(8,128)S(1)}, f32[2,64,1024]{2,1,0:T(8,128)S(1)}, u32[]{:S(2)}, u32[]{:S(2)}) collective-permute-start(f32[2,64,1024]{2,1,0:T(8,128)S(1)} %get-tuple-element.45), channel_id=1, source_target_pairs={{0,3},{1,2},{2,1},{3,0},{4,7},{5,6},{6,5},{7,4},{8,11},{9,10},{10,... | collective-permute-start | bytes 1572872 | tf_op jit(solution)/shard_map/ppermute | solution.py:361
  143.8 31.6 %collective-permute-start.6 = (f32[2,96,1024]{2,1,0:T(8,128)S(1)}, f32[2,96,1024]{2,1,0:T(8,128)S(1)}, u32[]{:S(2)}, u32[]{:S(2)}) collective-permute-start(f32[2,96,1024]{2,1,0:T(8,128)S(1)} %flip.13), channel_id=1, source_target_pairs={{0,1},{1,0},{2,3},{3,2},{4,5},{5,4},{6,7},{7,6},{8,9},{9,8},{10,11... | collective-permute-start | bytes 2359304 | tf_op jit(solution)/shard_map/ppermute | solution.py:361
  145.0 32.8 %collective-permute-start.7 = (f32[2,96,1024]{2,1,0:T(8,128)S(1)}, f32[2,96,1024]{2,1,0:T(8,128)S(1)}, u32[]{:S(2)}, u32[]{:S(2)}) collective-permute-start(f32[2,96,1024]{2,1,0:T(8,128)S(1)} %flip.14), channel_id=1, source_target_pairs={{0,2},{1,3},{2,0},{3,1},{4,6},{5,7},{6,4},{7,5},{8,10},{9,11},{10,... | collective-permute-start | bytes 2359304 | tf_op jit(solution)/shard_map/ppermute | solution.py:361
  145.9 50.9 %collective-permute-start.8 = (f32[2,96,1024]{2,1,0:T(8,128)S(1)}, f32[2,96,1024]{2,1,0:T(8,128)S(1)}, u32[]{:S(2)}, u32[]{:S(2)}) collective-permute-start(f32[2,96,1024]{2,1,0:T(8,128)S(1)} %flip.15), channel_id=1, source_target_pairs={{0,3},{1,2},{2,1},{3,0},{4,7},{5,6},{6,5},{7,4},{8,11},{9,10},{10,... | collective-permute-start | bytes 2359304 | tf_op jit(solution)/shard_map/ppermute | solution.py:361
  205.3 20.8 %collective-permute-start.9 = (f32[2,96,1024]{2,1,0:T(8,128)}, f32[2,96,1024]{2,1,0:T(8,128)}, u32[]{:S(2)}, u32[]{:S(2)}) collective-permute-start(f32[2,96,1024]{2,1,0:T(8,128)} %get-tuple-element.47), channel_id=1, source_target_pairs={{0,1},{1,0},{2,3},{3,2},{4,5},{5,4},{6,7},{7,6},{8,9},{9,8},{10,11... | collective-permute-start | bytes 2359304 | tf_op jit(solution)/shard_map/ppermute | solution.py:361
  206.4 34.8 %collective-permute-start.10 = (f32[2,96,1024]{2,1,0:T(8,128)}, f32[2,96,1024]{2,1,0:T(8,128)}, u32[]{:S(2)}, u32[]{:S(2)}) collective-permute-start(f32[2,96,1024]{2,1,0:T(8,128)} %get-tuple-element.48), channel_id=1, source_target_pairs={{0,2},{1,3},{2,0},{3,1},{4,6},{5,7},{6,4},{7,5},{8,10},{9,11},{10,... | collective-permute-start | bytes 2359304 | tf_op jit(solution)/shard_map/ppermute | solution.py:361
  206.9 34.2 %collective-permute-start.11 = (f32[2,96,1024]{2,1,0:T(8,128)}, f32[2,96,1024]{2,1,0:T(8,128)}, u32[]{:S(2)}, u32[]{:S(2)}) collective-permute-start(f32[2,96,1024]{2,1,0:T(8,128)} %get-tuple-element.49), channel_id=1, source_target_pairs={{0,3},{1,2},{2,1},{3,0},{4,7},{5,6},{6,5},{7,4},{8,11},{9,10},{10,... | collective-permute-start | bytes 2359304 | tf_op jit(solution)/shard_map/ppermute | solution.py:361
  208.8 53.7 %all-to-all-start.3 = ((f32[8,64,1024]{2,1,0:T(8,128)}), f32[8,64,1024]{2,1,0:T(8,128)S(1)}, u32[]{:S(2)}, u32[]{:S(2)}) async-start(f32[8,64,1024]{2,1,0:T(8,128)} %bitcast.9), calls=%async_computation.3 | async-start | bytes 4194304 | tf_op jit(solution)/shard_map/all_to_all | solution.py:355
  213.4 137.5 %reduce-scatter.9.cloned.1.call-start = ((), (), s32[]{:S(2)}) async-start(), calls=%async_computation.14 | async-start | bytes 3932160
  270.7 48.6 %all-to-all-start.4 = ((f32[8,32,1024]{2,1,0:T(8,128)}), f32[8,32,1024]{2,1,0:T(8,128)}, u32[]{:S(2)}, u32[]{:S(2)}) async-start(f32[8,32,1024]{2,1,0:T(8,128)} %bitcast.11), calls=%async_computation.4 | async-start | bytes 2097152 | tf_op jit(solution)/shard_map/all_to_all | solution.py:355
  275.1 51.9 %collective-permute-start.12 = (f32[2,64,1024]{2,1,0:T(8,128)}, f32[2,64,1024]{2,1,0:T(8,128)}, u32[]{:S(2)}, u32[]{:S(2)}) collective-permute-start(f32[2,64,1024]{2,1,0:T(8,128)} %get-tuple-element.51), channel_id=1, source_target_pairs={{0,1},{1,0},{2,3},{3,2},{4,5},{5,4},{6,7},{7,6},{8,9},{9,8},{10,11... | collective-permute-start | bytes 1572872 | tf_op jit(solution)/shard_map/ppermute | solution.py:361
  276.1 50.9 %collective-permute-start.13 = (f32[2,64,1024]{2,1,0:T(8,128)}, f32[2,64,1024]{2,1,0:T(8,128)}, u32[]{:S(2)}, u32[]{:S(2)}) collective-permute-start(f32[2,64,1024]{2,1,0:T(8,128)} %get-tuple-element.52), channel_id=1, source_target_pairs={{0,2},{1,3},{2,0},{3,1},{4,6},{5,7},{6,4},{7,5},{8,10},{9,11},{10,... | collective-permute-start | bytes 1572872 | tf_op jit(solution)/shard_map/ppermute | solution.py:361
  276.6 50.4 %collective-permute-start.14 = (f32[2,64,1024]{2,1,0:T(8,128)}, f32[2,64,1024]{2,1,0:T(8,128)}, u32[]{:S(2)}, u32[]{:S(2)}) collective-permute-start(f32[2,64,1024]{2,1,0:T(8,128)} %get-tuple-element.53), channel_id=1, source_target_pairs={{0,3},{1,2},{2,1},{3,0},{4,7},{5,6},{6,5},{7,4},{8,11},{9,10},{10,... | collective-permute-start | bytes 1572872 | tf_op jit(solution)/shard_map/ppermute | solution.py:361
  280.7 32.0 %collective-permute-start.15 = (f32[2,2,32,256]{3,2,1,0:T(8,128)}, f32[2,2,32,256]{3,2,1,0:T(8,128)S(1)}, u32[]{:S(2)}, u32[]{:S(2)}) collective-permute-start(f32[2,2,32,256]{3,2,1,0:T(8,128)} %get-tuple-element.55), channel_id=1, source_target_pairs={{0,1},{1,0},{2,3},{3,2},{4,5},{5,4},{6,7},{7,6},{8,9},{9,8},{10,11... | collective-permute-start | bytes 393224 | tf_op jit(solution)/shard_map/ppermute | solution.py:361
  282.5 31.7 %collective-permute-start.16 = (f32[2,2,32,256]{3,2,1,0:T(8,128)}, f32[2,2,32,256]{3,2,1,0:T(8,128)S(1)}, u32[]{:S(2)}, u32[]{:S(2)}) collective-permute-start(f32[2,2,32,256]{3,2,1,0:T(8,128)} %copy-done.29), channel_id=1, source_target_pairs={{0,2},{1,3},{2,0},{3,1},{4,6},{5,7},{6,4},{7,5},{8,10},{9,11},{10,... | collective-permute-start | bytes 393224 | tf_op jit(solution)/shard_map/ppermute | solution.py:361
  322.5 19.9 %all-to-all-start.5 = ((f32[8,2,32,256]{3,2,1,0:T(8,128)}), f32[8,2,32,256]{3,2,1,0:T(8,128)S(1)}, u32[]{:S(2)}, u32[]{:S(2)}) async-start(f32[8,2,32,256]{3,2,1,0:T(8,128)} %bitcast.27), calls=%async_computation.5 | async-start | bytes 1048576 | tf_op jit(solution)/shard_map/all_to_all | solution.py:355
  343.8 19.4 %all-to-all-start.6 = ((f32[8,2,32,256]{3,2,1,0:T(8,128)}), f32[8,2,32,256]{3,2,1,0:T(8,128)S(1)}, u32[]{:S(2)}, u32[]{:S(2)}) async-start(f32[8,2,32,256]{3,2,1,0:T(8,128)} %broadcast_select_fusion.2), calls=%async_computation.6 | async-start | bytes 1048576 | tf_op jit(solution)/shard_map/all_to_all | solution.py:355
  352.9 17.8 %collective-permute-start.27 = (f32[2,2,48,256]{3,2,1,0:T(8,128)}, f32[2,2,48,256]{3,2,1,0:T(8,128)S(1)}, u32[]{:S(2)}, u32[]{:S(2)}) collective-permute-start(f32[2,2,48,256]{3,2,1,0:T(8,128)} %get-tuple-element.71), channel_id=1, source_target_pairs={{0,1},{1,0},{2,3},{3,2},{4,5},{5,4},{6,7},{7,6},{8,9},{9,8},{10,11... | collective-permute-start | bytes 589832 | tf_op jit(solution)/shard_map/ppermute | solution.py:361
  372.1 25.8 %all-to-all-start.7 = ((f32[8,2,48,256]{3,2,1,0:T(8,128)}), f32[8,2,48,256]{3,2,1,0:T(8,128)S(1)}, u32[]{:S(2)}, u32[]{:S(2)}) async-start(f32[8,2,48,256]{3,2,1,0:T(8,128)} %bitcast.16), calls=%async_computation.7 | async-start | bytes 1572864 | tf_op jit(solution)/shard_map/all_to_all | solution.py:355
  401.4 52.7 %all-to-all-start.8 = ((f32[8,2,48,256]{3,2,1,0:T(8,128)}), f32[8,2,48,256]{3,2,1,0:T(8,128)S(1)}, u32[]{:S(2)}, u32[]{:S(2)}) async-start(f32[8,2,48,256]{3,2,1,0:T(8,128)} %bitcast.33), calls=%async_computation.8 | async-start | bytes 1572864 | tf_op jit(solution)/shard_map/all_to_all | solution.py:355
  405.7 26.0 %collective-permute-start.19 = (f32[2,64,1024]{2,1,0:T(8,128)S(1)}, f32[2,64,1024]{2,1,0:T(8,128)S(1)}, u32[]{:S(2)}, u32[]{:S(2)}) collective-permute-start(f32[2,64,1024]{2,1,0:T(8,128)S(1)} %copy-done.25), channel_id=1, source_target_pairs={{0,2},{1,3},{2,0},{3,1},{4,6},{5,7},{6,4},{7,5},{8,10},{9,11},{10,... | collective-permute-start | bytes 1572872 | tf_op jit(solution)/shard_map/ppermute | solution.py:361
  407.3 24.5 %collective-permute-start.20 = (f32[2,64,1024]{2,1,0:T(8,128)S(1)}, f32[2,64,1024]{2,1,0:T(8,128)S(1)}, u32[]{:S(2)}, u32[]{:S(2)}) collective-permute-start(f32[2,64,1024]{2,1,0:T(8,128)S(1)} %copy-done.23), channel_id=1, source_target_pairs={{0,3},{1,2},{2,1},{3,0},{4,7},{5,6},{6,5},{7,4},{8,11},{9,10},{10,... | collective-permute-start | bytes 1572872 | tf_op jit(solution)/shard_map/ppermute | solution.py:361
  408.5 28.4 %collective-permute-start.24 = (f32[2,32,1024]{2,1,0:T(8,128)}, f32[2,32,1024]{2,1,0:T(8,128)S(1)}, u32[]{:S(2)}, u32[]{:S(2)}) collective-permute-start(f32[2,32,1024]{2,1,0:T(8,128)} %get-tuple-element.67), channel_id=1, source_target_pairs={{0,1},{1,0},{2,3},{3,2},{4,5},{5,4},{6,7},{7,6},{8,9},{9,8},{10,11... | collective-permute-start | bytes 786440 | tf_op jit(solution)/shard_map/ppermute | solution.py:361
  409.2 27.8 %collective-permute-start.25 = (f32[2,32,1024]{2,1,0:T(8,128)}, f32[2,32,1024]{2,1,0:T(8,128)S(1)}, u32[]{:S(2)}, u32[]{:S(2)}) collective-permute-start(f32[2,32,1024]{2,1,0:T(8,128)} %get-tuple-element.68), channel_id=1, source_target_pairs={{0,2},{1,3},{2,0},{3,1},{4,6},{5,7},{6,4},{7,5},{8,10},{9,11},{10,... | collective-permute-start | bytes 786440 | tf_op jit(solution)/shard_map/ppermute | solution.py:361
  420.0 22.1 %collective-permute-start.26 = (f32[2,32,1024]{2,1,0:T(8,128)}, f32[2,32,1024]{2,1,0:T(8,128)S(1)}, u32[]{:S(2)}, u32[]{:S(2)}) collective-permute-start(f32[2,32,1024]{2,1,0:T(8,128)} %copy-done.27), channel_id=1, source_target_pairs={{0,3},{1,2},{2,1},{3,0},{4,7},{5,6},{6,5},{7,4},{8,11},{9,10},{10,... | collective-permute-start | bytes 786440 | tf_op jit(solution)/shard_map/ppermute | solution.py:361
  (42 other events, 360.1 us)
Sparse Core Ops, SparseCore 0:
  138.5 57.2 reduce-scatter.6
  253.4 60.5 reduce-scatter.8

commit v13 on v10

--- a/solution.py
+++ b/solution.py
@@ -173,7 +173,7 @@
 
 def product_kernel(sections, place_ref, *refs):
     own_refs, mirrored_refs, refs = refs[:sections], refs[sections : 2 * sections], refs[2 * sections :]
-    masked_ref, out_refs, split_ref = refs[0], refs[1:-1], refs[-1]
+    masked_ref, out_ref, split_ref = refs
     pairs, rows, _ = mirrored_refs[0].shape
     tall = sections * rows
 
@@ -192,8 +192,8 @@
         both = jnp.dot(split_ref[k], masked_ref[0, k], preferred_element_type=jnp.float32)
         both = both[:tall] + both[tall:]
         total = both if total is None else total + both
-    for e, out_ref in enumerate(out_refs):
-        out_ref[0] = total[e * rows : (e + 1) * rows]
+    for e in range(sections):
+        out_ref[place_ref[0] ^ e, 0] = total[e * rows : (e + 1) * rows]
 
 
 def product(place, own, mirrored, masked, start, after):
@@ -216,31 +216,11 @@
         ]
         + [whole(mirrored[0].shape)] * sections
         + [pl.BlockSpec((1, pairs, virtuals, wide), lambda s, n, at: (s, 0, 0, n))],
-        [pl.BlockSpec((1, rows, wide), lambda s, n, at: (s, 0, n))] * sections,
-        [jax.ShapeDtypeStruct((slots, rows, virtuals), jnp.float32)] * sections,
+        pl.BlockSpec((sections, 1, rows, wide), lambda s, n, at: (0, s, 0, n)),
+        jax.ShapeDtypeStruct((sections, slots, rows, virtuals), jnp.float32),
         (slots, virtuals // wide),
         scratch=[pltpu.VMEM((pairs, 2 * sections * rows, virtuals), jnp.bfloat16)],
         flops=4 * sections * rows * pairs * virtuals * virtuals * slots,
-        after=after,
-    )
-
-
-def add_kernel(place_ref, *refs):
-    refs[-1][...] = sum((part[...] for part in refs[1:-1]), refs[0][...])
-
-
-def add(place, parts, after):
-    slots, rows, virtuals = parts[0].shape
-    block = pl.BlockSpec((1, rows, virtuals), lambda s, at: (s, 0, 0))
-    return call(
-        add_kernel,
-        "add",
-        place,
-        parts,
-        [block] * len(parts),
-        block,
-        jax.ShapeDtypeStruct(parts[0].shape, jnp.float32),
-        (slots,),
         after=after,
     )
 
@@ -346,10 +326,10 @@
 
     def fetch(chunks, after):
         start, rows = spans[chunks[0]][0], sum(sizes[at] for at in chunks)
-        pieces = [flip(place, amplitudes, sections, e, start, rows, after) for e in range(sections)]
-        pieces = spread(pieces)
-        return [
-            functools.partial(part, place, pieces, spans[at][0] - start, sizes[at]) for at in chunks
+        sent = [flip(place, amplitudes, sections, e, start, rows, after) for e in range(sections)]
+        met = spread(sent)
+        return sent, [
+            functools.partial(part, place, met, spans[at][0] - start, sizes[at]) for at in chunks
         ]
 
     def hop(at):
@@ -362,7 +342,7 @@
 
     def multiply(at, mirrored, after):
         parts = product(place, amplitudes, mirrored, masked, spans[at][0], after)
-        return parts[0], spread(parts)
+        return parts, lax.psum_scatter(parts, "ka", scatter_dimension=0, tiled=False)
 
     def send(group):
         return spread(cut(place, [own[at] for at in group], sections, pairs))
@@ -378,30 +358,29 @@
     first = first_flip(place, amplitudes, sections, sizes[0])
     masked = mask_blocks(integrals, tile_mask, [first])
     across = [swap(first, "ka")]
-    (second,) = fetch(SETS[1], [first])
+    _, (second,) = fetch(SETS[1], [first])
     across.append(second([masked]))
-    waiting = fetch(SETS[2], [across[1]])
-    turned, mirrored = turn(0, hop(0), [across[1]])
-    begun, parts = multiply(0, mirrored, [])
-    across.append(waiting[0]([begun]))
-    turned, mirrored = turn(1, hop(1), [across[2]])
+    sent, (third, fourth) = fetch(SETS[2], [masked])
+    own = [None] * len(spans)
+    turned, mirrored = turn(0, hop(0), [across[1], *sent])
+    across.append(third([]))
+    begun, own[0] = multiply(0, mirrored, [across[2]])
+    turned, mirrored = turn(1, hop(1), [begun])
     turned, later = turn(2, hop(2), [turned])
-    across.append(waiting[1]([turned]))
-    own = [add(place, parts, [turned])]
-    begun, parts = multiply(1, mirrored, [turned])
+    leading = send(GROUPS[0])
+    across.append(fourth([turned, *leading]))
+    begun, own[1] = multiply(1, mirrored, [turned])
     crossed = hop(3)
-    leading = gather(place, send(GROUPS[0]), [crossed])
-    turned, mirrored = turn(3, crossed, [begun, leading])
-    own.append(add(place, parts, []))
+    leading = gather(place, leading, [crossed, begun])
+    turned, mirrored = turn(3, crossed, [leading])
     met = meet(leading)
-    begun, parts = multiply(2, later, [turned, met])
-    own.append(add(place, parts, []))
-    _, parts = multiply(3, mirrored, [begun])
-    own.append(add(place, parts, []))
-
+    begun, own[2] = multiply(2, later, [turned, met])
     delivered = [deliver(met)]
+    begun, own[3] = multiply(3, mirrored, [begun, *delivered])
+
     for group in GROUPS[1:]:
-        delivered.append(deliver(meet(gather(place, send(group), [delivered[-1]]))))
+        met = meet(gather(place, send(group), [delivered[-1]]))
+        delivered.append(deliver(met))
     return finish(place, spans, GROUPS, own, delivered)
 
 

time: 529 us -> 499 us (0.943)
  waiting for transfers between devices: 257 us -> 211 us
  blocking collectives: 79.3 us -> 111 us
  starting transfers between devices: 79 us -> 58.8 us
  between operations: 0.5 us -> 13.5 us
  local copies, waits for them, and re-layouts: 26.5 us -> 16.4 us
    ppermute x39 -> x27, waiting for transfers between devices: 185 us -> 95.2 us  [spread(): lax.ppermute(pieces[e], 'ka', [(q, q ^ e) for q in range(count)])]
    all_to_all x3 -> x4, blocking collectives: 79.3 us -> 111 us  [swap(): return lax.all_to_all(array, axis, split_axis=0, concat_axis=0, tiled=True)]
    all_to_all x8 -> x7, waiting for transfers between devices: 71.4 us -> 95.4 us  [swap(): return lax.all_to_all(array, axis, split_axis=0, concat_axis=0, tiled=True)]
    unnamed x0 -> x8, waiting for transfers between devices: none -> 20.8 us
    ppermute x39 -> x27, starting transfers between devices: 44.3 us -> 31 us  [spread(): lax.ppermute(pieces[e], 'ka', [(q, q ^ e) for q in range(count)])]
    unnamed x71 -> x49, local copies, waits for them, and re-layouts: 20.7 us -> 11.4 us
    all_to_all x8 -> x7, starting transfers between devices: 34.7 us -> 27.6 us  [swap(): return lax.all_to_all(array, axis, split_axis=0, concat_axis=0, tiled=True)]
    pallas_call x32 -> x28, Pallas kernels: 80.5 us -> 82.9 us  [call(): pl.pallas_call(trimmed, grid_spec=pltpu.PrefetchScalarGridSpec(num_scalar...]
  transfers between devices with their start and end apart: 47 -> 38, of which waited for: 22 -> 22; matrix products, arithmetic and copies ran while one was open for 1% -> 1% of each run, Pallas kernels for 13% -> 15%
where the time goes in v13:
time: 499 us; the launch traced here: 497 us
  waiting for transfers between devices  211 us (42%)
  blocking collectives  111 us (22%)
  Pallas kernels  82.9 us (17%)
  starting transfers between devices  58.8 us (12%)
  local copies, waits for them, and re-layouts  16.4 us (3%)
  between operations  13.5 us (3%)
    all_to_all x4, blocking collectives, swap(): return lax.all_to_all(array, axis, split_axis=0, concat_axis=0, tiled=True)  111 us
    all_to_all x7, waiting for transfers between devices, swap(): return lax.all_to_all(array, axis, split_axis=0, concat_axis=0, tiled=True)  95.4 us
    ppermute x27, waiting for transfers between devices, spread(): lax.ppermute(pieces[e], 'ka', [(q, q ^ e) for q in range(count)])  95.2 us
    pallas_call x28, Pallas kernels, call(): pl.pallas_call(trimmed, grid_spec=pltpu.PrefetchScalarGridSpec(num_scalar...  82.9 us
    ppermute x27, starting transfers between devices, spread(): lax.ppermute(pieces[e], 'ka', [(q, q ^ e) for q in range(count)])  31 us
    all_to_all x7, starting transfers between devices, swap(): return lax.all_to_all(array, axis, split_axis=0, concat_axis=0, tiled=True)  27.6 us
    unnamed x8, waiting for transfers between devices  20.8 us
    unnamed x49, local copies, waits for them, and re-layouts  11.4 us
  transfers between devices with their start and end apart: 38, of which 22 were waited for; matrix products, arithmetic and copies ran while one was open for 1% of the time, Pallas kernels for 15%

profile of v13, /device:TPU:0, one launch (start us, length us, event | category | flops | bytes accessed | tf_op | source)
XLA Modules:
  0.0 496.9 jit_solution(9714002213933781177)
XLA Ops:
  6.5 5.3 %first_flip.1.refs_2_ = f32[4,2,64,1024]{3,2,1,0:T(8,128)S(1)} custom-call(s32[1]{0:T(128)} %bitcast.refs_0_, f32[1,2,1024,1024]{3,2,1,0:T(8,128)} %refs_4_.7), custom_call_target="tpu_custom_call" | custom-call | bytes 4194304 | tf_op jit(solution)/shard_map/first_flip/pallas_call | solution.py:26
  11.8 30.4 %all_to_all.55 = f32[4,2,64,1024]{3,2,1,0:T(8,128)} all-to-all(f32[4,2,64,1024]{3,2,1,0:T(8,128)S(1)} %first_flip.1.refs_2_), channel_id=1, replica_groups=mesh['ia'=8,'ka'=4] {'ka'}, dimensions={0} | all-to-all | bytes 4194304 | tf_op jit(solution)/shard_map/all_to_all | solution.py:305
  42.2 4.9 all-to-all-start.1
  58.5 8.7 %mask.1.refs_5_.refs_2_.refs_9_ = bf16[2,2,1024,1024]{3,2,1,0:T(8,128)(2,1)} custom-call(s32[2,2,8,8]{3,2,1,0:T(8,128)S(1)} %bitcast.40, bf16[1,2,2,1024,1024]{4,3,2,1,0:T(8,128)(2,1)} %refs_1_.19, f32[4,2,64,1024]{3,2,1,0:T(8,128)S(1)} %first_flip.1.refs_2_), custom_call_target="tpu_custom_call" | custom-call | bytes 16777216 | tf_op jit(solution)/shard_map/mask/pallas_call | solution.py:26
  69.5 19.1 %collective-permute-done.1.refs_3_ = f32[2,96,1024]{2,1,0:T(8,128)S(1)} collective-permute-done((f32[2,96,1024]{2,1,0:T(8,128)S(1)}, f32[2,96,1024]{2,1,0:T(8,128)S(1)}, u32[]{:S(2)}, u32[]{:S(2)}) %collective-permute-start.1) | collective-permute-done | bytes 786464 | tf_op jit(solution)/shard_map/ppermute | solution.py:311
  90.3 6.0 %all-to-all-done.1 = f32[8,64,1024]{2,1,0:T(8,128)} async-done(((f32[8,64,1024]{2,1,0:T(8,128)}), f32[8,64,1024]{2,1,0:T(8,128)}, u32[]{:S(2)}, u32[]{:S(2)}) %all-to-all-start.1) | async-done | bytes 2097184 | tf_op jit(solution)/shard_map/all_to_all | solution.py:305
  96.3 4.5 all-to-all-start.2
  116.2 6.8 %collective-permute-done.6.refs_2_ = f32[2,96,1024]{2,1,0:T(8,128)S(1)} collective-permute-done((f32[2,96,1024]{2,1,0:T(8,128)S(1)}, f32[2,96,1024]{2,1,0:T(8,128)S(1)}, u32[]{:S(2)}, u32[]{:S(2)}) %collective-permute-start.6) | collective-permute-done | bytes 786464 | tf_op jit(solution)/shard_map/ppermute | solution.py:311
  123.9 18.7 %collective-permute-done.7.refs_3_ = f32[2,96,1024]{2,1,0:T(8,128)S(1)} collective-permute-done((f32[2,96,1024]{2,1,0:T(8,128)S(1)}, f32[2,96,1024]{2,1,0:T(8,128)S(1)}, u32[]{:S(2)}, u32[]{:S(2)}) %collective-permute-start.7) | collective-permute-done | bytes 786464 | tf_op jit(solution)/shard_map/ppermute | solution.py:311
  145.8 26.5 %all-to-all-done.2 = f32[8,96,1024]{2,1,0:T(8,128)} async-done(((f32[8,96,1024]{2,1,0:T(8,128)}), f32[8,96,1024]{2,1,0:T(8,128)}, u32[]{:S(2)}, u32[]{:S(2)}) %all-to-all-start.2) | async-done | bytes 3145760 | tf_op jit(solution)/shard_map/all_to_all | solution.py:305
  172.3 3.6 all-to-all-start.3
  176.0 9.6 %product.4.refs_2_ = f32[4,2,64,1024]{3,2,1,0:T(8,128)} custom-call(s32[1]{0:T(128)} %bitcast.refs_0_, f32[1,2,1024,1024]{3,2,1,0:T(8,128)} %refs_4_.7, f32[1,2,1024,1024]{3,2,1,0:T(8,128)} %refs_4_.7, f32[1,2,1024,1024]{3,2,1,0:T(8,128)} %refs_4_.7, f32[1,2,1024,1024]{3,2,1,0:T(8,128)} %refs_4_.7, f32[2,64,1024]{2,1,0:T(8,128)S(1)} %get-tuple-element.34.refs_5_, ...), custom_call_target="tpu_custom_call" | custom-call | flops 4294967296 | bytes 4194304 | tf_op jit(solution)/shard_map/product/pallas_call | solution.py:26
  185.6 3.5 scatter.5
  193.5 31.4 %all-to-all-done.3 = f32[8,64,1024]{2,1,0:T(8,128)S(1)} async-done(((f32[8,64,1024]{2,1,0:T(8,128)}), f32[8,64,1024]{2,1,0:T(8,128)S(1)}, u32[]{:S(2)}, u32[]{:S(2)}) %all-to-all-start.3) | async-done | bytes 2097184 | tf_op jit(solution)/shard_map/all_to_all | solution.py:305
  227.3 16.9 %collective-permute-done.11.refs_8_ = f32[2,96,1024]{2,1,0:T(8,128)} collective-permute-done((f32[2,96,1024]{2,1,0:T(8,128)}, f32[2,96,1024]{2,1,0:T(8,128)}, u32[]{:S(2)}, u32[]{:S(2)}) %collective-permute-start.11) | collective-permute-done | bytes 786464 | tf_op jit(solution)/shard_map/ppermute | solution.py:311
  244.2 12.2 %product.5.refs_6_ = f32[4,2,96,1024]{3,2,1,0:T(8,128)} custom-call(s32[1]{0:T(128)} %bitcast.refs_0_, f32[1,2,1024,1024]{3,2,1,0:T(8,128)} %refs_4_.7, f32[1,2,1024,1024]{3,2,1,0:T(8,128)} %refs_4_.7, f32[1,2,1024,1024]{3,2,1,0:T(8,128)} %refs_4_.7, f32[1,2,1024,1024]{3,2,1,0:T(8,128)} %refs_4_.7, f32[2,96,1024]{2,1,0:T(8,128)S(1)} %copy-done.15, ...), custom_call_target="tpu_custom_call" | custom-call | flops 6442450944 | bytes 6291456 | tf_op jit(solution)/shard_map/product/pallas_call | solution.py:26
  269.4 31.4 %all_to_all.56 = f32[8,32,1024]{2,1,0:T(8,128)S(1)} all-to-all(f32[8,32,1024]{2,1,0:T(8,128)S(1)} %bitcast.30), channel_id=1, replica_groups=mesh['ia'=8,'ka'=4] {'ia'}, dimensions={0} | all-to-all | bytes 2097152 | tf_op jit(solution)/shard_map/all_to_all | solution.py:305
  301.9 3.5 all-to-all-start.5
  310.1 10.7 %all-to-all-done.5.refs_11_ = f32[8,2,32,256]{3,2,1,0:T(8,128)S(1)} async-done(((f32[8,2,32,256]{3,2,1,0:T(8,128)}), f32[8,2,32,256]{3,2,1,0:T(8,128)S(1)}, u32[]{:S(2)}, u32[]{:S(2)}) %all-to-all-start.5) | async-done | bytes 524320 | tf_op jit(solution)/shard_map/all_to_all | solution.py:305
  322.2 3.5 all-to-all-start.6
  334.3 9.4 %product.6.refs_10_ = f32[4,2,64,1024]{3,2,1,0:T(8,128)} custom-call(s32[1]{0:T(128)} %bitcast.refs_0_, f32[1,2,1024,1024]{3,2,1,0:T(8,128)} %refs_4_.7, f32[1,2,1024,1024]{3,2,1,0:T(8,128)} %refs_4_.7, f32[1,2,1024,1024]{3,2,1,0:T(8,128)} %refs_4_.7, f32[1,2,1024,1024]{3,2,1,0:T(8,128)} %refs_4_.7, f32[2,64,1024]{2,1,0:T(8,128)S(1)} %copy-done.7, ...), custom_call_target="tpu_custom_call" | custom-call | flops 4294967296 | bytes 4194304 | tf_op jit(solution)/shard_map/product/pallas_call | solution.py:26
  345.1 6.9 %product.7 = f32[4,2,32,1024]{3,2,1,0:T(8,128)} custom-call(s32[1]{0:T(128)} %bitcast.refs_0_, f32[1,2,1024,1024]{3,2,1,0:T(8,128)} %refs_4_.7, f32[1,2,1024,1024]{3,2,1,0:T(8,128)} %refs_4_.7, f32[1,2,1024,1024]{3,2,1,0:T(8,128)} %refs_4_.7, f32[1,2,1024,1024]{3,2,1,0:T(8,128)} %refs_4_.7, f32[2,32,1024]{2,1,0:T(8,128)S(1)} %get-tuple-element.50.refs_10_.refs_5_, ...), custom_call_target="tpu_custom_call" | custom-call | flops 2147483648 | bytes 2097152 | tf_op jit(solution)/shard_map/product/pallas_call | solution.py:26
  357.4 4.9 collective-permute-done.21.refs_2_
  362.3 4.5 collective-permute-done.22.refs_3_
  370.8 4.2 all-to-all-start.7
  375.1 20.9 %all-to-all-done.7 = f32[8,2,48,256]{3,2,1,0:T(8,128)S(1)} async-done(((f32[8,2,48,256]{3,2,1,0:T(8,128)}), f32[8,2,48,256]{3,2,1,0:T(8,128)S(1)}, u32[]{:S(2)}, u32[]{:S(2)}) %all-to-all-start.7) | async-done | bytes 786464 | tf_op jit(solution)/shard_map/all_to_all | solution.py:305
  397.5 3.5 all-to-all-start.8
  401.1 20.2 %reduce-scatter.17.cloned.1.call-done = f32[1,2,64,1024]{3,2,1,0:T(8,128)} async-done(((f32[4,2,64,1024]{3,2,1,0:T(8,128)}), f32[1,2,64,1024]{3,2,1,0:T(8,128)}) %reduce-scatter.17.cloned.1.call-update) | async-done | bytes 524304
  426.9 4.3 collective-permute-done.24.refs_2_
  431.2 4.2 collective-permute-done.25.refs_3_
  435.5 25.5 %all_to_all.57 = f32[8,2,48,256]{3,2,1,0:T(8,128)} all-to-all(f32[8,2,48,256]{3,2,1,0:T(8,128)S(1)} %bitcast.31), channel_id=1, replica_groups=mesh['ia'=8,'ka'=4] {'ia'}, dimensions={0} | all-to-all | bytes 1572864 | tf_op jit(solution)/shard_map/all_to_all | solution.py:305
  465.0 23.4 %all_to_all.58.refs_7_ = f32[8,2,48,256]{3,2,1,0:T(8,128)S(1)} all-to-all(f32[8,2,48,256]{3,2,1,0:T(8,128)S(1)} %bitcast.45), channel_id=1, replica_groups=mesh['ia'=8,'ka'=4] {'ia'}, dimensions={0} | all-to-all | bytes 1572864 | tf_op jit(solution)/shard_map/all_to_all | solution.py:305
  (147 shorter events, 94.4 us)
Async XLA Ops:
  42.2 54.1 %all-to-all-start.1 = ((f32[8,64,1024]{2,1,0:T(8,128)}), f32[8,64,1024]{2,1,0:T(8,128)}, u32[]{:S(2)}, u32[]{:S(2)}) async-start(f32[8,64,1024]{2,1,0:T(8,128)} %bitcast.42), calls=%async_computation.1 | async-start | bytes 4194304 | tf_op jit(solution)/shard_map/all_to_all | solution.py:305
  49.1 20.4 %collective-permute-start = (f32[2,96,1024]{2,1,0:T(8,128)S(1)}, f32[2,96,1024]{2,1,0:T(8,128)S(1)}, u32[]{:S(2)}, u32[]{:S(2)}) collective-permute-start(f32[2,96,1024]{2,1,0:T(8,128)S(1)} %flip.9), channel_id=1, source_target_pairs={{0,1},{1,0},{2,3},{3,2},{4,5},{5,4},{6,7},{7,6},{8,9},{9,8},{10,11... | collective-permute-start | bytes 2359304 | tf_op jit(solution)/shard_map/ppermute | solution.py:311
  51.9 36.6 %collective-permute-start.1 = (f32[2,96,1024]{2,1,0:T(8,128)S(1)}, f32[2,96,1024]{2,1,0:T(8,128)S(1)}, u32[]{:S(2)}, u32[]{:S(2)}) collective-permute-start(f32[2,96,1024]{2,1,0:T(8,128)S(1)} %flip.10), channel_id=1, source_target_pairs={{0,2},{1,3},{2,0},{3,1},{4,6},{5,7},{6,4},{7,5},{8,10},{9,11},{10,... | collective-permute-start | bytes 2359304 | tf_op jit(solution)/shard_map/ppermute | solution.py:311
  54.5 34.0 %collective-permute-start.2 = (f32[2,96,1024]{2,1,0:T(8,128)S(1)}, f32[2,96,1024]{2,1,0:T(8,128)S(1)}, u32[]{:S(2)}, u32[]{:S(2)}) collective-permute-start(f32[2,96,1024]{2,1,0:T(8,128)S(1)} %flip.11), channel_id=1, source_target_pairs={{0,3},{1,2},{2,1},{3,0},{4,7},{5,6},{6,5},{7,4},{8,11},{9,10},{10,... | collective-permute-start | bytes 2359304 | tf_op jit(solution)/shard_map/ppermute | solution.py:311
  96.3 76.0 %all-to-all-start.2 = ((f32[8,96,1024]{2,1,0:T(8,128)}), f32[8,96,1024]{2,1,0:T(8,128)}, u32[]{:S(2)}, u32[]{:S(2)}) async-start(f32[8,96,1024]{2,1,0:T(8,128)} %bitcast.41), calls=%async_computation.2 | async-start | bytes 6291456 | tf_op jit(solution)/shard_map/all_to_all | solution.py:305
  102.6 20.4 %collective-permute-start.6 = (f32[2,96,1024]{2,1,0:T(8,128)S(1)}, f32[2,96,1024]{2,1,0:T(8,128)S(1)}, u32[]{:S(2)}, u32[]{:S(2)}) collective-permute-start(f32[2,96,1024]{2,1,0:T(8,128)S(1)} %flip.13.refs_4_), channel_id=1, source_target_pairs={{0,1},{1,0},{2,3},{3,2},{4,5},{5,4},{6,7},{7,6},{8,9},{9,8},{10,11... | collective-permute-start | bytes 2359304 | tf_op jit(solution)/shard_map/ppermute | solution.py:311
  105.3 37.3 %collective-permute-start.7 = (f32[2,96,1024]{2,1,0:T(8,128)S(1)}, f32[2,96,1024]{2,1,0:T(8,128)S(1)}, u32[]{:S(2)}, u32[]{:S(2)}) collective-permute-start(f32[2,96,1024]{2,1,0:T(8,128)S(1)} %flip.14.refs_5_), channel_id=1, source_target_pairs={{0,2},{1,3},{2,0},{3,1},{4,6},{5,7},{6,4},{7,5},{8,10},{9,11},{10,... | collective-permute-start | bytes 2359304 | tf_op jit(solution)/shard_map/ppermute | solution.py:311
  107.7 34.9 %collective-permute-start.8 = (f32[2,96,1024]{2,1,0:T(8,128)S(1)}, f32[2,96,1024]{2,1,0:T(8,128)S(1)}, u32[]{:S(2)}, u32[]{:S(2)}) collective-permute-start(f32[2,96,1024]{2,1,0:T(8,128)S(1)} %flip.15.refs_6_), channel_id=1, source_target_pairs={{0,3},{1,2},{2,1},{3,0},{4,7},{5,6},{6,5},{7,4},{8,11},{9,10},{10,... | collective-permute-start | bytes 2359304 | tf_op jit(solution)/shard_map/ppermute | solution.py:311
  114.7 61.2 %collective-permute-start.3 = (f32[2,64,1024]{2,1,0:T(8,128)}, f32[2,64,1024]{2,1,0:T(8,128)}, u32[]{:S(2)}, u32[]{:S(2)}) collective-permute-start(f32[2,64,1024]{2,1,0:T(8,128)} %get-tuple-element.35), channel_id=1, source_target_pairs={{0,1},{1,0},{2,3},{3,2},{4,5},{5,4},{6,7},{7,6},{8,9},{9,8},{10,11... | collective-permute-start | bytes 1572872 | tf_op jit(solution)/shard_map/ppermute | solution.py:311
  115.7 60.3 %collective-permute-start.4 = (f32[2,64,1024]{2,1,0:T(8,128)}, f32[2,64,1024]{2,1,0:T(8,128)}, u32[]{:S(2)}, u32[]{:S(2)}) collective-permute-start(f32[2,64,1024]{2,1,0:T(8,128)} %get-tuple-element.36), channel_id=1, source_target_pairs={{0,2},{1,3},{2,0},{3,1},{4,6},{5,7},{6,4},{7,5},{8,10},{9,11},{10,... | collective-permute-start | bytes 1572872 | tf_op jit(solution)/shard_map/ppermute | solution.py:311
  123.0 53.0 %collective-permute-start.5 = (f32[2,64,1024]{2,1,0:T(8,128)}, f32[2,64,1024]{2,1,0:T(8,128)}, u32[]{:S(2)}, u32[]{:S(2)}) collective-permute-start(f32[2,64,1024]{2,1,0:T(8,128)} %get-tuple-element.37), channel_id=1, source_target_pairs={{0,3},{1,2},{2,1},{3,0},{4,7},{5,6},{6,5},{7,4},{8,11},{9,10},{10,... | collective-permute-start | bytes 1572872 | tf_op jit(solution)/shard_map/ppermute | solution.py:311
  172.3 52.6 %all-to-all-start.3 = ((f32[8,64,1024]{2,1,0:T(8,128)}), f32[8,64,1024]{2,1,0:T(8,128)S(1)}, u32[]{:S(2)}, u32[]{:S(2)}) async-start(f32[8,64,1024]{2,1,0:T(8,128)} %bitcast.8), calls=%async_computation.3 | async-start | bytes 4194304 | tf_op jit(solution)/shard_map/all_to_all | solution.py:305
  175.9 81.4 %reduce-scatter.13.cloned.1.call-start = ((), (), s32[]{:S(2)}) async-start(), calls=%async_computation.15 | async-start | bytes 2621440
  185.6 167.0 %reduce-scatter.15.cloned.1.call-start = ((), (), s32[]{:S(2)}) async-start(), calls=%async_computation.16 | async-start | bytes 3932160
  190.0 37.3 %collective-permute-start.9 = (f32[2,96,1024]{2,1,0:T(8,128)}, f32[2,96,1024]{2,1,0:T(8,128)}, u32[]{:S(2)}, u32[]{:S(2)}) collective-permute-start(f32[2,96,1024]{2,1,0:T(8,128)} %get-tuple-element.39), channel_id=1, source_target_pairs={{0,1},{1,0},{2,3},{3,2},{4,5},{5,4},{6,7},{7,6},{8,9},{9,8},{10,11... | collective-permute-start | bytes 2359304 | tf_op jit(solution)/shard_map/ppermute | solution.py:311
  190.9 36.4 %collective-permute-start.10 = (f32[2,96,1024]{2,1,0:T(8,128)}, f32[2,96,1024]{2,1,0:T(8,128)}, u32[]{:S(2)}, u32[]{:S(2)}) collective-permute-start(f32[2,96,1024]{2,1,0:T(8,128)} %get-tuple-element.40), channel_id=1, source_target_pairs={{0,2},{1,3},{2,0},{3,1},{4,6},{5,7},{6,4},{7,5},{8,10},{9,11},{10,... | collective-permute-start | bytes 2359304 | tf_op jit(solution)/shard_map/ppermute | solution.py:311
  191.4 52.8 %collective-permute-start.11 = (f32[2,96,1024]{2,1,0:T(8,128)}, f32[2,96,1024]{2,1,0:T(8,128)}, u32[]{:S(2)}, u32[]{:S(2)}) collective-permute-start(f32[2,96,1024]{2,1,0:T(8,128)} %get-tuple-element.41), channel_id=1, source_target_pairs={{0,3},{1,2},{2,1},{3,0},{4,7},{5,6},{6,5},{7,4},{8,11},{9,10},{10,... | collective-permute-start | bytes 2359304 | tf_op jit(solution)/shard_map/ppermute | solution.py:311
  301.9 18.8 %all-to-all-start.5 = ((f32[8,2,32,256]{3,2,1,0:T(8,128)}), f32[8,2,32,256]{3,2,1,0:T(8,128)S(1)}, u32[]{:S(2)}, u32[]{:S(2)}) async-start(f32[8,2,32,256]{3,2,1,0:T(8,128)} %bitcast.13), calls=%async_computation.5 | async-start | bytes 1048576 | tf_op jit(solution)/shard_map/all_to_all | solution.py:305
  306.5 23.5 %collective-permute-start.12 = (f32[2,64,1024]{2,1,0:T(8,128)}, f32[2,64,1024]{2,1,0:T(8,128)S(1)}, u32[]{:S(2)}, u32[]{:S(2)}) collective-permute-start(f32[2,64,1024]{2,1,0:T(8,128)} %get-tuple-element.43), channel_id=1, source_target_pairs={{0,1},{1,0},{2,3},{3,2},{4,5},{5,4},{6,7},{7,6},{8,9},{9,8},{10,11... | collective-permute-start | bytes 1572872 | tf_op jit(solution)/shard_map/ppermute | solution.py:311
  308.3 25.3 %collective-permute-start.13 = (f32[2,64,1024]{2,1,0:T(8,128)}, f32[2,64,1024]{2,1,0:T(8,128)}, u32[]{:S(2)}, u32[]{:S(2)}) collective-permute-start(f32[2,64,1024]{2,1,0:T(8,128)} %get-tuple-element.44), channel_id=1, source_target_pairs={{0,2},{1,3},{2,0},{3,1},{4,6},{5,7},{6,4},{7,5},{8,10},{9,11},{10,... | collective-permute-start | bytes 1572872 | tf_op jit(solution)/shard_map/ppermute | solution.py:311
  309.8 24.5 %collective-permute-start.14 = (f32[2,64,1024]{2,1,0:T(8,128)}, f32[2,64,1024]{2,1,0:T(8,128)}, u32[]{:S(2)}, u32[]{:S(2)}) collective-permute-start(f32[2,64,1024]{2,1,0:T(8,128)} %get-tuple-element.45), channel_id=1, source_target_pairs={{0,3},{1,2},{2,1},{3,0},{4,7},{5,6},{6,5},{7,4},{8,11},{9,10},{10,... | collective-permute-start | bytes 1572872 | tf_op jit(solution)/shard_map/ppermute | solution.py:311
  322.2 22.9 %all-to-all-start.6 = ((f32[8,2,32,256]{3,2,1,0:T(8,128)}), f32[8,2,32,256]{3,2,1,0:T(8,128)S(1)}, u32[]{:S(2)}, u32[]{:S(2)}) async-start(f32[8,2,32,256]{3,2,1,0:T(8,128)} %broadcast_select_fusion.2), calls=%async_computation.6 | async-start | bytes 1048576 | tf_op jit(solution)/shard_map/all_to_all | solution.py:305
  325.7 75.4 %reduce-scatter.19.cloned.1.call-start = ((), (), s32[]{:S(2)}) async-start(), calls=%async_computation.18 | async-start | bytes 1310720
  326.8 16.9 %collective-permute-start.18 = (f32[2,32,1024]{2,1,0:T(8,128)}, f32[2,32,1024]{2,1,0:T(8,128)S(1)}, u32[]{:S(2)}, u32[]{:S(2)}) collective-permute-start(f32[2,32,1024]{2,1,0:T(8,128)} %get-tuple-element.51), channel_id=1, source_target_pairs={{0,1},{1,0},{2,3},{3,2},{4,5},{5,4},{6,7},{7,6},{8,9},{9,8},{10,11... | collective-permute-start | bytes 786440 | tf_op jit(solution)/shard_map/ppermute | solution.py:311
  328.5 15.6 %collective-permute-start.19 = (f32[2,32,1024]{2,1,0:T(8,128)}, f32[2,32,1024]{2,1,0:T(8,128)S(1)}, u32[]{:S(2)}, u32[]{:S(2)}) collective-permute-start(f32[2,32,1024]{2,1,0:T(8,128)} %get-tuple-element.52), channel_id=1, source_target_pairs={{0,2},{1,3},{2,0},{3,1},{4,6},{5,7},{6,4},{7,5},{8,10},{9,11},{10,... | collective-permute-start | bytes 786440 | tf_op jit(solution)/shard_map/ppermute | solution.py:311
  330.0 15.1 %collective-permute-start.20 = (f32[2,32,1024]{2,1,0:T(8,128)}, f32[2,32,1024]{2,1,0:T(8,128)}, u32[]{:S(2)}, u32[]{:S(2)}) collective-permute-start(f32[2,32,1024]{2,1,0:T(8,128)} %get-tuple-element.53), channel_id=1, source_target_pairs={{0,3},{1,2},{2,1},{3,0},{4,7},{5,6},{6,5},{7,4},{8,11},{9,10},{10,... | collective-permute-start | bytes 786440 | tf_op jit(solution)/shard_map/ppermute | solution.py:311
  352.0 69.3 %reduce-scatter.17.cloned.1.call-start = ((), (), s32[]{:S(2)}) async-start(), calls=%async_computation.17 | async-start | bytes 2621440
  355.1 11.7 %collective-permute-start.22 = (f32[2,2,48,256]{3,2,1,0:T(8,128)S(1)}, f32[2,2,48,256]{3,2,1,0:T(8,128)S(1)}, u32[]{:S(2)}, u32[]{:S(2)}) collective-permute-start(f32[2,2,48,256]{3,2,1,0:T(8,128)S(1)} %get-tuple-element.56), channel_id=1, source_target_pairs={{0,2},{1,3},{2,0},{3,1},{4,6},{5,7},{6,4},{7,5},{8,10},{9,11},{10,... | collective-permute-start | bytes 589832 | tf_op jit(solution)/shard_map/ppermute | solution.py:311
  356.0 13.8 %collective-permute-start.23 = (f32[2,2,48,256]{3,2,1,0:T(8,128)S(1)}, f32[2,2,48,256]{3,2,1,0:T(8,128)S(1)}, u32[]{:S(2)}, u32[]{:S(2)}) collective-permute-start(f32[2,2,48,256]{3,2,1,0:T(8,128)S(1)} %get-tuple-element.57), channel_id=1, source_target_pairs={{0,3},{1,2},{2,1},{3,0},{4,7},{5,6},{6,5},{7,4},{8,11},{9,10},{10,... | collective-permute-start | bytes 589832 | tf_op jit(solution)/shard_map/ppermute | solution.py:311
  370.8 25.2 %all-to-all-start.7 = ((f32[8,2,48,256]{3,2,1,0:T(8,128)}), f32[8,2,48,256]{3,2,1,0:T(8,128)S(1)}, u32[]{:S(2)}, u32[]{:S(2)}) async-start(f32[8,2,48,256]{3,2,1,0:T(8,128)} %bitcast.19), calls=%async_computation.7 | async-start | bytes 1572864 | tf_op jit(solution)/shard_map/all_to_all | solution.py:305
  397.5 29.4 %all-to-all-start.8 = ((f32[8,2,48,256]{3,2,1,0:T(8,128)}), f32[8,2,48,256]{3,2,1,0:T(8,128)S(1)}, u32[]{:S(2)}, u32[]{:S(2)}) async-start(f32[8,2,48,256]{3,2,1,0:T(8,128)} %bitcast.21), calls=%async_computation.8 | async-start | bytes 1572864 | tf_op jit(solution)/shard_map/all_to_all | solution.py:305
  424.9 10.6 %collective-permute-start.25 = (f32[2,2,48,256]{3,2,1,0:T(8,128)S(1)}, f32[2,2,48,256]{3,2,1,0:T(8,128)S(1)}, u32[]{:S(2)}, u32[]{:S(2)}) collective-permute-start(f32[2,2,48,256]{3,2,1,0:T(8,128)S(1)} %get-tuple-element.60), channel_id=1, source_target_pairs={{0,2},{1,3},{2,0},{3,1},{4,6},{5,7},{6,4},{7,5},{8,10},{9,11},{10,... | collective-permute-start | bytes 589832 | tf_op jit(solution)/shard_map/ppermute | solution.py:311
  (30 other events, 292.3 us)
Sparse Core Ops, SparseCore 0:
  185.7 59.7 reduce-scatter.12
  257.4 45.1 reduce-scatter.14
  352.1 31.0 reduce-scatter.18
  386.1 35.1 reduce-scatter.16

commit v14 on v13

--- a/solution.py
+++ b/solution.py
@@ -7,9 +7,8 @@
 from jax.experimental.pallas import tpu as pltpu
 from jax.sharding import PartitionSpec as P
 
-CHUNKS = (2, 3, 2, 1)
-SETS = ((0,), (1,), (2, 3))
-GROUPS = ((0,), (1,), (2, 3))
+CHUNKS = (3, 3, 2)
+GROUPS = ((0,), (1,), (2,))
 LANES = 128
 VMEM_BYTES = 48 * 1024 * 1024
 
@@ -326,9 +325,10 @@
 
     def fetch(chunks, after):
         start, rows = spans[chunks[0]][0], sum(sizes[at] for at in chunks)
-        sent = [flip(place, amplitudes, sections, e, start, rows, after) for e in range(sections)]
-        met = spread(sent)
-        return sent, [
+        met = spread(
+            [flip(place, amplitudes, sections, e, start, rows, after) for e in range(sections)]
+        )
+        return [
             functools.partial(part, place, met, spans[at][0] - start, sizes[at]) for at in chunks
         ]
 
@@ -358,26 +358,18 @@
     first = first_flip(place, amplitudes, sections, sizes[0])
     masked = mask_blocks(integrals, tile_mask, [first])
     across = [swap(first, "ka")]
-    _, (second,) = fetch(SETS[1], [first])
-    across.append(second([masked]))
-    sent, (third, fourth) = fetch(SETS[2], [masked])
+    second, third = fetch((1, 2), [first])
     own = [None] * len(spans)
-    turned, mirrored = turn(0, hop(0), [across[1], *sent])
-    across.append(third([]))
-    begun, own[0] = multiply(0, mirrored, [across[2]])
-    turned, mirrored = turn(1, hop(1), [begun])
-    turned, later = turn(2, hop(2), [turned])
-    leading = send(GROUPS[0])
-    across.append(fourth([turned, *leading]))
-    begun, own[1] = multiply(1, mirrored, [turned])
-    crossed = hop(3)
-    leading = gather(place, leading, [crossed, begun])
-    turned, mirrored = turn(3, crossed, [leading])
-    met = meet(leading)
-    begun, own[2] = multiply(2, later, [turned, met])
+    across += [second([masked]), third([masked])]
+    turned, early = turn(0, hop(0), across[1:2])
+    turned, middle = turn(1, hop(1), [turned])
+    _, own[0] = multiply(0, early, [turned])
+    crossed = hop(2)
+    turned, late = turn(2, crossed, [turned])
+    begun, own[1] = multiply(1, middle, [turned])
+    met = meet(gather(place, send(GROUPS[0]), [crossed]))
+    _, own[2] = multiply(2, late, [begun, met])
     delivered = [deliver(met)]
-    begun, own[3] = multiply(3, mirrored, [begun, *delivered])
-
     for group in GROUPS[1:]:
         met = meet(gather(place, send(group), [delivered[-1]]))
         delivered.append(deliver(met))

time: 499 us -> 491 us (0.984)
  waiting for transfers between devices: 211 us -> 246 us
  blocking collectives: 111 us -> 84.6 us
  Pallas kernels: 82.9 us -> 67.9 us
    all_to_all x7, waiting for transfers between devices: 95.4 us -> 160 us  [swap(): return lax.all_to_all(array, axis, split_axis=0, concat_axis=0, tiled=True)]
    all_to_all x4 -> x3, blocking collectives: 111 us -> 84.6 us  [swap(): return lax.all_to_all(array, axis, split_axis=0, concat_axis=0, tiled=True)]
    unnamed x8 -> x6, waiting for transfers between devices: 20.8 us -> 0.11 us
    pallas_call x28 -> x21, Pallas kernels: 82.9 us -> 67.9 us  [call(): pl.pallas_call(trimmed, grid_spec=pltpu.PrefetchScalarGridSpec(num_scalar...]
    ppermute x27 -> x21, waiting for transfers between devices: 95.2 us -> 85.5 us  [spread(): lax.ppermute(pieces[e], 'ka', [(q, q ^ e) for q in range(count)])]
    ppermute x27 -> x21, starting transfers between devices: 31 us -> 25.3 us  [spread(): lax.ppermute(pieces[e], 'ka', [(q, q ^ e) for q in range(count)])]
    unnamed x49 -> x41, local copies, waits for them, and re-layouts: 11.4 us -> 15.5 us
  transfers between devices with their start and end apart: 38 -> 31, of which waited for: 22 -> 16; matrix products, arithmetic and copies ran while one was open for 1% -> 1% of each run, Pallas kernels for 15% -> 10%
where the time goes in v14:
time: 491 us; the launch traced here: 489 us
  waiting for transfers between devices  246 us (50%)
  blocking collectives  84.6 us (17%)
  Pallas kernels  67.9 us (14%)
  starting transfers between devices  54.3 us (11%)
  local copies, waits for them, and re-layouts  20.1 us (4%)
  between operations  13.4 us (3%)
    all_to_all x7, waiting for transfers between devices, swap(): return lax.all_to_all(array, axis, split_axis=0, concat_axis=0, tiled=True)  160 us
    ppermute x21, waiting for transfers between devices, spread(): lax.ppermute(pieces[e], 'ka', [(q, q ^ e) for q in range(count)])  85.5 us
    all_to_all x3, blocking collectives, swap(): return lax.all_to_all(array, axis, split_axis=0, concat_axis=0, tiled=True)  84.6 us
    pallas_call x21, Pallas kernels, call(): pl.pallas_call(trimmed, grid_spec=pltpu.PrefetchScalarGridSpec(num_scalar...  67.9 us
    all_to_all x7, starting transfers between devices, swap(): return lax.all_to_all(array, axis, split_axis=0, concat_axis=0, tiled=True)  28.9 us
    ppermute x21, starting transfers between devices, spread(): lax.ppermute(pieces[e], 'ka', [(q, q ^ e) for q in range(count)])  25.3 us
    unnamed x41, local copies, waits for them, and re-layouts  15.5 us
  transfers between devices with their start and end apart: 31, of which 16 were waited for; matrix products, arithmetic and copies ran while one was open for 1% of the time, Pallas kernels for 10%

profile of v14, /device:TPU:0, one launch (start us, length us, event | category | flops | bytes accessed | tf_op | source)
XLA Modules:
  0.0 489.4 jit_solution(17289147158078600284)
XLA Ops:
  6.5 5.3 %first_flip.1.refs_2_ = f32[4,2,96,1024]{3,2,1,0:T(8,128)S(1)} custom-call(s32[1]{0:T(128)} %bitcast.refs_0_, f32[1,2,1024,1024]{3,2,1,0:T(8,128)} %refs_4_.5), custom_call_target="tpu_custom_call" | custom-call | bytes 6291456 | tf_op jit(solution)/shard_map/first_flip/pallas_call | solution.py:25
  11.8 41.7 %all_to_all.50 = f32[4,2,96,1024]{3,2,1,0:T(8,128)} all-to-all(f32[4,2,96,1024]{3,2,1,0:T(8,128)S(1)} %first_flip.1.refs_2_), channel_id=1, replica_groups=mesh['ia'=8,'ka'=4] {'ka'}, dimensions={0} | all-to-all | bytes 6291456 | tf_op jit(solution)/shard_map/all_to_all | solution.py:304
  53.5 4.9 all-to-all-start.1
  69.8 8.7 %mask.1.refs_5_.refs_9_ = bf16[2,2,1024,1024]{3,2,1,0:T(8,128)(2,1)} custom-call(s32[2,2,8,8]{3,2,1,0:T(8,128)S(1)} %bitcast.34, bf16[1,2,2,1024,1024]{4,3,2,1,0:T(8,128)(2,1)} %refs_1_.14, f32[4,2,96,1024]{3,2,1,0:T(8,128)S(1)} %first_flip.1.refs_2_), custom_call_target="tpu_custom_call" | custom-call | bytes 16777216 | tf_op jit(solution)/shard_map/mask/pallas_call | solution.py:25
  78.5 13.4 %collective-permute-done.refs_2_ = f32[2,160,1024]{2,1,0:T(8,128)S(1)} collective-permute-done((f32[2,160,1024]{2,1,0:T(8,128)S(1)}, f32[2,160,1024]{2,1,0:T(8,128)S(1)}, u32[]{:S(2)}, u32[]{:S(2)}) %collective-permute-start) | collective-permute-done | bytes 1310752 | tf_op jit(solution)/shard_map/ppermute | solution.py:310
  92.0 30.3 %collective-permute-done.1.refs_3_ = f32[2,160,1024]{2,1,0:T(8,128)S(1)} collective-permute-done((f32[2,160,1024]{2,1,0:T(8,128)S(1)}, f32[2,160,1024]{2,1,0:T(8,128)S(1)}, u32[]{:S(2)}, u32[]{:S(2)}) %collective-permute-start.1) | collective-permute-done | bytes 1310752 | tf_op jit(solution)/shard_map/ppermute | solution.py:310
  127.3 2.7 all-to-all-done.1
  130.1 4.5 all-to-all-start.2
  134.6 3.4 scatter.3
  141.5 64.5 %all-to-all-done.2 = f32[8,96,1024]{2,1,0:T(8,128)} async-done(((f32[8,96,1024]{2,1,0:T(8,128)}), f32[8,96,1024]{2,1,0:T(8,128)}, u32[]{:S(2)}, u32[]{:S(2)}) %all-to-all-start.2) | async-done | bytes 3145760 | tf_op jit(solution)/shard_map/all_to_all | solution.py:304
  210.9 11.7 %product.3 = f32[4,2,96,1024]{3,2,1,0:T(8,128)} custom-call(s32[1]{0:T(128)} %bitcast.refs_0_, f32[1,2,1024,1024]{3,2,1,0:T(8,128)} %refs_4_.5, f32[1,2,1024,1024]{3,2,1,0:T(8,128)} %refs_4_.5, f32[1,2,1024,1024]{3,2,1,0:T(8,128)} %refs_4_.5, f32[1,2,1024,1024]{3,2,1,0:T(8,128)} %refs_4_.5, f32[2,96,1024]{2,1,0:T(8,128)S(1)} %get-tuple-element.30.refs_2_.refs_5_, ...), custom_call_target="tpu_custom_call" | custom-call | flops 6442450944 | bytes 6291456 | tf_op jit(solution)/shard_map/product/pallas_call | solution.py:25
  229.3 3.6 all-to-all-start.3
  236.5 45.4 %all-to-all-done.3 = f32[8,64,1024]{2,1,0:T(8,128)S(1)} async-done(((f32[8,64,1024]{2,1,0:T(8,128)}), f32[8,64,1024]{2,1,0:T(8,128)S(1)}, u32[]{:S(2)}, u32[]{:S(2)}) %all-to-all-start.3) | async-done | bytes 2097184 | tf_op jit(solution)/shard_map/all_to_all | solution.py:304
  283.2 5.5 %collective-permute-done.8.refs_8_ = f32[2,96,1024]{2,1,0:T(8,128)} collective-permute-done((f32[2,96,1024]{2,1,0:T(8,128)}, f32[2,96,1024]{2,1,0:T(8,128)}, u32[]{:S(2)}, u32[]{:S(2)}) %collective-permute-start.8) | collective-permute-done | bytes 786464 | tf_op jit(solution)/shard_map/ppermute | solution.py:310
  288.7 12.1 %product.4.refs_10_ = f32[4,2,96,1024]{3,2,1,0:T(8,128)} custom-call(s32[1]{0:T(128)} %bitcast.refs_0_, f32[1,2,1024,1024]{3,2,1,0:T(8,128)} %refs_4_.5, f32[1,2,1024,1024]{3,2,1,0:T(8,128)} %refs_4_.5, f32[1,2,1024,1024]{3,2,1,0:T(8,128)} %refs_4_.5, f32[1,2,1024,1024]{3,2,1,0:T(8,128)} %refs_4_.5, ...), custom_call_target="tpu_custom_call" | custom-call | flops 6442450944 | bytes 6291456 | tf_op jit(solution)/shard_map/product/pallas_call | solution.py:25
  303.2 2.4 collective-permute-start.14
  305.6 5.4 %collective-permute-done.12.refs_2_ = f32[2,2,48,256]{3,2,1,0:T(8,128)S(1)} collective-permute-done((f32[2,2,48,256]{3,2,1,0:T(8,128)S(1)}, f32[2,2,48,256]{3,2,1,0:T(8,128)S(1)}, u32[]{:S(2)}, u32[]{:S(2)}) %collective-permute-start.12) | collective-permute-done | bytes 196640 | tf_op jit(solution)/shard_map/ppermute | solution.py:310
  311.1 2.6 collective-permute-done.13.refs_3_
  313.6 3.8 collective-permute-done.14.refs_4_
  318.4 4.6 all-to-all-start.4
  328.0 16.0 %all-to-all-done.4.refs_11_ = f32[8,2,48,256]{3,2,1,0:T(8,128)S(1)} async-done(((f32[8,2,48,256]{3,2,1,0:T(8,128)}), f32[8,2,48,256]{3,2,1,0:T(8,128)S(1)}, u32[]{:S(2)}, u32[]{:S(2)}) %all-to-all-start.4) | async-done | bytes 786464 | tf_op jit(solution)/shard_map/all_to_all | solution.py:304
  345.6 3.5 all-to-all-start.5
  349.2 11.8 %collective-permute-done.11.refs_8_ = f32[2,64,1024]{2,1,0:T(8,128)} collective-permute-done((f32[2,64,1024]{2,1,0:T(8,128)}, f32[2,64,1024]{2,1,0:T(8,128)}, u32[]{:S(2)}, u32[]{:S(2)}) %collective-permute-start.11) | collective-permute-done | bytes 524320 | tf_op jit(solution)/shard_map/ppermute | solution.py:310
  360.9 9.3 %product.5 = f32[4,2,64,1024]{3,2,1,0:T(8,128)} custom-call(s32[1]{0:T(128)} %bitcast.refs_0_, f32[1,2,1024,1024]{3,2,1,0:T(8,128)} %refs_4_.5, f32[1,2,1024,1024]{3,2,1,0:T(8,128)} %refs_4_.5, f32[1,2,1024,1024]{3,2,1,0:T(8,128)} %refs_4_.5, f32[1,2,1024,1024]{3,2,1,0:T(8,128)} %refs_4_.5, f32[2,64,1024]{2,1,0:T(8,128)S(1)} %get-tuple-element.38.refs_10_.refs_5_, ...), custom_call_target="tpu_custom_call" | custom-call | flops 4294967296 | bytes 4194304 | tf_op jit(solution)/shard_map/product/pallas_call | solution.py:25
  375.0 4.6 collective-permute-done.15.refs_2_
  381.8 5.9 %collective-permute-done.17.refs_4_ = f32[2,2,48,256]{3,2,1,0:T(8,128)S(1)} collective-permute-done((f32[2,2,48,256]{3,2,1,0:T(8,128)S(1)}, f32[2,2,48,256]{3,2,1,0:T(8,128)S(1)}, u32[]{:S(2)}, u32[]{:S(2)}) %collective-permute-start.17) | collective-permute-done | bytes 196640 | tf_op jit(solution)/shard_map/ppermute | solution.py:310
  387.7 25.2 %all_to_all.51 = f32[8,2,48,256]{3,2,1,0:T(8,128)S(1)} all-to-all(f32[8,2,48,256]{3,2,1,0:T(8,128)S(1)} %bitcast.26), channel_id=1, replica_groups=mesh['ia'=8,'ka'=4] {'ia'}, dimensions={0} | all-to-all | bytes 1572864 | tf_op jit(solution)/shard_map/all_to_all | solution.py:304
  414.6 3.5 all-to-all-start.7
  422.8 16.2 %all-to-all-done.7.refs_5_ = f32[8,2,48,256]{3,2,1,0:T(8,128)S(1)} async-done(((f32[8,2,48,256]{3,2,1,0:T(8,128)}), f32[8,2,48,256]{3,2,1,0:T(8,128)S(1)}, u32[]{:S(2)}, u32[]{:S(2)}) %all-to-all-start.7) | async-done | bytes 786464 | tf_op jit(solution)/shard_map/all_to_all | solution.py:304
  439.9 4.3 all-to-all-start.8
  444.3 15.3 %all-to-all-done.8 = f32[8,2,32,256]{3,2,1,0:T(8,128)} async-done(((f32[8,2,32,256]{3,2,1,0:T(8,128)}), f32[8,2,32,256]{3,2,1,0:T(8,128)}, u32[]{:S(2)}, u32[]{:S(2)}) %all-to-all-start.8) | async-done | bytes 524320 | tf_op jit(solution)/shard_map/all_to_all | solution.py:304
  463.1 17.8 %all_to_all.52.refs_6_ = f32[8,2,32,256]{3,2,1,0:T(8,128)S(1)} all-to-all(f32[8,2,32,256]{3,2,1,0:T(8,128)S(1)} %broadcast_select_fusion.2), channel_id=1, replica_groups=mesh['ia'=8,'ka'=4] {'ia'}, dimensions={0} | all-to-all | bytes 1048576 | tf_op jit(solution)/shard_map/all_to_all | solution.py:304
  (116 shorter events, 66.0 us)
Async XLA Ops:
  53.5 76.5 %all-to-all-start.1 = ((f32[8,96,1024]{2,1,0:T(8,128)}), f32[8,96,1024]{2,1,0:T(8,128)}, u32[]{:S(2)}, u32[]{:S(2)}) async-start(f32[8,96,1024]{2,1,0:T(8,128)} %bitcast.36), calls=%async_computation.1 | async-start | bytes 6291456 | tf_op jit(solution)/shard_map/all_to_all | solution.py:304
  60.3 31.6 %collective-permute-start = (f32[2,160,1024]{2,1,0:T(8,128)S(1)}, f32[2,160,1024]{2,1,0:T(8,128)S(1)}, u32[]{:S(2)}, u32[]{:S(2)}) collective-permute-start(f32[2,160,1024]{2,1,0:T(8,128)S(1)} %flip.5), channel_id=1, source_target_pairs={{0,1},{1,0},{2,3},{3,2},{4,5},{5,4},{6,7},{7,6},{8,9},{9,8},{10,11... | collective-permute-start | bytes 3932168 | tf_op jit(solution)/shard_map/ppermute | solution.py:310
  63.2 59.1 %collective-permute-start.1 = (f32[2,160,1024]{2,1,0:T(8,128)S(1)}, f32[2,160,1024]{2,1,0:T(8,128)S(1)}, u32[]{:S(2)}, u32[]{:S(2)}) collective-permute-start(f32[2,160,1024]{2,1,0:T(8,128)S(1)} %flip.6), channel_id=1, source_target_pairs={{0,2},{1,3},{2,0},{3,1},{4,6},{5,7},{6,4},{7,5},{8,10},{9,11},{10,... | collective-permute-start | bytes 3932168 | tf_op jit(solution)/shard_map/ppermute | solution.py:310
  65.8 56.5 %collective-permute-start.2 = (f32[2,160,1024]{2,1,0:T(8,128)S(1)}, f32[2,160,1024]{2,1,0:T(8,128)S(1)}, u32[]{:S(2)}, u32[]{:S(2)}) collective-permute-start(f32[2,160,1024]{2,1,0:T(8,128)S(1)} %flip.7), channel_id=1, source_target_pairs={{0,3},{1,2},{2,1},{3,0},{4,7},{5,6},{6,5},{7,4},{8,11},{9,10},{10,... | collective-permute-start | bytes 3932168 | tf_op jit(solution)/shard_map/ppermute | solution.py:310
  69.8 52.5 %copy-start = (f32[2,160,1024]{2,1,0:T(8,128)}, f32[2,160,1024]{2,1,0:T(8,128)S(1)}, u32[]{:S(2)}) copy-start(f32[2,160,1024]{2,1,0:T(8,128)S(1)} %flip.4.refs_1_) | copy-start | bytes 3932164
  130.1 76.0 %all-to-all-start.2 = ((f32[8,96,1024]{2,1,0:T(8,128)}), f32[8,96,1024]{2,1,0:T(8,128)}, u32[]{:S(2)}, u32[]{:S(2)}) async-start(f32[8,96,1024]{2,1,0:T(8,128)} %bitcast.35), calls=%async_computation.2 | async-start | bytes 6291456 | tf_op jit(solution)/shard_map/all_to_all | solution.py:304
  134.5 166.3 %reduce-scatter.10.cloned.1.call-start = ((), (), s32[]{:S(2)}) async-start(), calls=%async_computation.13 | async-start | bytes 3932160
  138.0 72.9 %collective-permute-start.3 = (f32[2,96,1024]{2,1,0:T(8,128)}, f32[2,96,1024]{2,1,0:T(8,128)S(1)}, u32[]{:S(2)}, u32[]{:S(2)}) collective-permute-start(f32[2,96,1024]{2,1,0:T(8,128)} %get-tuple-element.31), channel_id=1, source_target_pairs={{0,1},{1,0},{2,3},{3,2},{4,5},{5,4},{6,7},{7,6},{8,9},{9,8},{10,11... | collective-permute-start | bytes 2359304 | tf_op jit(solution)/shard_map/ppermute | solution.py:310
  138.9 72.0 %collective-permute-start.4 = (f32[2,96,1024]{2,1,0:T(8,128)}, f32[2,96,1024]{2,1,0:T(8,128)S(1)}, u32[]{:S(2)}, u32[]{:S(2)}) collective-permute-start(f32[2,96,1024]{2,1,0:T(8,128)} %get-tuple-element.32), channel_id=1, source_target_pairs={{0,2},{1,3},{2,0},{3,1},{4,6},{5,7},{6,4},{7,5},{8,10},{9,11},{10,... | collective-permute-start | bytes 2359304 | tf_op jit(solution)/shard_map/ppermute | solution.py:310
  139.5 71.4 %collective-permute-start.5 = (f32[2,96,1024]{2,1,0:T(8,128)}, f32[2,96,1024]{2,1,0:T(8,128)}, u32[]{:S(2)}, u32[]{:S(2)}) collective-permute-start(f32[2,96,1024]{2,1,0:T(8,128)} %get-tuple-element.33), channel_id=1, source_target_pairs={{0,3},{1,2},{2,1},{3,0},{4,7},{5,6},{6,5},{7,4},{8,11},{9,10},{10,... | collective-permute-start | bytes 2359304 | tf_op jit(solution)/shard_map/ppermute | solution.py:310
  229.3 52.6 %all-to-all-start.3 = ((f32[8,64,1024]{2,1,0:T(8,128)}), f32[8,64,1024]{2,1,0:T(8,128)S(1)}, u32[]{:S(2)}, u32[]{:S(2)}) async-start(f32[8,64,1024]{2,1,0:T(8,128)} %bitcast.37), calls=%async_computation.3 | async-start | bytes 4194304 | tf_op jit(solution)/shard_map/all_to_all | solution.py:304
  232.9 137.3 %reduce-scatter.12.cloned.1.call-start = ((), (), s32[]{:S(2)}) async-start(), calls=%async_computation.14 | async-start | bytes 3932160
  233.0 50.2 %collective-permute-start.6 = (f32[2,96,1024]{2,1,0:T(8,128)}, f32[2,96,1024]{2,1,0:T(8,128)}, u32[]{:S(2)}, u32[]{:S(2)}) collective-permute-start(f32[2,96,1024]{2,1,0:T(8,128)} %copy-done.18), channel_id=1, source_target_pairs={{0,1},{1,0},{2,3},{3,2},{4,5},{5,4},{6,7},{7,6},{8,9},{9,8},{10,11... | collective-permute-start | bytes 2359304 | tf_op jit(solution)/shard_map/ppermute | solution.py:310
  234.2 49.0 %collective-permute-start.7 = (f32[2,96,1024]{2,1,0:T(8,128)}, f32[2,96,1024]{2,1,0:T(8,128)}, u32[]{:S(2)}, u32[]{:S(2)}) collective-permute-start(f32[2,96,1024]{2,1,0:T(8,128)} %copy-done.17), channel_id=1, source_target_pairs={{0,2},{1,3},{2,0},{3,1},{4,6},{5,7},{6,4},{7,5},{8,10},{9,11},{10,... | collective-permute-start | bytes 2359304 | tf_op jit(solution)/shard_map/ppermute | solution.py:310
  234.5 54.2 %collective-permute-start.8 = (f32[2,96,1024]{2,1,0:T(8,128)}, f32[2,96,1024]{2,1,0:T(8,128)}, u32[]{:S(2)}, u32[]{:S(2)}) collective-permute-start(f32[2,96,1024]{2,1,0:T(8,128)} %copy-done.16), channel_id=1, source_target_pairs={{0,3},{1,2},{2,1},{3,0},{4,7},{5,6},{6,5},{7,4},{8,11},{9,10},{10,... | collective-permute-start | bytes 2359304 | tf_op jit(solution)/shard_map/ppermute | solution.py:310
  302.1 9.0 %collective-permute-start.12 = (f32[2,2,48,256]{3,2,1,0:T(8,128)S(1)}, f32[2,2,48,256]{3,2,1,0:T(8,128)S(1)}, u32[]{:S(2)}, u32[]{:S(2)}) collective-permute-start(f32[2,2,48,256]{3,2,1,0:T(8,128)S(1)} %get-tuple-element.43), channel_id=1, source_target_pairs={{0,1},{1,0},{2,3},{3,2},{4,5},{5,4},{6,7},{7,6},{8,9},{9,8},{10,11... | collective-permute-start | bytes 589832 | tf_op jit(solution)/shard_map/ppermute | solution.py:310
  302.7 10.9 %collective-permute-start.13 = (f32[2,2,48,256]{3,2,1,0:T(8,128)S(1)}, f32[2,2,48,256]{3,2,1,0:T(8,128)S(1)}, u32[]{:S(2)}, u32[]{:S(2)}) collective-permute-start(f32[2,2,48,256]{3,2,1,0:T(8,128)S(1)} %get-tuple-element.44), channel_id=1, source_target_pairs={{0,2},{1,3},{2,0},{3,1},{4,6},{5,7},{6,4},{7,5},{8,10},{9,11},{10,... | collective-permute-start | bytes 589832 | tf_op jit(solution)/shard_map/ppermute | solution.py:310
  303.2 14.3 %collective-permute-start.14 = (f32[2,2,48,256]{3,2,1,0:T(8,128)S(1)}, f32[2,2,48,256]{3,2,1,0:T(8,128)S(1)}, u32[]{:S(2)}, u32[]{:S(2)}) collective-permute-start(f32[2,2,48,256]{3,2,1,0:T(8,128)S(1)} %get-tuple-element.45), channel_id=1, source_target_pairs={{0,3},{1,2},{2,1},{3,0},{4,7},{5,6},{6,5},{7,4},{8,11},{9,10},{10,... | collective-permute-start | bytes 589832 | tf_op jit(solution)/shard_map/ppermute | solution.py:310
  318.4 25.5 %all-to-all-start.4 = ((f32[8,2,48,256]{3,2,1,0:T(8,128)}), f32[8,2,48,256]{3,2,1,0:T(8,128)S(1)}, u32[]{:S(2)}, u32[]{:S(2)}) async-start(f32[8,2,48,256]{3,2,1,0:T(8,128)} %bitcast.11), calls=%async_computation.4 | async-start | bytes 1572864 | tf_op jit(solution)/shard_map/all_to_all | solution.py:304
  324.0 25.1 %collective-permute-start.9 = (f32[2,64,1024]{2,1,0:T(8,128)}, f32[2,64,1024]{2,1,0:T(8,128)S(1)}, u32[]{:S(2)}, u32[]{:S(2)}) collective-permute-start(f32[2,64,1024]{2,1,0:T(8,128)} %get-tuple-element.39), channel_id=1, source_target_pairs={{0,1},{1,0},{2,3},{3,2},{4,5},{5,4},{6,7},{7,6},{8,9},{9,8},{10,11... | collective-permute-start | bytes 1572872 | tf_op jit(solution)/shard_map/ppermute | solution.py:310
  324.7 24.5 %collective-permute-start.10 = (f32[2,64,1024]{2,1,0:T(8,128)}, f32[2,64,1024]{2,1,0:T(8,128)S(1)}, u32[]{:S(2)}, u32[]{:S(2)}) collective-permute-start(f32[2,64,1024]{2,1,0:T(8,128)} %get-tuple-element.40), channel_id=1, source_target_pairs={{0,2},{1,3},{2,0},{3,1},{4,6},{5,7},{6,4},{7,5},{8,10},{9,11},{10,... | collective-permute-start | bytes 1572872 | tf_op jit(solution)/shard_map/ppermute | solution.py:310
  327.1 33.9 %collective-permute-start.11 = (f32[2,64,1024]{2,1,0:T(8,128)}, f32[2,64,1024]{2,1,0:T(8,128)}, u32[]{:S(2)}, u32[]{:S(2)}) collective-permute-start(f32[2,64,1024]{2,1,0:T(8,128)} %get-tuple-element.41), channel_id=1, source_target_pairs={{0,3},{1,2},{2,1},{3,0},{4,7},{5,6},{6,5},{7,4},{8,11},{9,10},{10,... | collective-permute-start | bytes 1572872 | tf_op jit(solution)/shard_map/ppermute | solution.py:310
  345.6 42.1 %all-to-all-start.5 = ((f32[8,2,48,256]{3,2,1,0:T(8,128)}), f32[8,2,48,256]{3,2,1,0:T(8,128)S(1)}, u32[]{:S(2)}, u32[]{:S(2)}) async-start(f32[8,2,48,256]{3,2,1,0:T(8,128)} %bitcast.38), calls=%async_computation.5 | async-start | bytes 1572864 | tf_op jit(solution)/shard_map/all_to_all | solution.py:304
  349.1 69.0 %reduce-scatter.14.cloned.1.call-start = ((), (), s32[]{:S(2)}) async-start(), calls=%async_computation.15 | async-start | bytes 2621440
  371.5 8.1 %collective-permute-start.15 = (f32[2,2,48,256]{3,2,1,0:T(8,128)S(1)}, f32[2,2,48,256]{3,2,1,0:T(8,128)S(1)}, u32[]{:S(2)}, u32[]{:S(2)}) collective-permute-start(f32[2,2,48,256]{3,2,1,0:T(8,128)S(1)} %get-tuple-element.47), channel_id=1, source_target_pairs={{0,1},{1,0},{2,3},{3,2},{4,5},{5,4},{6,7},{7,6},{8,9},{9,8},{10,11... | collective-permute-start | bytes 589832 | tf_op jit(solution)/shard_map/ppermute | solution.py:310
  371.9 9.9 %collective-permute-start.16 = (f32[2,2,48,256]{3,2,1,0:T(8,128)S(1)}, f32[2,2,48,256]{3,2,1,0:T(8,128)S(1)}, u32[]{:S(2)}, u32[]{:S(2)}) collective-permute-start(f32[2,2,48,256]{3,2,1,0:T(8,128)S(1)} %get-tuple-element.48), channel_id=1, source_target_pairs={{0,2},{1,3},{2,0},{3,1},{4,6},{5,7},{6,4},{7,5},{8,10},{9,11},{10,... | collective-permute-start | bytes 589832 | tf_op jit(solution)/shard_map/ppermute | solution.py:310
  373.6 14.1 %collective-permute-start.17 = (f32[2,2,48,256]{3,2,1,0:T(8,128)S(1)}, f32[2,2,48,256]{3,2,1,0:T(8,128)S(1)}, u32[]{:S(2)}, u32[]{:S(2)}) collective-permute-start(f32[2,2,48,256]{3,2,1,0:T(8,128)S(1)} %get-tuple-element.49), channel_id=1, source_target_pairs={{0,3},{1,2},{2,1},{3,0},{4,7},{5,6},{6,5},{7,4},{8,11},{9,10},{10,... | collective-permute-start | bytes 589832 | tf_op jit(solution)/shard_map/ppermute | solution.py:310
  414.6 24.4 %all-to-all-start.7 = ((f32[8,2,48,256]{3,2,1,0:T(8,128)}), f32[8,2,48,256]{3,2,1,0:T(8,128)S(1)}, u32[]{:S(2)}, u32[]{:S(2)}) async-start(f32[8,2,48,256]{3,2,1,0:T(8,128)} %bitcast.17), calls=%async_computation.7 | async-start | bytes 1572864 | tf_op jit(solution)/shard_map/all_to_all | solution.py:304
  419.2 19.8 %collective-permute-start.18 = (f32[2,2,32,256]{3,2,1,0:T(8,128)S(1)}, f32[2,2,32,256]{3,2,1,0:T(8,128)S(1)}, u32[]{:S(2)}, u32[]{:S(2)}) collective-permute-start(f32[2,2,32,256]{3,2,1,0:T(8,128)S(1)} %get-tuple-element.51), channel_id=1, source_target_pairs={{0,1},{1,0},{2,3},{3,2},{4,5},{5,4},{6,7},{7,6},{8,9},{9,8},{10,11... | collective-permute-start | bytes 393224 | tf_op jit(solution)/shard_map/ppermute | solution.py:310
  420.1 18.9 %collective-permute-start.19 = (f32[2,2,32,256]{3,2,1,0:T(8,128)S(1)}, f32[2,2,32,256]{3,2,1,0:T(8,128)S(1)}, u32[]{:S(2)}, u32[]{:S(2)}) collective-permute-start(f32[2,2,32,256]{3,2,1,0:T(8,128)S(1)} %get-tuple-element.52), channel_id=1, source_target_pairs={{0,2},{1,3},{2,0},{3,1},{4,6},{5,7},{6,4},{7,5},{8,10},{9,11},{10,... | collective-permute-start | bytes 393224 | tf_op jit(solution)/shard_map/ppermute | solution.py:310
  420.4 18.6 %collective-permute-start.20 = (f32[2,2,32,256]{3,2,1,0:T(8,128)S(1)}, f32[2,2,32,256]{3,2,1,0:T(8,128)S(1)}, u32[]{:S(2)}, u32[]{:S(2)}) collective-permute-start(f32[2,2,32,256]{3,2,1,0:T(8,128)S(1)} %get-tuple-element.53), channel_id=1, source_target_pairs={{0,3},{1,2},{2,1},{3,0},{4,7},{5,6},{6,5},{7,4},{8,11},{9,10},{10,... | collective-permute-start | bytes 393224 | tf_op jit(solution)/shard_map/ppermute | solution.py:310
  439.9 19.7 %all-to-all-start.8 = ((f32[8,2,32,256]{3,2,1,0:T(8,128)}), f32[8,2,32,256]{3,2,1,0:T(8,128)}, u32[]{:S(2)}, u32[]{:S(2)}) async-start(f32[8,2,32,256]{3,2,1,0:T(8,128)} %bitcast.33), calls=%async_computation.8 | async-start | bytes 1048576 | tf_op jit(solution)/shard_map/all_to_all | solution.py:304
  (19 other events, 126.0 us)
Sparse Core Ops, SparseCore 0:
  222.8 60.4 reduce-scatter.9
  301.0 61.3 reduce-scatter.11
  370.4 39.5 reduce-scatter.13

commit v15 on v14

--- a/solution.py
+++ b/solution.py
@@ -361,13 +361,14 @@
     second, third = fetch((1, 2), [first])
     own = [None] * len(spans)
     across += [second([masked]), third([masked])]
-    turned, early = turn(0, hop(0), across[1:2])
-    turned, middle = turn(1, hop(1), [turned])
-    _, own[0] = multiply(0, early, [turned])
+    turned, early = turn(0, hop(0), across[1:])
+    begun, own[0] = multiply(0, early, [])
+    turned, middle = turn(1, hop(1), [begun])
+    leading = send(GROUPS[0])
     crossed = hop(2)
-    turned, late = turn(2, crossed, [turned])
+    turned, late = turn(2, crossed, [turned, *leading])
     begun, own[1] = multiply(1, middle, [turned])
-    met = meet(gather(place, send(GROUPS[0]), [crossed]))
+    met = meet(gather(place, leading, [crossed]))
     _, own[2] = multiply(2, late, [begun, met])
     delivered = [deliver(met)]
     for group in GROUPS[1:]:

time: 491 us -> 470 us (0.957)
  waiting for transfers between devices: 246 us -> 222 us
    all_to_all x7, waiting for transfers between devices: 160 us -> 60.5 us  [swap(): return lax.all_to_all(array, axis, split_axis=0, concat_axis=0, tiled=True)]
    ppermute x21, waiting for transfers between devices: 85.5 us -> 130 us  [spread(): lax.ppermute(pieces[e], 'ka', [(q, q ^ e) for q in range(count)])]
    unnamed x6, waiting for transfers between devices: 0.11 us -> 31.1 us
    unnamed x41 -> x59, local copies, waits for them, and re-layouts: 15.5 us -> 17.6 us
  transfers between devices with their start and end apart: 31 -> 31, of which waited for: 16 -> 21; matrix products, arithmetic and copies ran while one was open for 1% -> 1% of each run, Pallas kernels for 10% -> 10%
where the time goes in v15:
time: 470 us; the launch traced here: 468 us
  waiting for transfers between devices  222 us (47%)
  blocking collectives  84.8 us (18%)
  Pallas kernels  68.4 us (15%)
  starting transfers between devices  53.7 us (11%)
  local copies, waits for them, and re-layouts  22.3 us (5%)
  between operations  13.4 us (3%)
    ppermute x21, waiting for transfers between devices, spread(): lax.ppermute(pieces[e], 'ka', [(q, q ^ e) for q in range(count)])  130 us
    all_to_all x3, blocking collectives, swap(): return lax.all_to_all(array, axis, split_axis=0, concat_axis=0, tiled=True)  84.8 us
    pallas_call x21, Pallas kernels, call(): pl.pallas_call(trimmed, grid_spec=pltpu.PrefetchScalarGridSpec(num_scalar...  68.4 us
    all_to_all x7, waiting for transfers between devices, swap(): return lax.all_to_all(array, axis, split_axis=0, concat_axis=0, tiled=True)  60.5 us
    unnamed x6, waiting for transfers between devices  31.1 us
    all_to_all x7, starting transfers between devices, swap(): return lax.all_to_all(array, axis, split_axis=0, concat_axis=0, tiled=True)  29.2 us
    ppermute x21, starting transfers between devices, spread(): lax.ppermute(pieces[e], 'ka', [(q, q ^ e) for q in range(count)])  24.4 us
    unnamed x59, local copies, waits for them, and re-layouts  17.6 us
  transfers between devices with their start and end apart: 31, of which 21 were waited for; matrix products, arithmetic and copies ran while one was open for 1% of the time, Pallas kernels for 10%

profile of v15, /device:TPU:0, one launch (start us, length us, event | category | flops | bytes accessed | tf_op | source)
XLA Modules:
  0.0 467.9 jit_solution(371031749762239127)
XLA Ops:
  6.5 5.3 %first_flip.1.refs_2_ = f32[4,2,96,1024]{3,2,1,0:T(8,128)S(1)} custom-call(s32[1]{0:T(128)} %bitcast.refs_0_, f32[1,2,1024,1024]{3,2,1,0:T(8,128)} %refs_4_.5), custom_call_target="tpu_custom_call" | custom-call | bytes 6291456 | tf_op jit(solution)/shard_map/first_flip/pallas_call | solution.py:25
  11.8 41.7 %all_to_all.50 = f32[4,2,96,1024]{3,2,1,0:T(8,128)} all-to-all(f32[4,2,96,1024]{3,2,1,0:T(8,128)S(1)} %first_flip.1.refs_2_), channel_id=1, replica_groups=mesh['ia'=8,'ka'=4] {'ka'}, dimensions={0} | all-to-all | bytes 6291456 | tf_op jit(solution)/shard_map/all_to_all | solution.py:304
  53.5 4.9 %all-to-all-start.1 = ((f32[8,96,1024]{2,1,0:T(8,128)}), f32[8,96,1024]{2,1,0:T(8,128)}, u32[]{:S(2)}, u32[]{:S(2)}) async-start(f32[8,96,1024]{2,1,0:T(8,128)} %bitcast.36), calls=%async_computation.1 | async-start | bytes 6291456 | tf_op jit(solution)/shard_map/all_to_all | solution.py:304
  69.8 8.7 %mask.1.refs_5_.refs_9_ = bf16[2,2,1024,1024]{3,2,1,0:T(8,128)(2,1)} custom-call(s32[2,2,8,8]{3,2,1,0:T(8,128)S(1)} %bitcast.34, bf16[1,2,2,1024,1024]{4,3,2,1,0:T(8,128)(2,1)} %refs_1_.14, f32[4,2,96,1024]{3,2,1,0:T(8,128)S(1)} %first_flip.1.refs_2_), custom_call_target="tpu_custom_call" | custom-call | bytes 16777216 | tf_op jit(solution)/shard_map/mask/pallas_call | solution.py:25
  78.5 13.4 %collective-permute-done.refs_2_ = f32[2,160,1024]{2,1,0:T(8,128)S(1)} collective-permute-done((f32[2,160,1024]{2,1,0:T(8,128)S(1)}, f32[2,160,1024]{2,1,0:T(8,128)S(1)}, u32[]{:S(2)}, u32[]{:S(2)}) %collective-permute-start) | collective-permute-done | bytes 1310752 | tf_op jit(solution)/shard_map/ppermute | solution.py:310
  92.0 30.3 %collective-permute-done.1.refs_3_ = f32[2,160,1024]{2,1,0:T(8,128)S(1)} collective-permute-done((f32[2,160,1024]{2,1,0:T(8,128)S(1)}, f32[2,160,1024]{2,1,0:T(8,128)S(1)}, u32[]{:S(2)}, u32[]{:S(2)}) %collective-permute-start.1) | collective-permute-done | bytes 1310752 | tf_op jit(solution)/shard_map/ppermute | solution.py:310
  130.1 4.7 %all-to-all-start.2 = ((f32[8,96,1024]{2,1,0:T(8,128)}), f32[8,96,1024]{2,1,0:T(8,128)}, u32[]{:S(2)}, u32[]{:S(2)}) async-start(f32[8,96,1024]{2,1,0:T(8,128)} %bitcast.35), calls=%async_computation.2 | async-start | bytes 6291456 | tf_op jit(solution)/shard_map/all_to_all | solution.py:304
  144.5 16.9 %collective-permute-done.3.refs_6_ = f32[2,96,1024]{2,1,0:T(8,128)S(1)} collective-permute-done((f32[2,96,1024]{2,1,0:T(8,128)S(1)}, f32[2,96,1024]{2,1,0:T(8,128)S(1)}, u32[]{:S(2)}, u32[]{:S(2)}) %collective-permute-start.3) | collective-permute-done | bytes 786464 | tf_op jit(solution)/shard_map/ppermute | solution.py:310
  161.4 16.9 %collective-permute-done.4.refs_7_ = f32[2,96,1024]{2,1,0:T(8,128)S(1)} collective-permute-done((f32[2,96,1024]{2,1,0:T(8,128)S(1)}, f32[2,96,1024]{2,1,0:T(8,128)S(1)}, u32[]{:S(2)}, u32[]{:S(2)}) %collective-permute-start.4) | collective-permute-done | bytes 786464 | tf_op jit(solution)/shard_map/ppermute | solution.py:310
  178.3 11.4 %product.3.refs_2_ = f32[4,2,96,1024]{3,2,1,0:T(8,128)} custom-call(s32[1]{0:T(128)} %bitcast.refs_0_, f32[1,2,1024,1024]{3,2,1,0:T(8,128)} %refs_4_.5, f32[1,2,1024,1024]{3,2,1,0:T(8,128)} %refs_4_.5, f32[1,2,1024,1024]{3,2,1,0:T(8,128)} %refs_4_.5, f32[1,2,1024,1024]{3,2,1,0:T(8,128)} %refs_4_.5, f32[2,96,1024]{2,1,0:T(8,128)S(1)} %get-tuple-element.30.refs_5_, ...), custom_call_target="tpu_custom_call" | custom-call | flops 6442450944 | bytes 6291456 | tf_op jit(solution)/shard_map/product/pallas_call | solution.py:25
  189.7 16.6 %all-to-all-done.2 = f32[8,96,1024]{2,1,0:T(8,128)} async-done(((f32[8,96,1024]{2,1,0:T(8,128)}), f32[8,96,1024]{2,1,0:T(8,128)}, u32[]{:S(2)}, u32[]{:S(2)}) %all-to-all-start.2) | async-done | bytes 3145760 | tf_op jit(solution)/shard_map/all_to_all | solution.py:304
  206.3 3.6 all-to-all-start.3
  210.0 3.5 scatter.4
  217.0 25.5 %reduce-scatter.10.cloned.1.call-done = f32[1,2,96,1024]{3,2,1,0:T(8,128)} async-done(((f32[4,2,96,1024]{3,2,1,0:T(8,128)}), f32[1,2,96,1024]{3,2,1,0:T(8,128)}) %reduce-scatter.10.cloned.1.call-update) | async-done | bytes 786448
  247.2 15.8 %collective-permute-done.9.refs_4_.refs_2_ = f32[2,2,48,256]{3,2,1,0:T(8,128)S(1)} collective-permute-done((f32[2,2,48,256]{3,2,1,0:T(8,128)S(1)}, f32[2,2,48,256]{3,2,1,0:T(8,128)S(1)}, u32[]{:S(2)}, u32[]{:S(2)}) %collective-permute-start.9) | collective-permute-done | bytes 196640 | tf_op jit(solution)/shard_map/ppermute | solution.py:310
  265.3 5.8 %collective-permute-done.11.refs_6_.refs_4_ = f32[2,2,48,256]{3,2,1,0:T(8,128)S(1)} collective-permute-done((f32[2,2,48,256]{3,2,1,0:T(8,128)}, f32[2,2,48,256]{3,2,1,0:T(8,128)S(1)}, u32[]{:S(2)}, u32[]{:S(2)}) %collective-permute-start.11) | collective-permute-done | bytes 196640 | tf_op jit(solution)/shard_map/ppermute | solution.py:310
  276.8 12.2 %product.4.refs_10_ = f32[4,2,96,1024]{3,2,1,0:T(8,128)} custom-call(s32[1]{0:T(128)} %bitcast.refs_0_, f32[1,2,1024,1024]{3,2,1,0:T(8,128)} %refs_4_.5, f32[1,2,1024,1024]{3,2,1,0:T(8,128)} %refs_4_.5, f32[1,2,1024,1024]{3,2,1,0:T(8,128)} %refs_4_.5, f32[1,2,1024,1024]{3,2,1,0:T(8,128)} %refs_4_.5, f32[2,96,1024]{2,1,0:T(8,128)S(1)} %get-tuple-element.34.refs_2_.refs_5_, ...), custom_call_target="tpu_custom_call" | custom-call | flops 6442450944 | bytes 6291456 | tf_op jit(solution)/shard_map/product/pallas_call | solution.py:25
  291.1 4.6 all-to-all-start.4
  300.3 16.4 %all-to-all-done.4.refs_11_ = f32[8,2,48,256]{3,2,1,0:T(8,128)S(1)} async-done(((f32[8,2,48,256]{3,2,1,0:T(8,128)}), f32[8,2,48,256]{3,2,1,0:T(8,128)S(1)}, u32[]{:S(2)}, u32[]{:S(2)}) %all-to-all-start.4) | async-done | bytes 786464 | tf_op jit(solution)/shard_map/all_to_all | solution.py:304
  318.3 3.5 all-to-all-start.5
  324.2 13.2 %collective-permute-done.14.refs_8_ = f32[2,64,1024]{2,1,0:T(8,128)} collective-permute-done((f32[2,64,1024]{2,1,0:T(8,128)}, f32[2,64,1024]{2,1,0:T(8,128)}, u32[]{:S(2)}, u32[]{:S(2)}) %collective-permute-start.14) | collective-permute-done | bytes 524320 | tf_op jit(solution)/shard_map/ppermute | solution.py:310
  337.4 9.2 %product.5 = f32[4,2,64,1024]{3,2,1,0:T(8,128)} custom-call(s32[1]{0:T(128)} %bitcast.refs_0_, f32[1,2,1024,1024]{3,2,1,0:T(8,128)} %refs_4_.5, f32[1,2,1024,1024]{3,2,1,0:T(8,128)} %refs_4_.5, f32[1,2,1024,1024]{3,2,1,0:T(8,128)} %refs_4_.5, f32[1,2,1024,1024]{3,2,1,0:T(8,128)} %refs_4_.5, f32[2,64,1024]{2,1,0:T(8,128)S(1)} %get-tuple-element.42.refs_10_.refs_5_, ...), custom_call_target="tpu_custom_call" | custom-call | flops 4294967296 | bytes 4194304 | tf_op jit(solution)/shard_map/product/pallas_call | solution.py:25
  346.6 5.5 %reduce-scatter.12.cloned.1.call-done = f32[1,2,96,1024]{3,2,1,0:T(8,128)} async-done(((f32[4,2,96,1024]{3,2,1,0:T(8,128)}), f32[1,2,96,1024]{3,2,1,0:T(8,128)}) %reduce-scatter.12.cloned.1.call-update) | async-done | bytes 786448
  356.9 4.3 collective-permute-done.15.refs_2_
  361.2 4.2 collective-permute-done.16.refs_3_
  366.1 25.4 %all_to_all.51 = f32[8,2,48,256]{3,2,1,0:T(8,128)S(1)} all-to-all(f32[8,2,48,256]{3,2,1,0:T(8,128)S(1)} %bitcast.26), channel_id=1, replica_groups=mesh['ia'=8,'ka'=4] {'ia'}, dimensions={0} | all-to-all | bytes 1572864 | tf_op jit(solution)/shard_map/all_to_all | solution.py:304
  393.1 3.5 all-to-all-start.7
  403.6 4.4 collective-permute-done.19.refs_3_
  408.0 9.6 %all-to-all-done.7.refs_5_ = f32[8,2,48,256]{3,2,1,0:T(8,128)S(1)} async-done(((f32[8,2,48,256]{3,2,1,0:T(8,128)}), f32[8,2,48,256]{3,2,1,0:T(8,128)S(1)}, u32[]{:S(2)}, u32[]{:S(2)}) %all-to-all-start.7) | async-done | bytes 786464 | tf_op jit(solution)/shard_map/all_to_all | solution.py:304
  418.4 4.3 all-to-all-start.8
  422.8 15.3 %all-to-all-done.8 = f32[8,2,32,256]{3,2,1,0:T(8,128)} async-done(((f32[8,2,32,256]{3,2,1,0:T(8,128)}), f32[8,2,32,256]{3,2,1,0:T(8,128)}, u32[]{:S(2)}, u32[]{:S(2)}) %all-to-all-start.8) | async-done | bytes 524320 | tf_op jit(solution)/shard_map/all_to_all | solution.py:304
  441.7 17.8 %all_to_all.52.refs_6_ = f32[8,2,32,256]{3,2,1,0:T(8,128)S(1)} all-to-all(f32[8,2,32,256]{3,2,1,0:T(8,128)S(1)} %broadcast_select_fusion.2), channel_id=1, replica_groups=mesh['ia'=8,'ka'=4] {'ia'}, dimensions={0} | all-to-all | bytes 1048576 | tf_op jit(solution)/shard_map/all_to_all | solution.py:304
  (134 shorter events, 76.3 us)
Async XLA Ops:
  53.5 76.5 %all-to-all-start.1 = ((f32[8,96,1024]{2,1,0:T(8,128)}), f32[8,96,1024]{2,1,0:T(8,128)}, u32[]{:S(2)}, u32[]{:S(2)}) async-start(f32[8,96,1024]{2,1,0:T(8,128)} %bitcast.36), calls=%async_computation.1 | async-start | bytes 6291456 | tf_op jit(solution)/shard_map/all_to_all | solution.py:304
  60.3 31.6 %collective-permute-start = (f32[2,160,1024]{2,1,0:T(8,128)S(1)}, f32[2,160,1024]{2,1,0:T(8,128)S(1)}, u32[]{:S(2)}, u32[]{:S(2)}) collective-permute-start(f32[2,160,1024]{2,1,0:T(8,128)S(1)} %flip.5), channel_id=1, source_target_pairs={{0,1},{1,0},{2,3},{3,2},{4,5},{5,4},{6,7},{7,6},{8,9},{9,8},{10,11... | collective-permute-start | bytes 3932168 | tf_op jit(solution)/shard_map/ppermute | solution.py:310
  63.2 59.1 %collective-permute-start.1 = (f32[2,160,1024]{2,1,0:T(8,128)S(1)}, f32[2,160,1024]{2,1,0:T(8,128)S(1)}, u32[]{:S(2)}, u32[]{:S(2)}) collective-permute-start(f32[2,160,1024]{2,1,0:T(8,128)S(1)} %flip.6), channel_id=1, source_target_pairs={{0,2},{1,3},{2,0},{3,1},{4,6},{5,7},{6,4},{7,5},{8,10},{9,11},{10,... | collective-permute-start | bytes 3932168 | tf_op jit(solution)/shard_map/ppermute | solution.py:310
  65.8 56.5 %collective-permute-start.2 = (f32[2,160,1024]{2,1,0:T(8,128)S(1)}, f32[2,160,1024]{2,1,0:T(8,128)S(1)}, u32[]{:S(2)}, u32[]{:S(2)}) collective-permute-start(f32[2,160,1024]{2,1,0:T(8,128)S(1)} %flip.7), channel_id=1, source_target_pairs={{0,3},{1,2},{2,1},{3,0},{4,7},{5,6},{6,5},{7,4},{8,11},{9,10},{10,... | collective-permute-start | bytes 3932168 | tf_op jit(solution)/shard_map/ppermute | solution.py:310
  69.8 52.5 %copy-start = (f32[2,160,1024]{2,1,0:T(8,128)}, f32[2,160,1024]{2,1,0:T(8,128)S(1)}, u32[]{:S(2)}) copy-start(f32[2,160,1024]{2,1,0:T(8,128)S(1)} %flip.4.refs_1_) | copy-start | bytes 3932164
  130.1 76.3 %all-to-all-start.2 = ((f32[8,96,1024]{2,1,0:T(8,128)}), f32[8,96,1024]{2,1,0:T(8,128)}, u32[]{:S(2)}, u32[]{:S(2)}) async-start(f32[8,96,1024]{2,1,0:T(8,128)} %bitcast.35), calls=%async_computation.2 | async-start | bytes 6291456 | tf_op jit(solution)/shard_map/all_to_all | solution.py:304
  134.8 107.8 %reduce-scatter.10.cloned.1.call-start = ((), (), s32[]{:S(2)}) async-start(), calls=%async_computation.13 | async-start | bytes 3932160
  141.0 20.4 %collective-permute-start.3 = (f32[2,96,1024]{2,1,0:T(8,128)S(1)}, f32[2,96,1024]{2,1,0:T(8,128)S(1)}, u32[]{:S(2)}, u32[]{:S(2)}) collective-permute-start(f32[2,96,1024]{2,1,0:T(8,128)S(1)} %get-tuple-element.31), channel_id=1, source_target_pairs={{0,1},{1,0},{2,3},{3,2},{4,5},{5,4},{6,7},{7,6},{8,9},{9,8},{10,11... | collective-permute-start | bytes 2359304 | tf_op jit(solution)/shard_map/ppermute | solution.py:310
  141.9 36.3 %collective-permute-start.4 = (f32[2,96,1024]{2,1,0:T(8,128)S(1)}, f32[2,96,1024]{2,1,0:T(8,128)S(1)}, u32[]{:S(2)}, u32[]{:S(2)}) collective-permute-start(f32[2,96,1024]{2,1,0:T(8,128)S(1)} %get-tuple-element.32), channel_id=1, source_target_pairs={{0,2},{1,3},{2,0},{3,1},{4,6},{5,7},{6,4},{7,5},{8,10},{9,11},{10,... | collective-permute-start | bytes 2359304 | tf_op jit(solution)/shard_map/ppermute | solution.py:310
  142.5 35.8 %collective-permute-start.5 = (f32[2,96,1024]{2,1,0:T(8,128)S(1)}, f32[2,96,1024]{2,1,0:T(8,128)S(1)}, u32[]{:S(2)}, u32[]{:S(2)}) collective-permute-start(f32[2,96,1024]{2,1,0:T(8,128)S(1)} %get-tuple-element.33), channel_id=1, source_target_pairs={{0,3},{1,2},{2,1},{3,0},{4,7},{5,6},{6,5},{7,4},{8,11},{9,10},{10,... | collective-permute-start | bytes 2359304 | tf_op jit(solution)/shard_map/ppermute | solution.py:310
  206.3 58.3 %all-to-all-start.3 = ((f32[8,64,1024]{2,1,0:T(8,128)}), f32[8,64,1024]{2,1,0:T(8,128)S(1)}, u32[]{:S(2)}, u32[]{:S(2)}) async-start(f32[8,64,1024]{2,1,0:T(8,128)} %bitcast.8), calls=%async_computation.3 | async-start | bytes 4194304 | tf_op jit(solution)/shard_map/all_to_all | solution.py:304
  210.0 142.2 %reduce-scatter.12.cloned.1.call-start = ((), (), s32[]{:S(2)}) async-start(), calls=%async_computation.14 | async-start | bytes 3932160
  213.5 63.3 %collective-permute-start.6 = (f32[2,96,1024]{2,1,0:T(8,128)}, f32[2,96,1024]{2,1,0:T(8,128)}, u32[]{:S(2)}, u32[]{:S(2)}) collective-permute-start(f32[2,96,1024]{2,1,0:T(8,128)} %get-tuple-element.35), channel_id=1, source_target_pairs={{0,1},{1,0},{2,3},{3,2},{4,5},{5,4},{6,7},{7,6},{8,9},{9,8},{10,11... | collective-permute-start | bytes 2359304 | tf_op jit(solution)/shard_map/ppermute | solution.py:310
  214.4 62.3 %collective-permute-start.7 = (f32[2,96,1024]{2,1,0:T(8,128)}, f32[2,96,1024]{2,1,0:T(8,128)}, u32[]{:S(2)}, u32[]{:S(2)}) collective-permute-start(f32[2,96,1024]{2,1,0:T(8,128)} %get-tuple-element.36), channel_id=1, source_target_pairs={{0,2},{1,3},{2,0},{3,1},{4,6},{5,7},{6,4},{7,5},{8,10},{9,11},{10,... | collective-permute-start | bytes 2359304 | tf_op jit(solution)/shard_map/ppermute | solution.py:310
  215.0 61.8 %collective-permute-start.8 = (f32[2,96,1024]{2,1,0:T(8,128)}, f32[2,96,1024]{2,1,0:T(8,128)}, u32[]{:S(2)}, u32[]{:S(2)}) collective-permute-start(f32[2,96,1024]{2,1,0:T(8,128)} %get-tuple-element.37), channel_id=1, source_target_pairs={{0,3},{1,2},{2,1},{3,0},{4,7},{5,6},{6,5},{7,4},{8,11},{9,10},{10,... | collective-permute-start | bytes 2359304 | tf_op jit(solution)/shard_map/ppermute | solution.py:310
  245.2 17.9 %collective-permute-start.9 = (f32[2,2,48,256]{3,2,1,0:T(8,128)S(1)}, f32[2,2,48,256]{3,2,1,0:T(8,128)S(1)}, u32[]{:S(2)}, u32[]{:S(2)}) collective-permute-start(f32[2,2,48,256]{3,2,1,0:T(8,128)S(1)} %get-tuple-element.39), channel_id=1, source_target_pairs={{0,1},{1,0},{2,3},{3,2},{4,5},{5,4},{6,7},{7,6},{8,9},{9,8},{10,11... | collective-permute-start | bytes 589832 | tf_op jit(solution)/shard_map/ppermute | solution.py:310
  246.9 17.7 %collective-permute-start.10 = (f32[2,2,48,256]{3,2,1,0:T(8,128)}, f32[2,2,48,256]{3,2,1,0:T(8,128)S(1)}, u32[]{:S(2)}, u32[]{:S(2)}) collective-permute-start(f32[2,2,48,256]{3,2,1,0:T(8,128)} %get-tuple-element.40), channel_id=1, source_target_pairs={{0,2},{1,3},{2,0},{3,1},{4,6},{5,7},{6,4},{7,5},{8,10},{9,11},{10,... | collective-permute-start | bytes 589832 | tf_op jit(solution)/shard_map/ppermute | solution.py:310
  263.7 7.4 %collective-permute-start.11 = (f32[2,2,48,256]{3,2,1,0:T(8,128)}, f32[2,2,48,256]{3,2,1,0:T(8,128)S(1)}, u32[]{:S(2)}, u32[]{:S(2)}) collective-permute-start(f32[2,2,48,256]{3,2,1,0:T(8,128)} %get-tuple-element.41), channel_id=1, source_target_pairs={{0,3},{1,2},{2,1},{3,0},{4,7},{5,6},{6,5},{7,4},{8,11},{9,10},{10,... | collective-permute-start | bytes 589832 | tf_op jit(solution)/shard_map/ppermute | solution.py:310
  291.1 25.6 %all-to-all-start.4 = ((f32[8,2,48,256]{3,2,1,0:T(8,128)}), f32[8,2,48,256]{3,2,1,0:T(8,128)S(1)}, u32[]{:S(2)}, u32[]{:S(2)}) async-start(f32[8,2,48,256]{3,2,1,0:T(8,128)} %bitcast.11), calls=%async_computation.4 | async-start | bytes 1572864 | tf_op jit(solution)/shard_map/all_to_all | solution.py:304
  296.7 26.3 %collective-permute-start.12 = (f32[2,64,1024]{2,1,0:T(8,128)}, f32[2,64,1024]{2,1,0:T(8,128)S(1)}, u32[]{:S(2)}, u32[]{:S(2)}) collective-permute-start(f32[2,64,1024]{2,1,0:T(8,128)} %get-tuple-element.43), channel_id=1, source_target_pairs={{0,1},{1,0},{2,3},{3,2},{4,5},{5,4},{6,7},{7,6},{8,9},{9,8},{10,11... | collective-permute-start | bytes 1572872 | tf_op jit(solution)/shard_map/ppermute | solution.py:310
  297.7 26.6 %collective-permute-start.13 = (f32[2,64,1024]{2,1,0:T(8,128)}, f32[2,64,1024]{2,1,0:T(8,128)S(1)}, u32[]{:S(2)}, u32[]{:S(2)}) collective-permute-start(f32[2,64,1024]{2,1,0:T(8,128)} %get-tuple-element.44), channel_id=1, source_target_pairs={{0,2},{1,3},{2,0},{3,1},{4,6},{5,7},{6,4},{7,5},{8,10},{9,11},{10,... | collective-permute-start | bytes 1572872 | tf_op jit(solution)/shard_map/ppermute | solution.py:310
  298.2 39.2 %collective-permute-start.14 = (f32[2,64,1024]{2,1,0:T(8,128)}, f32[2,64,1024]{2,1,0:T(8,128)}, u32[]{:S(2)}, u32[]{:S(2)}) collective-permute-start(f32[2,64,1024]{2,1,0:T(8,128)} %get-tuple-element.45), channel_id=1, source_target_pairs={{0,3},{1,2},{2,1},{3,0},{4,7},{5,6},{6,5},{7,4},{8,11},{9,10},{10,... | collective-permute-start | bytes 1572872 | tf_op jit(solution)/shard_map/ppermute | solution.py:310
  318.3 38.6 %all-to-all-start.5 = ((f32[8,2,48,256]{3,2,1,0:T(8,128)}), f32[8,2,48,256]{3,2,1,0:T(8,128)S(1)}, u32[]{:S(2)}, u32[]{:S(2)}) async-start(f32[8,2,48,256]{3,2,1,0:T(8,128)} %bitcast.37), calls=%async_computation.5 | async-start | bytes 1572864 | tf_op jit(solution)/shard_map/all_to_all | solution.py:304
  321.8 74.9 %reduce-scatter.14.cloned.1.call-start = ((), (), s32[]{:S(2)}) async-start(), calls=%async_computation.15 | async-start | bytes 2621440
  353.3 7.9 %collective-permute-start.15 = (f32[2,2,48,256]{3,2,1,0:T(8,128)S(1)}, f32[2,2,48,256]{3,2,1,0:T(8,128)S(1)}, u32[]{:S(2)}, u32[]{:S(2)}) collective-permute-start(f32[2,2,48,256]{3,2,1,0:T(8,128)S(1)} %get-tuple-element.47), channel_id=1, source_target_pairs={{0,1},{1,0},{2,3},{3,2},{4,5},{5,4},{6,7},{7,6},{8,9},{9,8},{10,11... | collective-permute-start | bytes 589832 | tf_op jit(solution)/shard_map/ppermute | solution.py:310
  354.8 10.6 %collective-permute-start.16 = (f32[2,2,48,256]{3,2,1,0:T(8,128)S(1)}, f32[2,2,48,256]{3,2,1,0:T(8,128)S(1)}, u32[]{:S(2)}, u32[]{:S(2)}) collective-permute-start(f32[2,2,48,256]{3,2,1,0:T(8,128)S(1)} %get-tuple-element.48), channel_id=1, source_target_pairs={{0,2},{1,3},{2,0},{3,1},{4,6},{5,7},{6,4},{7,5},{8,10},{9,11},{10,... | collective-permute-start | bytes 589832 | tf_op jit(solution)/shard_map/ppermute | solution.py:310
  355.4 10.7 %collective-permute-start.17 = (f32[2,2,48,256]{3,2,1,0:T(8,128)S(1)}, f32[2,2,48,256]{3,2,1,0:T(8,128)S(1)}, u32[]{:S(2)}, u32[]{:S(2)}) collective-permute-start(f32[2,2,48,256]{3,2,1,0:T(8,128)S(1)} %get-tuple-element.49), channel_id=1, source_target_pairs={{0,3},{1,2},{2,1},{3,0},{4,7},{5,6},{6,5},{7,4},{8,11},{9,10},{10,... | collective-permute-start | bytes 589832 | tf_op jit(solution)/shard_map/ppermute | solution.py:310
  393.1 24.4 %all-to-all-start.7 = ((f32[8,2,48,256]{3,2,1,0:T(8,128)}), f32[8,2,48,256]{3,2,1,0:T(8,128)S(1)}, u32[]{:S(2)}, u32[]{:S(2)}) async-start(f32[8,2,48,256]{3,2,1,0:T(8,128)} %bitcast.17), calls=%async_computation.7 | async-start | bytes 1572864 | tf_op jit(solution)/shard_map/all_to_all | solution.py:304
  397.8 5.8 %collective-permute-start.18 = (f32[2,2,32,256]{3,2,1,0:T(8,128)S(1)}, f32[2,2,32,256]{3,2,1,0:T(8,128)S(1)}, u32[]{:S(2)}, u32[]{:S(2)}) collective-permute-start(f32[2,2,32,256]{3,2,1,0:T(8,128)S(1)} %get-tuple-element.51), channel_id=1, source_target_pairs={{0,1},{1,0},{2,3},{3,2},{4,5},{5,4},{6,7},{7,6},{8,9},{9,8},{10,11... | collective-permute-start | bytes 393224 | tf_op jit(solution)/shard_map/ppermute | solution.py:310
  398.7 9.3 %collective-permute-start.19 = (f32[2,2,32,256]{3,2,1,0:T(8,128)S(1)}, f32[2,2,32,256]{3,2,1,0:T(8,128)S(1)}, u32[]{:S(2)}, u32[]{:S(2)}) collective-permute-start(f32[2,2,32,256]{3,2,1,0:T(8,128)S(1)} %get-tuple-element.52), channel_id=1, source_target_pairs={{0,2},{1,3},{2,0},{3,1},{4,6},{5,7},{6,4},{7,5},{8,10},{9,11},{10,... | collective-permute-start | bytes 393224 | tf_op jit(solution)/shard_map/ppermute | solution.py:310
  401.4 6.6 %collective-permute-start.20 = (f32[2,2,32,256]{3,2,1,0:T(8,128)S(1)}, f32[2,2,32,256]{3,2,1,0:T(8,128)S(1)}, u32[]{:S(2)}, u32[]{:S(2)}) collective-permute-start(f32[2,2,32,256]{3,2,1,0:T(8,128)S(1)} %get-tuple-element.53), channel_id=1, source_target_pairs={{0,3},{1,2},{2,1},{3,0},{4,7},{5,6},{6,5},{7,4},{8,11},{9,10},{10,... | collective-permute-start | bytes 393224 | tf_op jit(solution)/shard_map/ppermute | solution.py:310
  418.4 19.6 %all-to-all-start.8 = ((f32[8,2,32,256]{3,2,1,0:T(8,128)}), f32[8,2,32,256]{3,2,1,0:T(8,128)}, u32[]{:S(2)}, u32[]{:S(2)}) async-start(f32[8,2,32,256]{3,2,1,0:T(8,128)} %bitcast.33), calls=%async_computation.8 | async-start | bytes 1048576 | tf_op jit(solution)/shard_map/all_to_all | solution.py:304
  (28 other events, 140.8 us)
Sparse Core Ops, SparseCore 0:
  189.8 52.6 reduce-scatter.9
  289.1 62.9 reduce-scatter.11
  355.1 36.7 reduce-scatter.13

commit v16 on v15

--- a/solution.py
+++ b/solution.py
@@ -365,9 +365,9 @@
     begun, own[0] = multiply(0, early, [])
     turned, middle = turn(1, hop(1), [begun])
     leading = send(GROUPS[0])
+    begun, own[1] = multiply(1, middle, leading)
     crossed = hop(2)
-    turned, late = turn(2, crossed, [turned, *leading])
-    begun, own[1] = multiply(1, middle, [turned])
+    turned, late = turn(2, crossed, [begun])
     met = meet(gather(place, leading, [crossed]))
     _, own[2] = multiply(2, late, [begun, met])
     delivered = [deliver(met)]

time: 470 us -> 536 us (1.14)
  blocking collectives: 84.8 us -> 212 us
  waiting for transfers between devices: 222 us -> 179 us
  starting transfers between devices: 53.7 us -> 44.8 us
  local copies, waits for them, and re-layouts: 22.3 us -> 15.8 us
    all_to_all x3 -> x5, blocking collectives: 84.8 us -> 212 us  [swap(): return lax.all_to_all(array, axis, split_axis=0, concat_axis=0, tiled=True)]
    unnamed x6, waiting for transfers between devices: 31.1 us -> 0.09 us
    all_to_all x7 -> x5, waiting for transfers between devices: 60.5 us -> 47.7 us  [swap(): return lax.all_to_all(array, axis, split_axis=0, concat_axis=0, tiled=True)]
    all_to_all x7 -> x5, starting transfers between devices: 29.2 us -> 19.8 us  [swap(): return lax.all_to_all(array, axis, split_axis=0, concat_axis=0, tiled=True)]
    unnamed x59 -> x29, local copies, waits for them, and re-layouts: 17.6 us -> 11.2 us
  transfers between devices with their start and end apart: 31 -> 29, of which waited for: 21 -> 19; matrix products, arithmetic and copies ran while one was open for 1% -> 1% of each run, Pallas kernels for 10% -> 6%
where the time goes in v16:
time: 536 us; the launch traced here: 535 us
  blocking collectives  212 us (40%)
  waiting for transfers between devices  179 us (33%)
  Pallas kernels  67.4 us (13%)
  starting transfers between devices  44.8 us (8%)
  local copies, waits for them, and re-layouts  15.8 us (3%)
  between operations  13.4 us (2%)
    all_to_all x5, blocking collectives, swap(): return lax.all_to_all(array, axis, split_axis=0, concat_axis=0, tiled=True)  212 us
    ppermute x21, waiting for transfers between devices, spread(): lax.ppermute(pieces[e], 'ka', [(q, q ^ e) for q in range(count)])  131 us
    pallas_call x21, Pallas kernels, call(): pl.pallas_call(trimmed, grid_spec=pltpu.PrefetchScalarGridSpec(num_scalar...  67.4 us
    all_to_all x5, waiting for transfers between devices, swap(): return lax.all_to_all(array, axis, split_axis=0, concat_axis=0, tiled=True)  47.7 us
    ppermute x21, starting transfers between devices, spread(): lax.ppermute(pieces[e], 'ka', [(q, q ^ e) for q in range(count)])  24.9 us
    all_to_all x5, starting transfers between devices, swap(): return lax.all_to_all(array, axis, split_axis=0, concat_axis=0, tiled=True)  19.8 us
    unnamed x29, local copies, waits for them, and re-layouts  11.2 us
  transfers between devices with their start and end apart: 29, of which 19 were waited for; matrix products, arithmetic and copies ran while one was open for 1% of the time, Pallas kernels for 6%

profile of v16, /device:TPU:0, one launch (start us, length us, event | category | flops | bytes accessed | tf_op | source)
XLA Modules:
  0.0 535.0 jit_solution(4249366065377160260)
XLA Ops:
  6.5 5.3 first_flip.1.refs_2_
  11.8 41.7 %all_to_all.50 = f32[4,2,96,1024]{3,2,1,0:T(8,128)} all-to-all(f32[4,2,96,1024]{3,2,1,0:T(8,128)S(1)} %first_flip.1.refs_2_), channel_id=1, replica_groups=mesh['ia'=8,'ka'=4] {'ka'}, dimensions={0} | all-to-all | bytes 6291456 | tf_op jit(solution)/shard_map/all_to_all | solution.py:304
  53.5 4.9 all-to-all-start.1
  69.9 8.7 %mask.1.refs_5_.refs_9_ = bf16[2,2,1024,1024]{3,2,1,0:T(8,128)(2,1)} custom-call(s32[2,2,8,8]{3,2,1,0:T(8,128)S(1)} %bitcast.35, bf16[1,2,2,1024,1024]{4,3,2,1,0:T(8,128)(2,1)} %refs_1_.14, f32[4,2,96,1024]{3,2,1,0:T(8,128)S(1)} %first_flip.1.refs_2_), custom_call_target="tpu_custom_call" | custom-call | bytes 16777216 | tf_op jit(solution)/shard_map/mask/pallas_call | solution.py:25
  78.7 13.4 %collective-permute-done.refs_2_ = f32[2,160,1024]{2,1,0:T(8,128)S(1)} collective-permute-done((f32[2,160,1024]{2,1,0:T(8,128)S(1)}, f32[2,160,1024]{2,1,0:T(8,128)S(1)}, u32[]{:S(2)}, u32[]{:S(2)}) %collective-permute-start) | collective-permute-done | bytes 1310752 | tf_op jit(solution)/shard_map/ppermute | solution.py:310
  92.0 30.3 %collective-permute-done.1.refs_3_ = f32[2,160,1024]{2,1,0:T(8,128)S(1)} collective-permute-done((f32[2,160,1024]{2,1,0:T(8,128)S(1)}, f32[2,160,1024]{2,1,0:T(8,128)S(1)}, u32[]{:S(2)}, u32[]{:S(2)}) %collective-permute-start.1) | collective-permute-done | bytes 1310752 | tf_op jit(solution)/shard_map/ppermute | solution.py:310
  125.5 4.5 all-to-all-done.1
  137.3 17.0 %collective-permute-done.3.refs_6_ = f32[2,96,1024]{2,1,0:T(8,128)S(1)} collective-permute-done((f32[2,96,1024]{2,1,0:T(8,128)S(1)}, f32[2,96,1024]{2,1,0:T(8,128)S(1)}, u32[]{:S(2)}, u32[]{:S(2)}) %collective-permute-start.3) | collective-permute-done | bytes 786464 | tf_op jit(solution)/shard_map/ppermute | solution.py:310
  154.3 16.1 %collective-permute-done.4.refs_7_ = f32[2,96,1024]{2,1,0:T(8,128)S(1)} collective-permute-done((f32[2,96,1024]{2,1,0:T(8,128)S(1)}, f32[2,96,1024]{2,1,0:T(8,128)S(1)}, u32[]{:S(2)}, u32[]{:S(2)}) %collective-permute-start.4) | collective-permute-done | bytes 786464 | tf_op jit(solution)/shard_map/ppermute | solution.py:310
  170.4 11.6 %product.3.refs_2_ = f32[4,2,96,1024]{3,2,1,0:T(8,128)} custom-call(s32[1]{0:T(128)} %bitcast.refs_0_, f32[1,2,1024,1024]{3,2,1,0:T(8,128)} %refs_4_.5, f32[1,2,1024,1024]{3,2,1,0:T(8,128)} %refs_4_.5, f32[1,2,1024,1024]{3,2,1,0:T(8,128)} %refs_4_.5, f32[1,2,1024,1024]{3,2,1,0:T(8,128)} %refs_4_.5, f32[2,96,1024]{2,1,0:T(8,128)S(1)} %get-tuple-element.30.refs_5_, ...), custom_call_target="tpu_custom_call" | custom-call | flops 6442450944 | bytes 6291456 | tf_op jit(solution)/shard_map/product/pallas_call | solution.py:25
  183.9 74.7 %all_to_all.51 = f32[8,96,1024]{2,1,0:T(8,128)} all-to-all(f32[8,96,1024]{2,1,0:T(8,128)S(1)} %bitcast.36), channel_id=1, replica_groups=mesh['ia'=8,'ka'=4] {'ia'}, dimensions={0} | all-to-all | bytes 6291456 | tf_op jit(solution)/shard_map/all_to_all | solution.py:304
  258.6 3.2 scatter.4
  268.6 13.7 %collective-permute-done.6.refs_6_ = f32[2,96,1024]{2,1,0:T(8,128)S(1)} collective-permute-done((f32[2,96,1024]{2,1,0:T(8,128)S(1)}, f32[2,96,1024]{2,1,0:T(8,128)S(1)}, u32[]{:S(2)}, u32[]{:S(2)}) %collective-permute-start.6) | collective-permute-done | bytes 786464 | tf_op jit(solution)/shard_map/ppermute | solution.py:310
  283.8 16.8 %collective-permute-done.7.refs_7_ = f32[2,96,1024]{2,1,0:T(8,128)} collective-permute-done((f32[2,96,1024]{2,1,0:T(8,128)}, f32[2,96,1024]{2,1,0:T(8,128)}, u32[]{:S(2)}, u32[]{:S(2)}) %collective-permute-start.7) | collective-permute-done | bytes 786464 | tf_op jit(solution)/shard_map/ppermute | solution.py:310
  300.6 2.8 collective-permute-done.9.refs_11_.refs_2_
  303.4 3.6 collective-permute-done.10.refs_12_.refs_3_
  307.1 11.9 %product.4.refs_2_.refs_10_ = f32[4,2,96,1024]{3,2,1,0:T(8,128)} custom-call(s32[1]{0:T(128)} %bitcast.refs_0_, f32[1,2,1024,1024]{3,2,1,0:T(8,128)} %refs_4_.5, f32[1,2,1024,1024]{3,2,1,0:T(8,128)} %refs_4_.5, f32[1,2,1024,1024]{3,2,1,0:T(8,128)} %refs_4_.5, f32[1,2,1024,1024]{3,2,1,0:T(8,128)} %refs_4_.5, f32[2,96,1024]{2,1,0:T(8,128)S(1)} %get-tuple-element.34.refs_5_, ...), custom_call_target="tpu_custom_call" | custom-call | flops 6442450944 | bytes 6291456 | tf_op jit(solution)/shard_map/product/pallas_call | solution.py:25
  320.6 52.0 %all_to_all.52 = f32[8,64,1024]{2,1,0:T(8,128)S(1)} all-to-all(f32[8,64,1024]{2,1,0:T(8,128)S(1)} %bitcast.23), channel_id=1, replica_groups=mesh['ia'=8,'ka'=4] {'ia'}, dimensions={0} | all-to-all | bytes 4194304 | tf_op jit(solution)/shard_map/all_to_all | solution.py:304
  374.9 3.5 all-to-all-start.4
  384.9 14.4 %all-to-all-done.4.refs_11_ = f32[8,2,48,256]{3,2,1,0:T(8,128)S(1)} async-done(((f32[8,2,48,256]{3,2,1,0:T(8,128)}), f32[8,2,48,256]{3,2,1,0:T(8,128)S(1)}, u32[]{:S(2)}, u32[]{:S(2)}) %all-to-all-start.4) | async-done | bytes 786464 | tf_op jit(solution)/shard_map/all_to_all | solution.py:304
  400.9 3.5 all-to-all-start.5
  404.6 3.2 collective-permute-done.13.refs_7_
  407.8 9.2 %product.5 = f32[4,2,64,1024]{3,2,1,0:T(8,128)} custom-call(s32[1]{0:T(128)} %bitcast.refs_0_, f32[1,2,1024,1024]{3,2,1,0:T(8,128)} %refs_4_.5, f32[1,2,1024,1024]{3,2,1,0:T(8,128)} %refs_4_.5, f32[1,2,1024,1024]{3,2,1,0:T(8,128)} %refs_4_.5, f32[1,2,1024,1024]{3,2,1,0:T(8,128)} %refs_4_.5, f32[2,64,1024]{2,1,0:T(8,128)S(1)} %get-tuple-element.42.refs_5_, ...), custom_call_target="tpu_custom_call" | custom-call | flops 4294967296 | bytes 4194304 | tf_op jit(solution)/shard_map/product/pallas_call | solution.py:25
  421.8 3.6 all-to-all-done.5.refs_5_.refs_4_
  428.3 4.9 collective-permute-done.17.refs_4_
  433.2 25.4 %all_to_all.53 = f32[8,2,48,256]{3,2,1,0:T(8,128)S(1)} all-to-all(f32[8,2,48,256]{3,2,1,0:T(8,128)S(1)} %bitcast.27), channel_id=1, replica_groups=mesh['ia'=8,'ka'=4] {'ia'}, dimensions={0} | all-to-all | bytes 1572864 | tf_op jit(solution)/shard_map/all_to_all | solution.py:304
  460.2 3.5 all-to-all-start.7
  471.0 3.7 collective-permute-done.19.refs_3_
  474.7 9.9 %all-to-all-done.7.refs_5_ = f32[8,2,48,256]{3,2,1,0:T(8,128)S(1)} async-done(((f32[8,2,48,256]{3,2,1,0:T(8,128)}), f32[8,2,48,256]{3,2,1,0:T(8,128)S(1)}, u32[]{:S(2)}, u32[]{:S(2)}) %all-to-all-start.7) | async-done | bytes 786464 | tf_op jit(solution)/shard_map/all_to_all | solution.py:304
  485.5 4.3 all-to-all-start.8
  489.9 15.3 %all-to-all-done.8 = f32[8,2,32,256]{3,2,1,0:T(8,128)} async-done(((f32[8,2,32,256]{3,2,1,0:T(8,128)}), f32[8,2,32,256]{3,2,1,0:T(8,128)}, u32[]{:S(2)}, u32[]{:S(2)}) %all-to-all-start.8) | async-done | bytes 524320 | tf_op jit(solution)/shard_map/all_to_all | solution.py:304
  508.7 17.8 %all_to_all.54.refs_6_ = f32[8,2,32,256]{3,2,1,0:T(8,128)S(1)} all-to-all(f32[8,2,32,256]{3,2,1,0:T(8,128)S(1)} %broadcast_select_fusion.2), channel_id=1, replica_groups=mesh['ia'=8,'ka'=4] {'ia'}, dimensions={0} | all-to-all | bytes 1048576 | tf_op jit(solution)/shard_map/all_to_all | solution.py:304
  (102 shorter events, 67.1 us)
Async XLA Ops:
  53.5 76.5 %all-to-all-start.1 = ((f32[8,96,1024]{2,1,0:T(8,128)}), f32[8,96,1024]{2,1,0:T(8,128)}, u32[]{:S(2)}, u32[]{:S(2)}) async-start(f32[8,96,1024]{2,1,0:T(8,128)} %bitcast.37), calls=%async_computation.1 | async-start | bytes 6291456 | tf_op jit(solution)/shard_map/all_to_all | solution.py:304
  58.4 206.9 %reduce-scatter.10.cloned.1.call-start = ((), (), s32[]{:S(2)}) async-start(), calls=%async_computation.13 | async-start | bytes 3932160
  60.4 31.6 %collective-permute-start = (f32[2,160,1024]{2,1,0:T(8,128)S(1)}, f32[2,160,1024]{2,1,0:T(8,128)S(1)}, u32[]{:S(2)}, u32[]{:S(2)}) collective-permute-start(f32[2,160,1024]{2,1,0:T(8,128)S(1)} %flip.5), channel_id=1, source_target_pairs={{0,1},{1,0},{2,3},{3,2},{4,5},{5,4},{6,7},{7,6},{8,9},{9,8},{10,11... | collective-permute-start | bytes 3932168 | tf_op jit(solution)/shard_map/ppermute | solution.py:310
  63.3 59.0 %collective-permute-start.1 = (f32[2,160,1024]{2,1,0:T(8,128)S(1)}, f32[2,160,1024]{2,1,0:T(8,128)S(1)}, u32[]{:S(2)}, u32[]{:S(2)}) collective-permute-start(f32[2,160,1024]{2,1,0:T(8,128)S(1)} %flip.6), channel_id=1, source_target_pairs={{0,2},{1,3},{2,0},{3,1},{4,6},{5,7},{6,4},{7,5},{8,10},{9,11},{10,... | collective-permute-start | bytes 3932168 | tf_op jit(solution)/shard_map/ppermute | solution.py:310
  65.9 56.4 %collective-permute-start.2 = (f32[2,160,1024]{2,1,0:T(8,128)S(1)}, f32[2,160,1024]{2,1,0:T(8,128)S(1)}, u32[]{:S(2)}, u32[]{:S(2)}) collective-permute-start(f32[2,160,1024]{2,1,0:T(8,128)S(1)} %flip.7), channel_id=1, source_target_pairs={{0,3},{1,2},{2,1},{3,0},{4,7},{5,6},{6,5},{7,4},{8,11},{9,10},{10,... | collective-permute-start | bytes 3932168 | tf_op jit(solution)/shard_map/ppermute | solution.py:310
  133.7 20.5 %collective-permute-start.3 = (f32[2,96,1024]{2,1,0:T(8,128)S(1)}, f32[2,96,1024]{2,1,0:T(8,128)S(1)}, u32[]{:S(2)}, u32[]{:S(2)}) collective-permute-start(f32[2,96,1024]{2,1,0:T(8,128)S(1)} %get-tuple-element.31), channel_id=1, source_target_pairs={{0,1},{1,0},{2,3},{3,2},{4,5},{5,4},{6,7},{7,6},{8,9},{9,8},{10,11... | collective-permute-start | bytes 2359304 | tf_op jit(solution)/shard_map/ppermute | solution.py:310
  134.7 35.7 %collective-permute-start.4 = (f32[2,96,1024]{2,1,0:T(8,128)S(1)}, f32[2,96,1024]{2,1,0:T(8,128)S(1)}, u32[]{:S(2)}, u32[]{:S(2)}) collective-permute-start(f32[2,96,1024]{2,1,0:T(8,128)S(1)} %get-tuple-element.32), channel_id=1, source_target_pairs={{0,2},{1,3},{2,0},{3,1},{4,6},{5,7},{6,4},{7,5},{8,10},{9,11},{10,... | collective-permute-start | bytes 2359304 | tf_op jit(solution)/shard_map/ppermute | solution.py:310
  135.3 35.1 %collective-permute-start.5 = (f32[2,96,1024]{2,1,0:T(8,128)S(1)}, f32[2,96,1024]{2,1,0:T(8,128)S(1)}, u32[]{:S(2)}, u32[]{:S(2)}) collective-permute-start(f32[2,96,1024]{2,1,0:T(8,128)S(1)} %get-tuple-element.33), channel_id=1, source_target_pairs={{0,3},{1,2},{2,1},{3,0},{4,7},{5,6},{6,5},{7,4},{8,11},{9,10},{10,... | collective-permute-start | bytes 2359304 | tf_op jit(solution)/shard_map/ppermute | solution.py:310
  182.0 235.0 %reduce-scatter.12.cloned.1.call-start = ((), (), s32[]{:S(2)}) async-start(), calls=%async_computation.14 | async-start | bytes 3932160
  261.8 20.5 %collective-permute-start.6 = (f32[2,96,1024]{2,1,0:T(8,128)S(1)}, f32[2,96,1024]{2,1,0:T(8,128)S(1)}, u32[]{:S(2)}, u32[]{:S(2)}) collective-permute-start(f32[2,96,1024]{2,1,0:T(8,128)S(1)} %get-tuple-element.35), channel_id=1, source_target_pairs={{0,1},{1,0},{2,3},{3,2},{4,5},{5,4},{6,7},{7,6},{8,9},{9,8},{10,11... | collective-permute-start | bytes 2359304 | tf_op jit(solution)/shard_map/ppermute | solution.py:310
  262.9 37.6 %collective-permute-start.7 = (f32[2,96,1024]{2,1,0:T(8,128)}, f32[2,96,1024]{2,1,0:T(8,128)}, u32[]{:S(2)}, u32[]{:S(2)}) collective-permute-start(f32[2,96,1024]{2,1,0:T(8,128)} %get-tuple-element.36), channel_id=1, source_target_pairs={{0,2},{1,3},{2,0},{3,1},{4,6},{5,7},{6,4},{7,5},{8,10},{9,11},{10,... | collective-permute-start | bytes 2359304 | tf_op jit(solution)/shard_map/ppermute | solution.py:310
  263.8 36.7 %collective-permute-start.8 = (f32[2,96,1024]{2,1,0:T(8,128)}, f32[2,96,1024]{2,1,0:T(8,128)}, u32[]{:S(2)}, u32[]{:S(2)}) collective-permute-start(f32[2,96,1024]{2,1,0:T(8,128)} %get-tuple-element.37), channel_id=1, source_target_pairs={{0,3},{1,2},{2,1},{3,0},{4,7},{5,6},{6,5},{7,4},{8,11},{9,10},{10,... | collective-permute-start | bytes 2359304 | tf_op jit(solution)/shard_map/ppermute | solution.py:310
  266.5 36.9 %collective-permute-start.9 = (f32[2,2,48,256]{3,2,1,0:T(8,128)S(1)}, f32[2,2,48,256]{3,2,1,0:T(8,128)S(1)}, u32[]{:S(2)}, u32[]{:S(2)}) collective-permute-start(f32[2,2,48,256]{3,2,1,0:T(8,128)S(1)} %get-tuple-element.39), channel_id=1, source_target_pairs={{0,1},{1,0},{2,3},{3,2},{4,5},{5,4},{6,7},{7,6},{8,9},{9,8},{10,11... | collective-permute-start | bytes 589832 | tf_op jit(solution)/shard_map/ppermute | solution.py:310
  267.7 39.4 %collective-permute-start.10 = (f32[2,2,48,256]{3,2,1,0:T(8,128)S(1)}, f32[2,2,48,256]{3,2,1,0:T(8,128)S(1)}, u32[]{:S(2)}, u32[]{:S(2)}) collective-permute-start(f32[2,2,48,256]{3,2,1,0:T(8,128)S(1)} %get-tuple-element.40), channel_id=1, source_target_pairs={{0,2},{1,3},{2,0},{3,1},{4,6},{5,7},{6,4},{7,5},{8,10},{9,11},{10,... | collective-permute-start | bytes 589832 | tf_op jit(solution)/shard_map/ppermute | solution.py:310
  282.3 24.8 %collective-permute-start.11 = (f32[2,2,48,256]{3,2,1,0:T(8,128)S(1)}, f32[2,2,48,256]{3,2,1,0:T(8,128)S(1)}, u32[]{:S(2)}, u32[]{:S(2)}) collective-permute-start(f32[2,2,48,256]{3,2,1,0:T(8,128)S(1)} %get-tuple-element.41), channel_id=1, source_target_pairs={{0,3},{1,2},{2,1},{3,0},{4,7},{5,6},{6,5},{7,4},{8,11},{9,10},{10,... | collective-permute-start | bytes 589832 | tf_op jit(solution)/shard_map/ppermute | solution.py:310
  374.9 24.4 %all-to-all-start.4 = ((f32[8,2,48,256]{3,2,1,0:T(8,128)}), f32[8,2,48,256]{3,2,1,0:T(8,128)S(1)}, u32[]{:S(2)}, u32[]{:S(2)}) async-start(f32[8,2,48,256]{3,2,1,0:T(8,128)} %bitcast.11), calls=%async_computation.4 | async-start | bytes 1572864 | tf_op jit(solution)/shard_map/all_to_all | solution.py:304
  381.4 23.1 %collective-permute-start.12 = (f32[2,64,1024]{2,1,0:T(8,128)}, f32[2,64,1024]{2,1,0:T(8,128)S(1)}, u32[]{:S(2)}, u32[]{:S(2)}) collective-permute-start(f32[2,64,1024]{2,1,0:T(8,128)} %get-tuple-element.43), channel_id=1, source_target_pairs={{0,1},{1,0},{2,3},{3,2},{4,5},{5,4},{6,7},{7,6},{8,9},{9,8},{10,11... | collective-permute-start | bytes 1572872 | tf_op jit(solution)/shard_map/ppermute | solution.py:310
  382.4 25.4 %collective-permute-start.13 = (f32[2,64,1024]{2,1,0:T(8,128)}, f32[2,64,1024]{2,1,0:T(8,128)S(1)}, u32[]{:S(2)}, u32[]{:S(2)}) collective-permute-start(f32[2,64,1024]{2,1,0:T(8,128)} %get-tuple-element.44), channel_id=1, source_target_pairs={{0,2},{1,3},{2,0},{3,1},{4,6},{5,7},{6,4},{7,5},{8,10},{9,11},{10,... | collective-permute-start | bytes 1572872 | tf_op jit(solution)/shard_map/ppermute | solution.py:310
  383.2 24.6 %collective-permute-start.14 = (f32[2,64,1024]{2,1,0:T(8,128)}, f32[2,64,1024]{2,1,0:T(8,128)}, u32[]{:S(2)}, u32[]{:S(2)}) collective-permute-start(f32[2,64,1024]{2,1,0:T(8,128)} %get-tuple-element.45), channel_id=1, source_target_pairs={{0,3},{1,2},{2,1},{3,0},{4,7},{5,6},{6,5},{7,4},{8,11},{9,10},{10,... | collective-permute-start | bytes 1572872 | tf_op jit(solution)/shard_map/ppermute | solution.py:310
  400.9 24.4 %all-to-all-start.5 = ((f32[8,2,48,256]{3,2,1,0:T(8,128)}), f32[8,2,48,256]{3,2,1,0:T(8,128)S(1)}, u32[]{:S(2)}, u32[]{:S(2)}) async-start(f32[8,2,48,256]{3,2,1,0:T(8,128)} %bitcast.39), calls=%async_computation.5 | async-start | bytes 1572864 | tf_op jit(solution)/shard_map/all_to_all | solution.py:304
  404.5 59.3 %reduce-scatter.14.cloned.1.call-start = ((), (), s32[]{:S(2)}) async-start(), calls=%async_computation.15 | async-start | bytes 2621440
  418.2 8.0 %collective-permute-start.15 = (f32[2,2,48,256]{3,2,1,0:T(8,128)S(1)}, f32[2,2,48,256]{3,2,1,0:T(8,128)S(1)}, u32[]{:S(2)}, u32[]{:S(2)}) collective-permute-start(f32[2,2,48,256]{3,2,1,0:T(8,128)S(1)} %get-tuple-element.47), channel_id=1, source_target_pairs={{0,1},{1,0},{2,3},{3,2},{4,5},{5,4},{6,7},{7,6},{8,9},{9,8},{10,11... | collective-permute-start | bytes 589832 | tf_op jit(solution)/shard_map/ppermute | solution.py:310
  419.4 8.9 %collective-permute-start.16 = (f32[2,2,48,256]{3,2,1,0:T(8,128)S(1)}, f32[2,2,48,256]{3,2,1,0:T(8,128)S(1)}, u32[]{:S(2)}, u32[]{:S(2)}) collective-permute-start(f32[2,2,48,256]{3,2,1,0:T(8,128)S(1)} %get-tuple-element.48), channel_id=1, source_target_pairs={{0,2},{1,3},{2,0},{3,1},{4,6},{5,7},{6,4},{7,5},{8,10},{9,11},{10,... | collective-permute-start | bytes 589832 | tf_op jit(solution)/shard_map/ppermute | solution.py:310
  420.3 12.8 %collective-permute-start.17 = (f32[2,2,48,256]{3,2,1,0:T(8,128)S(1)}, f32[2,2,48,256]{3,2,1,0:T(8,128)S(1)}, u32[]{:S(2)}, u32[]{:S(2)}) collective-permute-start(f32[2,2,48,256]{3,2,1,0:T(8,128)S(1)} %get-tuple-element.49), channel_id=1, source_target_pairs={{0,3},{1,2},{2,1},{3,0},{4,7},{5,6},{6,5},{7,4},{8,11},{9,10},{10,... | collective-permute-start | bytes 589832 | tf_op jit(solution)/shard_map/ppermute | solution.py:310
  460.2 24.4 %all-to-all-start.7 = ((f32[8,2,48,256]{3,2,1,0:T(8,128)}), f32[8,2,48,256]{3,2,1,0:T(8,128)S(1)}, u32[]{:S(2)}, u32[]{:S(2)}) async-start(f32[8,2,48,256]{3,2,1,0:T(8,128)} %bitcast.17), calls=%async_computation.7 | async-start | bytes 1572864 | tf_op jit(solution)/shard_map/all_to_all | solution.py:304
  464.8 6.2 %collective-permute-start.18 = (f32[2,2,32,256]{3,2,1,0:T(8,128)S(1)}, f32[2,2,32,256]{3,2,1,0:T(8,128)S(1)}, u32[]{:S(2)}, u32[]{:S(2)}) collective-permute-start(f32[2,2,32,256]{3,2,1,0:T(8,128)S(1)} %get-tuple-element.51), channel_id=1, source_target_pairs={{0,1},{1,0},{2,3},{3,2},{4,5},{5,4},{6,7},{7,6},{8,9},{9,8},{10,11... | collective-permute-start | bytes 393224 | tf_op jit(solution)/shard_map/ppermute | solution.py:310
  466.4 8.3 %collective-permute-start.19 = (f32[2,2,32,256]{3,2,1,0:T(8,128)S(1)}, f32[2,2,32,256]{3,2,1,0:T(8,128)S(1)}, u32[]{:S(2)}, u32[]{:S(2)}) collective-permute-start(f32[2,2,32,256]{3,2,1,0:T(8,128)S(1)} %get-tuple-element.52), channel_id=1, source_target_pairs={{0,2},{1,3},{2,0},{3,1},{4,6},{5,7},{6,4},{7,5},{8,10},{9,11},{10,... | collective-permute-start | bytes 393224 | tf_op jit(solution)/shard_map/ppermute | solution.py:310
  467.8 6.9 %collective-permute-start.20 = (f32[2,2,32,256]{3,2,1,0:T(8,128)S(1)}, f32[2,2,32,256]{3,2,1,0:T(8,128)S(1)}, u32[]{:S(2)}, u32[]{:S(2)}) collective-permute-start(f32[2,2,32,256]{3,2,1,0:T(8,128)S(1)} %get-tuple-element.53), channel_id=1, source_target_pairs={{0,3},{1,2},{2,1},{3,0},{4,7},{5,6},{6,5},{7,4},{8,11},{9,10},{10,... | collective-permute-start | bytes 393224 | tf_op jit(solution)/shard_map/ppermute | solution.py:310
  485.5 41.0 %copy-start.5 = (f32[1,2,96,1024]{3,2,1,0:T(8,128)S(1)}, f32[1,2,96,1024]{3,2,1,0:T(8,128)}, u32[]{:S(2)}) copy-start(f32[1,2,96,1024]{3,2,1,0:T(8,128)} %reduce-scatter.10.cloned.1.call-done) | copy-start | bytes 2359300
  485.5 41.0 %copy-start.7 = (f32[1,2,96,1024]{3,2,1,0:T(8,128)S(1)}, f32[1,2,96,1024]{3,2,1,0:T(8,128)}, u32[]{:S(2)}) copy-start(f32[1,2,96,1024]{3,2,1,0:T(8,128)} %reduce-scatter.12.cloned.1.call-done) | copy-start | bytes 2359300
  485.5 19.7 %all-to-all-start.8 = ((f32[8,2,32,256]{3,2,1,0:T(8,128)}), f32[8,2,32,256]{3,2,1,0:T(8,128)}, u32[]{:S(2)}, u32[]{:S(2)}) async-start(f32[8,2,32,256]{3,2,1,0:T(8,128)} %bitcast.34), calls=%async_computation.8 | async-start | bytes 1048576 | tf_op jit(solution)/shard_map/all_to_all | solution.py:304
  507.5 19.0 %copy-start.9 = (f32[1,2,64,1024]{3,2,1,0:T(8,128)S(1)}, f32[1,2,64,1024]{3,2,1,0:T(8,128)}, u32[]{:S(2)}) copy-start(f32[1,2,64,1024]{3,2,1,0:T(8,128)} %reduce-scatter.14.cloned.1.call-done) | copy-start | bytes 1572868
  (11 other events, 22.0 us)
Sparse Core Ops, SparseCore 0:
  182.1 42.3 reduce-scatter.9
  319.2 42.1 reduce-scatter.11
  417.1 38.8 reduce-scatter.13

commit v17 on v15

--- a/solution.py
+++ b/solution.py
@@ -344,8 +344,8 @@
         parts = product(place, amplitudes, mirrored, masked, spans[at][0], after)
         return parts, lax.psum_scatter(parts, "ka", scatter_dimension=0, tiled=False)
 
-    def send(group):
-        return spread(cut(place, [own[at] for at in group], sections, pairs))
+    def columns_of(group):
+        return cut(place, [own[at] for at in group], sections, pairs)
 
     def meet(columns):
         return swap(columns.reshape(occupied, slots, *columns.shape[-2:]), "ia")
@@ -364,15 +364,15 @@
     turned, early = turn(0, hop(0), across[1:])
     begun, own[0] = multiply(0, early, [])
     turned, middle = turn(1, hop(1), [begun])
-    leading = send(GROUPS[0])
+    leading = columns_of(GROUPS[0])
     crossed = hop(2)
-    turned, late = turn(2, crossed, [turned, *leading])
+    turned, late = turn(2, crossed, [turned, leading[0]])
     begun, own[1] = multiply(1, middle, [turned])
-    met = meet(gather(place, leading, [crossed]))
+    met = meet(gather(place, spread(leading), [crossed]))
     _, own[2] = multiply(2, late, [begun, met])
     delivered = [deliver(met)]
     for group in GROUPS[1:]:
-        met = meet(gather(place, send(group), [delivered[-1]]))
+        met = meet(gather(place, spread(columns_of(group)), [delivered[-1]]))
         delivered.append(deliver(met))
     return finish(place, spans, GROUPS, own, delivered)
 

time: 470 us -> 468 us (level)
  starting transfers between devices: 53.7 us -> 61 us
  waiting for transfers between devices: 222 us -> 215 us
    ppermute x21, waiting for transfers between devices: 130 us -> 119 us  [spread(): lax.ppermute(pieces[e], 'ka', [(q, q ^ e) for q in range(count)])]
    all_to_all x7, waiting for transfers between devices: 60.5 us -> 68.3 us  [swap(): return lax.all_to_all(array, axis, split_axis=0, concat_axis=0, tiled=True)]
    ppermute x21, starting transfers between devices: 24.4 us -> 29.8 us  [spread(): lax.ppermute(pieces[e], 'ka', [(q, q ^ e) for q in range(count)])]
    unnamed x59 -> x55, local copies, waits for them, and re-layouts: 17.6 us -> 16.2 us
  transfers between devices with their start and end apart: 31 -> 31, of which waited for: 21 -> 17; matrix products, arithmetic and copies ran while one was open for 1% -> 1% of each run, Pallas kernels for 10% -> 10%
where the time goes in v17:
time: 468 us; the launch traced here: 466 us
  waiting for transfers between devices  215 us (46%)
  blocking collectives  84.6 us (18%)
  Pallas kernels  67.6 us (14%)
  starting transfers between devices  61 us (13%)
  local copies, waits for them, and re-layouts  20.8 us (4%)
  between operations  13.4 us (3%)
    ppermute x21, waiting for transfers between devices, spread(): lax.ppermute(pieces[e], 'ka', [(q, q ^ e) for q in range(count)])  119 us
    all_to_all x3, blocking collectives, swap(): return lax.all_to_all(array, axis, split_axis=0, concat_axis=0, tiled=True)  84.6 us
    all_to_all x7, waiting for transfers between devices, swap(): return lax.all_to_all(array, axis, split_axis=0, concat_axis=0, tiled=True)  68.3 us
    pallas_call x21, Pallas kernels, call(): pl.pallas_call(trimmed, grid_spec=pltpu.PrefetchScalarGridSpec(num_scalar...  67.6 us
    all_to_all x7, starting transfers between devices, swap(): return lax.all_to_all(array, axis, split_axis=0, concat_axis=0, tiled=True)  31 us
    ppermute x21, starting transfers between devices, spread(): lax.ppermute(pieces[e], 'ka', [(q, q ^ e) for q in range(count)])  29.8 us
    unnamed x6, waiting for transfers between devices  27.9 us
    unnamed x55, local copies, waits for them, and re-layouts  16.2 us
  transfers between devices with their start and end apart: 31, of which 17 were waited for; matrix products, arithmetic and copies ran while one was open for 1% of the time, Pallas kernels for 10%

profile of v17, /device:TPU:0, one launch (start us, length us, event | category | flops | bytes accessed | tf_op | source)
XLA Modules:
  0.0 466.1 jit_solution(12092372997755452982)
XLA Ops:
  6.5 5.3 %first_flip.1.refs_2_ = f32[4,2,96,1024]{3,2,1,0:T(8,128)S(1)} custom-call(s32[1]{0:T(128)} %bitcast.refs_0_, f32[1,2,1024,1024]{3,2,1,0:T(8,128)} %refs_4_.5), custom_call_target="tpu_custom_call" | custom-call | bytes 6291456 | tf_op jit(solution)/shard_map/first_flip/pallas_call | solution.py:25
  11.8 41.7 %all_to_all.50 = f32[4,2,96,1024]{3,2,1,0:T(8,128)} all-to-all(f32[4,2,96,1024]{3,2,1,0:T(8,128)S(1)} %first_flip.1.refs_2_), channel_id=1, replica_groups=mesh['ia'=8,'ka'=4] {'ka'}, dimensions={0} | all-to-all | bytes 6291456 | tf_op jit(solution)/shard_map/all_to_all | solution.py:304
  53.5 4.9 %all-to-all-start.1 = ((f32[8,96,1024]{2,1,0:T(8,128)}), f32[8,96,1024]{2,1,0:T(8,128)}, u32[]{:S(2)}, u32[]{:S(2)}) async-start(f32[8,96,1024]{2,1,0:T(8,128)} %bitcast.37), calls=%async_computation.1 | async-start | bytes 6291456 | tf_op jit(solution)/shard_map/all_to_all | solution.py:304
  69.8 8.7 %mask.1.refs_5_.refs_9_ = bf16[2,2,1024,1024]{3,2,1,0:T(8,128)(2,1)} custom-call(s32[2,2,8,8]{3,2,1,0:T(8,128)S(1)} %bitcast.35, bf16[1,2,2,1024,1024]{4,3,2,1,0:T(8,128)(2,1)} %refs_1_.14, f32[4,2,96,1024]{3,2,1,0:T(8,128)S(1)} %first_flip.1.refs_2_), custom_call_target="tpu_custom_call" | custom-call | bytes 16777216 | tf_op jit(solution)/shard_map/mask/pallas_call | solution.py:25
  78.5 13.5 %collective-permute-done.refs_2_ = f32[2,160,1024]{2,1,0:T(8,128)S(1)} collective-permute-done((f32[2,160,1024]{2,1,0:T(8,128)S(1)}, f32[2,160,1024]{2,1,0:T(8,128)S(1)}, u32[]{:S(2)}, u32[]{:S(2)}) %collective-permute-start) | collective-permute-done | bytes 1310752 | tf_op jit(solution)/shard_map/ppermute | solution.py:310
  92.0 30.3 %collective-permute-done.1.refs_3_ = f32[2,160,1024]{2,1,0:T(8,128)S(1)} collective-permute-done((f32[2,160,1024]{2,1,0:T(8,128)S(1)}, f32[2,160,1024]{2,1,0:T(8,128)S(1)}, u32[]{:S(2)}, u32[]{:S(2)}) %collective-permute-start.1) | collective-permute-done | bytes 1310752 | tf_op jit(solution)/shard_map/ppermute | solution.py:310
  130.1 4.7 %all-to-all-start.2 = ((f32[8,96,1024]{2,1,0:T(8,128)}), f32[8,96,1024]{2,1,0:T(8,128)}, u32[]{:S(2)}, u32[]{:S(2)}) async-start(f32[8,96,1024]{2,1,0:T(8,128)} %bitcast.36), calls=%async_computation.2 | async-start | bytes 6291456 | tf_op jit(solution)/shard_map/all_to_all | solution.py:304
  146.1 16.9 %collective-permute-done.3.refs_6_ = f32[2,96,1024]{2,1,0:T(8,128)S(1)} collective-permute-done((f32[2,96,1024]{2,1,0:T(8,128)S(1)}, f32[2,96,1024]{2,1,0:T(8,128)S(1)}, u32[]{:S(2)}, u32[]{:S(2)}) %collective-permute-start.3) | collective-permute-done | bytes 786464 | tf_op jit(solution)/shard_map/ppermute | solution.py:310
  163.0 16.9 %collective-permute-done.4.refs_7_ = f32[2,96,1024]{2,1,0:T(8,128)S(1)} collective-permute-done((f32[2,96,1024]{2,1,0:T(8,128)S(1)}, f32[2,96,1024]{2,1,0:T(8,128)S(1)}, u32[]{:S(2)}, u32[]{:S(2)}) %collective-permute-start.4) | collective-permute-done | bytes 786464 | tf_op jit(solution)/shard_map/ppermute | solution.py:310
  179.9 11.4 %product.3.refs_2_ = f32[4,2,96,1024]{3,2,1,0:T(8,128)} custom-call(s32[1]{0:T(128)} %bitcast.refs_0_, f32[1,2,1024,1024]{3,2,1,0:T(8,128)} %refs_4_.5, f32[1,2,1024,1024]{3,2,1,0:T(8,128)} %refs_4_.5, f32[1,2,1024,1024]{3,2,1,0:T(8,128)} %refs_4_.5, f32[1,2,1024,1024]{3,2,1,0:T(8,128)} %refs_4_.5, f32[2,96,1024]{2,1,0:T(8,128)S(1)} %get-tuple-element.30.refs_5_, ...), custom_call_target="tpu_custom_call" | custom-call | flops 6442450944 | bytes 6291456 | tf_op jit(solution)/shard_map/product/pallas_call | solution.py:25
  191.3 15.0 %all-to-all-done.2 = f32[8,96,1024]{2,1,0:T(8,128)} async-done(((f32[8,96,1024]{2,1,0:T(8,128)}), f32[8,96,1024]{2,1,0:T(8,128)}, u32[]{:S(2)}, u32[]{:S(2)}) %all-to-all-start.2) | async-done | bytes 3145760 | tf_op jit(solution)/shard_map/all_to_all | solution.py:304
  206.3 3.6 all-to-all-start.3
  210.0 3.5 scatter.4
  216.9 27.8 %reduce-scatter.10.cloned.1.call-done = f32[1,2,96,1024]{3,2,1,0:T(8,128)} async-done(((f32[4,2,96,1024]{3,2,1,0:T(8,128)}), f32[1,2,96,1024]{3,2,1,0:T(8,128)}) %reduce-scatter.10.cloned.1.call-update) | async-done | bytes 786448
  248.6 10.3 %all-to-all-done.3 = f32[8,64,1024]{2,1,0:T(8,128)S(1)} async-done(((f32[8,64,1024]{2,1,0:T(8,128)}), f32[8,64,1024]{2,1,0:T(8,128)S(1)}, u32[]{:S(2)}, u32[]{:S(2)}) %all-to-all-start.3) | async-done | bytes 2097184 | tf_op jit(solution)/shard_map/all_to_all | solution.py:304
  261.1 12.2 %product.4.refs_10_ = f32[4,2,96,1024]{3,2,1,0:T(8,128)} custom-call(s32[1]{0:T(128)} %bitcast.refs_0_, f32[1,2,1024,1024]{3,2,1,0:T(8,128)} %refs_4_.5, f32[1,2,1024,1024]{3,2,1,0:T(8,128)} %refs_4_.5, f32[1,2,1024,1024]{3,2,1,0:T(8,128)} %refs_4_.5, f32[1,2,1024,1024]{3,2,1,0:T(8,128)} %refs_4_.5, f32[2,96,1024]{2,1,0:T(8,128)S(1)} %get-tuple-element.34.refs_2_.refs_5_, ...), custom_call_target="tpu_custom_call" | custom-call | flops 6442450944 | bytes 6291456 | tf_op jit(solution)/shard_map/product/pallas_call | solution.py:25
  275.2 6.7 %collective-permute-start.13 = (f32[2,2,48,256]{3,2,1,0:T(8,128)S(1)}, f32[2,2,48,256]{3,2,1,0:T(8,128)S(1)}, u32[]{:S(2)}, u32[]{:S(2)}) collective-permute-start(f32[2,2,48,256]{3,2,1,0:T(8,128)S(1)} %copy-done.23), channel_id=1, source_target_pairs={{0,2},{1,3},{2,0},{3,1},{4,6},{5,7},{6,4},{7,5},{8,10},{9,11},{10,... | collective-permute-start | bytes 589832 | tf_op jit(solution)/shard_map/ppermute | solution.py:310
  281.9 12.5 %collective-permute-done.13.refs_3_ = f32[2,2,48,256]{3,2,1,0:T(8,128)S(1)} collective-permute-done((f32[2,2,48,256]{3,2,1,0:T(8,128)S(1)}, f32[2,2,48,256]{3,2,1,0:T(8,128)S(1)}, u32[]{:S(2)}, u32[]{:S(2)}) %collective-permute-start.13) | collective-permute-done | bytes 196640 | tf_op jit(solution)/shard_map/ppermute | solution.py:310
  295.3 6.5 %all-to-all-start.4 = ((f32[8,2,48,256]{3,2,1,0:T(8,128)}), f32[8,2,48,256]{3,2,1,0:T(8,128)S(1)}, u32[]{:S(2)}, u32[]{:S(2)}) async-start(f32[8,2,48,256]{3,2,1,0:T(8,128)} %bitcast.11), calls=%async_computation.4 | async-start | bytes 1572864 | tf_op jit(solution)/shard_map/all_to_all | solution.py:304
  306.4 16.4 %all-to-all-done.4.refs_11_ = f32[8,2,48,256]{3,2,1,0:T(8,128)S(1)} async-done(((f32[8,2,48,256]{3,2,1,0:T(8,128)}), f32[8,2,48,256]{3,2,1,0:T(8,128)S(1)}, u32[]{:S(2)}, u32[]{:S(2)}) %all-to-all-start.4) | async-done | bytes 786464 | tf_op jit(solution)/shard_map/all_to_all | solution.py:304
  324.4 3.5 all-to-all-start.5
  328.0 10.6 %collective-permute-done.11.refs_8_ = f32[2,64,1024]{2,1,0:T(8,128)} collective-permute-done((f32[2,64,1024]{2,1,0:T(8,128)}, f32[2,64,1024]{2,1,0:T(8,128)}, u32[]{:S(2)}, u32[]{:S(2)}) %collective-permute-start.11) | collective-permute-done | bytes 524320 | tf_op jit(solution)/shard_map/ppermute | solution.py:310
  338.6 9.3 %product.5 = f32[4,2,64,1024]{3,2,1,0:T(8,128)} custom-call(s32[1]{0:T(128)} %bitcast.refs_0_, f32[1,2,1024,1024]{3,2,1,0:T(8,128)} %refs_4_.5, f32[1,2,1024,1024]{3,2,1,0:T(8,128)} %refs_4_.5, f32[1,2,1024,1024]{3,2,1,0:T(8,128)} %refs_4_.5, f32[1,2,1024,1024]{3,2,1,0:T(8,128)} %refs_4_.5, f32[2,64,1024]{2,1,0:T(8,128)S(1)} %get-tuple-element.39.refs_10_.refs_5_, ...), custom_call_target="tpu_custom_call" | custom-call | flops 4294967296 | bytes 4194304 | tf_op jit(solution)/shard_map/product/pallas_call | solution.py:25
  352.7 4.3 collective-permute-done.15.refs_2_
  357.0 7.4 %collective-permute-done.16.refs_3_ = f32[2,2,48,256]{3,2,1,0:T(8,128)S(1)} collective-permute-done((f32[2,2,48,256]{3,2,1,0:T(8,128)S(1)}, f32[2,2,48,256]{3,2,1,0:T(8,128)S(1)}, u32[]{:S(2)}, u32[]{:S(2)}) %collective-permute-start.16) | collective-permute-done | bytes 196640 | tf_op jit(solution)/shard_map/ppermute | solution.py:310
  364.4 25.2 %all_to_all.51 = f32[8,2,48,256]{3,2,1,0:T(8,128)S(1)} all-to-all(f32[8,2,48,256]{3,2,1,0:T(8,128)S(1)} %bitcast.27), channel_id=1, replica_groups=mesh['ia'=8,'ka'=4] {'ia'}, dimensions={0} | all-to-all | bytes 1572864 | tf_op jit(solution)/shard_map/all_to_all | solution.py:304
  391.2 3.5 all-to-all-start.7
  402.9 4.2 collective-permute-done.19.refs_3_
  407.1 8.6 %all-to-all-done.7.refs_5_ = f32[8,2,48,256]{3,2,1,0:T(8,128)S(1)} async-done(((f32[8,2,48,256]{3,2,1,0:T(8,128)}), f32[8,2,48,256]{3,2,1,0:T(8,128)S(1)}, u32[]{:S(2)}, u32[]{:S(2)}) %all-to-all-start.7) | async-done | bytes 786464 | tf_op jit(solution)/shard_map/all_to_all | solution.py:304
  416.5 4.3 all-to-all-start.8
  420.9 15.3 %all-to-all-done.8 = f32[8,2,32,256]{3,2,1,0:T(8,128)} async-done(((f32[8,2,32,256]{3,2,1,0:T(8,128)}), f32[8,2,32,256]{3,2,1,0:T(8,128)}, u32[]{:S(2)}, u32[]{:S(2)}) %all-to-all-start.8) | async-done | bytes 524320 | tf_op jit(solution)/shard_map/all_to_all | solution.py:304
  439.8 17.8 %all_to_all.52.refs_6_ = f32[8,2,32,256]{3,2,1,0:T(8,128)S(1)} all-to-all(f32[8,2,32,256]{3,2,1,0:T(8,128)S(1)} %broadcast_select_fusion.2), channel_id=1, replica_groups=mesh['ia'=8,'ka'=4] {'ia'}, dimensions={0} | all-to-all | bytes 1048576 | tf_op jit(solution)/shard_map/all_to_all | solution.py:304
  (130 shorter events, 70.1 us)
Async XLA Ops:
  53.5 76.5 %all-to-all-start.1 = ((f32[8,96,1024]{2,1,0:T(8,128)}), f32[8,96,1024]{2,1,0:T(8,128)}, u32[]{:S(2)}, u32[]{:S(2)}) async-start(f32[8,96,1024]{2,1,0:T(8,128)} %bitcast.37), calls=%async_computation.1 | async-start | bytes 6291456 | tf_op jit(solution)/shard_map/all_to_all | solution.py:304
  60.3 31.6 %collective-permute-start = (f32[2,160,1024]{2,1,0:T(8,128)S(1)}, f32[2,160,1024]{2,1,0:T(8,128)S(1)}, u32[]{:S(2)}, u32[]{:S(2)}) collective-permute-start(f32[2,160,1024]{2,1,0:T(8,128)S(1)} %flip.5), channel_id=1, source_target_pairs={{0,1},{1,0},{2,3},{3,2},{4,5},{5,4},{6,7},{7,6},{8,9},{9,8},{10,11... | collective-permute-start | bytes 3932168 | tf_op jit(solution)/shard_map/ppermute | solution.py:310
  63.2 59.1 %collective-permute-start.1 = (f32[2,160,1024]{2,1,0:T(8,128)S(1)}, f32[2,160,1024]{2,1,0:T(8,128)S(1)}, u32[]{:S(2)}, u32[]{:S(2)}) collective-permute-start(f32[2,160,1024]{2,1,0:T(8,128)S(1)} %flip.6), channel_id=1, source_target_pairs={{0,2},{1,3},{2,0},{3,1},{4,6},{5,7},{6,4},{7,5},{8,10},{9,11},{10,... | collective-permute-start | bytes 3932168 | tf_op jit(solution)/shard_map/ppermute | solution.py:310
  65.8 56.5 %collective-permute-start.2 = (f32[2,160,1024]{2,1,0:T(8,128)S(1)}, f32[2,160,1024]{2,1,0:T(8,128)S(1)}, u32[]{:S(2)}, u32[]{:S(2)}) collective-permute-start(f32[2,160,1024]{2,1,0:T(8,128)S(1)} %flip.7), channel_id=1, source_target_pairs={{0,3},{1,2},{2,1},{3,0},{4,7},{5,6},{6,5},{7,4},{8,11},{9,10},{10,... | collective-permute-start | bytes 3932168 | tf_op jit(solution)/shard_map/ppermute | solution.py:310
  69.8 52.5 %copy-start.1 = (f32[2,160,1024]{2,1,0:T(8,128)}, f32[2,160,1024]{2,1,0:T(8,128)S(1)}, u32[]{:S(2)}) copy-start(f32[2,160,1024]{2,1,0:T(8,128)S(1)} %flip.4.refs_1_) | copy-start | bytes 3932164
  130.1 76.2 %all-to-all-start.2 = ((f32[8,96,1024]{2,1,0:T(8,128)}), f32[8,96,1024]{2,1,0:T(8,128)}, u32[]{:S(2)}, u32[]{:S(2)}) async-start(f32[8,96,1024]{2,1,0:T(8,128)} %bitcast.36), calls=%async_computation.2 | async-start | bytes 6291456 | tf_op jit(solution)/shard_map/all_to_all | solution.py:304
  134.8 109.9 %reduce-scatter.10.cloned.1.call-start = ((), (), s32[]{:S(2)}) async-start(), calls=%async_computation.13 | async-start | bytes 3932160
  142.5 20.4 %collective-permute-start.3 = (f32[2,96,1024]{2,1,0:T(8,128)S(1)}, f32[2,96,1024]{2,1,0:T(8,128)S(1)}, u32[]{:S(2)}, u32[]{:S(2)}) collective-permute-start(f32[2,96,1024]{2,1,0:T(8,128)S(1)} %get-tuple-element.31), channel_id=1, source_target_pairs={{0,1},{1,0},{2,3},{3,2},{4,5},{5,4},{6,7},{7,6},{8,9},{9,8},{10,11... | collective-permute-start | bytes 2359304 | tf_op jit(solution)/shard_map/ppermute | solution.py:310
  143.5 36.3 %collective-permute-start.4 = (f32[2,96,1024]{2,1,0:T(8,128)S(1)}, f32[2,96,1024]{2,1,0:T(8,128)S(1)}, u32[]{:S(2)}, u32[]{:S(2)}) collective-permute-start(f32[2,96,1024]{2,1,0:T(8,128)S(1)} %get-tuple-element.32), channel_id=1, source_target_pairs={{0,2},{1,3},{2,0},{3,1},{4,6},{5,7},{6,4},{7,5},{8,10},{9,11},{10,... | collective-permute-start | bytes 2359304 | tf_op jit(solution)/shard_map/ppermute | solution.py:310
  144.1 35.8 %collective-permute-start.5 = (f32[2,96,1024]{2,1,0:T(8,128)S(1)}, f32[2,96,1024]{2,1,0:T(8,128)S(1)}, u32[]{:S(2)}, u32[]{:S(2)}) collective-permute-start(f32[2,96,1024]{2,1,0:T(8,128)S(1)} %get-tuple-element.33), channel_id=1, source_target_pairs={{0,3},{1,2},{2,1},{3,0},{4,7},{5,6},{6,5},{7,4},{8,11},{9,10},{10,... | collective-permute-start | bytes 2359304 | tf_op jit(solution)/shard_map/ppermute | solution.py:310
  206.3 52.6 %all-to-all-start.3 = ((f32[8,64,1024]{2,1,0:T(8,128)}), f32[8,64,1024]{2,1,0:T(8,128)S(1)}, u32[]{:S(2)}, u32[]{:S(2)}) async-start(f32[8,64,1024]{2,1,0:T(8,128)} %bitcast.25), calls=%async_computation.3 | async-start | bytes 4194304 | tf_op jit(solution)/shard_map/all_to_all | solution.py:304
  209.9 138.0 %reduce-scatter.12.cloned.1.call-start = ((), (), s32[]{:S(2)}) async-start(), calls=%async_computation.14 | async-start | bytes 3932160
  213.4 47.7 %collective-permute-start.6 = (f32[2,96,1024]{2,1,0:T(8,128)}, f32[2,96,1024]{2,1,0:T(8,128)}, u32[]{:S(2)}, u32[]{:S(2)}) collective-permute-start(f32[2,96,1024]{2,1,0:T(8,128)} %get-tuple-element.35), channel_id=1, source_target_pairs={{0,1},{1,0},{2,3},{3,2},{4,5},{5,4},{6,7},{7,6},{8,9},{9,8},{10,11... | collective-permute-start | bytes 2359304 | tf_op jit(solution)/shard_map/ppermute | solution.py:310
  214.5 46.6 %collective-permute-start.7 = (f32[2,96,1024]{2,1,0:T(8,128)}, f32[2,96,1024]{2,1,0:T(8,128)}, u32[]{:S(2)}, u32[]{:S(2)}) collective-permute-start(f32[2,96,1024]{2,1,0:T(8,128)} %get-tuple-element.36), channel_id=1, source_target_pairs={{0,2},{1,3},{2,0},{3,1},{4,6},{5,7},{6,4},{7,5},{8,10},{9,11},{10,... | collective-permute-start | bytes 2359304 | tf_op jit(solution)/shard_map/ppermute | solution.py:310
  215.1 46.0 %collective-permute-start.8 = (f32[2,96,1024]{2,1,0:T(8,128)}, f32[2,96,1024]{2,1,0:T(8,128)}, u32[]{:S(2)}, u32[]{:S(2)}) collective-permute-start(f32[2,96,1024]{2,1,0:T(8,128)} %get-tuple-element.37), channel_id=1, source_target_pairs={{0,3},{1,2},{2,1},{3,0},{4,7},{5,6},{6,5},{7,4},{8,11},{9,10},{10,... | collective-permute-start | bytes 2359304 | tf_op jit(solution)/shard_map/ppermute | solution.py:310
  274.2 7.6 %collective-permute-start.12 = (f32[2,2,48,256]{3,2,1,0:T(8,128)S(1)}, f32[2,2,48,256]{3,2,1,0:T(8,128)S(1)}, u32[]{:S(2)}, u32[]{:S(2)}) collective-permute-start(f32[2,2,48,256]{3,2,1,0:T(8,128)S(1)} %copy-done.25), channel_id=1, source_target_pairs={{0,1},{1,0},{2,3},{3,2},{4,5},{5,4},{6,7},{7,6},{8,9},{9,8},{10,11... | collective-permute-start | bytes 589832 | tf_op jit(solution)/shard_map/ppermute | solution.py:310
  275.2 19.2 %collective-permute-start.13 = (f32[2,2,48,256]{3,2,1,0:T(8,128)S(1)}, f32[2,2,48,256]{3,2,1,0:T(8,128)S(1)}, u32[]{:S(2)}, u32[]{:S(2)}) collective-permute-start(f32[2,2,48,256]{3,2,1,0:T(8,128)S(1)} %copy-done.23), channel_id=1, source_target_pairs={{0,2},{1,3},{2,0},{3,1},{4,6},{5,7},{6,4},{7,5},{8,10},{9,11},{10,... | collective-permute-start | bytes 589832 | tf_op jit(solution)/shard_map/ppermute | solution.py:310
  281.8 12.5 %collective-permute-start.14 = (f32[2,2,48,256]{3,2,1,0:T(8,128)S(1)}, f32[2,2,48,256]{3,2,1,0:T(8,128)S(1)}, u32[]{:S(2)}, u32[]{:S(2)}) collective-permute-start(f32[2,2,48,256]{3,2,1,0:T(8,128)S(1)} %copy-done.21), channel_id=1, source_target_pairs={{0,3},{1,2},{2,1},{3,0},{4,7},{5,6},{6,5},{7,4},{8,11},{9,10},{10,... | collective-permute-start | bytes 589832 | tf_op jit(solution)/shard_map/ppermute | solution.py:310
  295.3 27.5 %all-to-all-start.4 = ((f32[8,2,48,256]{3,2,1,0:T(8,128)}), f32[8,2,48,256]{3,2,1,0:T(8,128)S(1)}, u32[]{:S(2)}, u32[]{:S(2)}) async-start(f32[8,2,48,256]{3,2,1,0:T(8,128)} %bitcast.11), calls=%async_computation.4 | async-start | bytes 1572864 | tf_op jit(solution)/shard_map/all_to_all | solution.py:304
  302.8 25.1 %collective-permute-start.9 = (f32[2,64,1024]{2,1,0:T(8,128)}, f32[2,64,1024]{2,1,0:T(8,128)S(1)}, u32[]{:S(2)}, u32[]{:S(2)}) collective-permute-start(f32[2,64,1024]{2,1,0:T(8,128)} %get-tuple-element.40), channel_id=1, source_target_pairs={{0,1},{1,0},{2,3},{3,2},{4,5},{5,4},{6,7},{7,6},{8,9},{9,8},{10,11... | collective-permute-start | bytes 1572872 | tf_op jit(solution)/shard_map/ppermute | solution.py:310
  303.0 25.0 %collective-permute-start.10 = (f32[2,64,1024]{2,1,0:T(8,128)}, f32[2,64,1024]{2,1,0:T(8,128)S(1)}, u32[]{:S(2)}, u32[]{:S(2)}) collective-permute-start(f32[2,64,1024]{2,1,0:T(8,128)} %get-tuple-element.41), channel_id=1, source_target_pairs={{0,2},{1,3},{2,0},{3,1},{4,6},{5,7},{6,4},{7,5},{8,10},{9,11},{10,... | collective-permute-start | bytes 1572872 | tf_op jit(solution)/shard_map/ppermute | solution.py:310
  305.4 33.2 %collective-permute-start.11 = (f32[2,64,1024]{2,1,0:T(8,128)}, f32[2,64,1024]{2,1,0:T(8,128)}, u32[]{:S(2)}, u32[]{:S(2)}) collective-permute-start(f32[2,64,1024]{2,1,0:T(8,128)} %get-tuple-element.42), channel_id=1, source_target_pairs={{0,3},{1,2},{2,1},{3,0},{4,7},{5,6},{6,5},{7,4},{8,11},{9,10},{10,... | collective-permute-start | bytes 1572872 | tf_op jit(solution)/shard_map/ppermute | solution.py:310
  324.4 28.3 %all-to-all-start.5 = ((f32[8,2,48,256]{3,2,1,0:T(8,128)}), f32[8,2,48,256]{3,2,1,0:T(8,128)S(1)}, u32[]{:S(2)}, u32[]{:S(2)}) async-start(f32[8,2,48,256]{3,2,1,0:T(8,128)} %bitcast.38), calls=%async_computation.5 | async-start | bytes 1572864 | tf_op jit(solution)/shard_map/all_to_all | solution.py:304
  327.9 66.9 %reduce-scatter.14.cloned.1.call-start = ((), (), s32[]{:S(2)}) async-start(), calls=%async_computation.15 | async-start | bytes 2621440
  349.1 7.8 %collective-permute-start.15 = (f32[2,2,48,256]{3,2,1,0:T(8,128)S(1)}, f32[2,2,48,256]{3,2,1,0:T(8,128)S(1)}, u32[]{:S(2)}, u32[]{:S(2)}) collective-permute-start(f32[2,2,48,256]{3,2,1,0:T(8,128)S(1)} %get-tuple-element.47), channel_id=1, source_target_pairs={{0,1},{1,0},{2,3},{3,2},{4,5},{5,4},{6,7},{7,6},{8,9},{9,8},{10,11... | collective-permute-start | bytes 589832 | tf_op jit(solution)/shard_map/ppermute | solution.py:310
  350.7 13.6 %collective-permute-start.16 = (f32[2,2,48,256]{3,2,1,0:T(8,128)S(1)}, f32[2,2,48,256]{3,2,1,0:T(8,128)S(1)}, u32[]{:S(2)}, u32[]{:S(2)}) collective-permute-start(f32[2,2,48,256]{3,2,1,0:T(8,128)S(1)} %get-tuple-element.48), channel_id=1, source_target_pairs={{0,2},{1,3},{2,0},{3,1},{4,6},{5,7},{6,4},{7,5},{8,10},{9,11},{10,... | collective-permute-start | bytes 589832 | tf_op jit(solution)/shard_map/ppermute | solution.py:310
  350.7 13.6 %collective-permute-start.17 = (f32[2,2,48,256]{3,2,1,0:T(8,128)S(1)}, f32[2,2,48,256]{3,2,1,0:T(8,128)S(1)}, u32[]{:S(2)}, u32[]{:S(2)}) collective-permute-start(f32[2,2,48,256]{3,2,1,0:T(8,128)S(1)} %get-tuple-element.49), channel_id=1, source_target_pairs={{0,3},{1,2},{2,1},{3,0},{4,7},{5,6},{6,5},{7,4},{8,11},{9,10},{10,... | collective-permute-start | bytes 589832 | tf_op jit(solution)/shard_map/ppermute | solution.py:310
  391.2 24.4 %all-to-all-start.7 = ((f32[8,2,48,256]{3,2,1,0:T(8,128)}), f32[8,2,48,256]{3,2,1,0:T(8,128)S(1)}, u32[]{:S(2)}, u32[]{:S(2)}) async-start(f32[8,2,48,256]{3,2,1,0:T(8,128)} %bitcast.17), calls=%async_computation.7 | async-start | bytes 1572864 | tf_op jit(solution)/shard_map/all_to_all | solution.py:304
  395.9 7.0 %collective-permute-start.18 = (f32[2,2,32,256]{3,2,1,0:T(8,128)S(1)}, f32[2,2,32,256]{3,2,1,0:T(8,128)S(1)}, u32[]{:S(2)}, u32[]{:S(2)}) collective-permute-start(f32[2,2,32,256]{3,2,1,0:T(8,128)S(1)} %get-tuple-element.51), channel_id=1, source_target_pairs={{0,1},{1,0},{2,3},{3,2},{4,5},{5,4},{6,7},{7,6},{8,9},{9,8},{10,11... | collective-permute-start | bytes 393224 | tf_op jit(solution)/shard_map/ppermute | solution.py:310
  398.8 8.3 %collective-permute-start.19 = (f32[2,2,32,256]{3,2,1,0:T(8,128)S(1)}, f32[2,2,32,256]{3,2,1,0:T(8,128)S(1)}, u32[]{:S(2)}, u32[]{:S(2)}) collective-permute-start(f32[2,2,32,256]{3,2,1,0:T(8,128)S(1)} %get-tuple-element.52), channel_id=1, source_target_pairs={{0,2},{1,3},{2,0},{3,1},{4,6},{5,7},{6,4},{7,5},{8,10},{9,11},{10,... | collective-permute-start | bytes 393224 | tf_op jit(solution)/shard_map/ppermute | solution.py:310
  398.8 8.3 %collective-permute-start.20 = (f32[2,2,32,256]{3,2,1,0:T(8,128)S(1)}, f32[2,2,32,256]{3,2,1,0:T(8,128)S(1)}, u32[]{:S(2)}, u32[]{:S(2)}) collective-permute-start(f32[2,2,32,256]{3,2,1,0:T(8,128)S(1)} %get-tuple-element.53), channel_id=1, source_target_pairs={{0,3},{1,2},{2,1},{3,0},{4,7},{5,6},{6,5},{7,4},{8,11},{9,10},{10,... | collective-permute-start | bytes 393224 | tf_op jit(solution)/shard_map/ppermute | solution.py:310
  416.5 19.6 %all-to-all-start.8 = ((f32[8,2,32,256]{3,2,1,0:T(8,128)}), f32[8,2,32,256]{3,2,1,0:T(8,128)}, u32[]{:S(2)}, u32[]{:S(2)}) async-start(f32[8,2,32,256]{3,2,1,0:T(8,128)} %bitcast.34), calls=%async_computation.8 | async-start | bytes 1048576 | tf_op jit(solution)/shard_map/all_to_all | solution.py:304
  (26 other events, 182.2 us)
Sparse Core Ops, SparseCore 0:
  191.4 53.2 reduce-scatter.9
  273.5 66.4 reduce-scatter.11
  348.0 39.8 reduce-scatter.13

commit v18 on v17

--- a/solution.py
+++ b/solution.py
@@ -369,7 +369,7 @@
     turned, late = turn(2, crossed, [turned, leading[0]])
     begun, own[1] = multiply(1, middle, [turned])
     met = meet(gather(place, spread(leading), [crossed]))
-    _, own[2] = multiply(2, late, [begun, met])
+    _, own[2] = multiply(2, late, [begun])
     delivered = [deliver(met)]
     for group in GROUPS[1:]:
         met = meet(gather(place, spread(columns_of(group)), [delivered[-1]]))

time: 468 us -> 459 us (0.981)
  waiting for transfers between devices: 215 us -> 209 us
    ppermute x21, waiting for transfers between devices: 119 us -> 108 us  [spread(): lax.ppermute(pieces[e], 'ka', [(q, q ^ e) for q in range(count)])]
    all_to_all x7, waiting for transfers between devices: 68.3 us -> 73.2 us  [swap(): return lax.all_to_all(array, axis, split_axis=0, concat_axis=0, tiled=True)]
    unnamed x55 -> x59, local copies, waits for them, and re-layouts: 16.2 us -> 17 us
  transfers between devices with their start and end apart: 31 -> 31, of which waited for: 17 -> 19; matrix products, arithmetic and copies ran while one was open for 1% -> 1% of each run, Pallas kernels for 10% -> 10%
where the time goes in v18:
time: 459 us; the launch traced here: 458 us
  waiting for transfers between devices  209 us (46%)
  blocking collectives  82.8 us (18%)
  Pallas kernels  67.3 us (15%)
  starting transfers between devices  58.7 us (13%)
  local copies, waits for them, and re-layouts  22.5 us (5%)
  between operations  13.4 us (3%)
    ppermute x21, waiting for transfers between devices, spread(): lax.ppermute(pieces[e], 'ka', [(q, q ^ e) for q in range(count)])  108 us
    all_to_all x3, blocking collectives, swap(): return lax.all_to_all(array, axis, split_axis=0, concat_axis=0, tiled=True)  82.8 us
    all_to_all x7, waiting for transfers between devices, swap(): return lax.all_to_all(array, axis, split_axis=0, concat_axis=0, tiled=True)  73.2 us
    pallas_call x21, Pallas kernels, call(): pl.pallas_call(trimmed, grid_spec=pltpu.PrefetchScalarGridSpec(num_scalar...  67.3 us
    ppermute x21, starting transfers between devices, spread(): lax.ppermute(pieces[e], 'ka', [(q, q ^ e) for q in range(count)])  29.4 us
    all_to_all x7, starting transfers between devices, swap(): return lax.all_to_all(array, axis, split_axis=0, concat_axis=0, tiled=True)  29.2 us
    unnamed x6, waiting for transfers between devices  27.8 us
    unnamed x59, local copies, waits for them, and re-layouts  17 us
  transfers between devices with their start and end apart: 31, of which 19 were waited for; matrix products, arithmetic and copies ran while one was open for 1% of the time, Pallas kernels for 10%

profile of v18, /device:TPU:0, one launch (start us, length us, event | category | flops | bytes accessed | tf_op | source)
XLA Modules:
  0.0 457.9 jit_solution(2143830113936330898)
XLA Ops:
  6.5 5.3 %first_flip.1.refs_2_ = f32[4,2,96,1024]{3,2,1,0:T(8,128)S(1)} custom-call(s32[1]{0:T(128)} %bitcast.refs_0_, f32[1,2,1024,1024]{3,2,1,0:T(8,128)} %refs_4_.5), custom_call_target="tpu_custom_call" | custom-call | bytes 6291456 | tf_op jit(solution)/shard_map/first_flip/pallas_call | solution.py:25
  11.8 41.7 %all_to_all.50 = f32[4,2,96,1024]{3,2,1,0:T(8,128)} all-to-all(f32[4,2,96,1024]{3,2,1,0:T(8,128)S(1)} %first_flip.1.refs_2_), channel_id=1, replica_groups=mesh['ia'=8,'ka'=4] {'ka'}, dimensions={0} | all-to-all | bytes 6291456 | tf_op jit(solution)/shard_map/all_to_all | solution.py:304
  53.5 4.9 %all-to-all-start.1 = ((f32[8,96,1024]{2,1,0:T(8,128)}), f32[8,96,1024]{2,1,0:T(8,128)}, u32[]{:S(2)}, u32[]{:S(2)}) async-start(f32[8,96,1024]{2,1,0:T(8,128)} %bitcast.36), calls=%async_computation.1 | async-start | bytes 6291456 | tf_op jit(solution)/shard_map/all_to_all | solution.py:304
  69.8 8.7 %mask.1.refs_5_.refs_9_ = bf16[2,2,1024,1024]{3,2,1,0:T(8,128)(2,1)} custom-call(s32[2,2,8,8]{3,2,1,0:T(8,128)S(1)} %bitcast.34, bf16[1,2,2,1024,1024]{4,3,2,1,0:T(8,128)(2,1)} %refs_1_.14, f32[4,2,96,1024]{3,2,1,0:T(8,128)S(1)} %first_flip.1.refs_2_), custom_call_target="tpu_custom_call" | custom-call | bytes 16777216 | tf_op jit(solution)/shard_map/mask/pallas_call | solution.py:25
  78.5 13.4 %collective-permute-done.refs_2_ = f32[2,160,1024]{2,1,0:T(8,128)S(1)} collective-permute-done((f32[2,160,1024]{2,1,0:T(8,128)S(1)}, f32[2,160,1024]{2,1,0:T(8,128)S(1)}, u32[]{:S(2)}, u32[]{:S(2)}) %collective-permute-start) | collective-permute-done | bytes 1310752 | tf_op jit(solution)/shard_map/ppermute | solution.py:310
  92.0 30.3 %collective-permute-done.1.refs_3_ = f32[2,160,1024]{2,1,0:T(8,128)S(1)} collective-permute-done((f32[2,160,1024]{2,1,0:T(8,128)S(1)}, f32[2,160,1024]{2,1,0:T(8,128)S(1)}, u32[]{:S(2)}, u32[]{:S(2)}) %collective-permute-start.1) | collective-permute-done | bytes 1310752 | tf_op jit(solution)/shard_map/ppermute | solution.py:310
  130.1 4.7 %all-to-all-start.2 = ((f32[8,96,1024]{2,1,0:T(8,128)}), f32[8,96,1024]{2,1,0:T(8,128)}, u32[]{:S(2)}, u32[]{:S(2)}) async-start(f32[8,96,1024]{2,1,0:T(8,128)} %bitcast.35), calls=%async_computation.2 | async-start | bytes 6291456 | tf_op jit(solution)/shard_map/all_to_all | solution.py:304
  146.1 16.9 %collective-permute-done.3.refs_6_ = f32[2,96,1024]{2,1,0:T(8,128)S(1)} collective-permute-done((f32[2,96,1024]{2,1,0:T(8,128)S(1)}, f32[2,96,1024]{2,1,0:T(8,128)S(1)}, u32[]{:S(2)}, u32[]{:S(2)}) %collective-permute-start.3) | collective-permute-done | bytes 786464 | tf_op jit(solution)/shard_map/ppermute | solution.py:310
  163.0 16.9 %collective-permute-done.4.refs_7_ = f32[2,96,1024]{2,1,0:T(8,128)S(1)} collective-permute-done((f32[2,96,1024]{2,1,0:T(8,128)S(1)}, f32[2,96,1024]{2,1,0:T(8,128)S(1)}, u32[]{:S(2)}, u32[]{:S(2)}) %collective-permute-start.4) | collective-permute-done | bytes 786464 | tf_op jit(solution)/shard_map/ppermute | solution.py:310
  179.9 11.4 %product.3.refs_2_ = f32[4,2,96,1024]{3,2,1,0:T(8,128)} custom-call(s32[1]{0:T(128)} %bitcast.refs_0_, f32[1,2,1024,1024]{3,2,1,0:T(8,128)} %refs_4_.5, f32[1,2,1024,1024]{3,2,1,0:T(8,128)} %refs_4_.5, f32[1,2,1024,1024]{3,2,1,0:T(8,128)} %refs_4_.5, f32[1,2,1024,1024]{3,2,1,0:T(8,128)} %refs_4_.5, f32[2,96,1024]{2,1,0:T(8,128)S(1)} %get-tuple-element.30.refs_5_, ...), custom_call_target="tpu_custom_call" | custom-call | flops 6442450944 | bytes 6291456 | tf_op jit(solution)/shard_map/product/pallas_call | solution.py:25
  191.3 15.0 %all-to-all-done.2 = f32[8,96,1024]{2,1,0:T(8,128)} async-done(((f32[8,96,1024]{2,1,0:T(8,128)}), f32[8,96,1024]{2,1,0:T(8,128)}, u32[]{:S(2)}, u32[]{:S(2)}) %all-to-all-start.2) | async-done | bytes 3145760 | tf_op jit(solution)/shard_map/all_to_all | solution.py:304
  206.3 3.6 all-to-all-start.3
  210.0 3.5 scatter.4
  217.0 27.7 %reduce-scatter.10.cloned.1.call-done = f32[1,2,96,1024]{3,2,1,0:T(8,128)} async-done(((f32[4,2,96,1024]{3,2,1,0:T(8,128)}), f32[1,2,96,1024]{3,2,1,0:T(8,128)}) %reduce-scatter.10.cloned.1.call-update) | async-done | bytes 786448
  248.6 10.3 %all-to-all-done.3 = f32[8,64,1024]{2,1,0:T(8,128)S(1)} async-done(((f32[8,64,1024]{2,1,0:T(8,128)}), f32[8,64,1024]{2,1,0:T(8,128)S(1)}, u32[]{:S(2)}, u32[]{:S(2)}) %all-to-all-start.3) | async-done | bytes 2097184 | tf_op jit(solution)/shard_map/all_to_all | solution.py:304
  261.7 12.2 %product.4.refs_10_ = f32[4,2,96,1024]{3,2,1,0:T(8,128)} custom-call(s32[1]{0:T(128)} %bitcast.refs_0_, f32[1,2,1024,1024]{3,2,1,0:T(8,128)} %refs_4_.5, f32[1,2,1024,1024]{3,2,1,0:T(8,128)} %refs_4_.5, f32[1,2,1024,1024]{3,2,1,0:T(8,128)} %refs_4_.5, f32[1,2,1024,1024]{3,2,1,0:T(8,128)} %refs_4_.5, f32[2,96,1024]{2,1,0:T(8,128)S(1)} %get-tuple-element.34.refs_2_.refs_5_, ...), custom_call_target="tpu_custom_call" | custom-call | flops 6442450944 | bytes 6291456 | tf_op jit(solution)/shard_map/product/pallas_call | solution.py:25
  275.8 6.7 %collective-permute-start.13 = (f32[2,2,48,256]{3,2,1,0:T(8,128)S(1)}, f32[2,2,48,256]{3,2,1,0:T(8,128)S(1)}, u32[]{:S(2)}, u32[]{:S(2)}) collective-permute-start(f32[2,2,48,256]{3,2,1,0:T(8,128)S(1)} %copy-done.25), channel_id=1, source_target_pairs={{0,2},{1,3},{2,0},{3,1},{4,6},{5,7},{6,4},{7,5},{8,10},{9,11},{10,... | collective-permute-start | bytes 589832 | tf_op jit(solution)/shard_map/ppermute | solution.py:310
  282.5 12.5 %collective-permute-done.13.refs_3_ = f32[2,2,48,256]{3,2,1,0:T(8,128)S(1)} collective-permute-done((f32[2,2,48,256]{3,2,1,0:T(8,128)S(1)}, f32[2,2,48,256]{3,2,1,0:T(8,128)S(1)}, u32[]{:S(2)}, u32[]{:S(2)}) %collective-permute-start.13) | collective-permute-done | bytes 196640 | tf_op jit(solution)/shard_map/ppermute | solution.py:310
  295.9 4.6 %all-to-all-start.4 = ((f32[8,2,48,256]{3,2,1,0:T(8,128)}), f32[8,2,48,256]{3,2,1,0:T(8,128)S(1)}, u32[]{:S(2)}, u32[]{:S(2)}) async-start(f32[8,2,48,256]{3,2,1,0:T(8,128)} %bitcast.12), calls=%async_computation.4 | async-start | bytes 1572864 | tf_op jit(solution)/shard_map/all_to_all | solution.py:304
  305.2 16.3 %all-to-all-done.4 = f32[8,2,48,256]{3,2,1,0:T(8,128)S(1)} async-done(((f32[8,2,48,256]{3,2,1,0:T(8,128)}), f32[8,2,48,256]{3,2,1,0:T(8,128)S(1)}, u32[]{:S(2)}, u32[]{:S(2)}) %all-to-all-start.4) | async-done | bytes 786464 | tf_op jit(solution)/shard_map/all_to_all | solution.py:304
  325.1 3.5 all-to-all-start.5
  328.7 3.2 collective-permute-done.10.refs_7_
  331.9 9.1 %product.5 = f32[4,2,64,1024]{3,2,1,0:T(8,128)} custom-call(s32[1]{0:T(128)} %bitcast.refs_0_, f32[1,2,1024,1024]{3,2,1,0:T(8,128)} %refs_4_.5, f32[1,2,1024,1024]{3,2,1,0:T(8,128)} %refs_4_.5, f32[1,2,1024,1024]{3,2,1,0:T(8,128)} %refs_4_.5, f32[1,2,1024,1024]{3,2,1,0:T(8,128)} %refs_4_.5, f32[2,64,1024]{2,1,0:T(8,128)S(1)} %get-tuple-element.39.refs_10_.refs_5_, ...), custom_call_target="tpu_custom_call" | custom-call | flops 4294967296 | bytes 4194304 | tf_op jit(solution)/shard_map/product/pallas_call | solution.py:25
  346.2 3.3 all-to-all-done.5.refs_5_.refs_4_
  350.1 4.8 %collective-permute-done.16.refs_3_ = f32[2,2,48,256]{3,2,1,0:T(8,128)S(1)} collective-permute-done((f32[2,2,48,256]{3,2,1,0:T(8,128)S(1)}, f32[2,2,48,256]{3,2,1,0:T(8,128)S(1)}, u32[]{:S(2)}, u32[]{:S(2)}) %collective-permute-start.16) | collective-permute-done | bytes 196640 | tf_op jit(solution)/shard_map/ppermute | solution.py:310
  358.1 23.4 %all_to_all.51 = f32[8,2,48,256]{3,2,1,0:T(8,128)S(1)} all-to-all(f32[8,2,48,256]{3,2,1,0:T(8,128)S(1)} %bitcast.26), channel_id=1, replica_groups=mesh['ia'=8,'ka'=4] {'ia'}, dimensions={0} | all-to-all | bytes 1572864 | tf_op jit(solution)/shard_map/all_to_all | solution.py:304
  383.1 3.5 all-to-all-start.7
  394.1 3.2 collective-permute-done.20.refs_4_
  397.3 10.2 %all-to-all-done.7.refs_5_ = f32[8,2,48,256]{3,2,1,0:T(8,128)S(1)} async-done(((f32[8,2,48,256]{3,2,1,0:T(8,128)}), f32[8,2,48,256]{3,2,1,0:T(8,128)S(1)}, u32[]{:S(2)}, u32[]{:S(2)}) %all-to-all-start.7) | async-done | bytes 786464 | tf_op jit(solution)/shard_map/all_to_all | solution.py:304
  408.4 4.3 all-to-all-start.8
  412.7 15.3 %all-to-all-done.8 = f32[8,2,32,256]{3,2,1,0:T(8,128)} async-done(((f32[8,2,32,256]{3,2,1,0:T(8,128)}), f32[8,2,32,256]{3,2,1,0:T(8,128)}, u32[]{:S(2)}, u32[]{:S(2)}) %all-to-all-start.8) | async-done | bytes 524320 | tf_op jit(solution)/shard_map/all_to_all | solution.py:304
  431.6 17.8 %all_to_all.52.refs_6_ = f32[8,2,32,256]{3,2,1,0:T(8,128)S(1)} all-to-all(f32[8,2,32,256]{3,2,1,0:T(8,128)S(1)} %broadcast_select_fusion.2), channel_id=1, replica_groups=mesh['ia'=8,'ka'=4] {'ia'}, dimensions={0} | all-to-all | bytes 1048576 | tf_op jit(solution)/shard_map/all_to_all | solution.py:304
  (134 shorter events, 76.2 us)
Async XLA Ops:
  53.5 76.5 %all-to-all-start.1 = ((f32[8,96,1024]{2,1,0:T(8,128)}), f32[8,96,1024]{2,1,0:T(8,128)}, u32[]{:S(2)}, u32[]{:S(2)}) async-start(f32[8,96,1024]{2,1,0:T(8,128)} %bitcast.36), calls=%async_computation.1 | async-start | bytes 6291456 | tf_op jit(solution)/shard_map/all_to_all | solution.py:304
  60.3 31.6 %collective-permute-start = (f32[2,160,1024]{2,1,0:T(8,128)S(1)}, f32[2,160,1024]{2,1,0:T(8,128)S(1)}, u32[]{:S(2)}, u32[]{:S(2)}) collective-permute-start(f32[2,160,1024]{2,1,0:T(8,128)S(1)} %flip.5), channel_id=1, source_target_pairs={{0,1},{1,0},{2,3},{3,2},{4,5},{5,4},{6,7},{7,6},{8,9},{9,8},{10,11... | collective-permute-start | bytes 3932168 | tf_op jit(solution)/shard_map/ppermute | solution.py:310
  63.2 59.1 %collective-permute-start.1 = (f32[2,160,1024]{2,1,0:T(8,128)S(1)}, f32[2,160,1024]{2,1,0:T(8,128)S(1)}, u32[]{:S(2)}, u32[]{:S(2)}) collective-permute-start(f32[2,160,1024]{2,1,0:T(8,128)S(1)} %flip.6), channel_id=1, source_target_pairs={{0,2},{1,3},{2,0},{3,1},{4,6},{5,7},{6,4},{7,5},{8,10},{9,11},{10,... | collective-permute-start | bytes 3932168 | tf_op jit(solution)/shard_map/ppermute | solution.py:310
  65.8 56.5 %collective-permute-start.2 = (f32[2,160,1024]{2,1,0:T(8,128)S(1)}, f32[2,160,1024]{2,1,0:T(8,128)S(1)}, u32[]{:S(2)}, u32[]{:S(2)}) collective-permute-start(f32[2,160,1024]{2,1,0:T(8,128)S(1)} %flip.7), channel_id=1, source_target_pairs={{0,3},{1,2},{2,1},{3,0},{4,7},{5,6},{6,5},{7,4},{8,11},{9,10},{10,... | collective-permute-start | bytes 3932168 | tf_op jit(solution)/shard_map/ppermute | solution.py:310
  69.8 52.5 %copy-start.1 = (f32[2,160,1024]{2,1,0:T(8,128)}, f32[2,160,1024]{2,1,0:T(8,128)S(1)}, u32[]{:S(2)}) copy-start(f32[2,160,1024]{2,1,0:T(8,128)S(1)} %flip.4.refs_1_) | copy-start | bytes 3932164
  130.1 76.3 %all-to-all-start.2 = ((f32[8,96,1024]{2,1,0:T(8,128)}), f32[8,96,1024]{2,1,0:T(8,128)}, u32[]{:S(2)}, u32[]{:S(2)}) async-start(f32[8,96,1024]{2,1,0:T(8,128)} %bitcast.35), calls=%async_computation.2 | async-start | bytes 6291456 | tf_op jit(solution)/shard_map/all_to_all | solution.py:304
  134.8 109.9 %reduce-scatter.10.cloned.1.call-start = ((), (), s32[]{:S(2)}) async-start(), calls=%async_computation.13 | async-start | bytes 3932160
  142.5 20.4 %collective-permute-start.3 = (f32[2,96,1024]{2,1,0:T(8,128)S(1)}, f32[2,96,1024]{2,1,0:T(8,128)S(1)}, u32[]{:S(2)}, u32[]{:S(2)}) collective-permute-start(f32[2,96,1024]{2,1,0:T(8,128)S(1)} %get-tuple-element.31), channel_id=1, source_target_pairs={{0,1},{1,0},{2,3},{3,2},{4,5},{5,4},{6,7},{7,6},{8,9},{9,8},{10,11... | collective-permute-start | bytes 2359304 | tf_op jit(solution)/shard_map/ppermute | solution.py:310
  143.5 36.3 %collective-permute-start.4 = (f32[2,96,1024]{2,1,0:T(8,128)S(1)}, f32[2,96,1024]{2,1,0:T(8,128)S(1)}, u32[]{:S(2)}, u32[]{:S(2)}) collective-permute-start(f32[2,96,1024]{2,1,0:T(8,128)S(1)} %get-tuple-element.32), channel_id=1, source_target_pairs={{0,2},{1,3},{2,0},{3,1},{4,6},{5,7},{6,4},{7,5},{8,10},{9,11},{10,... | collective-permute-start | bytes 2359304 | tf_op jit(solution)/shard_map/ppermute | solution.py:310
  144.1 35.8 %collective-permute-start.5 = (f32[2,96,1024]{2,1,0:T(8,128)S(1)}, f32[2,96,1024]{2,1,0:T(8,128)S(1)}, u32[]{:S(2)}, u32[]{:S(2)}) collective-permute-start(f32[2,96,1024]{2,1,0:T(8,128)S(1)} %get-tuple-element.33), channel_id=1, source_target_pairs={{0,3},{1,2},{2,1},{3,0},{4,7},{5,6},{6,5},{7,4},{8,11},{9,10},{10,... | collective-permute-start | bytes 2359304 | tf_op jit(solution)/shard_map/ppermute | solution.py:310
  206.3 52.6 %all-to-all-start.3 = ((f32[8,64,1024]{2,1,0:T(8,128)}), f32[8,64,1024]{2,1,0:T(8,128)S(1)}, u32[]{:S(2)}, u32[]{:S(2)}) async-start(f32[8,64,1024]{2,1,0:T(8,128)} %bitcast.25), calls=%async_computation.3 | async-start | bytes 4194304 | tf_op jit(solution)/shard_map/all_to_all | solution.py:304
  209.9 131.1 %reduce-scatter.12.cloned.1.call-start = ((), (), s32[]{:S(2)}) async-start(), calls=%async_computation.14 | async-start | bytes 3932160
  213.5 48.3 %collective-permute-start.6 = (f32[2,96,1024]{2,1,0:T(8,128)}, f32[2,96,1024]{2,1,0:T(8,128)}, u32[]{:S(2)}, u32[]{:S(2)}) collective-permute-start(f32[2,96,1024]{2,1,0:T(8,128)} %get-tuple-element.35), channel_id=1, source_target_pairs={{0,1},{1,0},{2,3},{3,2},{4,5},{5,4},{6,7},{7,6},{8,9},{9,8},{10,11... | collective-permute-start | bytes 2359304 | tf_op jit(solution)/shard_map/ppermute | solution.py:310
  214.6 47.2 %collective-permute-start.7 = (f32[2,96,1024]{2,1,0:T(8,128)}, f32[2,96,1024]{2,1,0:T(8,128)}, u32[]{:S(2)}, u32[]{:S(2)}) collective-permute-start(f32[2,96,1024]{2,1,0:T(8,128)} %get-tuple-element.36), channel_id=1, source_target_pairs={{0,2},{1,3},{2,0},{3,1},{4,6},{5,7},{6,4},{7,5},{8,10},{9,11},{10,... | collective-permute-start | bytes 2359304 | tf_op jit(solution)/shard_map/ppermute | solution.py:310
  215.1 46.6 %collective-permute-start.8 = (f32[2,96,1024]{2,1,0:T(8,128)}, f32[2,96,1024]{2,1,0:T(8,128)}, u32[]{:S(2)}, u32[]{:S(2)}) collective-permute-start(f32[2,96,1024]{2,1,0:T(8,128)} %get-tuple-element.37), channel_id=1, source_target_pairs={{0,3},{1,2},{2,1},{3,0},{4,7},{5,6},{6,5},{7,4},{8,11},{9,10},{10,... | collective-permute-start | bytes 2359304 | tf_op jit(solution)/shard_map/ppermute | solution.py:310
  274.8 7.6 %collective-permute-start.12 = (f32[2,2,48,256]{3,2,1,0:T(8,128)S(1)}, f32[2,2,48,256]{3,2,1,0:T(8,128)S(1)}, u32[]{:S(2)}, u32[]{:S(2)}) collective-permute-start(f32[2,2,48,256]{3,2,1,0:T(8,128)S(1)} %copy-done.27), channel_id=1, source_target_pairs={{0,1},{1,0},{2,3},{3,2},{4,5},{5,4},{6,7},{7,6},{8,9},{9,8},{10,11... | collective-permute-start | bytes 589832 | tf_op jit(solution)/shard_map/ppermute | solution.py:310
  275.8 19.2 %collective-permute-start.13 = (f32[2,2,48,256]{3,2,1,0:T(8,128)S(1)}, f32[2,2,48,256]{3,2,1,0:T(8,128)S(1)}, u32[]{:S(2)}, u32[]{:S(2)}) collective-permute-start(f32[2,2,48,256]{3,2,1,0:T(8,128)S(1)} %copy-done.25), channel_id=1, source_target_pairs={{0,2},{1,3},{2,0},{3,1},{4,6},{5,7},{6,4},{7,5},{8,10},{9,11},{10,... | collective-permute-start | bytes 589832 | tf_op jit(solution)/shard_map/ppermute | solution.py:310
  282.5 12.5 %collective-permute-start.14 = (f32[2,2,48,256]{3,2,1,0:T(8,128)S(1)}, f32[2,2,48,256]{3,2,1,0:T(8,128)S(1)}, u32[]{:S(2)}, u32[]{:S(2)}) collective-permute-start(f32[2,2,48,256]{3,2,1,0:T(8,128)S(1)} %copy-done.23), channel_id=1, source_target_pairs={{0,3},{1,2},{2,1},{3,0},{4,7},{5,6},{6,5},{7,4},{8,11},{9,10},{10,... | collective-permute-start | bytes 589832 | tf_op jit(solution)/shard_map/ppermute | solution.py:310
  295.9 25.6 %all-to-all-start.4 = ((f32[8,2,48,256]{3,2,1,0:T(8,128)}), f32[8,2,48,256]{3,2,1,0:T(8,128)S(1)}, u32[]{:S(2)}, u32[]{:S(2)}) async-start(f32[8,2,48,256]{3,2,1,0:T(8,128)} %bitcast.12), calls=%async_computation.4 | async-start | bytes 1572864 | tf_op jit(solution)/shard_map/all_to_all | solution.py:304
  301.6 30.3 %collective-permute-start.10 = (f32[2,64,1024]{2,1,0:T(8,128)}, f32[2,64,1024]{2,1,0:T(8,128)S(1)}, u32[]{:S(2)}, u32[]{:S(2)}) collective-permute-start(f32[2,64,1024]{2,1,0:T(8,128)} %get-tuple-element.41), channel_id=1, source_target_pairs={{0,2},{1,3},{2,0},{3,1},{4,6},{5,7},{6,4},{7,5},{8,10},{9,11},{10,... | collective-permute-start | bytes 1572872 | tf_op jit(solution)/shard_map/ppermute | solution.py:310
  303.1 28.8 %collective-permute-start.11 = (f32[2,64,1024]{2,1,0:T(8,128)}, f32[2,64,1024]{2,1,0:T(8,128)S(1)}, u32[]{:S(2)}, u32[]{:S(2)}) collective-permute-start(f32[2,64,1024]{2,1,0:T(8,128)} %get-tuple-element.42), channel_id=1, source_target_pairs={{0,3},{1,2},{2,1},{3,0},{4,7},{5,6},{6,5},{7,4},{8,11},{9,10},{10,... | collective-permute-start | bytes 1572872 | tf_op jit(solution)/shard_map/ppermute | solution.py:310
  304.2 27.7 %collective-permute-start.9 = (f32[2,64,1024]{2,1,0:T(8,128)S(1)}, f32[2,64,1024]{2,1,0:T(8,128)S(1)}, u32[]{:S(2)}, u32[]{:S(2)}) collective-permute-start(f32[2,64,1024]{2,1,0:T(8,128)S(1)} %copy-done.21), channel_id=1, source_target_pairs={{0,1},{1,0},{2,3},{3,2},{4,5},{5,4},{6,7},{7,6},{8,9},{9,8},{10,11... | collective-permute-start | bytes 1572872 | tf_op jit(solution)/shard_map/ppermute | solution.py:310
  325.1 24.4 %all-to-all-start.5 = ((f32[8,2,48,256]{3,2,1,0:T(8,128)}), f32[8,2,48,256]{3,2,1,0:T(8,128)S(1)}, u32[]{:S(2)}, u32[]{:S(2)}) async-start(f32[8,2,48,256]{3,2,1,0:T(8,128)} %bitcast.37), calls=%async_computation.5 | async-start | bytes 1572864 | tf_op jit(solution)/shard_map/all_to_all | solution.py:304
  328.7 58.0 %reduce-scatter.14.cloned.1.call-start = ((), (), s32[]{:S(2)}) async-start(), calls=%async_computation.15 | async-start | bytes 2621440
  342.2 7.9 %collective-permute-start.15 = (f32[2,2,48,256]{3,2,1,0:T(8,128)S(1)}, f32[2,2,48,256]{3,2,1,0:T(8,128)S(1)}, u32[]{:S(2)}, u32[]{:S(2)}) collective-permute-start(f32[2,2,48,256]{3,2,1,0:T(8,128)S(1)} %get-tuple-element.47), channel_id=1, source_target_pairs={{0,1},{1,0},{2,3},{3,2},{4,5},{5,4},{6,7},{7,6},{8,9},{9,8},{10,11... | collective-permute-start | bytes 589832 | tf_op jit(solution)/shard_map/ppermute | solution.py:310
  343.3 11.6 %collective-permute-start.16 = (f32[2,2,48,256]{3,2,1,0:T(8,128)S(1)}, f32[2,2,48,256]{3,2,1,0:T(8,128)S(1)}, u32[]{:S(2)}, u32[]{:S(2)}) collective-permute-start(f32[2,2,48,256]{3,2,1,0:T(8,128)S(1)} %get-tuple-element.48), channel_id=1, source_target_pairs={{0,2},{1,3},{2,0},{3,1},{4,6},{5,7},{6,4},{7,5},{8,10},{9,11},{10,... | collective-permute-start | bytes 589832 | tf_op jit(solution)/shard_map/ppermute | solution.py:310
  344.8 13.2 %collective-permute-start.17 = (f32[2,2,48,256]{3,2,1,0:T(8,128)S(1)}, f32[2,2,48,256]{3,2,1,0:T(8,128)S(1)}, u32[]{:S(2)}, u32[]{:S(2)}) collective-permute-start(f32[2,2,48,256]{3,2,1,0:T(8,128)S(1)} %get-tuple-element.49), channel_id=1, source_target_pairs={{0,3},{1,2},{2,1},{3,0},{4,7},{5,6},{6,5},{7,4},{8,11},{9,10},{10,... | collective-permute-start | bytes 589832 | tf_op jit(solution)/shard_map/ppermute | solution.py:310
  383.1 24.4 %all-to-all-start.7 = ((f32[8,2,48,256]{3,2,1,0:T(8,128)}), f32[8,2,48,256]{3,2,1,0:T(8,128)S(1)}, u32[]{:S(2)}, u32[]{:S(2)}) async-start(f32[8,2,48,256]{3,2,1,0:T(8,128)} %bitcast.17), calls=%async_computation.7 | async-start | bytes 1572864 | tf_op jit(solution)/shard_map/all_to_all | solution.py:304
  387.7 6.4 %collective-permute-start.18 = (f32[2,2,32,256]{3,2,1,0:T(8,128)S(1)}, f32[2,2,32,256]{3,2,1,0:T(8,128)S(1)}, u32[]{:S(2)}, u32[]{:S(2)}) collective-permute-start(f32[2,2,32,256]{3,2,1,0:T(8,128)S(1)} %get-tuple-element.51), channel_id=1, source_target_pairs={{0,1},{1,0},{2,3},{3,2},{4,5},{5,4},{6,7},{7,6},{8,9},{9,8},{10,11... | collective-permute-start | bytes 393224 | tf_op jit(solution)/shard_map/ppermute | solution.py:310
  387.8 6.3 %collective-permute-start.19 = (f32[2,2,32,256]{3,2,1,0:T(8,128)S(1)}, f32[2,2,32,256]{3,2,1,0:T(8,128)S(1)}, u32[]{:S(2)}, u32[]{:S(2)}) collective-permute-start(f32[2,2,32,256]{3,2,1,0:T(8,128)S(1)} %get-tuple-element.52), channel_id=1, source_target_pairs={{0,2},{1,3},{2,0},{3,1},{4,6},{5,7},{6,4},{7,5},{8,10},{9,11},{10,... | collective-permute-start | bytes 393224 | tf_op jit(solution)/shard_map/ppermute | solution.py:310
  389.7 7.6 %collective-permute-start.20 = (f32[2,2,32,256]{3,2,1,0:T(8,128)S(1)}, f32[2,2,32,256]{3,2,1,0:T(8,128)S(1)}, u32[]{:S(2)}, u32[]{:S(2)}) collective-permute-start(f32[2,2,32,256]{3,2,1,0:T(8,128)S(1)} %get-tuple-element.53), channel_id=1, source_target_pairs={{0,3},{1,2},{2,1},{3,0},{4,7},{5,6},{6,5},{7,4},{8,11},{9,10},{10,... | collective-permute-start | bytes 393224 | tf_op jit(solution)/shard_map/ppermute | solution.py:310
  408.4 19.6 %all-to-all-start.8 = ((f32[8,2,32,256]{3,2,1,0:T(8,128)}), f32[8,2,32,256]{3,2,1,0:T(8,128)}, u32[]{:S(2)}, u32[]{:S(2)}) async-start(f32[8,2,32,256]{3,2,1,0:T(8,128)} %bitcast.33), calls=%async_computation.8 | async-start | bytes 1048576 | tf_op jit(solution)/shard_map/all_to_all | solution.py:304
  (28 other events, 184.6 us)
Sparse Core Ops, SparseCore 0:
  191.4 53.2 reduce-scatter.9
  274.1 66.4 reduce-scatter.11
  343.6 36.6 reduce-scatter.13
